TPU v7x, 32 devices: a whole 2x2x4 slice. The times are simulated.
32 devices in a mesh: rows: 16 (over z, x, core), pair: 2 (over y).
Axes of the slice: x: 2, y: 2, z: 4, core: 2. Of those that a mesh axis runs over, the one named last changes fastest.
Arguments:
- tokens: bfloat16 [16, 1024, 1024], P('rows', 'pair'), may hold values from -6 to 6
- cotangent: bfloat16 [16, 1024, 1024], P('rows', 'pair'), may hold values from -6 to 6
- gains: bfloat16 [1024, 2], P('rows', 'pair'), may hold values from 0.099609375 to 1.8984375
- w_qkv: bfloat16 [1024, 3072], P('rows', 'pair'), may hold values from -0.1875 to 0.1875
- w_out: bfloat16 [1024, 1024], P('rows', 'pair'), may hold values from -3 to 3
- w_up: bfloat16 [1024, 4096], P('rows', 'pair'), may hold values from -0.1875 to 0.1875
- w_down: bfloat16 [4096, 1024], P('rows', 'pair'), may hold values from -0.09375 to 0.09375
- phone_len: int32 [16, 2], P('rows'), may hold values from 20 to 400, as said below
- prompt_len: int32 [16, 2], P('rows'), may hold values from 1 to 471, as said below
- target_len: int32 [16, 2], P('rows'), may hold values from 1 to 511, as said below
Outputs:
- mixed: bfloat16 [16, 1024, 1024], P('rows', 'pair')
- grad_tokens: float32 [16, 1024, 1024], P('rows', 'pair')
- grad_gains: float32 [1024, 2], P('rows', 'pair')
- grad_qkv: float32 [1024, 3072], P('rows', 'pair')
- grad_out: float32 [1024, 1024], P('rows', 'pair')
- grad_up: float32 [1024, 4096], P('rows', 'pair')
- grad_down: float32 [4096, 1024], P('rows', 'pair')
Inputs may be any that keep to these rules, and one draw needn't show every extreme that they name: `phone_len`: some row, drawn from the seed, has a segment of exactly 400 phonemes, and some other row has 20 in every segment; a row's phoneme and prompt lengths sum to 512. `prompt_len`: A row's phoneme and prompt lengths sum to 512. `target_len`: A row's target lengths sum to 512.
All inputs are finite; a program needn't handle non-finite values.
Results may differ from a plain program's by a relative error of at most 0.014.
Values may be sent and summed in bfloat16 or wider, within the bound.
No kernel may reach another device: no remote copies, remote signals or barrier semaphores. Data moves between devices by JAX's collectives and lax.ppermute only.
A program may use at most 192 MiB of HBM per device.

v0:
```python
import jax
import jax.numpy as jnp
from jax import lax
from jax.sharding import PartitionSpec as P

HEADS = 16
HEAD_DIM = 64


epsilon = 1e-05


def passed_along(value, axis, steps):
    count = lax.axis_size(axis)
    leading, last = (max(0, -steps), min(count, count - steps))
    return lax.ppermute(value, axis, [(source, source + steps) for source in range(leading, last)])


def slot_layout(side_index, phones, prompts, targets, slot_count):
    lengths = jnp.where(side_index == 0, phones + prompts, targets)
    seg_ends = jnp.cumsum(lengths)
    starts = seg_ends - lengths
    places = jnp.arange(slot_count, dtype=jnp.int32)
    segment = jnp.sum((places[:, None] >= seg_ends[None, :]).astype(jnp.int32), axis=1)
    onehot = (segment[:, None] == jnp.arange(lengths.shape[0], dtype=jnp.int32)[None, :]).astype(
        jnp.int32
    )
    within = places - jnp.sum(onehot * starts[None, :], axis=1)
    phone_here = jnp.sum(onehot * phones[None, :], axis=1)
    is_phone = jnp.logical_and(side_index == 0, within < phone_here)
    ordering = places + side_index * slot_count
    return (segment, is_phone, ordering)


def permitted(query_side, key_side):
    query_seg, query_phone, query_order = query_side
    key_seg, key_phone, key_order = key_side
    same_seg = query_seg[:, None] == key_seg[None, :]
    earlier = key_order[None, :] <= query_order[:, None]
    return same_seg & (key_phone[None, :] | jnp.logical_not(query_phone)[:, None] & earlier)


def normalize(values, gain_row):
    centred = values - jnp.mean(values, axis=-1, keepdims=True)
    spread = jnp.mean(centred * centred, axis=-1, keepdims=True)
    return centred * lax.rsqrt(spread + epsilon) * gain_row


def exact_gelu(values):
    return jax.nn.gelu(values, approximate=False)


def softmax_rows(query_piece, key_piece, allowed):
    scores = jnp.einsum(
        "qhd,khd->hqk", query_piece, key_piece, preferred_element_type=jnp.float32
    ) * HEAD_DIM ** (-0.5)
    scores = jnp.where(allowed[None], scores, -1e30)
    row_max = jnp.max(scores, axis=-1, keepdims=True)
    exponents = jnp.exp(scores - row_max)
    return exponents / jnp.sum(exponents, axis=-1, keepdims=True)


def shards(tokens, cotangent, gains, w_qkv, w_out, w_up, w_down, phone_len, prompt_len, target_len):
    slot_count = tokens.shape[1]
    model_width = tokens.shape[2]
    inputs = tokens[0].astype(jnp.float32)
    side_index = lax.axis_index("pair")
    paired = (
        lax.all_gather(gains, "pair", axis=1, tiled=True),
        lax.all_gather(w_qkv, "pair", axis=1, tiled=True),
        lax.all_gather(w_out, "pair", axis=1, tiled=True),
        lax.all_gather(w_up, "pair", axis=1, tiled=True),
        lax.all_gather(w_down, "pair", axis=1, tiled=True),
    )
    gain_all, qkv_all, out_all, up_all, down_all = (
        lax.all_gather(paired[0], "rows", axis=0, tiled=True),
        lax.all_gather(paired[1], "rows", axis=0, tiled=True),
        lax.all_gather(paired[2], "rows", axis=0, tiled=True),
        lax.all_gather(paired[3], "rows", axis=0, tiled=True),
        lax.all_gather(paired[4], "rows", axis=0, tiled=True),
    )
    gain_first = gain_all[:, 0].astype(jnp.float32)
    gain_second = gain_all[:, 1].astype(jnp.float32)
    phones = phone_len[0]
    prompts = prompt_len[0]
    targets = target_len[0]
    own_layout = slot_layout(side_index, phones, prompts, targets, slot_count)
    far_layout = slot_layout(0, phones, prompts, targets, slot_count)
    key_layout = tuple(
        (
            jnp.concatenate([far_part, own_part])
            for far_part, own_part in zip(far_layout, own_layout)
        )
    )
    far_live = jnp.concatenate(
        [jnp.full((slot_count,), side_index == 1), jnp.ones((slot_count,), dtype=bool)]
    )
    normed_in, norm_first_back = jax.vjp(normalize, inputs, gain_first)
    normed_low = normed_in.astype(jnp.bfloat16)
    projected = jnp.dot(normed_low, qkv_all, preferred_element_type=jnp.float32).astype(
        jnp.bfloat16
    )
    queries = projected[:, :model_width]
    near_pairs = projected[:, model_width:]
    far_pairs = passed_along(near_pairs, "pair", 1)
    key_value = jnp.concatenate([far_pairs, near_pairs], axis=0)
    block_rows = min(512, slot_count)
    per_group = min(4, HEADS)
    group_width = per_group * HEAD_DIM
    groups = HEADS // per_group
    steps_total = slot_count // block_rows * groups
    key_count = 2 * slot_count

    def piece_of(item_index):
        row_start = item_index // groups * block_rows
        col_start = item_index % groups * group_width
        query_piece = lax.dynamic_slice(
            queries, (row_start, col_start), (block_rows, group_width)
        ).reshape(block_rows, per_group, HEAD_DIM)
        key_piece = lax.dynamic_slice(key_value, (0, col_start), (key_count, group_width)).reshape(
            key_count, per_group, HEAD_DIM
        )
        value_piece = lax.dynamic_slice(
            key_value, (0, model_width + col_start), (key_count, group_width)
        ).reshape(key_count, per_group, HEAD_DIM)
        query_layout = tuple((member for member in own_layout))
        allowed = permitted(query_layout, key_layout) & far_live[None, :]
        attn_probs = softmax_rows(query_piece, key_piece, allowed)
        return (row_start, col_start, query_piece, key_piece, value_piece, attn_probs)

    def forward_step(item_index, attended):
        row_start, col_start, query_piece, key_piece, value_piece, attn_probs = piece_of(item_index)
        head_mix = jnp.einsum(
            "hqk,khd->qhd",
            attn_probs.astype(jnp.bfloat16),
            value_piece,
            preferred_element_type=jnp.float32,
        )
        return lax.dynamic_update_slice(
            attended, head_mix.reshape(block_rows, group_width), (row_start, col_start)
        )

    attended = lax.fori_loop(
        0, steps_total, forward_step, jnp.zeros((slot_count, model_width), jnp.float32)
    )
    attended_low = attended.astype(jnp.bfloat16)
    middle = inputs + jnp.dot(attended_low, out_all, preferred_element_type=jnp.float32)
    normed_mid, norm_second_back = jax.vjp(normalize, middle, gain_second)
    normed_mid_low = normed_mid.astype(jnp.bfloat16)
    pre_act = jnp.dot(normed_mid_low, up_all, preferred_element_type=jnp.float32)
    activated, gelu_back = jax.vjp(exact_gelu, pre_act)
    activated_low = activated.astype(jnp.bfloat16)
    result = middle + jnp.dot(activated_low, down_all, preferred_element_type=jnp.float32)
    mixed_out = result.astype(jnp.bfloat16)[None]
    paired_again = (
        lax.all_gather(w_qkv, "pair", axis=1, tiled=True),
        lax.all_gather(w_out, "pair", axis=1, tiled=True),
        lax.all_gather(w_up, "pair", axis=1, tiled=True),
        lax.all_gather(w_down, "pair", axis=1, tiled=True),
    )
    qkv_back, out_back, up_back, down_back = (
        lax.all_gather(paired_again[0], "rows", axis=0, tiled=True),
        lax.all_gather(paired_again[1], "rows", axis=0, tiled=True),
        lax.all_gather(paired_again[2], "rows", axis=0, tiled=True),
        lax.all_gather(paired_again[3], "rows", axis=0, tiled=True),
    )
    grad_result = cotangent[0]
    grad_down = jnp.dot(activated_low.T, grad_result, preferred_element_type=jnp.float32)
    grad_act = jnp.dot(grad_result, down_back.T, preferred_element_type=jnp.float32)
    grad_pre = gelu_back(grad_act)[0].astype(jnp.bfloat16)
    grad_up = jnp.dot(normed_mid_low.T, grad_pre, preferred_element_type=jnp.float32)
    grad_normed_mid = jnp.dot(grad_pre, up_back.T, preferred_element_type=jnp.float32)
    grad_middle_norm, grad_gain_second = norm_second_back(grad_normed_mid)
    grad_middle = grad_result.astype(jnp.float32) + grad_middle_norm
    grad_branch = grad_middle.astype(jnp.bfloat16)
    grad_out = jnp.dot(attended_low.T, grad_branch, preferred_element_type=jnp.float32)
    grad_attended = jnp.dot(grad_branch, out_back.T, preferred_element_type=jnp.float32).astype(
        jnp.bfloat16
    )

    def backward_step(item_index, running):
        grad_queries, grad_pairs = running
        row_start, col_start, query_piece, key_piece, value_piece, attn_probs = piece_of(item_index)
        grad_piece = lax.dynamic_slice(
            grad_attended, (row_start, col_start), (block_rows, group_width)
        ).reshape(block_rows, per_group, HEAD_DIM)
        grad_probs = jnp.einsum(
            "qhd,khd->hqk", grad_piece, value_piece, preferred_element_type=jnp.float32
        )
        centre = jnp.sum(grad_probs * attn_probs, axis=-1, keepdims=True)
        grad_scores = (attn_probs * (grad_probs - centre)).astype(jnp.bfloat16)
        score_scale = HEAD_DIM ** (-0.5)
        query_grad = (
            jnp.einsum("hqk,khd->qhd", grad_scores, key_piece, preferred_element_type=jnp.float32)
            * score_scale
        )
        key_grad = (
            jnp.einsum("hqk,qhd->khd", grad_scores, query_piece, preferred_element_type=jnp.float32)
            * score_scale
        )
        value_grad = jnp.einsum(
            "hqk,qhd->khd",
            attn_probs.astype(jnp.bfloat16),
            grad_piece,
            preferred_element_type=jnp.float32,
        )
        grad_queries = lax.dynamic_update_slice(
            grad_queries, query_grad.reshape(block_rows, group_width), (row_start, col_start)
        )
        key_old = lax.dynamic_slice(grad_pairs, (0, col_start), (key_count, group_width))
        grad_pairs = lax.dynamic_update_slice(
            grad_pairs, key_old + key_grad.reshape(key_count, group_width), (0, col_start)
        )
        value_old = lax.dynamic_slice(
            grad_pairs, (0, model_width + col_start), (key_count, group_width)
        )
        grad_pairs = lax.dynamic_update_slice(
            grad_pairs,
            value_old + value_grad.reshape(key_count, group_width),
            (0, model_width + col_start),
        )
        return (grad_queries, grad_pairs)

    start_state = (
        jnp.zeros((slot_count, model_width), jnp.float32),
        jnp.zeros((key_count, 2 * model_width), jnp.float32),
    )
    grad_queries, grad_pairs = lax.fori_loop(0, steps_total, backward_step, start_state)
    returned = passed_along(grad_pairs[:slot_count].astype(jnp.bfloat16), "pair", -1).astype(
        jnp.float32
    )
    grad_near = (grad_pairs[slot_count:] + returned).astype(jnp.bfloat16)
    grad_projected = jnp.concatenate([grad_queries.astype(jnp.bfloat16), grad_near], axis=1)
    grad_qkv = jnp.dot(normed_low.T, grad_projected, preferred_element_type=jnp.float32)
    grad_normed_in = jnp.dot(grad_projected, qkv_back.T, preferred_element_type=jnp.float32)
    grad_inputs_norm, grad_gain_first = norm_first_back(grad_normed_in)
    grad_tokens = (grad_middle + grad_inputs_norm)[None]
    grad_gains = jnp.stack([grad_gain_first, grad_gain_second], axis=1)
    strips = (
        lax.psum_scatter(grad_gains, "rows", scatter_dimension=0, tiled=True),
        lax.psum_scatter(grad_qkv, "rows", scatter_dimension=0, tiled=True),
        lax.psum_scatter(grad_out, "rows", scatter_dimension=0, tiled=True),
        lax.psum_scatter(grad_up, "rows", scatter_dimension=0, tiled=True),
        lax.psum_scatter(grad_down, "rows", scatter_dimension=0, tiled=True),
    )
    owned = (
        lax.psum_scatter(
            strips[0].astype(jnp.bfloat16), "pair", scatter_dimension=1, tiled=True
        ).astype(jnp.float32),
        lax.psum_scatter(
            strips[1].astype(jnp.bfloat16), "pair", scatter_dimension=1, tiled=True
        ).astype(jnp.float32),
        lax.psum_scatter(
            strips[2].astype(jnp.bfloat16), "pair", scatter_dimension=1, tiled=True
        ).astype(jnp.float32),
        lax.psum_scatter(
            strips[3].astype(jnp.bfloat16), "pair", scatter_dimension=1, tiled=True
        ).astype(jnp.float32),
        lax.psum_scatter(
            strips[4].astype(jnp.bfloat16), "pair", scatter_dimension=1, tiled=True
        ).astype(jnp.float32),
    )
    return (mixed_out, grad_tokens, owned[0], owned[1], owned[2], owned[3], owned[4])


def solution(mesh):
    return jax.shard_map(
        shards,
        mesh=mesh,
        in_specs=(
            P("rows", "pair", None),
            P("rows", "pair", None),
            P("rows", "pair"),
            P("rows", "pair"),
            P("rows", "pair"),
            P("rows", "pair"),
            P("rows", "pair"),
            P("rows", None),
            P("rows", None),
            P("rows", None),
        ),
        out_specs=(
            P("rows", "pair", None),
            P("rows", "pair", None),
            P("rows", "pair"),
            P("rows", "pair"),
            P("rows", "pair"),
            P("rows", "pair"),
            P("rows", "pair"),
        ),
        check_vma=False,
    )
```

profile of v0, /device:TPU:8, one launch (start us, length us, event | category | flops | bytes accessed | tf_op | source)
XLA Modules:
  0.0 1113.4 jit_solution(6771182337995517362)
XLA Ops:
  7.2 9.0 all_gather.40
  16.3 5.3 all_gather.42
  21.6 9.0 all_gather.44
  30.7 4.4 all-gather
  35.1 18.7 %all-gather.1 = bf16[16,64,2]{1,2,0:T(2,128)(2,1)S(1)} all-gather(bf16[1,64,2]{1,2,0:T(2,128)(2,1)S(1)} %bitcast.208), channel_id=1, replica_groups=mesh['rows'=16,'pair'=2] {'rows'}, dimensions={0}, use_global_device_ids=true | all-gather | bytes 4352 | tf_op jit(solution)/shard_map/all_gather | solution.py:76
  57.6 20.9 %all-gather.7.cloned.1.call-done = bf16[1024,3072]{1,0:T(8,128)(2,1)} async-done(((bf16[64,3072]{1,0:T(8,128)(2,1)}), bf16[1024,3072]{1,0:T(8,128)(2,1)}) %all-gather.7.cloned.1.call-update) | async-done | bytes 6291472 | tf_op jit(solution)/shard_map/all_gather | solution.py:77
  78.5 6.6 convolution_convert_fusion
  87.0 4.7 collective-permute-start
  91.7 49.6 %all_gather.46 = bf16[256,1024]{1,0:T(8,128)(2,1)} all-gather(bf16[256,512]{1,0:T(8,128)(2,1)S(1)} %copy-done.16), channel_id=1, replica_groups=mesh['rows'=16,'pair'=2] {'pair'}, dimensions={1}, use_global_device_ids=true | all-gather | bytes 786432 | tf_op jit(solution)/shard_map/all_gather | solution.py:73
  149.1 6.4 copy.35
  156.6 62.3 %while.34 = (s32[]{:T(128)}, bf16[512,1024]{0,1:T(8,128)(2,1)}, bf16[1024,2048]{0,1:T(8,128)(2,1)}, s32[512]{0:T(512)S(1)}, s32[1024]{0:T(1024)S(1)}, /*index=5*...) while((s32[]{:T(128)}, bf16[512,1024]{0,1:T(8,128)(2,1)}, ...), condition=%wide.region_13.14_spmd.clone, body=%wide.region_10.13_spmd.clone.sunk | while | flops 552601088 | bytes 22579060 | solution.py:143
  161.3 5.3 fusion.129
  166.6 4.8 fusion.130
  176.8 5.3 fusion.129
  182.1 4.8 fusion.130
  192.4 5.3 fusion.129
  197.7 4.8 fusion.130
  208.0 5.3 fusion.129
  213.3 4.9 fusion.130
  222.6 27.9 %multiply_convert_fusion.1 = (bf16[512,4096]{1,0:T(8,128)(2,1)}, f32[512,4096]{1,0:T(8,128)}, f32[512,4096]{1,0:T(8,128)}) fusion(bf16[1024,4096]{1,0:T(8,128)(2,1)} %all-gather.11.cloned.1.call-done, f32[512,1024]{1,0:T(8,128)S(1)} %get-tuple-element.820, f32[1024]{0:T(1024)S(1)} %bitcast.199, f32[512]{0:T(512)S(1)} %fusion.60, ...), kind=kOutput, calls=%fused_computation.51 | convolution fusion | flops 4433379328 | bytes 31465472 | tf_op jit(solution)/shard_map/dot_general | solution.py:150
  250.4 20.6 %all-gather.13.cloned.1.call-done = bf16[4096,1024]{1,0:T(8,128)(2,1)} async-done(((bf16[256,1024]{1,0:T(8,128)(2,1)}), bf16[4096,1024]{1,0:T(8,128)(2,1)}) %all-gather.13.cloned.1.call-update) | async-done | bytes 8388624 | tf_op jit(solution)/shard_map/all_gather | solution.py:80
  271.0 14.5 %add_convert_fusion = bf16[512,4096]{1,0:T(8,128)(2,1)} fusion(f32[512,4096]{1,0:T(8,128)} %get-tuple-element.800, f32[512,4096]{1,0:T(8,128)} %get-tuple-element.821, bf16[4096,1024]{1,0:T(8,128)(2,1)} %all-gather.13.cloned.1.call-done, bf16[1,512,1024]{2,1,0:T(8,128)(2,1)S(1)} %copy-done.8), kind=kOutput, calls=%fused_computation.50 | convolution fusion | flops 4324327424 | bytes 30408704 | tf_op jit(solution)/shard_map/dot_general | solution.py:169
  285.5 7.6 multiply_reduce_fusion.1
  303.5 4.4 broadcast_in_dim.170
  307.8 112.3 %while.35 = (s32[]{:T(128)}, bf16[512,1024]{0,1:T(8,128)(2,1)}, f32[1024,2048]{0,1:T(8,128)}, bf16[1024,2048]{0,1:T(8,128)(2,1)}, s32[512]{0:T(512)S(1)}, /*inde...) while((s32[]{:T(128)}, bf16[512,1024]{0,1:T(8,128)(2,1)}, ...), condition=%wide.region_22.23_spmd.clone, body=%wide.region_18.22_spmd.clone.sunk | while | flops 1373634048 | bytes 104662968 | solution.py:228
  312.5 5.3 fusion.141
  318.0 4.5 multiply_reduce_fusion.5
  340.6 5.3 fusion.141
  346.1 4.4 multiply_reduce_fusion.5
  368.8 5.3 fusion.141
  374.3 4.4 multiply_reduce_fusion.5
  396.8 5.3 fusion.141
  402.3 4.4 multiply_reduce_fusion.5
  424.3 48.2 %collective-permute-done.1 = bf16[512,2048]{0,1:T(8,128)(2,1)S(1)} collective-permute-done((bf16[512,2048]{0,1:T(8,128)(2,1)S(1)}, bf16[512,2048]{0,1:T(8,128)(2,1)S(1)}, u32[]{:S(2)}, u32[]{:S(2)}) %collective-permute-start.1) | collective-permute-done | bytes 2097184 | tf_op jit(solution)/shard_map/ppermute | solution.py:16
  476.9 8.0 fusion.43
  486.5 12.6 %fusion.69 = f32[1024,4096]{1,0:T(8,128)} fusion(bf16[512,4096]{1,0:T(8,128)(2,1)} %add_convert_fusion, f32[512,1024]{1,0:T(8,128)S(1)} %copy-done.5, f32[1024]{0:T(1024)S(1)} %bitcast.202, f32[512]{0:T(512)S(1)} %copy-done.32, f32[512]{0:T(512)S(1)} %copy-done.28), kind=kOutput, calls=%fused_computation.147 | convolution fusion | flops 4297064448 | bytes 23076864 | tf_op jit(solution)/shard_map/dot_general | solution.py:171
  499.2 13.9 %fusion.47 = f32[4096,1024]{1,0:T(8,128)} fusion(bf16[512,4096]{1,0:T(8,128)(2,1)} %get-tuple-element.799, bf16[1,512,1024]{2,1,0:T(8,128)(2,1)} %param.15), kind=kOutput, calls=%fused_computation.98 | convolution fusion | flops 4294967296 | bytes 22020096 | tf_op jit(solution)/shard_map/dot_general | solution.py:168
  513.5 6.8 fusion.42
  525.4 92.6 %reduce-scatter.12.cloned.1.call-done = f32[64,3072]{1,0:T(8,128)} async-done(((f32[1024,3072]{1,0:T(8,128)}), f32[64,3072]{1,0:T(8,128)}) %reduce-scatter.12.cloned.1.call-update) | async-done | bytes 786448 | tf_op jit(solution)/shard_map/reduce_scatter | solution.py:241
  620.0 179.8 %reduce-scatter.20.cloned.1.call-done = f32[64,4096]{1,0:T(8,128)} async-done(((f32[1024,4096]{1,0:T(8,128)}), f32[64,4096]{1,0:T(8,128)}) %reduce-scatter.20.cloned.1.call-update) | async-done | bytes 1048592 | tf_op jit(solution)/shard_map/reduce_scatter | solution.py:243
  802.5 179.5 %reduce-scatter.24.cloned.1.call-done = f32[256,1024]{1,0:T(8,128)} async-done(((f32[4096,1024]{1,0:T(8,128)}), f32[256,1024]{1,0:T(8,128)}) %reduce-scatter.24.cloned.1.call-update) | async-done | bytes 1048592 | tf_op jit(solution)/shard_map/reduce_scatter | solution.py:244
  984.2 10.3 fusion.45
  996.7 45.9 %reduce-scatter.28.cloned.1.call-done = f32[64,2]{1,0:T(8,128)} async-done(((f32[1024,2]{1,0:T(8,128)}), f32[64,2]{1,0:T(8,128)}) %reduce-scatter.28.cloned.1.call-update) | async-done | bytes 528
  1043.4 4.9 all-reduce.1
  1049.4 5.2 reduce-scatter.18.cloned.1.call-done
  1056.1 14.5 %reduce-scatter.14.cloned.1.call-done = bf16[64,1536]{1,0:T(8,128)(2,1)} async-done(((bf16[64,3072]{1,0:T(8,128)(2,1)}), bf16[64,1536]{1,0:T(8,128)(2,1)}) %reduce-scatter.14.cloned.1.call-update) | async-done | bytes 196624 | tf_op jit(solution)/shard_map/reduce_scatter | solution.py:250
  1072.3 15.7 %reduce-scatter.22.cloned.1.call-done = bf16[64,2048]{1,0:T(8,128)(2,1)} async-done(((bf16[64,4096]{1,0:T(8,128)(2,1)}), bf16[64,2048]{1,0:T(8,128)(2,1)}) %reduce-scatter.22.cloned.1.call-update) | async-done | bytes 262160 | tf_op jit(solution)/shard_map/reduce_scatter | solution.py:256
  1089.7 15.0 %reduce-scatter.26.cloned.1.call-done = bf16[256,512]{1,0:T(8,128)(2,1)} async-done(((bf16[256,1024]{1,0:T(8,128)(2,1)}), bf16[256,512]{1,0:T(8,128)(2,1)}) %reduce-scatter.26.cloned.1.call-update) | async-done | bytes 262160 | tf_op jit(solution)/shard_map/reduce_scatter | solution.py:259
  (268 shorter events, 156.5 us)
Async XLA Ops:
  7.2 71.3 %all-gather.7.cloned.1.call-start = ((), (), s32[]{:S(2)}) async-start(), calls=%async_computation.9 | async-start | bytes 6684672 | tf_op jit(solution)/shard_map/all_gather | solution.py:77
  16.2 202.6 %all-gather.9.cloned.1.call-start = ((), (), s32[]{:S(2)}) async-start(), calls=%async_computation.10 | async-start | bytes 2228224 | tf_op jit(solution)/shard_map/all_gather | solution.py:78
  21.6 201.0 %all-gather.11.cloned.1.call-start = ((), (), s32[]{:S(2)}) async-start(), calls=%async_computation.11 | async-start | bytes 8912896 | tf_op jit(solution)/shard_map/all_gather | solution.py:79
  30.7 240.3 %all-gather.13.cloned.1.call-start = ((), (), s32[]{:S(2)}) async-start(), calls=%async_computation.12 | async-start | bytes 8912896 | tf_op jit(solution)/shard_map/all_gather | solution.py:80
  55.3 23.2 %copy-start.19 = (f32[512]{0:T(512)}, f32[512]{0:T(512)S(1)}, u32[]{:S(2)}) copy-start(f32[512]{0:T(512)S(1)} %broadcast_multiply_fusion.1) | copy-start | bytes 6148
  57.5 20.9 %copy-start.21 = (f32[512]{0:T(512)}, f32[512]{0:T(512)S(1)}, u32[]{:S(2)}) copy-start(f32[512]{0:T(512)S(1)} %fusion.59) | copy-start | bytes 6148
  57.6 20.9 %copy-start.17 = (f32[1024,1]{0,1:T(1,128)}, f32[1024,1]{0,1:T(1,128)S(1)}, u32[]{:S(2)}) copy-start(f32[1024,1]{0,1:T(1,128)S(1)} %get-tuple-element.814) | copy-start | bytes 12292
  57.6 235.6 %copy-start.29 = (f32[1024,1]{0,1:T(1,128)}, f32[1024,1]{0,1:T(1,128)S(1)}, u32[]{:S(2)}) copy-start(f32[1024,1]{0,1:T(1,128)S(1)} %get-tuple-element.813) | copy-start | bytes 12292
  78.5 13.2 %copy-start.16 = (bf16[256,512]{1,0:T(8,128)(2,1)S(1)}, bf16[256,512]{1,0:T(8,128)(2,1)}, u32[]{:S(2)}) copy-start(bf16[256,512]{1,0:T(8,128)(2,1)} %param.20) | copy-start | bytes 786436
  78.5 63.2 %copy-start.34 = (s32[1,2]{1,0:T(1,128)S(1)}, s32[1,2]{1,0:T(1,128)}, u32[]{:S(2)}) copy-start(s32[1,2]{1,0:T(1,128)} %param.21) | copy-start | bytes 28
  78.5 63.2 %copy-start.35 = (s32[1,2]{1,0:T(1,128)S(1)}, s32[1,2]{1,0:T(1,128)}, u32[]{:S(2)}) copy-start(s32[1,2]{1,0:T(1,128)} %param.23) | copy-start | bytes 28
  78.5 63.2 %copy-start.36 = (s32[1,2]{1,0:T(1,128)S(1)}, s32[1,2]{1,0:T(1,128)}, u32[]{:S(2)}) copy-start(s32[1,2]{1,0:T(1,128)} %param.22) | copy-start | bytes 28
  87.0 58.0 %collective-permute-start = (bf16[512,2048]{1,0:T(8,128)(2,1)S(1)}, bf16[512,2048]{1,0:T(8,128)(2,1)}, u32[]{:S(2)}, u32[]{:S(2)}) collective-permute-start(bf16[512,2048]{1,0:T(8,128)(2,1)S(1)} %slice.26), channel_id=1, source_target_pairs={{0,1},{2,3},{4,5},{6,7},{8,9},{10,11},{12,13},{14,15},{16,17},{18,... | collective-permute-start | bytes 6291464 | tf_op jit(solution)/shard_map/ppermute | solution.py:16
  141.3 382.4 %reduce-scatter.16.cloned.1.call-start = ((), (), s32[]{:S(2)}) async-start(), calls=%async_computation.15 | async-start | bytes 4456448 | tf_op jit(solution)/shard_map/reduce_scatter | solution.py:242
  156.6 62.3 %copy-start = (bf16[1,512,1024]{2,1,0:T(8,128)(2,1)S(1)}, bf16[1,512,1024]{2,1,0:T(8,128)(2,1)}, u32[]{:S(2)}) copy-start(bf16[1,512,1024]{2,1,0:T(8,128)(2,1)} %param.14) | copy-start | bytes 3145732
  222.1 71.0 %copy-start.4 = (f32[512,1024]{1,0:T(8,128)}, f32[512,1024]{1,0:T(8,128)S(1)}, u32[]{:S(2)}) copy-start(f32[512,1024]{1,0:T(8,128)S(1)} %get-tuple-element.820) | copy-start | bytes 6291460
  222.2 71.0 %copy-start.27 = (f32[512]{0:T(512)}, f32[512]{0:T(512)S(1)}, u32[]{:S(2)}) copy-start(f32[512]{0:T(512)S(1)} %broadcast_multiply_fusion) | copy-start | bytes 6148
  222.5 70.6 %copy-start.31 = (f32[512]{0:T(512)}, f32[512]{0:T(512)S(1)}, u32[]{:S(2)}) copy-start(f32[512]{0:T(512)S(1)} %fusion.60) | copy-start | bytes 6148
  222.6 48.4 %copy-start.8 = (bf16[1,512,1024]{2,1,0:T(8,128)(2,1)S(1)}, bf16[1,512,1024]{2,1,0:T(8,128)(2,1)}, u32[]{:S(2)}) copy-start(bf16[1,512,1024]{2,1,0:T(8,128)(2,1)} %param.15) | copy-start | bytes 3145732
  271.0 14.5 %copy-start.37 = (bf16[1024,4096]{1,0:T(8,128)(2,1)S(1)}, bf16[1024,4096]{1,0:T(8,128)(2,1)}, u32[]{:S(2)}) copy-start(bf16[1024,4096]{1,0:T(8,128)(2,1)} %all-gather.11.cloned.1.call-done) | copy-start | bytes 25165828
  299.8 318.2 %reduce-scatter.12.cloned.1.call-start = ((), (), s32[]{:S(2)}) async-start(), calls=%async_computation.13 | async-start | bytes 13369344 | tf_op jit(solution)/shard_map/reduce_scatter | solution.py:241
  326.7 5.7 slice-start
  328.9 3.6 slice-start.1
  354.8 5.7 slice-start
  357.0 3.6 slice-start.1
  382.8 5.7 slice-start
  385.0 3.6 slice-start.1
  410.9 5.7 slice-start
  420.2 56.7 %copy-start.1 = (bf16[1,512,1024]{2,1,0:T(8,128)(2,1)S(1)}, bf16[1,512,1024]{2,1,0:T(8,128)(2,1)}, u32[]{:S(2)}) copy-start(bf16[1,512,1024]{2,1,0:T(8,128)(2,1)} %param.14) | copy-start | bytes 3145732
  420.2 56.7 %copy-start.14 = (bf16[512,1024]{0,1:T(8,128)(2,1)S(1)}, bf16[512,1024]{0,1:T(8,128)(2,1)}, u32[]{:S(2)}) copy-start(bf16[512,1024]{0,1:T(8,128)(2,1)} %get-tuple-element.589) | copy-start | bytes 3145732
  420.2 56.7 %copy-start.18 = (f32[1024,1]{0,1:T(1,128)S(1)}, f32[1024,1]{0,1:T(1,128)}, u32[]{:S(2)}) copy-start(f32[1024,1]{0,1:T(1,128)} %copy-done.17) | copy-start | bytes 12292
  420.2 56.7 %copy-start.20 = (f32[512]{0:T(512)S(1)}, f32[512]{0:T(512)}, u32[]{:S(2)}) copy-start(f32[512]{0:T(512)} %copy-done.19) | copy-start | bytes 6148
  420.2 56.7 %copy-start.22 = (f32[512]{0:T(512)S(1)}, f32[512]{0:T(512)}, u32[]{:S(2)}) copy-start(f32[512]{0:T(512)} %copy-done.21) | copy-start | bytes 6148
  422.8 49.7 %collective-permute-start.1 = (bf16[512,2048]{0,1:T(8,128)(2,1)S(1)}, bf16[512,2048]{0,1:T(8,128)(2,1)S(1)}, u32[]{:S(2)}, u32[]{:S(2)}) collective-permute-start(bf16[512,2048]{0,1:T(8,128)(2,1)S(1)} %slice.34), channel_id=1, source_target_pairs={{1,0},{3,2},{5,4},{7,6},{9,8},{11,10},{13,12},{15,14},{17,16},{19,... | collective-permute-start | bytes 6291464 | tf_op jit(solution)/shard_map/ppermute | solution.py:16
  484.9 314.8 %reduce-scatter.20.cloned.1.call-start = ((), (), s32[]{:S(2)}) async-start(), calls=%async_computation.17 | async-start | bytes 17825792 | tf_op jit(solution)/shard_map/reduce_scatter | solution.py:243
  499.2 482.8 %reduce-scatter.24.cloned.1.call-start = ((), (), s32[]{:S(2)}) async-start(), calls=%async_computation.19 | async-start | bytes 17825792 | tf_op jit(solution)/shard_map/reduce_scatter | solution.py:244
  513.1 7.1 copy-start.26
  513.2 9.4 copy-start.33
  513.2 529.4 %reduce-scatter.28.cloned.1.call-start = ((), (), s32[]{:S(2)}) async-start(), calls=%async_computation.21 | async-start | bytes 557056
  520.2 281.7 %copy-start.38 = (u32[32]{0:T(128)S(1)}, u32[32]{0:T(128)}, u32[]{:S(2)}) copy-start(u32[32]{0:T(128)} %constant.376) | copy-start | bytes 388
  523.6 531.0 %reduce-scatter.18.cloned.1.call-start = ((), (), s32[]{:S(2)}) async-start(), calls=%async_computation.16 | async-start | bytes 196608 | tf_op jit(solution)/shard_map/reduce_scatter | solution.py:253
  525.3 545.3 %reduce-scatter.14.cloned.1.call-start = ((), (), s32[]{:S(2)}) async-start(), calls=%async_computation.14 | async-start | bytes 589824 | tf_op jit(solution)/shard_map/reduce_scatter | solution.py:250
  619.9 468.0 %reduce-scatter.22.cloned.1.call-start = ((), (), s32[]{:S(2)}) async-start(), calls=%async_computation.18 | async-start | bytes 786432 | tf_op jit(solution)/shard_map/reduce_scatter | solution.py:256
  801.9 302.9 %reduce-scatter.26.cloned.1.call-start = ((), (), s32[]{:S(2)}) async-start(), calls=%async_computation.20 | async-start | bytes 786432 | tf_op jit(solution)/shard_map/reduce_scatter | solution.py:259
  984.1 10.3 copy-start.3
  984.1 10.3 copy-start.7
  984.1 10.3 copy-start.9
  984.2 10.3 copy-start.24
  (14 other events, 25.3 us)
Sparse Core Ops, SparseCore 0:
  16.4 62.0 all-gather.6
  80.6 38.9 all-gather.8
  121.7 74.0 all-gather.10
  197.8 73.1 all-gather.12
  300.0 70.6 reduce-scatter.15
  485.1 132.8 reduce-scatter.11
  622.7 177.0 reduce-scatter.19
  804.4 177.4 reduce-scatter.23
  986.5 56.0 reduce-scatter.27
  1045.2 9.3 reduce-scatter.17
  1057.4 13.1 reduce-scatter.13
  1073.3 14.5 reduce-scatter.21
  1090.2 14.5 reduce-scatter.25
where the time goes:
time: 1120 us; the launch traced here: 1110 us
  waiting for transfers between devices  638 us (57%)
  matrix products  211 us (19%)
  blocking collectives  101 us (9%)
  other arithmetic  87.2 us (8%)
  local copies, waits for them, and re-layouts  54.4 us (5%)
  between operations  14.7 us (1%)
    reduce_scatter x1, waiting for transfers between devices, shards(): lax.psum_scatter(grad_up, 'rows', scatter_dimension=0, tiled=True)  180 us
    reduce_scatter x1, waiting for transfers between devices, shards(): lax.psum_scatter(grad_down, 'rows', scatter_dimension=0, tiled=True)  179 us
    reduce_scatter x1, waiting for transfers between devices, shards(): lax.psum_scatter(grad_qkv, 'rows', scatter_dimension=0, tiled=True)  92.6 us
    all_gather x1, blocking collectives, shards(): lax.all_gather(w_down, 'pair', axis=1, tiled=True)  49.6 us
    ppermute x2, waiting for transfers between devices, passed_along(): lax.ppermute(value, axis, [(source, source + steps) for source in range(l...  48.2 us
    unnamed x14, waiting for transfers between devices  46.1 us
    sub x8, matrix products, softmax_rows(): exponents = jnp.exp(scores - row_max)  42.5 us
    dot_general x1, matrix products, shards(): jnp.dot(normed_mid_low, up_all, preferred_element_type=jnp.float32)  27.9 us
  transfers between devices with their start and end apart: 15, of which 11 were waited for; matrix products, arithmetic and copies ran while one was open for 28% of the time, Pallas kernels for 0%

commit v1 on v0

--- a/solution.py
+++ b/solution.py
@@ -18,7 +18,8 @@
 
 def slot_layout(side_index, phones, prompts, targets, slot_count):
     lengths = jnp.where(side_index == 0, phones + prompts, targets)
-    seg_ends = jnp.cumsum(lengths)
+    count = lengths.shape[0]
+    seg_ends = jnp.stack([sum(lengths[i] for i in range(upto + 1)) for upto in range(count)])
     starts = seg_ends - lengths
     places = jnp.arange(slot_count, dtype=jnp.int32)
     segment = jnp.sum((places[:, None] >= seg_ends[None, :]).astype(jnp.int32), axis=1)
@@ -152,18 +153,7 @@
     activated_low = activated.astype(jnp.bfloat16)
     result = middle + jnp.dot(activated_low, down_all, preferred_element_type=jnp.float32)
     mixed_out = result.astype(jnp.bfloat16)[None]
-    paired_again = (
-        lax.all_gather(w_qkv, "pair", axis=1, tiled=True),
-        lax.all_gather(w_out, "pair", axis=1, tiled=True),
-        lax.all_gather(w_up, "pair", axis=1, tiled=True),
-        lax.all_gather(w_down, "pair", axis=1, tiled=True),
-    )
-    qkv_back, out_back, up_back, down_back = (
-        lax.all_gather(paired_again[0], "rows", axis=0, tiled=True),
-        lax.all_gather(paired_again[1], "rows", axis=0, tiled=True),
-        lax.all_gather(paired_again[2], "rows", axis=0, tiled=True),
-        lax.all_gather(paired_again[3], "rows", axis=0, tiled=True),
-    )
+    qkv_back, out_back, up_back, down_back = (qkv_all, out_all, up_all, down_all)
     grad_result = cotangent[0]
     grad_down = jnp.dot(activated_low.T, grad_result, preferred_element_type=jnp.float32)
     grad_act = jnp.dot(grad_result, down_back.T, preferred_element_type=jnp.float32)
@@ -238,10 +228,10 @@
     grad_gains = jnp.stack([grad_gain_first, grad_gain_second], axis=1)
     strips = (
         lax.psum_scatter(grad_gains, "rows", scatter_dimension=0, tiled=True),
-        lax.psum_scatter(grad_qkv, "rows", scatter_dimension=0, tiled=True),
-        lax.psum_scatter(grad_out, "rows", scatter_dimension=0, tiled=True),
-        lax.psum_scatter(grad_up, "rows", scatter_dimension=0, tiled=True),
-        lax.psum_scatter(grad_down, "rows", scatter_dimension=0, tiled=True),
+        lax.psum_scatter(grad_qkv.astype(jnp.bfloat16), "rows", scatter_dimension=0, tiled=True),
+        lax.psum_scatter(grad_out.astype(jnp.bfloat16), "rows", scatter_dimension=0, tiled=True),
+        lax.psum_scatter(grad_up.astype(jnp.bfloat16), "rows", scatter_dimension=0, tiled=True),
+        lax.psum_scatter(grad_down.astype(jnp.bfloat16), "rows", scatter_dimension=0, tiled=True),
     )
     owned = (
         lax.psum_scatter(

time: 1120 us -> 931 us (0.83)
  waiting for transfers between devices: 638 us -> 496 us
  blocking collectives: 101 us -> 59 us
    reduce_scatter x4, waiting for transfers between devices: 452 us -> 278 us  [the longest x1 108 us: shards(): lax.psum_scatter(grad_up.astype(jnp.bfloat16), 'rows', scatter_dimension=...]
    all_gather x1, blocking collectives: 49.6 us -> 7.54 us  [shards(): lax.all_gather(w_down, 'pair', axis=1, tiled=True)]
    ppermute x2, waiting for transfers between devices: 48.2 us -> 79.3 us  [passed_along(): lax.ppermute(value, axis, [(source, source + steps) for source in range(l...]
  transfers between devices with their start and end apart: 15 -> 15, of which waited for: 11 -> 12; matrix products, arithmetic and copies ran while one was open for 28% -> 20% of each run, Pallas kernels for 0% -> 0%
where the time goes in v1:
time: 931 us; the launch traced here: 924 us
  waiting for transfers between devices  496 us (53%)
  matrix products  204 us (22%)
  other arithmetic  82.5 us (9%)
  blocking collectives  59 us (6%)
  local copies, waits for them, and re-layouts  57.3 us (6%)
  between operations  17.2 us (2%)
    reduce_scatter x1, waiting for transfers between devices, shards(): lax.psum_scatter(grad_up.astype(jnp.bfloat16), 'rows', scatter_dimension=...  108 us
    reduce_scatter x1, waiting for transfers between devices, shards(): lax.psum_scatter(grad_down.astype(jnp.bfloat16), 'rows', scatter_dimensio...  108 us
    ppermute x2, waiting for transfers between devices, passed_along(): lax.ppermute(value, axis, [(source, source + steps) for source in range(l...  79.3 us
    reduce_scatter x1, waiting for transfers between devices, shards(): lax.psum_scatter(grad_qkv.astype(jnp.bfloat16), 'rows', scatter_dimension...  61.7 us
    unnamed x14, waiting for transfers between devices  47.5 us
    sub x8, matrix products, softmax_rows(): exponents = jnp.exp(scores - row_max)  42.7 us
    all_gather x1, waiting for transfers between devices, shards(): lax.all_gather(paired[4], 'rows', axis=0, tiled=True)  29.3 us
    dot_general x1, matrix products, shards(): jnp.dot(normed_mid_low, up_all, preferred_element_type=jnp.float32)  27.9 us
  transfers between devices with their start and end apart: 15, of which 12 were waited for; matrix products, arithmetic and copies ran while one was open for 20% of the time, Pallas kernels for 0%

profile of v1, /device:TPU:8, one launch (start us, length us, event | category | flops | bytes accessed | tf_op | source)
XLA Modules:
  0.0 924.1 jit_solution(1258898478308388590)
XLA Ops:
  7.2 9.0 all_gather.32
  16.3 5.3 all_gather.34
  21.6 9.0 all_gather.36
  30.7 7.5 all_gather.38
  38.3 4.4 all-gather
  42.6 18.9 %all-gather.1 = bf16[16,64,2]{1,2,0:T(2,128)(2,1)S(1)} all-gather(bf16[1,64,2]{1,2,0:T(2,128)(2,1)S(1)} %bitcast.204), channel_id=1, replica_groups=mesh['rows'=16,'pair'=2] {'rows'}, dimensions={0}, use_global_device_ids=true | all-gather | bytes 4352 | tf_op jit(solution)/shard_map/all_gather | solution.py:77
  64.8 13.7 %all-gather.7.cloned.1.call-done = bf16[1024,3072]{1,0:T(8,128)(2,1)} async-done(((bf16[64,3072]{1,0:T(8,128)(2,1)}), bf16[1024,3072]{1,0:T(8,128)(2,1)}) %all-gather.7.cloned.1.call-update) | async-done | bytes 6291472 | tf_op jit(solution)/shard_map/all_gather | solution.py:78
  78.5 6.6 convolution_convert_fusion.3
  87.0 4.9 collective-permute-start
  101.0 34.7 %collective-permute-done = bf16[512,2048]{1,0:T(8,128)(2,1)} collective-permute-done((bf16[512,2048]{1,0:T(8,128)(2,1)S(1)}, bf16[512,2048]{1,0:T(8,128)(2,1)}, u32[]{:S(2)}, u32[]{:S(2)}) %collective-permute-start) | collective-permute-done | bytes 2097184 | tf_op jit(solution)/shard_map/ppermute | solution.py:16
  139.8 6.4 copy.35
  147.3 62.9 %while.34 = (s32[]{:T(128)}, bf16[512,1024]{0,1:T(8,128)(2,1)}, bf16[1024,2048]{0,1:T(8,128)(2,1)}, s32[512]{0:T(512)S(1)}, s32[1024]{0:T(1024)S(1)}, /*index=5*...) while((s32[]{:T(128)}, bf16[512,1024]{0,1:T(8,128)(2,1)}, ...), condition=%wide.region_11.12_spmd.clone, body=%wide.region_8.11_spmd.clone.sunk | while | flops 552601088 | bytes 22579060 | solution.py:144
  152.0 5.4 fusion.126
  157.3 4.8 fusion.127
  167.5 5.3 fusion.126
  172.9 4.9 fusion.127
  183.1 5.3 fusion.126
  188.5 5.0 fusion.127
  198.9 5.3 fusion.126
  204.3 5.2 fusion.127
  213.9 27.9 %multiply_convert_fusion.1 = (bf16[512,4096]{1,0:T(8,128)(2,1)}, f32[512,4096]{1,0:T(8,128)}, f32[512,4096]{1,0:T(8,128)}) fusion(bf16[1024,4096]{1,0:T(8,128)(2,1)} %all-gather.11.cloned.1.call-done, f32[512,1024]{1,0:T(8,128)S(1)} %get-tuple-element.824, f32[1024]{0:T(1024)S(1)} %bitcast.198, f32[512]{0:T(512)S(1)} %fusion.57, ...), kind=kOutput, calls=%fused_computation.51 | convolution fusion | flops 4433379328 | bytes 31465472 | tf_op jit(solution)/shard_map/dot_general | solution.py:151
  241.8 29.3 %all-gather.13.cloned.1.call-done = bf16[4096,1024]{1,0:T(8,128)(2,1)} async-done(((bf16[256,1024]{1,0:T(8,128)(2,1)}), bf16[4096,1024]{1,0:T(8,128)(2,1)}) %all-gather.13.cloned.1.call-update) | async-done | bytes 8388624 | tf_op jit(solution)/shard_map/all_gather | solution.py:81
  271.1 14.5 %add_convert_fusion = bf16[512,4096]{1,0:T(8,128)(2,1)} fusion(f32[512,4096]{1,0:T(8,128)} %get-tuple-element.800, f32[512,4096]{1,0:T(8,128)} %get-tuple-element.825, bf16[4096,1024]{1,0:T(8,128)(2,1)} %all-gather.13.cloned.1.call-done, bf16[1,512,1024]{2,1,0:T(8,128)(2,1)S(1)} %copy-done.8), kind=kOutput, calls=%fused_computation.50 | convolution fusion | flops 4324327424 | bytes 30408704 | tf_op jit(solution)/shard_map/dot_general | solution.py:159
  285.6 7.6 multiply_reduce_fusion.1
  302.5 115.8 %while.35 = (s32[]{:T(128)}, bf16[512,1024]{0,1:T(8,128)(2,1)}, f32[1024,2048]{0,1:T(8,128)}, bf16[1024,2048]{0,1:T(8,128)(2,1)}, s32[512]{0:T(512)S(1)}, /*inde...) while((s32[]{:T(128)}, bf16[512,1024]{0,1:T(8,128)(2,1)}, ...), condition=%wide.region_20.21_spmd.clone, body=%wide.region_16.20_spmd.clone.sunk | while | flops 1373634048 | bytes 104662968 | solution.py:218
  307.2 5.3 fusion.138
  313.7 4.4 multiply_reduce_fusion.5
  336.3 5.3 fusion.138
  342.7 4.4 multiply_reduce_fusion.5
  365.1 5.3 fusion.138
  371.6 4.4 multiply_reduce_fusion.5
  394.0 5.3 fusion.138
  400.5 4.4 multiply_reduce_fusion.5
  427.5 44.6 %collective-permute-done.1 = bf16[512,2048]{0,1:T(8,128)(2,1)} collective-permute-done((bf16[512,2048]{0,1:T(8,128)(2,1)}, bf16[512,2048]{0,1:T(8,128)(2,1)}, u32[]{:S(2)}, u32[]{:S(2)}) %collective-permute-start.1) | collective-permute-done | bytes 2097184 | tf_op jit(solution)/shard_map/ppermute | solution.py:16
  476.9 7.0 convolution_convert_fusion.2
  485.5 9.2 convolution_convert_fusion.1
  494.8 10.5 %convolution_convert_fusion = bf16[4096,1024]{1,0:T(8,128)(2,1)} fusion(bf16[512,4096]{1,0:T(8,128)(2,1)} %get-tuple-element.799, bf16[1,512,1024]{2,1,0:T(8,128)(2,1)} %param.15), kind=kOutput, calls=%fused_computation.65 | convolution fusion | flops 4299161600 | bytes 13631488 | tf_op jit(solution)/shard_map/dot_general | solution.py:158
  505.6 7.2 fusion.42
  516.9 61.7 %reduce-scatter.12.cloned.1.call-done = bf16[64,3072]{1,0:T(8,128)(2,1)} async-done(((bf16[1024,3072]{1,0:T(8,128)(2,1)}), bf16[64,3072]{1,0:T(8,128)(2,1)}) %reduce-scatter.12.cloned.1.call-update) | async-done | bytes 393232 | tf_op jit(solution)/shard_map/reduce_scatter | solution.py:231
  578.6 108.4 %reduce-scatter.20.cloned.1.call-done = bf16[64,4096]{1,0:T(8,128)(2,1)} async-done(((bf16[1024,4096]{1,0:T(8,128)(2,1)}), bf16[64,4096]{1,0:T(8,128)(2,1)}) %reduce-scatter.20.cloned.1.call-update) | async-done | bytes 524304 | tf_op jit(solution)/shard_map/reduce_scatter | solution.py:233
  687.7 107.8 %reduce-scatter.24.cloned.1.call-done = bf16[256,1024]{1,0:T(8,128)(2,1)} async-done(((bf16[4096,1024]{1,0:T(8,128)(2,1)}), bf16[256,1024]{1,0:T(8,128)(2,1)}) %reduce-scatter.24.cloned.1.call-update) | async-done | bytes 524304 | tf_op jit(solution)/shard_map/reduce_scatter | solution.py:234
  795.6 10.3 %fusion.44 = bf16[1,512,1024]{2,1,0:T(8,128)(2,1)} fusion(f32[512,1024]{1,0:T(8,128)S(1)} %copy-done.5, bf16[512,4096]{1,0:T(8,128)(2,1)} %get-tuple-element.799, bf16[4096,1024]{1,0:T(8,128)(2,1)} %all-gather.13.cloned.1.call-done), kind=kOutput, calls=%fused_computation.99 | convolution fusion | flops 4296015872 | bytes 15728640 | tf_op jit(solution)/shard_map/dot_general | solution.py:154
  808.1 46.8 %reduce-scatter.28.cloned.1.call-done = f32[64,2]{1,0:T(8,128)} async-done(((f32[1024,2]{1,0:T(8,128)}), f32[64,2]{1,0:T(8,128)}) %reduce-scatter.28.cloned.1.call-update) | async-done | bytes 528
  855.7 4.9 all-reduce.1
  861.8 4.6 reduce-scatter.18.cloned.1.call-done
  867.9 14.0 %reduce-scatter.14.cloned.1.call-done = bf16[64,1536]{1,0:T(8,128)(2,1)} async-done(((bf16[64,3072]{1,0:T(8,128)(2,1)}), bf16[64,1536]{1,0:T(8,128)(2,1)}) %reduce-scatter.14.cloned.1.call-update) | async-done | bytes 196624 | tf_op jit(solution)/shard_map/reduce_scatter | solution.py:240
  883.6 15.0 %reduce-scatter.22.cloned.1.call-done = bf16[64,2048]{1,0:T(8,128)(2,1)} async-done(((bf16[64,4096]{1,0:T(8,128)(2,1)}), bf16[64,2048]{1,0:T(8,128)(2,1)}) %reduce-scatter.22.cloned.1.call-update) | async-done | bytes 262160 | tf_op jit(solution)/shard_map/reduce_scatter | solution.py:246
  900.4 15.1 %reduce-scatter.26.cloned.1.call-done = bf16[256,512]{1,0:T(8,128)(2,1)} async-done(((bf16[256,1024]{1,0:T(8,128)(2,1)}), bf16[256,512]{1,0:T(8,128)(2,1)}) %reduce-scatter.26.cloned.1.call-update) | async-done | bytes 262160 | tf_op jit(solution)/shard_map/reduce_scatter | solution.py:249
  (264 shorter events, 159.7 us)
Async XLA Ops:
  7.2 71.3 %all-gather.7.cloned.1.call-start = ((), (), s32[]{:S(2)}) async-start(), calls=%async_computation.9 | async-start | bytes 6684672 | tf_op jit(solution)/shard_map/all_gather | solution.py:78
  16.2 193.9 %all-gather.9.cloned.1.call-start = ((), (), s32[]{:S(2)}) async-start(), calls=%async_computation.10 | async-start | bytes 2228224 | tf_op jit(solution)/shard_map/all_gather | solution.py:79
  21.6 192.3 %all-gather.11.cloned.1.call-start = ((), (), s32[]{:S(2)}) async-start(), calls=%async_computation.11 | async-start | bytes 8912896 | tf_op jit(solution)/shard_map/all_gather | solution.py:80
  30.6 240.5 %all-gather.13.cloned.1.call-start = ((), (), s32[]{:S(2)}) async-start(), calls=%async_computation.12 | async-start | bytes 8912896 | tf_op jit(solution)/shard_map/all_gather | solution.py:81
  38.2 478.1 %reduce-scatter.16.cloned.1.call-start = ((), (), s32[]{:S(2)}) async-start(), calls=%async_computation.15 | async-start | bytes 2228224 | tf_op jit(solution)/shard_map/reduce_scatter | solution.py:232
  61.7 23.5 %copy-start.16 = (f32[1024,1]{0,1:T(1,128)}, f32[1024,1]{0,1:T(1,128)S(1)}, u32[]{:S(2)}) copy-start(f32[1024,1]{0,1:T(1,128)S(1)} %get-tuple-element.814) | copy-start | bytes 12292
  61.7 231.6 %copy-start.28 = (f32[1024,1]{0,1:T(1,128)}, f32[1024,1]{0,1:T(1,128)S(1)}, u32[]{:S(2)}) copy-start(f32[1024,1]{0,1:T(1,128)S(1)} %get-tuple-element.813) | copy-start | bytes 12292
  63.1 22.0 %copy-start.18 = (f32[512]{0:T(512)}, f32[512]{0:T(512)S(1)}, u32[]{:S(2)}) copy-start(f32[512]{0:T(512)S(1)} %broadcast_multiply_fusion.1) | copy-start | bytes 6148
  64.8 20.4 %copy-start.24 = (f32[512]{0:T(512)}, f32[512]{0:T(512)S(1)}, u32[]{:S(2)}) copy-start(f32[512]{0:T(512)S(1)} %fusion.41) | copy-start | bytes 6148
  64.8 20.4 %copy-start.20 = (f32[512]{0:T(512)}, f32[512]{0:T(512)S(1)}, u32[]{:S(2)}) copy-start(f32[512]{0:T(512)S(1)} %fusion.56) | copy-start | bytes 6148
  78.5 13.5 %copy-start.32 = (s32[1,2]{1,0:T(1,128)S(1)}, s32[1,2]{1,0:T(1,128)}, u32[]{:S(2)}) copy-start(s32[1,2]{1,0:T(1,128)} %param.21) | copy-start | bytes 28
  78.5 13.5 %copy-start.34 = (s32[1,2]{1,0:T(1,128)S(1)}, s32[1,2]{1,0:T(1,128)}, u32[]{:S(2)}) copy-start(s32[1,2]{1,0:T(1,128)} %param.23) | copy-start | bytes 28
  78.5 13.5 %copy-start.35 = (s32[1,2]{1,0:T(1,128)S(1)}, s32[1,2]{1,0:T(1,128)}, u32[]{:S(2)}) copy-start(s32[1,2]{1,0:T(1,128)} %param.22) | copy-start | bytes 28
  87.0 48.7 %collective-permute-start = (bf16[512,2048]{1,0:T(8,128)(2,1)S(1)}, bf16[512,2048]{1,0:T(8,128)(2,1)}, u32[]{:S(2)}, u32[]{:S(2)}) collective-permute-start(bf16[512,2048]{1,0:T(8,128)(2,1)S(1)} %slice.44), channel_id=1, source_target_pairs={{0,1},{2,3},{4,5},{6,7},{8,9},{10,11},{12,13},{14,15},{16,17},{18,... | collective-permute-start | bytes 6291464 | tf_op jit(solution)/shard_map/ppermute | solution.py:16
  147.3 62.9 %copy-start = (bf16[1,512,1024]{2,1,0:T(8,128)(2,1)S(1)}, bf16[1,512,1024]{2,1,0:T(8,128)(2,1)}, u32[]{:S(2)}) copy-start(bf16[1,512,1024]{2,1,0:T(8,128)(2,1)} %param.14) | copy-start | bytes 3145732
  213.5 79.8 %copy-start.4 = (f32[512,1024]{1,0:T(8,128)}, f32[512,1024]{1,0:T(8,128)S(1)}, u32[]{:S(2)}) copy-start(f32[512,1024]{1,0:T(8,128)S(1)} %get-tuple-element.824) | copy-start | bytes 6291460
  213.5 79.8 %copy-start.26 = (f32[512]{0:T(512)}, f32[512]{0:T(512)S(1)}, u32[]{:S(2)}) copy-start(f32[512]{0:T(512)S(1)} %broadcast_multiply_fusion) | copy-start | bytes 6148
  213.9 79.4 %copy-start.30 = (f32[512]{0:T(512)}, f32[512]{0:T(512)S(1)}, u32[]{:S(2)}) copy-start(f32[512]{0:T(512)S(1)} %fusion.57) | copy-start | bytes 6148
  213.9 57.2 %copy-start.8 = (bf16[1,512,1024]{2,1,0:T(8,128)(2,1)S(1)}, bf16[1,512,1024]{2,1,0:T(8,128)(2,1)}, u32[]{:S(2)}) copy-start(bf16[1,512,1024]{2,1,0:T(8,128)(2,1)} %param.15) | copy-start | bytes 3145732
  271.1 14.5 %copy-start.36 = (bf16[1024,4096]{1,0:T(8,128)(2,1)S(1)}, bf16[1024,4096]{1,0:T(8,128)(2,1)}, u32[]{:S(2)}) copy-start(bf16[1024,4096]{1,0:T(8,128)(2,1)} %all-gather.11.cloned.1.call-done) | copy-start | bytes 25165828
  302.5 120.9 %copy-start.10 = (bf16[512,1024]{0,1:T(8,128)(2,1)S(1)}, bf16[512,1024]{0,1:T(8,128)(2,1)}, u32[]{:S(2)}) copy-start(bf16[512,1024]{0,1:T(8,128)(2,1)} %get-tuple-element.588) | copy-start | bytes 3145732
  322.2 5.7 slice-start
  324.4 3.6 slice-start.1
  351.3 5.6 slice-start
  380.2 5.7 slice-start
  382.3 3.5 slice-start.1
  409.1 5.7 slice-start
  422.1 50.0 %collective-permute-start.1 = (bf16[512,2048]{0,1:T(8,128)(2,1)}, bf16[512,2048]{0,1:T(8,128)(2,1)}, u32[]{:S(2)}, u32[]{:S(2)}) collective-permute-start(bf16[512,2048]{0,1:T(8,128)(2,1)} %slice.52), channel_id=1, source_target_pairs={{1,0},{3,2},{5,4},{7,6},{9,8},{11,10},{13,12},{15,14},{17,16},{19,... | collective-permute-start | bytes 6291464 | tf_op jit(solution)/shard_map/ppermute | solution.py:16
  427.2 49.8 %copy-start.1 = (bf16[1,512,1024]{2,1,0:T(8,128)(2,1)S(1)}, bf16[1,512,1024]{2,1,0:T(8,128)(2,1)}, u32[]{:S(2)}) copy-start(bf16[1,512,1024]{2,1,0:T(8,128)(2,1)} %param.14) | copy-start | bytes 3145732
  427.2 49.8 %copy-start.14 = (bf16[512,1024]{0,1:T(8,128)(2,1)S(1)}, bf16[512,1024]{0,1:T(8,128)(2,1)}, u32[]{:S(2)}) copy-start(bf16[512,1024]{0,1:T(8,128)(2,1)} %get-tuple-element.589) | copy-start | bytes 3145732
  427.2 49.8 %copy-start.17 = (f32[1024,1]{0,1:T(1,128)S(1)}, f32[1024,1]{0,1:T(1,128)}, u32[]{:S(2)}) copy-start(f32[1024,1]{0,1:T(1,128)} %copy-done.16) | copy-start | bytes 12292
  427.2 49.8 %copy-start.19 = (f32[512]{0:T(512)S(1)}, f32[512]{0:T(512)}, u32[]{:S(2)}) copy-start(f32[512]{0:T(512)} %copy-done.18) | copy-start | bytes 6148
  427.2 49.8 %copy-start.21 = (f32[512]{0:T(512)S(1)}, f32[512]{0:T(512)}, u32[]{:S(2)}) copy-start(f32[512]{0:T(512)} %copy-done.20) | copy-start | bytes 6148
  427.2 151.3 %reduce-scatter.12.cloned.1.call-start = ((), (), s32[]{:S(2)}) async-start(), calls=%async_computation.13 | async-start | bytes 6684672 | tf_op jit(solution)/shard_map/reduce_scatter | solution.py:231
  483.9 203.1 %reduce-scatter.20.cloned.1.call-start = ((), (), s32[]{:S(2)}) async-start(), calls=%async_computation.17 | async-start | bytes 8912896 | tf_op jit(solution)/shard_map/reduce_scatter | solution.py:233
  494.7 300.8 %reduce-scatter.24.cloned.1.call-start = ((), (), s32[]{:S(2)}) async-start(), calls=%async_computation.19 | async-start | bytes 8912896 | tf_op jit(solution)/shard_map/reduce_scatter | solution.py:234
  505.3 7.6 copy-start.25
  505.3 9.9 %copy-start.33 = (f32[1024]{0:T(1024)S(1)}, f32[1024]{0:T(1024)}, u32[]{:S(2)}) copy-start(f32[1024]{0:T(1024)} %get-tuple-element.741) | copy-start | bytes 12292
  505.3 181.8 %copy-start.37 = (u32[32]{0:T(128)S(1)}, u32[32]{0:T(128)}, u32[]{:S(2)}) copy-start(u32[32]{0:T(128)} %constant.372) | copy-start | bytes 388
  505.3 349.6 %reduce-scatter.28.cloned.1.call-start = ((), (), s32[]{:S(2)}) async-start(), calls=%async_computation.21 | async-start | bytes 557056
  516.2 350.2 %reduce-scatter.18.cloned.1.call-start = ((), (), s32[]{:S(2)}) async-start(), calls=%async_computation.16 | async-start | bytes 196608 | tf_op jit(solution)/shard_map/reduce_scatter | solution.py:243
  516.8 365.1 %reduce-scatter.14.cloned.1.call-start = ((), (), s32[]{:S(2)}) async-start(), calls=%async_computation.14 | async-start | bytes 589824 | tf_op jit(solution)/shard_map/reduce_scatter | solution.py:240
  578.6 320.0 %reduce-scatter.22.cloned.1.call-start = ((), (), s32[]{:S(2)}) async-start(), calls=%async_computation.18 | async-start | bytes 786432 | tf_op jit(solution)/shard_map/reduce_scatter | solution.py:246
  687.1 228.5 %reduce-scatter.26.cloned.1.call-start = ((), (), s32[]{:S(2)}) async-start(), calls=%async_computation.20 | async-start | bytes 786432 | tf_op jit(solution)/shard_map/reduce_scatter | solution.py:249
  795.5 10.3 %copy-start.3 = (f32[512,1024]{1,0:T(8,128)S(1)}, f32[512,1024]{1,0:T(8,128)}, u32[]{:S(2)}) copy-start(f32[512,1024]{1,0:T(8,128)} %copy-done.2) | copy-start | bytes 6291460
  795.5 10.3 %copy-start.7 = (f32[512,1024]{1,0:T(8,128)S(1)}, f32[512,1024]{1,0:T(8,128)}, u32[]{:S(2)}) copy-start(f32[512,1024]{1,0:T(8,128)} %copy-done.6) | copy-start | bytes 6291460
  795.5 10.3 %copy-start.9 = (bf16[1,512,1024]{2,1,0:T(8,128)(2,1)S(1)}, bf16[1,512,1024]{2,1,0:T(8,128)(2,1)}, u32[]{:S(2)}) copy-start(bf16[1,512,1024]{2,1,0:T(8,128)(2,1)} %param.15) | copy-start | bytes 3145732
  795.6 10.3 %copy-start.23 = (f32[512]{0:T(512)S(1)}, f32[512]{0:T(512)}, u32[]{:S(2)}) copy-start(f32[512]{0:T(512)} %copy-done.22) | copy-start | bytes 6148
  (13 other events, 28.0 us)
Sparse Core Ops, SparseCore 0:
  16.4 62.0 all-gather.6
  80.6 38.9 all-gather.8
  121.8 74.0 all-gather.10
  197.9 73.1 all-gather.12
  427.3 62.8 reduce-scatter.15
  494.5 83.9 reduce-scatter.11
  582.6 104.3 reduce-scatter.19
  691.1 104.3 reduce-scatter.23
  799.6 55.2 reduce-scatter.27
  857.0 9.3 reduce-scatter.17
  868.8 13.1 reduce-scatter.13
  884.0 14.5 reduce-scatter.21
  900.9 14.5 reduce-scatter.25

commit v2 on v1

--- a/solution.py
+++ b/solution.py
@@ -1,6 +1,10 @@
+import functools
+
 import jax
 import jax.numpy as jnp
 from jax import lax
+from jax.experimental import pallas as pl
+from jax.experimental.pallas import tpu as pltpu
 from jax.sharding import PartitionSpec as P
 
 HEADS = 16
@@ -253,9 +257,860 @@
     return (mixed_out, grad_tokens, owned[0], owned[1], owned[2], owned[3], owned[4])
 
 
+LINE = 4
+HALF = 512
+NEG = -1e30
+bf16 = jnp.bfloat16
+f32 = jnp.float32
+VMEM_LIMIT = 56 * 1024 * 1024
+
+
+def params(limit=VMEM_LIMIT):
+    return pltpu.CompilerParams(vmem_limit_bytes=limit)
+
+
+def cost(flops, nbytes, trans=0):
+    return pl.CostEstimate(flops=flops // 64, bytes_accessed=nbytes // 64, transcendentals=trans // 64)
+
+
+def whole():
+    return pl.BlockSpec(memory_space=pltpu.VMEM)
+
+
+def hbm():
+    return pl.BlockSpec(memory_space=pl.ANY)
+
+
+def dot(a, b, contract):
+    return lax.dot_general(a, b, ((contract[:1], contract[1:]), ((), ())), preferred_element_type=f32)
+
+
+def row_pairs(target):
+    pairs = []
+    for r in range(LINE * 4):
+        z, x, c = target(r // 4, r // 2 % 2, r % 2)
+        pairs.append((r, z % LINE * 4 + x * 2 + c))
+    return pairs
+
+
+def shift_z(v, k):
+    return lax.ppermute(v, "rows", row_pairs(lambda z, x, c: (z + k, x, c)))
+
+
+def swap_x(v):
+    return lax.ppermute(v, "rows", row_pairs(lambda z, x, c: (z, 1 - x, c)))
+
+
+def swap_c(v):
+    return lax.ppermute(v, "rows", row_pairs(lambda z, x, c: (z, x, 1 - c)))
+
+
+def swap_y(v):
+    return lax.ppermute(v, "pair", [(0, 1), (1, 0)])
+
+
+def along_line(shard):
+    return jnp.stack([shard] + [shift_z(shard, k) for k in range(1, LINE)])
+
+
+def summed_line(parts):
+    total = parts[0].astype(f32)
+    for k in range(1, LINE):
+        total = total + shift_z(parts[k], k).astype(f32)
+    return total
+
+
+def plus(a, b):
+    return (a.astype(f32) + b.astype(f32)).astype(bf16)
+
+
+def after(value, *others):
+    return lax.optimization_barrier((value, others))[0]
+
+
+def place_of(info, z_abs, x_abs):
+    dx = lax.rem(info[1] + x_abs, 2)
+    return dx, lax.rem(info[0] - z_abs + LINE, LINE), lax.rem(z_abs - info[0] + LINE, LINE)
+
+
+def weight_copies(info, a_ref, b_ref, w_ref, sems, halves, start_col=0, cols=None):
+    rows = a_ref.shape[1]
+    cols = cols or a_ref.shape[2]
+    out = []
+    for y_abs in range(halves):
+        out.append([])
+        for z_abs in range(LINE):
+            group = []
+            for x_abs in range(2):
+                dx, dz, _ = place_of(info, z_abs, x_abs)
+                index = dx * LINE + dz
+                if halves == 2:
+                    index = index + lax.rem(info[3] + y_abs, 2) * 2 * LINE
+                for own in (0, 1):
+                    core = info[2] if own == 0 else 1 - info[2]
+                    start = pl.multiple_of((z_abs * 2 + x_abs) * 2 * rows + core * rows, rows)
+                    group.append(
+                        pltpu.make_async_copy(
+                            (a_ref, b_ref)[own].at[index, :, pl.ds(start_col, cols)],
+                            w_ref.at[pl.ds(start, rows), pl.ds(y_abs * cols, cols)],
+                            sems.at[(y_abs * LINE * 2 + z_abs * 2 + x_abs) * 2 + own],
+                        )
+                    )
+            out[-1].append(group)
+    return out
+
+
+def start(copies):
+    for y in copies:
+        for group in y:
+            for c in group:
+                c.start()
+
+
+def wait(copies, y=None, z=None):
+    for i, by_z in enumerate(copies):
+        for j, group in enumerate(by_z):
+            if y in (None, i) and z in (None, j):
+                for c in group:
+                    c.wait()
+
+
+def project_kernel(info, xo_ref, xt_ref, a_ref, b_ref, out_ref, g_ref, w_ref, gcol_ref, nin_ref, sems):
+    copies = weight_copies(info, a_ref, b_ref, w_ref, sems, 1, 0, 1536)
+    gains = weight_copies(info, a_ref, b_ref, gcol_ref, sems.at[pl.ds(16, 16)], 1, 1536, 128)
+    start(gains)
+    start(copies)
+    wait(gains)
+    both = gcol_ref[...].T.astype(f32)[:2]
+    g_ref[...] = both
+    side = info[3]
+    for part, x_ref in ((0, xo_ref), (1, xt_ref)):
+        at = side if part == 0 else 1 - side
+        tokens = pl.ds(pl.multiple_of(at * HALF, HALF), HALF)
+        nin_ref[tokens, :] = (centred(x_ref[...].astype(f32))[0] * both[:1]).astype(bf16)
+        if part == 0:
+            wait(copies)
+        for n in range(2):
+            cols = slice(n * 768, n * 768 + 768)
+            out_ref[tokens, cols] = dot(nin_ref[tokens, :], w_ref[:, cols], (1, 0)).astype(bf16)
+
+
+def project(info, x_own, x_other, a, b):
+    block = lambda *shape: pl.BlockSpec(shape, lambda i, s: (0,) * len(shape))
+    return pl.pallas_call(
+        project_kernel,
+        grid_spec=pltpu.PrefetchScalarGridSpec(
+            num_scalar_prefetch=1,
+            grid=(1,),
+            in_specs=[block(HALF, 1024), block(HALF, 1024), hbm(), hbm()],
+            out_specs=[block(1024, 1536), block(2, 1024)],
+            scratch_shapes=[
+                pltpu.VMEM((1024, 1536), bf16),
+                pltpu.VMEM((1024, 128), bf16),
+                pltpu.VMEM((1024, 1024), bf16),
+                pltpu.SemaphoreType.DMA((32,)),
+            ],
+        ),
+        out_shape=[jax.ShapeDtypeStruct((1024, 1536), bf16), jax.ShapeDtypeStruct((2, 1024), f32)],
+        compiler_params=params(),
+        cost_estimate=cost(2 * 1024 * 1024 * 1536, 8 << 20),
+        name="project",
+    )(info, x_own, x_other, a, b)
+
+
+TILES = ((0, 512), (256, 512), (512, 768), (768, 1024))
+
+
+def own_lanes(v, head):
+    lane = lax.broadcasted_iota(jnp.int32, v.shape, 1)
+    return jnp.where((lane >= 64) if head else (lane < 64), v, jnp.zeros_like(v))
+
+
+def attend_kernel(info, q_ref, k_ref, v_ref, bias_ref, keep_ref, send_ref, lse_ref):
+    side = info[3]
+    v_t = v_ref[...].T
+    for tile, (start, seen) in enumerate(TILES):
+        q_tile = q_ref[start : start + 256, :] * jnp.asarray(0.125, bf16)
+        pieces = []
+        for head in range(2):
+            s = dot(k_ref[:seen, :], own_lanes(q_tile, head), (1, 1))
+            s = s + bias_ref[:seen, start : start + 256]
+            top = jnp.max(s, axis=0, keepdims=True)
+            p = jnp.exp(s - top)
+            total = jnp.sum(p, axis=0, keepdims=True)
+            lse_ref[0, head : head + 1, start : start + 256] = top + jnp.log(total)
+            mixed = dot(v_t[head * 64 : head * 64 + 64, :seen], p.astype(bf16), (1, 0))
+            pieces.append(mixed * (1.0 / total))
+        done = jnp.concatenate(pieces, axis=0).T.astype(bf16)
+        half, row = tile // 2, tile % 2 * 256
+
+        @pl.when(side == half)
+        def _():
+            keep_ref[row : row + 256, :] = done
+
+        @pl.when(side != half)
+        def _():
+            send_ref[row : row + 256, :] = done
+
+
+def head_parts(group):
+    return [pl.BlockSpec((1024, 128), lambda h, s, j=j: (0, 6 * group + 2 * j + h)) for j in range(3)]
+
+
+def attend(info, projected, bias, group):
+    piece = pl.BlockSpec((HALF, 128), lambda h, s: (0, h))
+    return pl.pallas_call(
+        attend_kernel,
+        grid_spec=pltpu.PrefetchScalarGridSpec(
+            num_scalar_prefetch=1,
+            grid=(2,),
+            in_specs=[*head_parts(group), pl.BlockSpec((1024, 1024), lambda h, s: (0, 0))],
+            out_specs=[piece, piece, pl.BlockSpec((1, 2, 1024), lambda h, s: (h, 0, 0))],
+        ),
+        out_shape=[
+            jax.ShapeDtypeStruct((HALF, 256), bf16),
+            jax.ShapeDtypeStruct((HALF, 256), bf16),
+            jax.ShapeDtypeStruct((2, 2, 1024), f32),
+        ],
+        compiler_params=params(),
+        cost_estimate=cost(4 * 1024 * 768 * 64 * 4 * 4, 8 << 20, 4 * 768 * 1024),
+        name="attend",
+    )(info, projected, projected, projected, bias)
+
+
+def attend_back_kernel(info, q_ref, k_ref, v_ref, bias_ref, lse_ref, keep_ref, send_ref, out_ref, dk_ref, dv_ref):
+    side = info[3]
+    pair = pl.program_id(0)
+    k_t = k_ref[...].T
+    dk_ref[...] = jnp.zeros_like(dk_ref)
+    dv_ref[...] = jnp.zeros_like(dv_ref)
+    for tile, (start, seen) in enumerate(TILES):
+        half, row = tile // 2, tile % 2 * 256
+        q_tile = q_ref[start : start + 256, :] * jnp.asarray(0.125, bf16)
+        g_tile = jnp.where(side == half, keep_ref[row : row + 256, :], send_ref[row : row + 256, :])
+        pieces = []
+        for head in range(2):
+            q_head = own_lanes(q_tile, head)
+            g_head = own_lanes(g_tile, head)
+            s = dot(k_ref[:seen, :], q_head, (1, 1))
+            p = jnp.exp(s + bias_ref[:seen, start : start + 256] - lse_ref[0, head : head + 1, start : start + 256])
+            dp = dot(v_ref[:seen, :], g_head, (1, 1))
+            centre = jnp.sum(p * dp, axis=0, keepdims=True)
+            ds = (p * (dp - centre)).astype(bf16)
+            dv_ref[:seen, :] += dot(p.astype(bf16), g_head, (1, 0))
+            dk_ref[:seen, :] += dot(ds, q_head, (1, 0))
+            pieces.append(dot(k_t[head * 64 : head * 64 + 64, :seen], ds, (1, 0)) * 0.125)
+        cols = pl.ds(pl.multiple_of(pair * 128, 128), 128)
+        out_ref[start : start + 256, cols] = jnp.concatenate(pieces, axis=0).T.astype(bf16)
+    out_ref[:, pl.ds(pl.multiple_of(256 + pair * 128, 128), 128)] = dk_ref[...].astype(bf16)
+    out_ref[:, pl.ds(pl.multiple_of(512 + pair * 128, 128), 128)] = dv_ref[...].astype(bf16)
+
+
+def attend_back(info, projected, bias, lse, keep, other, group):
+    piece = pl.BlockSpec((HALF, 128), lambda h, s: (0, h))
+    return pl.pallas_call(
+        attend_back_kernel,
+        grid_spec=pltpu.PrefetchScalarGridSpec(
+            num_scalar_prefetch=1,
+            grid=(2,),
+            in_specs=[
+                *head_parts(group),
+                pl.BlockSpec((1024, 1024), lambda h, s: (0, 0)),
+                pl.BlockSpec((1, 2, 1024), lambda h, s: (h, 0, 0)),
+                piece,
+                piece,
+            ],
+            out_specs=pl.BlockSpec((1024, 768), lambda h, s: (0, 0)),
+            scratch_shapes=[pltpu.VMEM((1024, 128), f32), pltpu.VMEM((1024, 128), f32)],
+        ),
+        out_shape=jax.ShapeDtypeStruct((1024, 768), bf16),
+        compiler_params=params(),
+        cost_estimate=cost(10 * 1024 * 768 * 64 * 4 * 4, 10 << 20, 4 * 768 * 1024),
+        name="attend_back",
+    )(info, projected, projected, projected, bias, lse, keep, other)
+
+
+def centred(v):
+    off = v - jnp.mean(v, axis=-1, keepdims=True)
+    scale = lax.rsqrt(jnp.mean(off * off, axis=-1, keepdims=True) + epsilon)
+    return off * scale, scale
+
+
+def out_kernel(
+    info, x_ref, k0, k1, g0, g1, a_ref, b_ref, g_ref, mid_ref, nm_ref, own_ref, oth_ref, w_ref, t_ref, sems
+):
+    side = info[3]
+    copies = weight_copies(info, a_ref, b_ref, w_ref, sems, 2, 2048, 512)
+    start(copies)
+    for i, ref in enumerate((k0, k1, g0, g1)):
+        at = (side if i < 2 else 1 - side) * HALF + i % 2 * 256
+        t_ref[pl.ds(pl.multiple_of(at, 256), 256), :] = ref[...].T
+    put_parities(info, t_ref, own_ref, oth_ref, 0)
+    wait(copies)
+    for half in range(2):
+        cols = slice(half * 512, half * 512 + 512)
+        branch = x_ref[:, cols].astype(f32)
+        for i, ref in enumerate((k0, k1, g0, g1)):
+            at = (side if i < 2 else 1 - side) * HALF + i % 2 * 256
+            branch = branch + dot(ref[...], w_ref[pl.ds(pl.multiple_of(at, 256), 256), cols], (1, 0))
+        mid_ref[:, cols] = branch
+    normed = (centred(mid_ref[...])[0] * g_ref[1:]).astype(bf16)
+    nm_ref[...] = normed
+    t_ref[...] = normed.T
+    put_parities(info, t_ref, own_ref, oth_ref, 1)
+
+
+def put_parities(info, t_ref, own_ref, oth_ref, slot):
+    for dx in range(2):
+        for dz in range(LINE):
+            chip = lax.rem(info[0] + dz, LINE) * 2 + lax.rem(info[1] + dx, 2)
+            here = pl.multiple_of(chip * 128 + info[2] * 64, 64)
+            there = pl.multiple_of(chip * 128 + (1 - info[2]) * 64, 64)
+            own_ref[slot, dx * LINE + dz] = t_ref[pl.ds(here, 64), :]
+            oth_ref[slot, dx * LINE + dz] = t_ref[pl.ds(there, 64), :]
+
+
+def attention_out(info, x, keeps, gots, a, b, gain):
+    block = lambda *shape: pl.BlockSpec(shape, lambda i, s: (0,) * len(shape))
+    return pl.pallas_call(
+        out_kernel,
+        grid_spec=pltpu.PrefetchScalarGridSpec(
+            num_scalar_prefetch=1,
+            grid=(1,),
+            in_specs=[block(HALF, 1024)] + [block(HALF, 256)] * 4 + [hbm(), hbm(), block(2, 1024)],
+            out_specs=[block(HALF, 1024), block(HALF, 1024), block(2, 8, 64, HALF), block(2, 8, 64, HALF)],
+            scratch_shapes=[
+                pltpu.VMEM((1024, 1024), bf16),
+                pltpu.VMEM((1024, HALF), bf16),
+                pltpu.SemaphoreType.DMA((32,)),
+            ],
+        ),
+        out_shape=[
+            jax.ShapeDtypeStruct((HALF, 1024), f32),
+            jax.ShapeDtypeStruct((HALF, 1024), bf16),
+            jax.ShapeDtypeStruct((2, 8, 64, HALF), bf16),
+            jax.ShapeDtypeStruct((2, 8, 64, HALF), bf16),
+        ],
+        compiler_params=params(),
+        cost_estimate=cost(2 * 512 * 1024 * 1024, 8 << 20),
+        name="attention_out",
+    )(info, x, *keeps, *gots, a, b, gain)
+
+
+def up_kernel(info, x_ref, a_ref, b_ref, act0_ref, act1_ref, slope0_ref, slope1_ref, w_ref, sems):
+    step = pl.program_id(0)
+    copies = weight_copies(info, a_ref, b_ref, w_ref, sems, 2, 0, 2048)
+
+    @pl.when(step == 0)
+    def _():
+        start(copies)
+        wait(copies, y=0)
+
+    @pl.when(step == 2)
+    def _():
+        wait(copies, y=1)
+
+    for x_abs in range(2):
+        dx = lax.rem(info[1] + x_abs, 2)
+        for own, act_ref, slope_ref in ((0, act0_ref, slope0_ref), (1, act1_ref, slope1_ref)):
+            core = info[2] if own == 0 else 1 - info[2]
+            cols = pl.ds(pl.multiple_of(step * 1024 + x_abs * 512 + core * 256, 256), 256)
+            pre = dot(x_ref[...], w_ref[:, cols], (1, 0))
+            below = 0.5 * (1.0 + lax.erf(pre * 0.7071067811865476))
+            act_ref[dx] = (pre * below).astype(bf16)
+            slope_ref[dx] = (below + pre * (0.3989422804014327 * jnp.exp(-0.5 * pre * pre))).astype(bf16)
+
+
+def ff_tile():
+    return pl.BlockSpec((2, HALF, 256), lambda n, s: (0, 0, place_of(s, n, 0)[2]))
+
+
+def up(info, x, a, b):
+    shape = jax.ShapeDtypeStruct((2, HALF, 1024), bf16)
+    return pl.pallas_call(
+        up_kernel,
+        grid_spec=pltpu.PrefetchScalarGridSpec(
+            num_scalar_prefetch=1,
+            grid=(4,),
+            in_specs=[pl.BlockSpec((HALF, 1024), lambda n, s: (0, 0)), hbm(), hbm()],
+            out_specs=[ff_tile()] * 4,
+            scratch_shapes=[pltpu.VMEM((1024, 4096), bf16), pltpu.SemaphoreType.DMA((32,))],
+        ),
+        out_shape=[shape] * 4,
+        compiler_params=params(),
+        cost_estimate=cost(2 * 512 * 1024 * 4096 * 2, 17 << 20, 512 * 4096),
+        name="up",
+    )(info, x, a, b)
+
+
+def down_kernel(info, act0, act1, slope0, slope1, *refs):
+    a, b = refs[:4], refs[4:8]
+    cot_ref, mid_ref, out_ref, gp_ref, acc_ref = refs[8:]
+    step = pl.program_id(0)
+    side = info[3]
+    mine = pl.ds(pl.multiple_of(side * 512, 512), 512)
+    theirs = pl.ds(pl.multiple_of((1 - side) * 512, 512), 512)
+    for dy in range(2):
+        total = sum(
+            dot(act[dx], shard[dx + 2 * dy][0], (1, 0)) for dx in range(2) for act, shard in ((act0, a), (act1, b))
+        )
+
+        @pl.when(step == 0)
+        def _():
+            acc_ref[dy] = total
+
+        @pl.when(step > 0)
+        def _():
+            acc_ref[dy] += total
+
+    for dx in range(2):
+        for own, shard, slope in ((0, a, slope0), (1, b, slope1)):
+            core = info[2] if own == 0 else 1 - info[2]
+            back = dot(cot_ref[:, mine], shard[dx][0], (1, 1)) + dot(cot_ref[:, theirs], shard[dx + 2][0], (1, 1))
+            cols = pl.ds(pl.multiple_of(lax.rem(info[1] + dx, 2) * 512 + core * 256, 256), 256)
+            gp_ref[:, cols] = (back * slope[dx].astype(f32)).astype(bf16)
+
+    @pl.when(step == 3)
+    def _():
+        out_ref[:, mine] = (mid_ref[:, mine] + acc_ref[0]).astype(bf16)
+        out_ref[:, theirs] = (mid_ref[:, theirs] + acc_ref[1]).astype(bf16)
+
+
+def down(info, acts, slopes, a, b, cot, mid):
+    shards = [
+        pl.BlockSpec((1, 256, 512), lambda n, s, xy=xy: (xy * LINE + place_of(s, n, 0)[1], 0, 0)) for xy in range(4)
+    ]
+    full = pl.BlockSpec((HALF, 1024), lambda n, s: (0, 0))
+    return pl.pallas_call(
+        down_kernel,
+        grid_spec=pltpu.PrefetchScalarGridSpec(
+            num_scalar_prefetch=1,
+            grid=(4,),
+            in_specs=[ff_tile()] * 4 + shards + shards + [full, full],
+            out_specs=[full, pl.BlockSpec((HALF, 1024), lambda n, s: (0, n))],
+            scratch_shapes=[pltpu.VMEM((2, HALF, 512), f32)],
+        ),
+        out_shape=[jax.ShapeDtypeStruct((HALF, 1024), bf16), jax.ShapeDtypeStruct((HALF, 4096), bf16)],
+        compiler_params=params(),
+        cost_estimate=cost(4 * 512 * 1024 * 4096, 25 << 20),
+        name="down",
+    )(info, *acts, *slopes, *[a] * 4, *[b] * 4, cot, mid)
+
+
+def middle_back_kernel(
+    info, gp_ref, a_ref, b_ref, cot_ref, mid_ref, g_ref, gm_ref, gb_ref, keep0, keep1, send0, send1, w_ref, wo_ref, e_ref, sems
+):
+    copies = weight_copies(info, a_ref, b_ref, w_ref, sems, 2, 0, 2048)
+    more = weight_copies(info, a_ref, b_ref, wo_ref, sems.at[pl.ds(32, 32)], 2, 2048, 512)
+    start(copies)
+    start(more)
+    for n in range(4):
+        wait(copies, z=n)
+        rows = slice(n * 256, n * 256 + 256)
+        e_ref[:, rows] = dot(gp_ref[...], w_ref[rows, :], (1, 1))
+
+    e = e_ref[...]
+    n, scale = centred(mid_ref[...])
+    eg = e * g_ref[1:]
+    lean = eg - jnp.mean(eg, axis=-1, keepdims=True) - n * jnp.mean(eg * n, axis=-1, keepdims=True)
+    grad = cot_ref[...].astype(f32) + scale * lean
+    gm_ref[...] = grad
+    low = grad.astype(bf16)
+    gb_ref[...] = low
+    wait(more)
+    side = info[3]
+    for i, out in enumerate((keep0, keep1, send0, send1)):
+        at = (side if i < 2 else 1 - side) * HALF + i % 2 * 256
+        out[...] = dot(low, wo_ref[pl.ds(pl.multiple_of(at, 256), 256), :], (1, 1)).astype(bf16)
+
+
+def middle_back(info, gp, a, b, cot, mid, gain):
+    block = lambda *shape: pl.BlockSpec(shape, lambda i, s: (0,) * len(shape))
+    return pl.pallas_call(
+        middle_back_kernel,
+        grid_spec=pltpu.PrefetchScalarGridSpec(
+            num_scalar_prefetch=1,
+            grid=(1,),
+            in_specs=[
+                block(HALF, 4096),
+                hbm(),
+                hbm(),
+                block(HALF, 1024),
+                block(HALF, 1024),
+                block(2, 1024),
+            ],
+            out_specs=[block(HALF, 1024), block(HALF, 1024)] + [block(HALF, 256)] * 4,
+            scratch_shapes=[
+                pltpu.VMEM((1024, 4096), bf16),
+                pltpu.VMEM((1024, 1024), bf16),
+                pltpu.VMEM((HALF, 1024), f32),
+                pltpu.SemaphoreType.DMA((64,)),
+            ],
+        ),
+        out_shape=[jax.ShapeDtypeStruct((HALF, 1024), f32), jax.ShapeDtypeStruct((HALF, 1024), bf16)]
+        + [jax.ShapeDtypeStruct((HALF, 256), bf16)] * 4,
+        compiler_params=params(),
+        cost_estimate=cost(2 * 512 * 1024 * 5120, 20 << 20),
+        name="middle_back",
+    )(info, gp, a, b, cot, mid, gain)
+
+
+def down_grad_kernel(info, l0_ref, r0_ref, l1_ref, r1_ref, far_a, far_b, beside, across, own, part_ref, sems):
+    g = pl.program_id(0)
+    total = (dot(l0_ref[...], r0_ref[0], (1, 0)) + dot(l1_ref[...], r1_ref[0], (1, 0))).astype(bf16)
+    for dz in range(LINE):
+        part_ref[g, dz] = total[:, dz * 256 : dz * 256 + 256]
+    outs = (
+        (0, part_ref.at[0, pl.ds(0, 2)], far_a, 0),
+        (0, part_ref.at[0, pl.ds(2, 2)], far_b, 1),
+        (1, part_ref.at[1], across, 2),
+        (2, part_ref.at[2], beside, 3),
+        (3, part_ref.at[3], own, 4),
+    )
+    for at, source, out, sem in outs:
+
+        @pl.when(g == at)
+        def _():
+            pltpu.make_async_copy(source, out, sems.at[sem]).start()
+
+    @pl.when(g == 3)
+    def _():
+        for _, source, out, sem in outs:
+            pltpu.make_async_copy(source, out, sems.at[sem]).wait()
+
+
+def down_grad(info, cot_t, act, cot_t_sib, act_sib):
+    left = pl.BlockSpec((512, HALF), lambda g, s: (lax.rem(s[3] + 1 - g // 2, 2), 0))
+    right = pl.BlockSpec((1, HALF, 1024), lambda g, s: (1 - lax.rem(g, 2), 0, 0))
+    return pl.pallas_call(
+        down_grad_kernel,
+        grid_spec=pltpu.PrefetchScalarGridSpec(
+            num_scalar_prefetch=1,
+            grid=(4,),
+            in_specs=[left, right, left, right],
+            out_specs=[hbm()] * 5,
+            scratch_shapes=[pltpu.VMEM((4, LINE, 512, 256), bf16), pltpu.SemaphoreType.DMA((5,))],
+        ),
+        out_shape=[jax.ShapeDtypeStruct((n, 512, 256), bf16) for n in (2, 2, 4, 4, 4)],
+        compiler_params=params(),
+        cost_estimate=cost(2 * 1024 * 1024 * 2048, 12 << 20),
+        name="down_grad",
+    )(info, cot_t, act, cot_t_sib, act_sib)
+
+
+def up_grad_kernel(info, l0_ref, r0_ref, l1_ref, r1_ref, far_a, far_b, beside, across, own):
+    g = pl.program_id(0)
+    total = dot(l0_ref[...], r0_ref[...], (1, 0)) + dot(l1_ref[...], r1_ref[...], (1, 0))
+    total = total.astype(bf16).reshape(8, 64, 1024)
+
+    @pl.when(g < 2)
+    def _():
+        across[...] = total[:4]
+        far_a[...] = total[4:6]
+        far_b[...] = total[6:]
+
+    @pl.when(g >= 2)
+    def _():
+        own[...] = total[:4]
+        beside[...] = total[4:]
+
+
+def up_grad(info, sides_t, gp, sides_t_sib, gp_sib):
+    left = pl.BlockSpec((512, HALF), lambda g, s: (1, 0))
+    right = pl.BlockSpec((HALF, 1024), lambda g, s: (0, lax.rem(s[3] + 1 - g // 2, 2) * 2 + lax.rem(g, 2)))
+    outs = ((2, 0), (2, 0), (4, 2), (4, 0), (4, 2))
+
+    def spec(n, first):
+        return pl.BlockSpec((n, 64, 1024), lambda g, s: (0, 0, lax.max(0, lax.min(g - first, 1))))
+
+    return pl.pallas_call(
+        up_grad_kernel,
+        grid_spec=pltpu.PrefetchScalarGridSpec(
+            num_scalar_prefetch=1,
+            grid=(4,),
+            in_specs=[left, right, left, right],
+            out_specs=[spec(n, f) for n, f in outs],
+        ),
+        out_shape=[jax.ShapeDtypeStruct((n, 64, 2048), bf16) for n, _ in outs],
+        compiler_params=params(),
+        cost_estimate=cost(2 * 1024 * 512 * 4096, 14 << 20),
+        name="up_grad",
+    )(info, sides_t.reshape(1024, HALF), gp, sides_t_sib.reshape(1024, HALF), gp_sib)
+
+
+def out_grad_kernel(info, l0_ref, r0_ref, l1_ref, r1_ref, keep_ref, send_ref):
+    for out, at in ((keep_ref, info[3]), (send_ref, 1 - info[3])):
+        cols = pl.ds(pl.multiple_of(at * 512, 512), 512)
+        total = dot(l0_ref[...], r0_ref[:, cols], (1, 0)) + dot(l1_ref[...], r1_ref[:, cols], (1, 0))
+        out[...] = total.astype(bf16).reshape(8, 64, 512)
+
+
+def out_grad(info, sides_t, gb, sides_t_sib, gb_sib):
+    block = lambda *shape: pl.BlockSpec(shape, lambda i, s: (0,) * len(shape))
+    return pl.pallas_call(
+        out_grad_kernel,
+        grid_spec=pltpu.PrefetchScalarGridSpec(
+            num_scalar_prefetch=1,
+            grid=(1,),
+            in_specs=[block(512, HALF), block(HALF, 1024)] * 2,
+            out_specs=[block(8, 64, 512)] * 2,
+        ),
+        out_shape=[jax.ShapeDtypeStruct((8, 64, 512), bf16)] * 2,
+        compiler_params=params(),
+        cost_estimate=cost(2 * 512 * 1024 * 1024, 4 << 20),
+        name="out_grad",
+    )(info, sides_t.reshape(1024, HALF), gb, sides_t_sib.reshape(1024, HALF), gb_sib)
+
+
+def input_part_kernel(group, part, info, d_ref, a_ref, b_ref, *refs):
+    out_ref, w_ref, sems = refs[-3:]
+    copies = weight_copies(info, a_ref, b_ref, w_ref, sems, 1, group * 768, 768)
+    start(copies)
+    wait(copies)
+    if part is None:
+        for half in range(2):
+            rows = slice(half * HALF, half * HALF + HALF)
+            out_ref[rows, :] = dot(d_ref[rows, :], w_ref[...], (1, 1))
+    else:
+        out_ref[...] = (refs[0][...] + dot(d_ref[...], w_ref[...], (1, 1))).astype(out_ref.dtype)
+
+
+def input_part(info, d, a, b, group, part=None, earlier=None):
+    side = lambda s: s[3] if part == 0 else 1 - s[3]
+    tokens = 2 * HALF if part is None else HALF
+    at = (lambda i, s: (0, 0)) if part is None else (lambda i, s: (side(s), 0))
+    kind = bf16 if part == 1 else f32
+    more = [] if part is None else [earlier]
+    return pl.pallas_call(
+        functools.partial(input_part_kernel, group, part),
+        grid_spec=pltpu.PrefetchScalarGridSpec(
+            num_scalar_prefetch=1,
+            grid=(1,),
+            in_specs=[pl.BlockSpec((tokens, 768), at), hbm(), hbm()] + [pl.BlockSpec((tokens, 1024), at)] * len(more),
+            out_specs=pl.BlockSpec((tokens, 1024), lambda i, s: (0, 0)),
+            scratch_shapes=[pltpu.VMEM((1024, 768), bf16), pltpu.SemaphoreType.DMA((16,))],
+        ),
+        out_shape=jax.ShapeDtypeStruct((tokens, 1024), kind),
+        compiler_params=params(),
+        cost_estimate=cost(2 * tokens * 1024 * 768, 8 << 20),
+        name="input_part",
+    )(info, d, a, b, *more)
+
+
+def qkv_grad_kernel(info, l0_ref, r0_ref, l1_ref, r1_ref, *refs):
+    beside, own = refs[-2:]
+    total = dot(l0_ref[...], r0_ref[...], (1, 0)) + dot(l1_ref[...], r1_ref[...], (1, 0))
+    total = total.astype(bf16).reshape(8, 64, 768)
+    own[:, :, :768] = total[:4]
+    beside[:, :, :768] = total[4:]
+    if len(refs) == 4:
+        both = (refs[0][...].astype(f32) + refs[1][...].astype(f32)).astype(bf16)
+        own[:, :, 768:] = both[:4]
+        beside[:, :, 768:] = both[4:]
+
+
+def qkv_grad(info, nin_t, dproj, nin_t_sib, dproj_sib, more=()):
+    block = lambda *shape: pl.BlockSpec(shape, lambda i, s: (0,) * len(shape))
+    width = 768 + 512 * bool(more)
+    return pl.pallas_call(
+        qkv_grad_kernel,
+        grid_spec=pltpu.PrefetchScalarGridSpec(
+            num_scalar_prefetch=1,
+            grid=(1,),
+            in_specs=[block(512, 1024), block(1024, 768)] * 2 + [block(8, 64, 512)] * len(more),
+            out_specs=[block(4, 64, width)] * 2,
+        ),
+        out_shape=[jax.ShapeDtypeStruct((4, 64, width), bf16)] * 2,
+        compiler_params=params(),
+        cost_estimate=cost(2 * 2048 * 512 * 768, 8 << 20),
+        name="qkv_grad",
+    )(info, nin_t.reshape(512, 1024), dproj, nin_t_sib.reshape(512, 1024), dproj_sib, *more)
+
+
+def input_norm_kernel(info, xo_ref, xt_ref, g_ref, own_ref, oth_ref, t_ref):
+    side = info[3]
+    for part, x_ref in ((0, xo_ref), (1, xt_ref)):
+        at = side if part == 0 else 1 - side
+        normed = (centred(x_ref[...].astype(f32))[0] * g_ref[:1]).astype(bf16)
+        t_ref[:, pl.ds(pl.multiple_of(at * HALF, HALF), HALF)] = normed.T
+    put_parities(info, t_ref, own_ref, oth_ref, 0)
+
+
+def input_norm(info, x_own, x_other, gains):
+    block = lambda *shape: pl.BlockSpec(shape, lambda i, s: (0,) * len(shape))
+    return pl.pallas_call(
+        input_norm_kernel,
+        grid_spec=pltpu.PrefetchScalarGridSpec(
+            num_scalar_prefetch=1,
+            grid=(1,),
+            in_specs=[block(HALF, 1024), block(HALF, 1024), block(2, 1024)],
+            out_specs=[block(1, 8, 64, 1024)] * 2,
+            scratch_shapes=[pltpu.VMEM((1024, 1024), bf16)],
+        ),
+        out_shape=[jax.ShapeDtypeStruct((1, 8, 64, 1024), bf16)] * 2,
+        compiler_params=params(),
+        cost_estimate=cost(20 << 20, 8 << 20),
+        name="input_norm",
+    )(info, x_own, x_other, gains)
+
+
+def slot_bias(phones, prompts, targets):
+    places = jnp.arange(HALF, dtype=jnp.int32)
+    count = phones.shape[0]
+    segs, is_phone = [], None
+    for lengths in (phones + prompts, targets):
+        ends = jnp.stack([sum(lengths[i] for i in range(upto + 1)) for upto in range(count)])
+        seg = jnp.sum((places[:, None] >= ends[None, :]).astype(jnp.int32), axis=1)
+        segs.append(seg)
+        if is_phone is None:
+            onehot = seg[:, None] == jnp.arange(count, dtype=jnp.int32)[None, :]
+            phone_ends = jnp.sum(jnp.where(onehot, (ends - lengths + phones)[None, :], 0), axis=1)
+            is_phone = places < phone_ends
+    seg = jnp.concatenate(segs)
+    phone = jnp.concatenate([is_phone, jnp.zeros((HALF,), dtype=bool)])
+    order = jnp.arange(2 * HALF, dtype=jnp.int32)
+    allowed = (seg[:, None] == seg[None, :]) & (
+        phone[:, None] | (jnp.logical_not(phone)[None, :] & (order[:, None] <= order[None, :]))
+    )
+    return jnp.where(allowed, 0.0, NEG).astype(f32)
+
+
+def line_shards(tokens, cotangent, gains, w_qkv, w_out, w_up, w_down, phone_len, prompt_len, target_len):
+    r = lax.axis_index("rows")
+    side = lax.axis_index("pair")
+    info = jnp.stack([r // 4, r // 2 % 2, r % 2, side]).astype(jnp.int32)
+    x_own = tokens[0]
+    cot = cotangent[0]
+
+    gain_lanes = jnp.pad(gains, ((0, 0), (0, 127)))
+    crossed = swap_y(jnp.concatenate([w_qkv[:, 512:1024], gain_lanes], axis=1))
+    first, middle, last = w_qkv[:, :512], crossed[:, :512], w_qkv[:, 1024:]
+    q = jnp.where(side == 0, first, middle)
+    k = jnp.where(side == 0, last, first)
+    v = jnp.where(side == 0, middle, last)
+    gain_own, gain_got = gains, crossed[:, 512:513]
+    gain_pair = jnp.where(
+        side == 0, jnp.concatenate([gain_own, gain_got], axis=1), jnp.concatenate([gain_got, gain_own], axis=1)
+    )
+    heads = jnp.concatenate(
+        [m[:, i : i + 256] for i in (0, 256) for m in (q, k, v)] + [jnp.pad(gain_pair, ((0, 0), (0, 126)))], axis=1
+    )
+    heads, x_send = lax.optimization_barrier((heads, x_own))
+    pieces = [heads] + [shift_z(heads, j) for j in range(1, LINE)]
+    x_other = swap_y(x_send)
+    beside = [swap_x(p) for p in pieces]
+    pieces, up_out, w_down_in = lax.optimization_barrier((pieces, jnp.concatenate([w_up, w_out], axis=1), w_down))
+    up_line = along_line(up_out)
+    qkv_line = jnp.stack(pieces)
+    qkv_line_sib = swap_c(qkv_line)
+    beside = jnp.stack(beside)
+    beside_sib = swap_c(beside)
+    qkv_a = jnp.concatenate([qkv_line, beside])
+    qkv_b = jnp.concatenate([qkv_line_sib, beside_sib])
+
+    bias = slot_bias(phone_len[0], prompt_len[0], target_len[0])
+    cot_t = cot.T
+    projected, gain_all = project(info, after(x_own, cot_t, bias), x_other, qkv_a, qkv_b)
+    projected, up_line, w_down_in = lax.optimization_barrier((projected, up_line, w_down_in))
+    up_x, up_y = swap_x(up_line), swap_y(up_line)
+    down_line = along_line(w_down_in)
+    keep0, send0, lse0 = attend(info, projected, bias, 0)
+    bias, keep0, send0, up_x, up_y = lax.optimization_barrier((bias, keep0, send0, up_x, up_y))
+    got0 = swap_y(send0)
+    up_far = [swap_y(up_x[:2]), swap_x(up_y[2:])]
+    keep1, send1, lse1 = attend(info, projected, after(bias, keep0), 1)
+    keep1, send1, up_far, down_line = lax.optimization_barrier((keep1, send1, up_far, down_line))
+    got1 = swap_y(send1)
+    up_a = jnp.concatenate([up_line, up_x, up_y, *up_far])
+    up_b = swap_c(up_a)
+    down_x, down_y = swap_x(down_line), swap_y(down_line)
+    nin_t, nin_t_oth = input_norm(info, after(x_own, keep1, up_a), x_other, gain_all)
+    got0, got1, nin_t_oth, cot_t, up_b = lax.optimization_barrier((got0, got1, nin_t_oth, cot_t, up_b))
+    nin_t_sib = swap_c(nin_t_oth)
+    cot_t_sib = swap_c(cot_t)
+    mid, normed_mid, sides_t, sides_t_oth = attention_out(info, x_own, (keep0, keep1), (got0, got1), up_a, up_b, gain_all)
+    sides_t_sib = swap_c(sides_t_oth)
+    down_x, down_y, normed_mid = lax.optimization_barrier((down_x, down_y, normed_mid))
+    down_far = [swap_y(down_x[:2]), swap_x(down_y[2:])]
+    act, act_oth, slope, slope_oth = up(info, normed_mid, up_a, up_b)
+    down_far, act_oth = lax.optimization_barrier((down_far, act_oth))
+    down_a = jnp.concatenate([down_line, down_x, down_y, *down_far])
+    down_b = swap_c(down_a)
+    act_sib = swap_c(act_oth)
+    mixed, gp = down(info, (act, act_oth), (slope, slope_oth), down_a, down_b, cot, mid)
+    gp_sib = swap_c(gp)
+
+    far_a, far_b, beside, across, own = down_grad(info, cot_t, after(act, gp), cot_t_sib, act_sib)
+    got_a, got_b = swap_x(far_a), swap_y(far_b)
+    gm, gb, ga_keep0, ga_keep1, ga_send0, ga_send1 = middle_back(info, after(gp, own), up_a, up_b, cot, mid, gain_all)
+    ga_got0, ga_got1 = swap_y(ga_send0), swap_y(ga_send1)
+    gb_sib = swap_c(gb)
+    got_a, got_b, gb = lax.optimization_barrier((got_a, got_b, gb))
+    down_x = swap_x(jnp.concatenate([beside[:2], plus(beside[2:], got_b)]))
+    down_y = swap_y(jnp.concatenate([plus(across[:2], got_a), across[2:]]))
+    down_own = own
+    far_a, far_b, beside, across, own = up_grad(info, sides_t, after(gp, gb), sides_t_sib, gp_sib)
+    out_keep, out_send = out_grad(info, sides_t, after(gb, own), sides_t_sib, gb_sib)
+    out_got = swap_y(out_send)
+    got_a, got_b = swap_x(far_a), swap_y(far_b)
+    dproj0 = attend_back(info, projected, after(bias, out_keep), lse0, ga_keep0, ga_got0, 0)
+    dproj0_sib = swap_c(dproj0)
+    dproj0, down_x, down_y, got_a, got_b = lax.optimization_barrier((dproj0, down_x, down_y, got_a, got_b))
+    down_parts = [
+        (down_own[k].astype(f32) + down_x[k].astype(f32) + down_y[k].astype(f32)).astype(bf16) for k in range(LINE)
+    ]
+    down_shift = [shift_z(down_parts[k], k) for k in range(1, LINE)]
+    up_x = swap_x(jnp.concatenate([beside[:2], plus(beside[2:], got_b)]))
+    up_y = swap_y(jnp.concatenate([plus(across[:2], got_a), across[2:]]))
+    up_own = own
+    e_first = input_part(info, after(dproj0, down_parts), qkv_a, qkv_b, 0)
+    beside, own = qkv_grad(info, nin_t, after(dproj0, e_first), nin_t_sib, dproj0_sib, (out_keep, out_got))
+    first_x = swap_x(beside)
+    first_own = own
+    dproj1 = attend_back(info, projected, after(bias, own), lse1, ga_keep1, ga_got1, 1)
+    dproj1_sib = swap_c(dproj1)
+    dproj1, up_x, up_y, first_x, down_shift = lax.optimization_barrier((dproj1, up_x, up_y, first_x, down_shift))
+    e_send = input_part(info, dproj1, qkv_a, qkv_b, 1, 1, e_first)
+    e_got = swap_y(e_send)
+    up_parts = [
+        (up_own[k].astype(f32) + up_x[k].astype(f32) + up_y[k].astype(f32)).astype(bf16) for k in range(LINE)
+    ]
+    first_parts = [plus(first_own[k], first_x[k]) for k in range(LINE)]
+    up_parts, first_parts, dproj1_late = lax.optimization_barrier((up_parts, first_parts, dproj1))
+    up_shift = [shift_z(up_parts[k], k) for k in range(1, LINE)]
+    first_shift = [shift_z(first_parts[k], k) for k in range(1, LINE)]
+    beside, own = qkv_grad(info, nin_t, after(dproj1_late, e_send), nin_t_sib, dproj1_sib)
+    second_x = swap_x(beside)
+    e_own = input_part(info, after(dproj1, own), qkv_a, qkv_b, 1, 0, e_first)
+    g_down = sum([p.astype(f32) for p in down_shift], down_parts[0].astype(f32)).T
+    g_second = summed_line([plus(own[k], after(second_x, e_own)[k]) for k in range(LINE)])
+    g_up = sum([p.astype(f32) for p in up_shift], up_parts[0].astype(f32))
+    g_first = sum([p.astype(f32) for p in first_shift], first_parts[0].astype(f32))
+    g_out = g_first[:, 768:]
+    gq, gk, gv = (
+        jnp.concatenate([g_first[:, j : j + 256], g_second[:, j : j + 256]], axis=1) for j in (0, 256, 512)
+    )
+
+    crossed = swap_y(jnp.where(side == 0, gv, gq))
+    g_qkv = jnp.where(
+        side == 0, jnp.concatenate([gq, crossed, gk], axis=1), jnp.concatenate([gk, crossed, gv], axis=1)
+    )
+    in_sum = jnp.sum(w_qkv.astype(f32) * g_qkv, axis=1, keepdims=True)
+    mid_sum = jnp.sum(w_up.astype(f32) * g_up, axis=1, keepdims=True)
+    gain_sum = jnp.where(side == 0, in_sum, mid_sum) + swap_y(jnp.where(side == 0, mid_sum, in_sum))
+    grad_gains = gain_sum / gains.astype(f32)
+
+    n, scale = centred(x_own.astype(f32))
+    eg = (e_own + e_got.astype(f32)) * lax.dynamic_slice_in_dim(gain_all, 0, 1, 0)
+    lean = eg - jnp.mean(eg, axis=-1, keepdims=True) - n * jnp.mean(eg * n, axis=-1, keepdims=True)
+    grad_tokens = gm + scale * lean
+    return (mixed[None], grad_tokens[None], grad_gains, g_qkv, g_out, g_up, g_down)
+
+
 def solution(mesh):
+    lined = mesh.shape["rows"] == 4 * LINE and mesh.shape["pair"] == 2
     return jax.shard_map(
-        shards,
+        line_shards if lined else shards,
         mesh=mesh,
         in_specs=(
             P("rows", "pair", None),

time: 931 us -> 480 us (0.52)
  waiting for transfers between devices: 496 us -> 146 us
  matrix products: 204 us -> 0 us
  Pallas kernels: 0 us -> 191 us
  starting transfers between devices: 7.22 us -> 69.2 us
  blocking collectives: 59 us -> 0 us
  other arithmetic: 82.5 us -> 29.4 us
  local copies, waits for them, and re-layouts: 57.3 us -> 30.6 us
  between operations: 17.2 us -> 4.7 us
    reduce_scatter x8 -> x0, waiting for transfers between devices: 327 us -> none  [the longest x1 108 us: shards(): lax.psum_scatter(grad_up.astype(jnp.bfloat16), 'rows', scatter_dimension=...]
    pallas_call x0 -> x18, Pallas kernels: none -> 191 us  [the longest x2 30.7 us: attend_back(): pl.pallas_call(attend_back_kernel, grid_spec=pltpu.PrefetchScalarGridSpec...]
    dot_general x32 -> x0, matrix products: 161 us -> none  [the longest x1 27.9 us: shards(): jnp.dot(normed_mid_low, up_all, preferred_element_type=jnp.float32)]
    ppermute x2 -> x65, waiting for transfers between devices: 79.3 us -> 146 us  [the longest x18 69.2 us: swap_y(): return lax.ppermute(v, 'pair', [(0, 1), (1, 0)])]
    ppermute x2 -> x65, starting transfers between devices: 6.23 us -> 69.2 us  [the longest x21 29.8 us: shift_z(): return lax.ppermute(v, 'rows', row_pairs(lambda z, x, c: (z + k, x, c)))]
    all_gather x6 -> x0, blocking collectives: 54 us -> none  [the longest x1 18.9 us: shards(): lax.all_gather(paired[0], 'rows', axis=0, tiled=True)]
    unnamed x14 -> x0, waiting for transfers between devices: 47.5 us -> none
    all_gather x4 -> x0, waiting for transfers between devices: 43 us -> none  [the longest x1 29.3 us: shards(): lax.all_gather(paired[4], 'rows', axis=0, tiled=True)]
  transfers between devices with their start and end apart: 15 -> 65, of which waited for: 12 -> 26; matrix products, arithmetic and copies ran while one was open for 20% -> 9% of each run, Pallas kernels for 0% -> 35%
where the time goes in v2:
time: 480 us; the launch traced here: 471 us
  Pallas kernels  191 us (40%)
  waiting for transfers between devices  146 us (30%)
  starting transfers between devices  69.2 us (14%)
  local copies, waits for them, and re-layouts  30.6 us (6%)
  other arithmetic  29.4 us (6%)
    ppermute x18, waiting for transfers between devices, swap_y(): return lax.ppermute(v, 'pair', [(0, 1), (1, 0)])  69.2 us
    ppermute x21, waiting for transfers between devices, shift_z(): return lax.ppermute(v, 'rows', row_pairs(lambda z, x, c: (z + k, x, c)))  43.8 us
    pallas_call x2, Pallas kernels, attend_back(): pl.pallas_call(attend_back_kernel, grid_spec=pltpu.PrefetchScalarGridSpec...  30.7 us
    ppermute x21, starting transfers between devices, shift_z(): return lax.ppermute(v, 'rows', row_pairs(lambda z, x, c: (z + k, x, c)))  29.8 us
    pallas_call x2, Pallas kernels, attend(): pl.pallas_call(attend_kernel, grid_spec=pltpu.PrefetchScalarGridSpec(num_...  28.6 us
    ppermute x18, starting transfers between devices, swap_y(): return lax.ppermute(v, 'pair', [(0, 1), (1, 0)])  20.7 us
    pallas_call x3, Pallas kernels, input_part(): pl.pallas_call(functools.partial(input_part_kernel, group, part), grid_sp...  20.2 us
    pallas_call x1, Pallas kernels, middle_back(): pl.pallas_call(middle_back_kernel, grid_spec=pltpu.PrefetchScalarGridSpec...  19.4 us
  transfers between devices with their start and end apart: 65, of which 26 were waited for; matrix products, arithmetic and copies ran while one was open for 9% of the time, Pallas kernels for 35%

profile of v2, /device:TPU:8, one launch (start us, length us, event | category | flops | bytes accessed | tf_op | source)
XLA Modules:
  0.0 471.5 jit_solution(12819694271478910022)
XLA Ops:
  18.8 2.9 fusion.3.bias_ref
  24.3 6.3 %collective-permute-done.2 = bf16[64,1664]{1,0:T(8,128)(2,1)S(1)} collective-permute-done((bf16[64,1664]{1,0:T(8,128)(2,1)S(1)}, bf16[64,1664]{1,0:T(8,128)(2,1)S(1)}, u32[]{:S(2)}, u32[]{:S(2)}) %collective-permute-start.2) | collective-permute-done | bytes 213024 | tf_op jit(solution)/shard_map/ppermute | solution.py:297
  30.6 3.1 collective-permute-done.3
  41.0 4.5 collective-permute-done.6
  47.0 5.5 %collective-permute-done.7 = bf16[64,1664]{1,0:T(8,128)(2,1)S(1)} collective-permute-done((bf16[64,1664]{1,0:T(8,128)(2,1)S(1)}, bf16[64,1664]{1,0:T(8,128)(2,1)S(1)}, u32[]{:S(2)}, u32[]{:S(2)}) %collective-permute-start.7) | collective-permute-done | bytes 213024 | tf_op jit(solution)/shard_map/ppermute | solution.py:301
  54.1 4.3 collective-permute-done.8
  59.2 4.8 %collective-permute-done.12 = bf16[64,2560]{1,0:T(8,128)(2,1)S(1)} collective-permute-done((bf16[64,2560]{1,0:T(8,128)(2,1)S(1)}, bf16[64,2560]{1,0:T(8,128)(2,1)S(1)}, u32[]{:S(2)}, u32[]{:S(2)}) %collective-permute-start.12) | collective-permute-done | bytes 327712 | tf_op jit(solution)/shard_map/ppermute | solution.py:297
  67.3 9.9 %project.1 = (bf16[1024,1536]{1,0:T(8,128)(2,1)}, f32[2,1024]{1,0:T(2,128)}) custom-call(s32[4]{0:T(128)} %pad_add_fusion.1.info, bf16[512,1024]{1,0:T(8,128)(2,1)} %bitcast.96, bf16[512,1024]{1,0:T(8,128)(2,1)} %copy-done.10, bf16[8,64,1664]{2,1,0:T(8,128)(2,1)} %copy-done.6, bf16[8,64,1664]{2,1,0:T(8,128)(2,1)} %copy-done.5), custom_call_target="tpu_custom_call" | custom-call | flops 50331648 | bytes 131072 | tf_op jit(solution)/shard_map/project/pallas_call | solution.py:400
  79.3 2.6 collective-permute-start.19
  82.0 2.2 collective-permute-start.20
  84.2 14.1 %attend.2 = (bf16[512,256]{1,0:T(8,128)(2,1)}, bf16[512,256]{1,0:T(8,128)(2,1)}, f32[2,2,1024]{2,1,0:T(2,128)}) custom-call(s32[4]{0:T(128)} %pad_add_fusion.1.info, bf16[1024,1536]{1,0:T(8,128)(2,1)} %get-tuple-element.129.q_ref.k_ref.v_ref, bf16[1024,1536]{1,0:T(8,128)(2,1)} %get-tuple-element.129.q_ref.k_ref.v_ref, ...), custom_call_target="tpu_custom_call" | custom-call | flops 50331648 | bytes 131072 | tf_op jit(solution)/shard_map/attend/pallas_call | solution.py:462
  98.4 3.3 collective-permute-done.19
  101.7 2.6 collective-permute-done.20
  113.6 14.5 %attend.3 = (bf16[512,256]{1,0:T(8,128)(2,1)}, bf16[512,256]{1,0:T(8,128)(2,1)}, f32[2,2,1024]{2,1,0:T(2,128)}) custom-call(s32[4]{0:T(128)} %pad_add_fusion.1.info, bf16[1024,1536]{1,0:T(8,128)(2,1)} %get-tuple-element.129.q_ref.k_ref.v_ref, bf16[1024,1536]{1,0:T(8,128)(2,1)} %get-tuple-element.129.q_ref.k_ref.v_ref, ...), custom_call_target="tpu_custom_call" | custom-call | flops 50331648 | bytes 131072 | tf_op jit(solution)/shard_map/attend/pallas_call | solution.py:462
  136.2 5.3 %input_norm.1 = (bf16[1,8,64,1024]{3,2,1,0:T(8,128)(2,1)}, bf16[1,8,64,1024]{3,2,1,0:T(8,128)(2,1)}) custom-call(s32[4]{0:T(128)} %pad_add_fusion.1.info, bf16[512,1024]{1,0:T(8,128)(2,1)} %bitcast.97, bf16[512,1024]{1,0:T(8,128)(2,1)} %copy-done.10, f32[2,1024]{1,0:T(2,128)} %get-tuple-element.148.g_ref), custom_call_target="tpu_custom_call" | custom-call | flops 327680 | bytes 131072 | tf_op jit(solution)/shard_map/input_norm/pallas_call | solution.py:941
  141.5 22.8 %collective-permute-done.23.g0 = bf16[512,256]{1,0:T(8,128)(2,1)S(1)} collective-permute-done((bf16[512,256]{1,0:T(8,128)(2,1)}, bf16[512,256]{1,0:T(8,128)(2,1)S(1)}, u32[]{:S(2)}, u32[]{:S(2)}) %collective-permute-start.23) | collective-permute-done | bytes 262176 | tf_op jit(solution)/shard_map/ppermute | solution.py:309
  164.2 4.8 %collective-permute-done.24.g1 = bf16[512,256]{1,0:T(8,128)(2,1)S(1)} collective-permute-done((bf16[512,256]{1,0:T(8,128)(2,1)}, bf16[512,256]{1,0:T(8,128)(2,1)S(1)}, u32[]{:S(2)}, u32[]{:S(2)}) %collective-permute-start.24) | collective-permute-done | bytes 262176 | tf_op jit(solution)/shard_map/ppermute | solution.py:309
  169.8 8.0 %attention_out.1 = (f32[512,1024]{1,0:T(8,128)}, bf16[512,1024]{1,0:T(8,128)(2,1)}, bf16[2,8,64,512]{3,2,1,0:T(8,128)(2,1)}, bf16[2,8,64,512]{3,2,1,0:T(8,128)(2,1)}) custom-call(s32[4]{0:T(128)} %pad_add_fusion.1.info, bf16[512,1024]{1,0:T(8,128)(2,1)} %bitcast.98, bf16[512,256]{1,0:T(8,128)(2,1)} %get-tuple-element.134.k0, ...), custom_call_target="tpu_custom_call" | custom-call | flops 16777216 | bytes 131072 | tf_op jit(solution)/shard_map/attention_out/pallas_call | solution.py:575
  181.9 13.8 %up.1 = (bf16[2,512,1024]{2,1,0:T(8,128)(2,1)}, bf16[2,512,1024]{2,1,0:T(8,128)(2,1)}, bf16[2,512,1024]{2,1,0:T(8,128)(2,1)}, bf16[2,512,1024]{2,1,0:T(8,128)(2,1)}) custom-call(s32[4]{0:T(128)} %pad_add_fusion.1.info, bf16[512,1024]{1,0:T(8,128)(2,1)} %get-tuple-element.154.x_ref, bf16[16,64,2560]{2,1,0:T(8,128)(2,1)} %copy-done.2, ...), custom_call_target="tpu_custom_call" | custom-call | flops 134217728 | bytes 278528 | tf_op jit(solution)/shard_map/up/pallas_call | solution.py:630
  197.3 7.1 %collective-permute-done.28.refs_4_.refs_5_.refs_6_.refs_7_ = bf16[16,256,512]{2,1,0:T(8,128)(2,1)S(1)} collective-permute-done((bf16[16,256,512]{2,1,0:T(8,128)(2,1)S(1)}, bf16[16,256,512]{2,1,0:T(8,128)(2,1)S(1)}, u32[]{:S(2)}, u32[]{:S(2)}) %collective-permute-start.28) | collective-permute-done | bytes 4194336 | tf_op jit(solution)/shard_map/ppermute | solution.py:305
  206.4 18.5 %down.1 = (bf16[512,1024]{1,0:T(8,128)(2,1)}, bf16[512,4096]{1,0:T(8,128)(2,1)}) custom-call(s32[4]{0:T(128)} %pad_add_fusion.1.info, bf16[2,512,1024]{2,1,0:T(8,128)(2,1)} %get-tuple-element.168.act0.r0_ref, bf16[2,512,1024]{2,1,0:T(8,128)(2,1)} %get-tuple-element.159.act1, bf16[2,512,1024]{2,1,0:T(8,128)(2,1)} %get-tuple-element.160.slope0, ...), custom_call_target="tpu_custom_call" | custom-call | flops 134217728 | bytes 409600 | tf_op jit(solution)/shard_map/down/pallas_call | solution.py:684
  227.0 9.7 %collective-permute-done.29 = bf16[1024,512]{0,1:T(8,128)(2,1)} collective-permute-done((bf16[1024,512]{0,1:T(8,128)(2,1)S(1)}, bf16[1024,512]{0,1:T(8,128)(2,1)}, u32[]{:S(2)}, u32[]{:S(2)}) %collective-permute-start.29) | collective-permute-done | bytes 1048608 | tf_op jit(solution)/shard_map/ppermute | solution.py:305
  236.7 2.3 copy.35.l1_ref
  239.0 9.8 %down_grad.1 = (bf16[2,512,256]{2,1,0:T(8,128)(2,1)}, bf16[2,512,256]{2,1,0:T(8,128)(2,1)}, bf16[4,512,256]{2,1,0:T(8,128)(2,1)}, bf16[4,512,256]{2,1,0:T(8,128)(2,1)}, bf16[4,512,256]{2,1,0:T(8,128)(2,1)}) custom-call(s32[4]{0:T(128)} %pad_add_fusion.1.info, bf16[1024,512]{1,0:T(8,128)(2,1)} %copy.34.l0_ref, ...), custom_call_target="tpu_custom_call" | custom-call | flops 67108864 | bytes 196608 | tf_op jit(solution)/shard_map/down_grad/pallas_call | solution.py:785
  253.1 19.4 %middle_back.1 = (f32[512,1024]{1,0:T(8,128)}, bf16[512,1024]{1,0:T(8,128)(2,1)}, bf16[512,256]{1,0:T(8,128)(2,1)}, bf16[512,256]{1,0:T(8,128)(2,1)}, bf16[512,2...) custom-call(s32[4]{0:T(128)} %pad_add_fusion.1.info, bf16[512,4096]{1,0:T(8,128)(2,1)} %get-tuple-element.178.gp_ref.r0_ref, ...), custom_call_target="tpu_custom_call" | custom-call | flops 83886080 | bytes 327680 | tf_op jit(solution)/shard_map/middle_back/pallas_call | solution.py:729
  276.7 10.1 %up_grad.1 = (bf16[2,64,2048]{2,1,0:T(8,128)(2,1)}, bf16[2,64,2048]{2,1,0:T(8,128)(2,1)}, bf16[4,64,2048]{2,1,0:T(8,128)(2,1)}, bf16[4,64,2048]{2,1,0:T(8,128)(2,1)}, bf16[4,64,2048]{2,1,0:T(8,128)(2,1)}) custom-call(s32[4]{0:T(128)} %pad_add_fusion.1.info, bf16[1024,512]{1,0:T(8,128)(2,1)} %bitcast.108, bf16[512,4096]{1,0:T(8,128)(2,1)} %get-tuple-element.178.gp_ref.r0_ref, ...), custom_call_target="tpu_custom_call" | custom-call | flops 67108864 | bytes 229376 | tf_op jit(solution)/shard_map/up_grad/pallas_call | solution.py:826
  290.4 4.7 out_grad.1
  295.2 20.1 %collective-permute-done.36.send_ref = bf16[512,256]{1,0:T(8,128)(2,1)S(1)} collective-permute-done((bf16[512,256]{1,0:T(8,128)(2,1)S(1)}, bf16[512,256]{1,0:T(8,128)(2,1)S(1)}, u32[]{:S(2)}, u32[]{:S(2)}) %collective-permute-start.36) | collective-permute-done | bytes 262176 | tf_op jit(solution)/shard_map/ppermute | solution.py:309
  316.1 15.3 %attend_back.2.d_ref.r0_ref = bf16[1024,768]{1,0:T(8,128)(2,1)} custom-call(s32[4]{0:T(128)} %pad_add_fusion.1.info, bf16[1024,1536]{1,0:T(8,128)(2,1)} %get-tuple-element.129.q_ref.k_ref.v_ref, bf16[1024,1536]{1,0:T(8,128)(2,1)} %get-tuple-element.129.q_ref.k_ref.v_ref, bf16[1024,1536]{1,0:T(8,128)(2,1)} %get-tuple-element.129.q_ref.k_ref.v_ref, ...), custom_call_target="tpu_custom_call" | custom-call | flops 125829120 | bytes 163840 | tf_op jit(solution)/shard_map/attend_back/pallas_call | solution.py:511
  338.7 7.7 %input_part.3.refs_0_ = f32[1024,1024]{1,0:T(8,128)} custom-call(s32[4]{0:T(128)} %pad_add_fusion.1.info, bf16[1024,768]{1,0:T(8,128)(2,1)} %attend_back.2.d_ref.r0_ref, bf16[8,64,1664]{2,1,0:T(8,128)(2,1)} %copy-done.6, bf16[8,64,1664]{2,1,0:T(8,128)(2,1)} %copy-done.5), custom_call_target="tpu_custom_call" | custom-call | flops 25165824 | bytes 131072 | tf_op jit(solution)/shard_map/input_part/pallas_call | solution.py:884
  349.2 6.5 %qkv_grad.2 = (bf16[4,64,1280]{2,1,0:T(8,128)(2,1)}, bf16[4,64,1280]{2,1,0:T(8,128)(2,1)}) custom-call(s32[4]{0:T(128)} %pad_add_fusion.1.info, bf16[512,1024]{1,0:T(8,128)(2,1)} %bitcast.104, bf16[1024,768]{1,0:T(8,128)(2,1)} %attend_back.2.d_ref.r0_ref, bf16[512,1024]{1,0:T(8,128)(2,1)} %bitcast.106, bf16[1024,768]{1,0:T(8,128)(2,1)} %copy-done.14, ...), custom_call_target="tpu_custom_call" | custom-call | flops 25165824 | bytes 131072 | tf_op jit(solution)/shard_map/qkv_grad/pallas_call | solution.py:915
  357.4 16.7 %collective-permute-done.44.send_ref = bf16[512,256]{1,0:T(8,128)(2,1)S(1)} collective-permute-done((bf16[512,256]{1,0:T(8,128)(2,1)S(1)}, bf16[512,256]{1,0:T(8,128)(2,1)S(1)}, u32[]{:S(2)}, u32[]{:S(2)}) %collective-permute-start.44) | collective-permute-done | bytes 262176 | tf_op jit(solution)/shard_map/ppermute | solution.py:309
  374.1 2.3 collective-permute-start.49
  376.9 15.4 %attend_back.3.d_ref.r0_ref = bf16[1024,768]{1,0:T(8,128)(2,1)} custom-call(s32[4]{0:T(128)} %pad_add_fusion.1.info, bf16[1024,1536]{1,0:T(8,128)(2,1)} %get-tuple-element.129.q_ref.k_ref.v_ref, bf16[1024,1536]{1,0:T(8,128)(2,1)} %get-tuple-element.129.q_ref.k_ref.v_ref, bf16[1024,1536]{1,0:T(8,128)(2,1)} %get-tuple-element.129.q_ref.k_ref.v_ref, ...), custom_call_target="tpu_custom_call" | custom-call | flops 125829120 | bytes 163840 | tf_op jit(solution)/shard_map/attend_back/pallas_call | solution.py:511
  393.5 2.8 fusion.22
  398.4 2.4 collective-permute-start.54
  400.8 6.1 %input_part.4 = bf16[512,1024]{1,0:T(8,128)(2,1)} custom-call(s32[4]{0:T(128)} %pad_add_fusion.1.info, bf16[1024,768]{1,0:T(8,128)(2,1)} %attend_back.3.d_ref.r0_ref, bf16[8,64,1664]{2,1,0:T(8,128)(2,1)} %copy-done.6, bf16[8,64,1664]{2,1,0:T(8,128)(2,1)} %copy-done.5, f32[1024,1024]{1,0:T(8,128)} %input_part.3.refs_0_), custom_call_target="tpu_custom_call" | custom-call | flops 12582912 | bytes 131072 | tf_op jit(solution)/shard_map/input_part/pallas_call | solution.py:884
  410.1 2.6 collective-permute-start.61
  413.8 3.4 collective-permute-start.62
  417.2 9.9 %collective-permute-done.55 = bf16[64,1280]{1,0:T(8,128)(2,1)} collective-permute-done((bf16[64,1280]{1,0:T(8,128)(2,1)S(1)}, bf16[64,1280]{1,0:T(8,128)(2,1)}, u32[]{:S(2)}, u32[]{:S(2)}) %collective-permute-start.55) | collective-permute-done | bytes 163872 | tf_op jit(solution)/shard_map/ppermute | solution.py:297
  429.6 5.9 %qkv_grad.3 = (bf16[4,64,768]{2,1,0:T(8,128)(2,1)}, bf16[4,64,768]{2,1,0:T(8,128)(2,1)}) custom-call(s32[4]{0:T(128)} %pad_add_fusion.1.info, bf16[512,1024]{1,0:T(8,128)(2,1)} %bitcast.105, bf16[1024,768]{1,0:T(8,128)(2,1)} %attend_back.3.d_ref.r0_ref, bf16[512,1024]{1,0:T(8,128)(2,1)} %bitcast.107, bf16[1024,768]{1,0:T(8,128)(2,1)} %collective-permute-done.51.r1_ref), custom_call_target="tpu_custom_call" | custom-call | flops 25165824 | bytes 131072 | tf_op jit(solution)/shard_map/qkv_grad/pallas_call | solution.py:915
  438.7 6.4 %input_part.5 = f32[512,1024]{1,0:T(8,128)} custom-call(s32[4]{0:T(128)} %pad_add_fusion.1.info, bf16[1024,768]{1,0:T(8,128)(2,1)} %attend_back.3.d_ref.r0_ref, bf16[8,64,1664]{2,1,0:T(8,128)(2,1)} %copy-done.6, bf16[8,64,1664]{2,1,0:T(8,128)(2,1)} %copy-done.5, f32[1024,1024]{1,0:T(8,128)} %input_part.3.refs_0_), custom_call_target="tpu_custom_call" | custom-call | flops 12582912 | bytes 131072 | tf_op jit(solution)/shard_map/input_part/pallas_call | solution.py:884
  445.2 2.4 fusion.14
  448.3 3.3 collective-permute-start.58
  453.2 4.1 collective-permute-done.58
  457.4 2.4 collective-permute-done.59
  462.3 3.5 collective-permute-done.60
  468.4 2.1 fusion.12
  (286 shorter events, 108.3 us)
Async XLA Ops:
  14.2 16.5 %collective-permute-start.2 = (bf16[64,1664]{1,0:T(8,128)(2,1)S(1)}, bf16[64,1664]{1,0:T(8,128)(2,1)S(1)}, u32[]{:S(2)}, u32[]{:S(2)}) collective-permute-start(bf16[64,1664]{1,0:T(8,128)(2,1)S(1)} %constant_dynamic-update-slice_fusion), channel_id=1, source_target_pairs={{0,8},{2,10},{4,12},{6,14},{8,16},{10,18},{12,20},{14,22},{16,24},... | collective-permute-start | bytes 638984 | tf_op jit(solution)/shard_map/ppermute | solution.py:297
  15.8 17.9 %collective-permute-start.3 = (bf16[64,1664]{1,0:T(8,128)(2,1)S(1)}, bf16[64,1664]{1,0:T(8,128)(2,1)S(1)}, u32[]{:S(2)}, u32[]{:S(2)}) collective-permute-start(bf16[64,1664]{1,0:T(8,128)(2,1)S(1)} %constant_dynamic-update-slice_fusion), channel_id=1, source_target_pairs={{0,16},{2,18},{4,20},{6,22},{8,24},{10,26},{12,28},{14,30},{16,0},... | collective-permute-start | bytes 638984 | tf_op jit(solution)/shard_map/ppermute | solution.py:297
  17.0 18.4 %collective-permute-start.4 = (bf16[64,1664]{1,0:T(8,128)(2,1)S(1)}, bf16[64,1664]{1,0:T(8,128)(2,1)S(1)}, u32[]{:S(2)}, u32[]{:S(2)}) collective-permute-start(bf16[64,1664]{1,0:T(8,128)(2,1)S(1)} %constant_dynamic-update-slice_fusion), channel_id=1, source_target_pairs={{0,24},{2,26},{4,28},{6,30},{8,0},{10,2},{12,4},{14,6},{16,8},{18,... | collective-permute-start | bytes 638984 | tf_op jit(solution)/shard_map/ppermute | solution.py:297
  22.3 16.9 %collective-permute-start.5 = (bf16[64,1664]{1,0:T(8,128)(2,1)S(1)}, bf16[64,1664]{1,0:T(8,128)(2,1)S(1)}, u32[]{:S(2)}, u32[]{:S(2)}) collective-permute-start(bf16[64,1664]{1,0:T(8,128)(2,1)S(1)} %constant_dynamic-update-slice_fusion), channel_id=1, source_target_pairs={{0,4},{2,6},{4,0},{6,2},{8,12},{10,14},{12,8},{14,10},{16,20},{18,... | collective-permute-start | bytes 638984 | tf_op jit(solution)/shard_map/ppermute | solution.py:301
  23.8 41.3 %collective-permute-start.1 = (bf16[512,1024]{1,0:T(8,128)(2,1)S(1)}, bf16[512,1024]{1,0:T(8,128)(2,1)S(1)}, u32[]{:S(2)}, u32[]{:S(2)}) collective-permute-start(bf16[512,1024]{1,0:T(8,128)(2,1)S(1)} %bitcast.99), channel_id=1, source_target_pairs={{0,1},{1,0},{2,3},{3,2},{4,5},{5,4},{6,7},{7,6},{8,9},{9,8},{10,11... | collective-permute-start | bytes 3145736 | tf_op jit(solution)/shard_map/ppermute | solution.py:309
  35.5 23.1 %collective-permute-start.11 = (bf16[64,2560]{1,0:T(8,128)(2,1)S(1)}, bf16[64,2560]{1,0:T(8,128)(2,1)S(1)}, u32[]{:S(2)}, u32[]{:S(2)}) collective-permute-start(bf16[64,2560]{1,0:T(8,128)(2,1)S(1)} %pad_maximum_fusion.8), channel_id=1, source_target_pairs={{0,8},{2,10},{4,12},{6,14},{8,16},{10,18},{12,20},{14,22},{16,24},... | collective-permute-start | bytes 983048 | tf_op jit(solution)/shard_map/ppermute | solution.py:297
  35.5 28.5 %collective-permute-start.12 = (bf16[64,2560]{1,0:T(8,128)(2,1)S(1)}, bf16[64,2560]{1,0:T(8,128)(2,1)S(1)}, u32[]{:S(2)}, u32[]{:S(2)}) collective-permute-start(bf16[64,2560]{1,0:T(8,128)(2,1)S(1)} %pad_maximum_fusion.8), channel_id=1, source_target_pairs={{0,16},{2,18},{4,20},{6,22},{8,24},{10,26},{12,28},{14,30},{16,0},... | collective-permute-start | bytes 983048 | tf_op jit(solution)/shard_map/ppermute | solution.py:297
  37.1 27.6 %collective-permute-start.13 = (bf16[64,2560]{1,0:T(8,128)(2,1)S(1)}, bf16[64,2560]{1,0:T(8,128)(2,1)S(1)}, u32[]{:S(2)}, u32[]{:S(2)}) collective-permute-start(bf16[64,2560]{1,0:T(8,128)(2,1)S(1)} %pad_maximum_fusion.8), channel_id=1, source_target_pairs={{0,24},{2,26},{4,28},{6,30},{8,0},{10,2},{12,4},{14,6},{16,8},{18,... | collective-permute-start | bytes 983048 | tf_op jit(solution)/shard_map/ppermute | solution.py:297
  77.3 30.9 %collective-permute-start.14 = (bf16[4,64,2560]{2,1,0:T(8,128)(2,1)S(1)}, bf16[4,64,2560]{2,1,0:T(8,128)(2,1)}, u32[]{:S(2)}, u32[]{:S(2)}) collective-permute-start(bf16[4,64,2560]{2,1,0:T(8,128)(2,1)S(1)} %pad_maximum_fusion), channel_id=1, source_target_pairs={{0,4},{2,6},{4,0},{6,2},{8,12},{10,14},{12,8},{14,10},{16,20},{18,... | collective-permute-start | bytes 3932168 | tf_op jit(solution)/shard_map/ppermute | solution.py:301
  78.8 30.5 %collective-permute-start.15 = (bf16[4,64,2560]{2,1,0:T(8,128)(2,1)S(1)}, bf16[4,64,2560]{2,1,0:T(8,128)(2,1)}, u32[]{:S(2)}, u32[]{:S(2)}) collective-permute-start(bf16[4,64,2560]{2,1,0:T(8,128)(2,1)S(1)} %pad_maximum_fusion), channel_id=1, source_target_pairs={{0,1},{1,0},{2,3},{3,2},{4,5},{5,4},{6,7},{7,6},{8,9},{9,8},{10,11... | collective-permute-start | bytes 3932168 | tf_op jit(solution)/shard_map/ppermute | solution.py:309
  79.3 19.0 %collective-permute-start.18 = (bf16[256,512]{1,0:T(8,128)(2,1)S(1)}, bf16[256,512]{1,0:T(8,128)(2,1)S(1)}, u32[]{:S(2)}, u32[]{:S(2)}) collective-permute-start(bf16[256,512]{1,0:T(8,128)(2,1)S(1)} %copy-done.36), channel_id=1, source_target_pairs={{0,8},{2,10},{4,12},{6,14},{8,16},{10,18},{12,20},{14,22},{16,24},... | collective-permute-start | bytes 786440 | tf_op jit(solution)/shard_map/ppermute | solution.py:297
  79.3 22.3 %collective-permute-start.19 = (bf16[256,512]{1,0:T(8,128)(2,1)S(1)}, bf16[256,512]{1,0:T(8,128)(2,1)S(1)}, u32[]{:S(2)}, u32[]{:S(2)}) collective-permute-start(bf16[256,512]{1,0:T(8,128)(2,1)S(1)} %copy-done.36), channel_id=1, source_target_pairs={{0,16},{2,18},{4,20},{6,22},{8,24},{10,26},{12,28},{14,30},{16,0},... | collective-permute-start | bytes 786440 | tf_op jit(solution)/shard_map/ppermute | solution.py:297
  82.0 22.3 %collective-permute-start.20 = (bf16[256,512]{1,0:T(8,128)(2,1)S(1)}, bf16[256,512]{1,0:T(8,128)(2,1)S(1)}, u32[]{:S(2)}, u32[]{:S(2)}) collective-permute-start(bf16[256,512]{1,0:T(8,128)(2,1)S(1)} %copy-done.36), channel_id=1, source_target_pairs={{0,24},{2,26},{4,28},{6,30},{8,0},{10,2},{12,4},{14,6},{16,8},{18,... | collective-permute-start | bytes 786440 | tf_op jit(solution)/shard_map/ppermute | solution.py:297
  110.5 20.4 %collective-permute-start.16 = (bf16[2,64,2560]{2,1,0:T(8,128)(2,1)S(1)}, bf16[2,64,2560]{2,1,0:T(8,128)(2,1)S(1)}, u32[]{:S(2)}, u32[]{:S(2)}) collective-permute-start(bf16[2,64,2560]{2,1,0:T(8,128)(2,1)S(1)} %slice.252), channel_id=1, source_target_pairs={{0,1},{1,0},{2,3},{3,2},{4,5},{5,4},{6,7},{7,6},{8,9},{9,8},{10,11... | collective-permute-start | bytes 1966088 | tf_op jit(solution)/shard_map/ppermute | solution.py:309
  113.0 17.8 %collective-permute-start.17 = (bf16[2,64,2560]{2,1,0:T(8,128)(2,1)}, bf16[2,64,2560]{2,1,0:T(8,128)(2,1)S(1)}, u32[]{:S(2)}, u32[]{:S(2)}) collective-permute-start(bf16[2,64,2560]{2,1,0:T(8,128)(2,1)} %slice.253), channel_id=1, source_target_pairs={{0,4},{2,6},{4,0},{6,2},{8,12},{10,14},{12,8},{14,10},{16,20},{18,... | collective-permute-start | bytes 1966088 | tf_op jit(solution)/shard_map/ppermute | solution.py:301
  131.0 38.1 %collective-permute-start.25 = (bf16[16,64,2560]{2,1,0:T(8,128)(2,1)S(1)}, bf16[16,64,2560]{2,1,0:T(8,128)(2,1)}, u32[]{:S(2)}, u32[]{:S(2)}) collective-permute-start(bf16[16,64,2560]{2,1,0:T(8,128)(2,1)S(1)} %constant_dynamic-update-slice_fusion.17.a_ref), channel_id=1, source_target_pairs={{0,2},{2,0},{4,6},{6,4},{8,10},{10,8},{12,14},{14,12},{16,18},{18,... | collective-permute-start | bytes 15728648 | tf_op jit(solution)/shard_map/ppermute | solution.py:305
  131.1 46.7 %collective-permute-start.21 = (bf16[4,256,512]{2,1,0:T(8,128)(2,1)S(1)}, bf16[4,256,512]{2,1,0:T(8,128)(2,1)S(1)}, u32[]{:S(2)}, u32[]{:S(2)}) collective-permute-start(bf16[4,256,512]{2,1,0:T(8,128)(2,1)S(1)} %pad_maximum_fusion.1), channel_id=1, source_target_pairs={{0,4},{2,6},{4,0},{6,2},{8,12},{10,14},{12,8},{14,10},{16,20},{18,... | collective-permute-start | bytes 3145736 | tf_op jit(solution)/shard_map/ppermute | solution.py:301
  132.6 45.2 %collective-permute-start.22 = (bf16[4,256,512]{2,1,0:T(8,128)(2,1)S(1)}, bf16[4,256,512]{2,1,0:T(8,128)(2,1)}, u32[]{:S(2)}, u32[]{:S(2)}) collective-permute-start(bf16[4,256,512]{2,1,0:T(8,128)(2,1)S(1)} %pad_maximum_fusion.1), channel_id=1, source_target_pairs={{0,1},{1,0},{2,3},{3,2},{4,5},{5,4},{6,7},{7,6},{8,9},{9,8},{10,11... | collective-permute-start | bytes 3145736 | tf_op jit(solution)/shard_map/ppermute | solution.py:309
  134.2 30.1 %collective-permute-start.23 = (bf16[512,256]{1,0:T(8,128)(2,1)}, bf16[512,256]{1,0:T(8,128)(2,1)S(1)}, u32[]{:S(2)}, u32[]{:S(2)}) collective-permute-start(bf16[512,256]{1,0:T(8,128)(2,1)} %get-tuple-element.143), channel_id=1, source_target_pairs={{0,1},{1,0},{2,3},{3,2},{4,5},{5,4},{6,7},{7,6},{8,9},{9,8},{10,11... | collective-permute-start | bytes 786440 | tf_op jit(solution)/shard_map/ppermute | solution.py:309
  134.6 34.4 %collective-permute-start.24 = (bf16[512,256]{1,0:T(8,128)(2,1)}, bf16[512,256]{1,0:T(8,128)(2,1)S(1)}, u32[]{:S(2)}, u32[]{:S(2)}) collective-permute-start(bf16[512,256]{1,0:T(8,128)(2,1)} %get-tuple-element.144), channel_id=1, source_target_pairs={{0,1},{1,0},{2,3},{3,2},{4,5},{5,4},{6,7},{7,6},{8,9},{9,8},{10,11... | collective-permute-start | bytes 786440 | tf_op jit(solution)/shard_map/ppermute | solution.py:309
  177.8 19.3 %collective-permute-start.26 = (bf16[2,256,512]{2,1,0:T(8,128)(2,1)S(1)}, bf16[2,256,512]{2,1,0:T(8,128)(2,1)S(1)}, u32[]{:S(2)}, u32[]{:S(2)}) collective-permute-start(bf16[2,256,512]{2,1,0:T(8,128)(2,1)S(1)} %slice.254), channel_id=1, source_target_pairs={{0,1},{1,0},{2,3},{3,2},{4,5},{5,4},{6,7},{7,6},{8,9},{9,8},{10,11... | collective-permute-start | bytes 1572872 | tf_op jit(solution)/shard_map/ppermute | solution.py:309
  181.3 15.8 %collective-permute-start.27 = (bf16[2,256,512]{2,1,0:T(8,128)(2,1)}, bf16[2,256,512]{2,1,0:T(8,128)(2,1)S(1)}, u32[]{:S(2)}, u32[]{:S(2)}) collective-permute-start(bf16[2,256,512]{2,1,0:T(8,128)(2,1)} %slice.255), channel_id=1, source_target_pairs={{0,4},{2,6},{4,0},{6,2},{8,12},{10,14},{12,8},{14,10},{16,20},{18,... | collective-permute-start | bytes 1572872 | tf_op jit(solution)/shard_map/ppermute | solution.py:301
  225.0 50.7 %collective-permute-start.34 = (bf16[512,4096]{1,0:T(8,128)(2,1)}, bf16[512,4096]{1,0:T(8,128)(2,1)}, u32[]{:S(2)}, u32[]{:S(2)}) collective-permute-start(bf16[512,4096]{1,0:T(8,128)(2,1)} %get-tuple-element.178.gp_ref.r0_ref), channel_id=1, source_target_pairs={{0,2},{2,0},{4,6},{6,4},{8,10},{10,8},{12,14},{14,12},{16,18},{18,... | collective-permute-start | bytes 12582920 | tf_op jit(solution)/shard_map/ppermute | solution.py:305
  248.8 24.3 %collective-permute-start.31 = (bf16[2,512,256]{2,1,0:T(8,128)(2,1)}, bf16[2,512,256]{2,1,0:T(8,128)(2,1)S(1)}, u32[]{:S(2)}, u32[]{:S(2)}) collective-permute-start(bf16[2,512,256]{2,1,0:T(8,128)(2,1)} %get-tuple-element.174), channel_id=1, source_target_pairs={{0,4},{2,6},{4,0},{6,2},{8,12},{10,14},{12,8},{14,10},{16,20},{18,... | collective-permute-start | bytes 1572872 | tf_op jit(solution)/shard_map/ppermute | solution.py:301
  250.4 22.7 %collective-permute-start.32 = (bf16[2,512,256]{2,1,0:T(8,128)(2,1)}, bf16[2,512,256]{2,1,0:T(8,128)(2,1)S(1)}, u32[]{:S(2)}, u32[]{:S(2)}) collective-permute-start(bf16[2,512,256]{2,1,0:T(8,128)(2,1)} %get-tuple-element.175), channel_id=1, source_target_pairs={{0,1},{1,0},{2,3},{3,2},{4,5},{5,4},{6,7},{7,6},{8,9},{9,8},{10,11... | collective-permute-start | bytes 1572872 | tf_op jit(solution)/shard_map/ppermute | solution.py:309
  250.9 24.7 %collective-permute-start.33 = (bf16[2,8,64,512]{3,2,1,0:T(8,128)(2,1)}, bf16[2,8,64,512]{3,2,1,0:T(8,128)(2,1)S(1)}, u32[]{:S(2)}, u32[]{:S(2)}) collective-permute-start(bf16[2,8,64,512]{3,2,1,0:T(8,128)(2,1)} %get-tuple-element.179), channel_id=1, source_target_pairs={{0,2},{2,0},{4,6},{6,4},{8,10},{10,8},{12,14},{14,12},{16,18},{18,... | collective-permute-start | bytes 3145736 | tf_op jit(solution)/shard_map/ppermute | solution.py:305
  272.5 16.3 %collective-permute-start.35 = (bf16[512,1024]{1,0:T(8,128)(2,1)}, bf16[512,1024]{1,0:T(8,128)(2,1)S(1)}, u32[]{:S(2)}, u32[]{:S(2)}) collective-permute-start(bf16[512,1024]{1,0:T(8,128)(2,1)} %get-tuple-element.181.r0_ref), channel_id=1, source_target_pairs={{0,2},{2,0},{4,6},{6,4},{8,10},{10,8},{12,14},{14,12},{16,18},{18,... | collective-permute-start | bytes 3145736 | tf_op jit(solution)/shard_map/ppermute | solution.py:305
  273.3 58.0 %collective-permute-start.38 = (bf16[4,512,256]{2,1,0:T(8,128)(2,1)S(1)}, bf16[4,512,256]{2,1,0:T(8,128)(2,1)}, u32[]{:S(2)}, u32[]{:S(2)}) collective-permute-start(bf16[4,512,256]{2,1,0:T(8,128)(2,1)S(1)} %pad_maximum_fusion.3), channel_id=1, source_target_pairs={{0,1},{1,0},{2,3},{3,2},{4,5},{5,4},{6,7},{7,6},{8,9},{9,8},{10,11... | collective-permute-start | bytes 3145736 | tf_op jit(solution)/shard_map/ppermute | solution.py:309
  275.1 56.4 %collective-permute-start.37 = (bf16[4,512,256]{2,1,0:T(8,128)(2,1)S(1)}, bf16[4,512,256]{2,1,0:T(8,128)(2,1)}, u32[]{:S(2)}, u32[]{:S(2)}) collective-permute-start(bf16[4,512,256]{2,1,0:T(8,128)(2,1)S(1)} %pad_maximum_fusion.2), channel_id=1, source_target_pairs={{0,4},{2,6},{4,0},{6,2},{8,12},{10,14},{12,8},{14,10},{16,20},{18,... | collective-permute-start | bytes 3145736 | tf_op jit(solution)/shard_map/ppermute | solution.py:301
  286.8 46.2 %collective-permute-start.39 = (bf16[2,64,2048]{2,1,0:T(8,128)(2,1)}, bf16[2,64,2048]{2,1,0:T(8,128)(2,1)}, u32[]{:S(2)}, u32[]{:S(2)}) collective-permute-start(bf16[2,64,2048]{2,1,0:T(8,128)(2,1)} %get-tuple-element.191), channel_id=1, source_target_pairs={{0,4},{2,6},{4,0},{6,2},{8,12},{10,14},{12,8},{14,10},{16,20},{18,... | collective-permute-start | bytes 1572872 | tf_op jit(solution)/shard_map/ppermute | solution.py:301
  288.3 44.7 %collective-permute-start.40 = (bf16[2,64,2048]{2,1,0:T(8,128)(2,1)}, bf16[2,64,2048]{2,1,0:T(8,128)(2,1)}, u32[]{:S(2)}, u32[]{:S(2)}) collective-permute-start(bf16[2,64,2048]{2,1,0:T(8,128)(2,1)} %get-tuple-element.192), channel_id=1, source_target_pairs={{0,1},{1,0},{2,3},{3,2},{4,5},{5,4},{6,7},{7,6},{8,9},{9,8},{10,11... | collective-permute-start | bytes 1572872 | tf_op jit(solution)/shard_map/ppermute | solution.py:309
  288.9 26.5 %collective-permute-start.36 = (bf16[512,256]{1,0:T(8,128)(2,1)S(1)}, bf16[512,256]{1,0:T(8,128)(2,1)S(1)}, u32[]{:S(2)}, u32[]{:S(2)}) collective-permute-start(bf16[512,256]{1,0:T(8,128)(2,1)S(1)} %copy-done.42), channel_id=1, source_target_pairs={{0,1},{1,0},{2,3},{3,2},{4,5},{5,4},{6,7},{7,6},{8,9},{9,8},{10,11... | collective-permute-start | bytes 786440 | tf_op jit(solution)/shard_map/ppermute | solution.py:309
  315.3 31.0 %collective-permute-start.41 = (bf16[1,8,64,1024]{3,2,1,0:T(8,128)(2,1)}, bf16[1,8,64,1024]{3,2,1,0:T(8,128)(2,1)S(1)}, u32[]{:S(2)}, u32[]{:S(2)}) collective-permute-start(bf16[1,8,64,1024]{3,2,1,0:T(8,128)(2,1)} %get-tuple-element.198), channel_id=1, source_target_pairs={{0,2},{2,0},{4,6},{6,4},{8,10},{10,8},{12,14},{14,12},{16,18},{18,... | collective-permute-start | bytes 3145736 | tf_op jit(solution)/shard_map/ppermute | solution.py:305
  331.4 16.5 %collective-permute-start.42 = (bf16[1024,768]{1,0:T(8,128)(2,1)}, bf16[1024,768]{1,0:T(8,128)(2,1)S(1)}, u32[]{:S(2)}, u32[]{:S(2)}) collective-permute-start(bf16[1024,768]{1,0:T(8,128)(2,1)} %attend_back.2.d_ref.r0_ref), channel_id=1, source_target_pairs={{0,2},{2,0},{4,6},{6,4},{8,10},{10,8},{12,14},{14,12},{16,18},{18,... | collective-permute-start | bytes 4718600 | tf_op jit(solution)/shard_map/ppermute | solution.py:305
  331.5 16.4 %collective-permute-start.43 = (bf16[8,64,512]{2,1,0:T(8,128)(2,1)}, bf16[8,64,512]{2,1,0:T(8,128)(2,1)S(1)}, u32[]{:S(2)}, u32[]{:S(2)}) collective-permute-start(bf16[8,64,512]{2,1,0:T(8,128)(2,1)} %get-tuple-element.199), channel_id=1, source_target_pairs={{0,1},{1,0},{2,3},{3,2},{4,5},{5,4},{6,7},{7,6},{8,9},{9,8},{10,11... | collective-permute-start | bytes 1572872 | tf_op jit(solution)/shard_map/ppermute | solution.py:309
  334.3 58.1 %collective-permute-start.46 = (bf16[4,64,2048]{2,1,0:T(8,128)(2,1)S(1)}, bf16[4,64,2048]{2,1,0:T(8,128)(2,1)}, u32[]{:S(2)}, u32[]{:S(2)}) collective-permute-start(bf16[4,64,2048]{2,1,0:T(8,128)(2,1)S(1)} %pad_maximum_fusion.5), channel_id=1, source_target_pairs={{0,1},{1,0},{2,3},{3,2},{4,5},{5,4},{6,7},{7,6},{8,9},{9,8},{10,11... | collective-permute-start | bytes 3145736 | tf_op jit(solution)/shard_map/ppermute | solution.py:309
  336.2 56.2 %collective-permute-start.45 = (bf16[4,64,2048]{2,1,0:T(8,128)(2,1)S(1)}, bf16[4,64,2048]{2,1,0:T(8,128)(2,1)}, u32[]{:S(2)}, u32[]{:S(2)}) collective-permute-start(bf16[4,64,2048]{2,1,0:T(8,128)(2,1)S(1)} %pad_maximum_fusion.4), channel_id=1, source_target_pairs={{0,4},{2,6},{4,0},{6,2},{8,12},{10,14},{12,8},{14,10},{16,20},{18,... | collective-permute-start | bytes 3145736 | tf_op jit(solution)/shard_map/ppermute | solution.py:301
  346.4 27.7 %collective-permute-start.44 = (bf16[512,256]{1,0:T(8,128)(2,1)S(1)}, bf16[512,256]{1,0:T(8,128)(2,1)S(1)}, u32[]{:S(2)}, u32[]{:S(2)}) collective-permute-start(bf16[512,256]{1,0:T(8,128)(2,1)S(1)} %copy-done.41), channel_id=1, source_target_pairs={{0,1},{1,0},{2,3},{3,2},{4,5},{5,4},{6,7},{7,6},{8,9},{9,8},{10,11... | collective-permute-start | bytes 786440 | tf_op jit(solution)/shard_map/ppermute | solution.py:309
  347.9 28.5 %collective-permute-start.48 = (bf16[512,256]{1,0:T(8,128)(2,1)S(1)}, bf16[512,256]{1,0:T(8,128)(2,1)S(1)}, u32[]{:S(2)}, u32[]{:S(2)}) collective-permute-start(bf16[512,256]{1,0:T(8,128)(2,1)S(1)} %get-tuple-element.264), channel_id=1, source_target_pairs={{0,8},{2,10},{4,12},{6,14},{8,16},{10,18},{12,20},{14,22},{16,24},... | collective-permute-start | bytes 786440 | tf_op jit(solution)/shard_map/ppermute | solution.py:297
  355.7 36.7 %collective-permute-start.47 = (bf16[4,64,1280]{2,1,0:T(8,128)(2,1)}, bf16[4,64,1280]{2,1,0:T(8,128)(2,1)S(1)}, u32[]{:S(2)}, u32[]{:S(2)}) collective-permute-start(bf16[4,64,1280]{2,1,0:T(8,128)(2,1)} %get-tuple-element.209), channel_id=1, source_target_pairs={{0,4},{2,6},{4,0},{6,2},{8,12},{10,14},{12,8},{14,10},{16,20},{18,... | collective-permute-start | bytes 1966088 | tf_op jit(solution)/shard_map/ppermute | solution.py:301
  374.1 18.2 %collective-permute-start.49 = (bf16[512,256]{1,0:T(8,128)(2,1)S(1)}, bf16[512,256]{1,0:T(8,128)(2,1)S(1)}, u32[]{:S(2)}, u32[]{:S(2)}) collective-permute-start(bf16[512,256]{1,0:T(8,128)(2,1)S(1)} %get-tuple-element.263), channel_id=1, source_target_pairs={{0,16},{2,18},{4,20},{6,22},{8,24},{10,26},{12,28},{14,30},{16,0},... | collective-permute-start | bytes 786440 | tf_op jit(solution)/shard_map/ppermute | solution.py:297
  376.4 16.0 %collective-permute-start.50 = (bf16[512,256]{1,0:T(8,128)(2,1)S(1)}, bf16[512,256]{1,0:T(8,128)(2,1)S(1)}, u32[]{:S(2)}, u32[]{:S(2)}) collective-permute-start(bf16[512,256]{1,0:T(8,128)(2,1)S(1)} %get-tuple-element.262), channel_id=1, source_target_pairs={{0,24},{2,26},{4,28},{6,30},{8,0},{10,2},{12,4},{14,6},{16,8},{18,... | collective-permute-start | bytes 786440 | tf_op jit(solution)/shard_map/ppermute | solution.py:297
  392.3 37.3 %collective-permute-start.51 = (bf16[1024,768]{1,0:T(8,128)(2,1)}, bf16[1024,768]{1,0:T(8,128)(2,1)}, u32[]{:S(2)}, u32[]{:S(2)}) collective-permute-start(bf16[1024,768]{1,0:T(8,128)(2,1)} %attend_back.3.d_ref.r0_ref), channel_id=1, source_target_pairs={{0,2},{2,0},{4,6},{6,4},{8,10},{10,8},{12,14},{14,12},{16,18},{18,... | collective-permute-start | bytes 4718600 | tf_op jit(solution)/shard_map/ppermute | solution.py:305
  398.4 15.4 %collective-permute-start.54 = (bf16[64,1280]{1,0:T(8,128)(2,1)}, bf16[64,1280]{1,0:T(8,128)(2,1)}, u32[]{:S(2)}, u32[]{:S(2)}) collective-permute-start(bf16[64,1280]{1,0:T(8,128)(2,1)} %get-tuple-element.220), channel_id=1, source_target_pairs={{0,16},{2,18},{4,20},{6,22},{8,24},{10,26},{12,28},{14,30},{16,0},... | collective-permute-start | bytes 491528 | tf_op jit(solution)/shard_map/ppermute | solution.py:297
  400.8 26.3 %collective-permute-start.55 = (bf16[64,1280]{1,0:T(8,128)(2,1)S(1)}, bf16[64,1280]{1,0:T(8,128)(2,1)}, u32[]{:S(2)}, u32[]{:S(2)}) collective-permute-start(bf16[64,1280]{1,0:T(8,128)(2,1)S(1)} %get-tuple-element.221), channel_id=1, source_target_pairs={{0,24},{2,26},{4,28},{6,30},{8,0},{10,2},{12,4},{14,6},{16,8},{18,... | collective-permute-start | bytes 491528 | tf_op jit(solution)/shard_map/ppermute | solution.py:297
  406.9 38.2 %collective-permute-start.52 = (bf16[512,1024]{1,0:T(8,128)(2,1)}, bf16[512,1024]{1,0:T(8,128)(2,1)S(1)}, u32[]{:S(2)}, u32[]{:S(2)}) collective-permute-start(bf16[512,1024]{1,0:T(8,128)(2,1)} %input_part.4), channel_id=1, source_target_pairs={{0,1},{1,0},{2,3},{3,2},{4,5},{5,4},{6,7},{7,6},{8,9},{9,8},{10,11... | collective-permute-start | bytes 3145736 | tf_op jit(solution)/shard_map/ppermute | solution.py:309
  410.1 25.9 %collective-permute-start.61 = (bf16[64,2048]{1,0:T(8,128)(2,1)}, bf16[64,2048]{1,0:T(8,128)(2,1)S(1)}, u32[]{:S(2)}, u32[]{:S(2)}) collective-permute-start(bf16[64,2048]{1,0:T(8,128)(2,1)} %get-tuple-element.225), channel_id=1, source_target_pairs={{0,8},{2,10},{4,12},{6,14},{8,16},{10,18},{12,20},{14,22},{16,24},... | collective-permute-start | bytes 786440 | tf_op jit(solution)/shard_map/ppermute | solution.py:297
  413.8 22.2 %collective-permute-start.62 = (bf16[64,2048]{1,0:T(8,128)(2,1)}, bf16[64,2048]{1,0:T(8,128)(2,1)S(1)}, u32[]{:S(2)}, u32[]{:S(2)}) collective-permute-start(bf16[64,2048]{1,0:T(8,128)(2,1)} %get-tuple-element.226), channel_id=1, source_target_pairs={{0,16},{2,18},{4,20},{6,22},{8,24},{10,26},{12,28},{14,30},{16,0},... | collective-permute-start | bytes 786440 | tf_op jit(solution)/shard_map/ppermute | solution.py:297
  (60 other events, 503.7 us)

commit v3 on v1

--- a/solution.py
+++ b/solution.py
@@ -1,6 +1,10 @@
+import functools
+
 import jax
 import jax.numpy as jnp
 from jax import lax
+from jax.experimental import pallas as pl
+from jax.experimental.pallas import tpu as pltpu
 from jax.sharding import PartitionSpec as P
 
 HEADS = 16
@@ -253,9 +257,1142 @@
     return (mixed_out, grad_tokens, owned[0], owned[1], owned[2], owned[3], owned[4])
 
 
+LINE = 4
+HALF = 512
+NEG = -1e30
+bf16 = jnp.bfloat16
+f32 = jnp.float32
+VMEM_LIMIT = 56 * 1024 * 1024
+
+
+def params(limit=VMEM_LIMIT):
+    return pltpu.CompilerParams(vmem_limit_bytes=limit)
+
+
+PLACES = dict(up_stack=20, attend_1=20, touch=20, attend_back_0=20, mixed=20, down_sum=20, up_parts=20, up_sum=20)
+
+
+def cost(name):
+    return pl.CostEstimate(flops=int(PLACES.get(name, 0.5) * 1.15e9), bytes_accessed=1 << 16, transcendentals=0)
+
+
+def hbm():
+    return pl.BlockSpec(memory_space=pl.ANY)
+
+
+def block(*shape):
+    return pl.BlockSpec(shape, lambda i, s: (0,) * len(shape))
+
+
+def call(kernel, name, ins, outs, scratch, flops, *args, grid=(1,)):
+    out = pl.pallas_call(
+        kernel,
+        grid_spec=pltpu.PrefetchScalarGridSpec(
+            num_scalar_prefetch=1,
+            grid=grid,
+            in_specs=ins,
+            out_specs=[spec for spec, _ in outs],
+            scratch_shapes=scratch,
+        ),
+        out_shape=[shape for _, shape in outs],
+        compiler_params=params(),
+        cost_estimate=cost(name),
+        name=name,
+    )(*args)
+    return out
+
+
+def of(kind, *shape):
+    return jax.ShapeDtypeStruct(shape, kind)
+
+
+def dot(a, b, contract):
+    return lax.dot_general(a, b, ((contract[:1], contract[1:]), ((), ())), preferred_element_type=f32)
+
+
+def row_pairs(target):
+    pairs = []
+    for r in range(LINE * 4):
+        z, x, c = target(r // 4, r // 2 % 2, r % 2)
+        pairs.append((r, z % LINE * 4 + x * 2 + c))
+    return pairs
+
+
+def shift_z(v, k):
+    return lax.ppermute(v, "rows", row_pairs(lambda z, x, c: (z + k, x, c)))
+
+
+def swap_x(v):
+    return lax.ppermute(v, "rows", row_pairs(lambda z, x, c: (z, 1 - x, c)))
+
+
+def swap_c(v):
+    return lax.ppermute(v, "rows", row_pairs(lambda z, x, c: (z, x, 1 - c)))
+
+
+def swap_y(v):
+    return lax.ppermute(v, "pair", [(0, 1), (1, 0)])
+
+
+def along_line(shard):
+    return [shard] + [shift_z(shard, k) for k in range(1, LINE)]
+
+
+def barrier(*values):
+    return lax.optimization_barrier(values)
+
+
+def after(value, *others):
+    return lax.optimization_barrier((value, others))[0]
+
+
+def qkv_copies(info, refs, w_ref, sems, start_col, cols):
+    out = []
+    for dx in range(2):
+        for dz in range(LINE):
+            chip = lax.rem(info[0] + LINE - dz, LINE) * 2 + lax.rem(info[1] + dx, 2)
+            for own in (0, 1):
+                core = info[2] if own == 0 else 1 - info[2]
+                out.append(
+                    pltpu.make_async_copy(
+                        refs[own * 2 + dx].at[dz, :, pl.ds(start_col, cols)],
+                        w_ref.at[pl.ds(pl.multiple_of(chip * 128 + core * 64, 64), 64), :],
+                        sems.at[(dx * LINE + dz) * 2 + own],
+                    )
+                )
+    return out
+
+
+def by_chip(z, x):
+    return z * 2 + x
+
+
+def by_unit(z, x):
+    return z // 2 * 4 + x * 2 + z % 2
+
+
+def piece_copies(info, refs, w_ref, sems, rows, cols, order):
+    line, beside, across, far_a, far_b = refs
+    out = [[], []]
+    for dy in range(2):
+        for dx in range(2):
+            for dz in range(LINE):
+                chip = order(lax.rem(info[0] + LINE - dz, LINE), lax.rem(info[1] + dx, 2))
+                ref, at = ((line, dz), (beside, dz), (across, dz), (far_a, dz) if dz < 2 else (far_b, dz + far_b.shape[0] - LINE))[dx + 2 * dy]
+                out[dy].append(
+                    pltpu.make_async_copy(
+                        ref.at[at, :, pl.ds(0, cols)],
+                        w_ref.at[pl.ds(pl.multiple_of(chip * rows, rows), rows), pl.ds(dy * cols, cols)],
+                        sems.at[(dy * 2 + dx) * LINE + dz],
+                    )
+                )
+    return out
+
+
+def start(copies):
+    for c in copies:
+        c.start()
+
+
+def wait(copies):
+    for c in copies:
+        c.wait()
+
+
+def project_kernel(info, xo_ref, xt_ref, *refs):
+    out_ref, g_ref, w_ref, gcol_ref, nin_ref, sems = refs[4:]
+    copies = qkv_copies(info, refs[:4], w_ref, sems, 0, 1536)
+    gains = qkv_copies(info, refs[:4], gcol_ref, sems.at[pl.ds(16, 16)], 1536, 128)
+    start(gains)
+    start(copies)
+    wait(gains)
+    both = gcol_ref[...].T.astype(f32)[:2]
+    g_ref[...] = both
+    side = info[3]
+    for part, x_ref in ((0, xo_ref), (1, xt_ref)):
+        at = side if part == 0 else 1 - side
+        tokens = pl.ds(pl.multiple_of(at * HALF, HALF), HALF)
+        nin_ref[tokens, :] = (centred(x_ref[...].astype(f32))[0] * both[:1]).astype(bf16)
+        if part == 0:
+            wait(copies)
+        for n in range(2):
+            cols = slice(n * 768, n * 768 + 768)
+            out_ref[tokens, cols] = dot(nin_ref[tokens, :], w_ref[:, cols], (1, 0)).astype(bf16)
+
+
+def project(info, x_own, x_other, pieces):
+    return call(
+        project_kernel,
+        "project",
+        [block(HALF, 1024), block(HALF, 1024)] + [hbm()] * 4,
+        [(block(1024, 1536), of(bf16, 1024, 1536)), (block(2, 1024), of(f32, 2, 1024))],
+        [
+            pltpu.VMEM((1024, 1536), bf16),
+            pltpu.VMEM((1024, 128), bf16),
+            pltpu.VMEM((1024, 1024), bf16),
+            pltpu.SemaphoreType.DMA((32,)),
+        ],
+        2 * 1024 * 1024 * 1536,
+        info,
+        x_own,
+        x_other,
+        *pieces,
+    )
+
+
+TILES = ((0, 512), (256, 512), (512, 768), (768, 1024))
+
+
+def own_lanes(v, head):
+    lane = lax.broadcasted_iota(jnp.int32, v.shape, 1)
+    return jnp.where((lane >= 64) if head else (lane < 64), v, jnp.zeros_like(v))
+
+
+def attend_kernel(info, q_ref, k_ref, v_ref, bias_ref, keep_ref, send_ref, lse_ref):
+    side = info[3]
+    lane = lax.broadcasted_iota(jnp.int32, (256, 128), 1)
+    for tile, (first, seen) in enumerate(TILES):
+        rows = slice(first, first + 256)
+        q_tile = q_ref[rows, :] * jnp.asarray(0.125, bf16)
+        done, lse = [], []
+        for head in range(2):
+            s = dot(own_lanes(q_tile, head), k_ref[:seen, :], (1, 1)) + bias_ref[rows, :seen]
+            top = jnp.max(s, axis=1, keepdims=True)
+            p = jnp.exp(s - top)
+            total = jnp.sum(p, axis=1, keepdims=True)
+            lse.append(top + jnp.log(total))
+            done.append(dot(p.astype(bf16), v_ref[:seen, :], (1, 0)) * (1.0 / total))
+        both = jnp.where(lane < 64, done[0], done[1]).astype(bf16)
+        lse_ref[0, :, rows] = jnp.where(lane == 0, lse[0], lse[1]).T[:2]
+        half, row = tile // 2, tile % 2 * 256
+
+        @pl.when(side == half)
+        def _():
+            keep_ref[row : row + 256, :] = both
+
+        @pl.when(side != half)
+        def _():
+            send_ref[row : row + 256, :] = both
+
+
+def head_parts(group):
+    return [pl.BlockSpec((1024, 128), lambda h, s, j=j: (0, 6 * group + 2 * j + h)) for j in range(3)]
+
+
+def attend(info, projected, bias, group):
+    piece = pl.BlockSpec((HALF, 128), lambda h, s: (0, h))
+    return call(
+        attend_kernel,
+        f"attend_{group}",
+        [*head_parts(group), block(1024, 1024)],
+        [
+            (piece, of(bf16, HALF, 256)),
+            (piece, of(bf16, HALF, 256)),
+            (pl.BlockSpec((1, 2, 1024), lambda h, s: (h, 0, 0)), of(f32, 2, 2, 1024)),
+        ],
+        [],
+        4 * 1024 * 768 * 64 * 4,
+        info,
+        projected,
+        projected,
+        projected,
+        bias,
+        grid=(2,),
+    )
+
+
+def attend_back_kernel(info, q_ref, k_ref, v_ref, bias_ref, lse_ref, keep_ref, send_ref, out_ref, dk_ref, dv_ref):
+    side = info[3]
+    pair = pl.program_id(0)
+    k_t = k_ref[...].T
+    dk_ref[...] = jnp.zeros_like(dk_ref)
+    dv_ref[...] = jnp.zeros_like(dv_ref)
+    for tile, (start, seen) in enumerate(TILES):
+        half, row = tile // 2, tile % 2 * 256
+        q_tile = q_ref[start : start + 256, :] * jnp.asarray(0.125, bf16)
+        g_tile = jnp.where(side == half, keep_ref[row : row + 256, :], send_ref[row : row + 256, :])
+        pieces = []
+        for head in range(2):
+            q_head = own_lanes(q_tile, head)
+            g_head = own_lanes(g_tile, head)
+            s = dot(k_ref[:seen, :], q_head, (1, 1))
+            p = jnp.exp(s + bias_ref[:seen, start : start + 256] - lse_ref[0, head : head + 1, start : start + 256])
+            dp = dot(v_ref[:seen, :], g_head, (1, 1))
+            centre = jnp.sum(p * dp, axis=0, keepdims=True)
+            ds = (p * (dp - centre)).astype(bf16)
+            dv_ref[:seen, :] += dot(p.astype(bf16), g_head, (1, 0))
+            dk_ref[:seen, :] += dot(ds, q_head, (1, 0))
+            pieces.append(dot(k_t[head * 64 : head * 64 + 64, :seen], ds, (1, 0)) * 0.125)
+        cols = pl.ds(pl.multiple_of(pair * 128, 128), 128)
+        out_ref[start : start + 256, cols] = jnp.concatenate(pieces, axis=0).T.astype(bf16)
+    out_ref[:, pl.ds(pl.multiple_of(256 + pair * 128, 128), 128)] = dk_ref[...].astype(bf16)
+    out_ref[:, pl.ds(pl.multiple_of(512 + pair * 128, 128), 128)] = dv_ref[...].astype(bf16)
+
+
+def attend_back(info, projected, bias, lse, keep, other, group):
+    piece = pl.BlockSpec((HALF, 128), lambda h, s: (0, 2 * group + h))
+    return pl.pallas_call(
+        attend_back_kernel,
+        grid_spec=pltpu.PrefetchScalarGridSpec(
+            num_scalar_prefetch=1,
+            grid=(2,),
+            in_specs=[
+                *head_parts(group),
+                pl.BlockSpec((1024, 1024), lambda h, s: (0, 0)),
+                pl.BlockSpec((1, 2, 1024), lambda h, s: (h, 0, 0)),
+                piece,
+                piece,
+            ],
+            out_specs=pl.BlockSpec((1024, 768), lambda h, s: (0, 0)),
+            scratch_shapes=[pltpu.VMEM((1024, 128), f32), pltpu.VMEM((1024, 128), f32)],
+        ),
+        out_shape=jax.ShapeDtypeStruct((1024, 768), bf16),
+        compiler_params=params(),
+        cost_estimate=cost(f"attend_back_{group}"),
+        name=f"attend_back_{group}",
+    )(info, projected, projected, projected, bias, lse, keep, other)
+
+
+def centred(v):
+    off = v - jnp.mean(v, axis=-1, keepdims=True)
+    scale = lax.rsqrt(jnp.mean(off * off, axis=-1, keepdims=True) + epsilon)
+    return off * scale, scale
+
+
+def out_kernel(info, x_ref, k0, k1, g0, g1, w_ref, g_ref, mid_ref, nm_ref, own_ref, oth_ref, t_ref):
+    places = [(info[3] if i < 2 else 1 - info[3]) * HALF + i % 2 * 256 for i in range(4)]
+    places = [pl.ds(pl.multiple_of(at, 256), 256) for at in places]
+    for half in range(2):
+        cols = slice(half * 512, half * 512 + 512)
+        branch = x_ref[:, cols].astype(f32)
+        for at, ref in zip(places, (k0, k1, g0, g1)):
+            branch = branch + dot(ref[...], w_ref[half, at, :], (1, 0))
+        mid_ref[:, cols] = branch
+    nm_ref[...] = (centred(mid_ref[...])[0] * g_ref[1:]).astype(bf16)
+    for at, ref in zip(places, (k0, k1, g0, g1)):
+        t_ref[at, :] = ref[...].T
+    put_parities(info, t_ref, own_ref, oth_ref)
+
+
+def put_parities(info, t_ref, own_ref, oth_ref):
+    for dx in range(2):
+        for dz in range(LINE):
+            chip = lax.rem(info[0] + dz, LINE) * 2 + lax.rem(info[1] + dx, 2)
+            here = pl.multiple_of(chip * 128 + info[2] * 64, 64)
+            there = pl.multiple_of(chip * 128 + (1 - info[2]) * 64, 64)
+            own_ref[dx * LINE + dz] = t_ref[pl.ds(here, 64), :]
+            oth_ref[dx * LINE + dz] = t_ref[pl.ds(there, 64), :]
+
+
+def attention_out(info, x, keeps, gots, w, gain):
+    return call(
+        out_kernel,
+        "attention_out",
+        [block(HALF, 1024)] + [block(HALF, 256)] * 4 + [block(2, 1024, 512), block(2, 1024)],
+        [
+            (block(HALF, 1024), of(f32, HALF, 1024)),
+            (block(HALF, 1024), of(bf16, HALF, 1024)),
+            (block(8, 64, HALF), of(bf16, 8, 64, HALF)),
+            (block(8, 64, HALF), of(bf16, 8, 64, HALF)),
+        ],
+        [pltpu.VMEM((1024, HALF), bf16)],
+        2 * 512 * 1024 * 1024,
+        info,
+        x,
+        *keeps,
+        *gots,
+        w,
+        gain,
+    )
+
+
+def up_kernel(info, x0_ref, x1_ref, *refs):
+    act_ref, slope_ref, w_ref, sems = refs[5:]
+    step = pl.program_id(0)
+    near, far = piece_copies(info, refs[:5], w_ref, sems, 128, 1024, by_chip)
+
+    @pl.when(step == 0)
+    def _():
+        start(near)
+        start(far)
+        wait(near)
+
+    @pl.when(step == 1)
+    def _():
+        wait(far)
+
+    for part, x_ref in enumerate((x0_ref, x1_ref)):
+        rows = slice(part * HALF, part * HALF + HALF)
+        for n in range(2):
+            cols = slice(n * 512, n * 512 + 512)
+            pre = dot(x_ref[...], w_ref[:, pl.ds(pl.multiple_of(step * 1024 + n * 512, 512), 512)], (1, 0))
+            below = 0.5 * (1.0 + lax.erf(pre * 0.7071067811865476))
+            act_ref[rows, cols] = (pre * below).astype(bf16)
+            slope_ref[rows, cols] = (below + pre * (0.3989422804014327 * jnp.exp(-0.5 * pre * pre))).astype(bf16)
+
+
+def up(info, x_own, x_sib, pieces):
+    out = pl.BlockSpec((1024, 1024), lambda n, s: (0, lax.rem(s[3] + n, 2)))
+    return call(
+        up_kernel,
+        "up",
+        [block(HALF, 1024)] * 2 + [hbm()] * 5,
+        [(out, of(bf16, 1024, 2048))] * 2,
+        [pltpu.VMEM((1024, 2048), bf16), pltpu.SemaphoreType.DMA((16,))],
+        4 * 512 * 1024 * 4096,
+        info,
+        x_own,
+        x_sib,
+        *pieces,
+        grid=(2,),
+    )
+
+
+def down_kernel(info, act_ref, slope_ref, c0_ref, c1_ref, mid_ref, *refs):
+    keep_ref, send_ref, gp_ref, w_ref, acc_ref, sems = refs[5:]
+    step = pl.program_id(0)
+    side = info[3]
+    near, far = piece_copies(info, refs[:5], w_ref, sems, 256, 512, by_unit)
+    mine = pl.ds(pl.multiple_of(side * 512, 512), 512)
+    theirs = pl.ds(pl.multiple_of((1 - side) * 512, 512), 512)
+
+    @pl.when(step == 0)
+    def _():
+        start(near)
+        start(far)
+        wait(near)
+        wait(far)
+
+    units = pl.ds(pl.multiple_of(step * 1024, 1024), 1024)
+    for part, cot_ref in enumerate((c0_ref, c1_ref)):
+        rows = slice(part * HALF, part * HALF + HALF)
+        for n in range(2):
+            here = pl.ds(pl.multiple_of(step * 1024 + n * 512, 512), 512)
+            cols = slice(n * 512, n * 512 + 512)
+            back = dot(cot_ref[:, mine], w_ref[here, :512], (1, 1)) + dot(cot_ref[:, theirs], w_ref[here, 512:], (1, 1))
+            gp_ref[rows, cols] = (back * slope_ref[rows, cols].astype(f32)).astype(bf16)
+        total = dot(act_ref[rows, :], w_ref[units, :], (1, 0))
+
+        @pl.when(step == 0)
+        def _():
+            acc_ref[rows, :] = total
+
+        @pl.when(step == 1)
+        def _():
+            done = total + acc_ref[rows, :]
+            if part == 0:
+                keep_ref[:, mine] = mid_ref[:, mine] + done[:, :512]
+                keep_ref[:, theirs] = mid_ref[:, theirs] + done[:, 512:]
+            else:
+                send_ref[:, mine] = done[:, :512].astype(bf16)
+                send_ref[:, theirs] = done[:, 512:].astype(bf16)
+
+
+def down(info, act, slope, cot_own, cot_sib, mid, pieces):
+    tile = pl.BlockSpec((1024, 1024), lambda n, s: (0, n))
+    return call(
+        down_kernel,
+        "down",
+        [tile, tile] + [block(HALF, 1024)] * 3 + [hbm()] * 5,
+        [
+            (block(HALF, 1024), of(f32, HALF, 1024)),
+            (block(HALF, 1024), of(bf16, HALF, 1024)),
+            (tile, of(bf16, 1024, 2048)),
+        ],
+        [pltpu.VMEM((2048, 1024), bf16), pltpu.VMEM((1024, 1024), f32), pltpu.SemaphoreType.DMA((16,))],
+        4 * 512 * 1024 * 4096,
+        info,
+        act,
+        slope,
+        cot_own,
+        cot_sib,
+        mid,
+        *pieces,
+        grid=(2,),
+    )
+
+
+def normed_back_kernel(info, gp_ref, *refs):
+    keep_ref, send_ref, w_ref, sems = refs[5:]
+    near, far = piece_copies(info, refs[:5], w_ref, sems, 128, 1024, by_chip)
+    start(near)
+    start(far)
+    wait(near)
+    wait(far)
+    mine = pl.ds(pl.multiple_of(info[3] * 1024, 1024), 1024)
+    theirs = pl.ds(pl.multiple_of((1 - info[3]) * 1024, 1024), 1024)
+    for part, out in ((1, send_ref), (0, keep_ref)):
+        rows = slice(part * HALF, part * HALF + HALF)
+        for n in range(2):
+            dims = slice(n * 512, n * 512 + 512)
+            total = dot(gp_ref[rows, mine], w_ref[dims, :1024], (1, 1)) + dot(gp_ref[rows, theirs], w_ref[dims, 1024:], (1, 1))
+            out[:, dims] = total.astype(out.dtype)
+
+
+def normed_back(info, gp, pieces):
+    return call(
+        normed_back_kernel,
+        "normed_back",
+        [block(1024, 2048)] + [hbm()] * 5,
+        [(block(HALF, 1024), of(f32, HALF, 1024)), (block(HALF, 1024), of(bf16, HALF, 1024))],
+        [pltpu.VMEM((1024, 2048), bf16), pltpu.SemaphoreType.DMA((16,))],
+        2 * 512 * 1024 * 4096,
+        info,
+        gp,
+        *pieces,
+    )
+
+
+def middle_back_kernel(info, e0_ref, e1_ref, cot_ref, mid_ref, g_ref, w_ref, gm_ref, gb_ref, keep, send):
+    n, scale = centred(mid_ref[...])
+    eg = (e0_ref[...] + e1_ref[...].astype(f32)) * g_ref[1:]
+    lean = eg - jnp.mean(eg, axis=-1, keepdims=True) - n * jnp.mean(eg * n, axis=-1, keepdims=True)
+    grad = cot_ref[...].astype(f32) + scale * lean
+    gm_ref[...] = grad
+    low = grad.astype(bf16)
+    gb_ref[...] = low
+    for out, at in ((keep, info[3]), (send, 1 - info[3])):
+        rows = pl.ds(pl.multiple_of(at * HALF, HALF), HALF)
+        out[...] = (dot(low[:, :512], w_ref[0, rows, :], (1, 1)) + dot(low[:, 512:], w_ref[1, rows, :], (1, 1))).astype(bf16)
+
+
+def middle_back(info, e_keep, e_got, cot, mid, gain, w):
+    return call(
+        middle_back_kernel,
+        "middle_back",
+        [block(HALF, 1024)] * 4 + [block(2, 1024), block(2, 1024, 512)],
+        [
+            (block(HALF, 1024), of(f32, HALF, 1024)),
+            (block(HALF, 1024), of(bf16, HALF, 1024)),
+            (block(HALF, 512), of(bf16, HALF, 512)),
+            (block(HALF, 512), of(bf16, HALF, 512)),
+        ],
+        [],
+        2 * 512 * 1024 * 1024,
+        info,
+        e_keep,
+        e_got,
+        cot,
+        mid,
+        gain,
+        w,
+    )
+
+
+def down_grad_kernel(info, c0_ref, c1_ref, act_ref, far, across, beside, own, t_ref):
+    g = pl.program_id(0)
+
+    @pl.when(g == 0)
+    def _():
+        t_ref[:, :HALF] = c0_ref[...].T
+        t_ref[:, HALF:] = c1_ref[...].T
+
+    x = lax.rem(info[1] + 1 - lax.rem(g, 2), 2)
+    side = lax.rem(info[3] + 1 - g // 2, 2)
+    rows = pl.ds(pl.multiple_of(side * 512, 512), 512)
+    for half in range(2):
+        units = pl.ds(pl.multiple_of(half * 1024 + x * 512, 512), 512)
+        total = dot(t_ref[rows, :], act_ref[:, units], (1, 0)).astype(bf16)
+        for j in range(2):
+            dz = lax.rem(half * 2 + j - info[0] + LINE, LINE)
+            for at, ref in enumerate((far, across, beside, own)):
+
+                @pl.when(g == at)
+                def _():
+                    ref[dz] = total[:, j * 256 : j * 256 + 256]
+
+
+def down_grad(info, cot_own, cot_sib, act):
+    return call(
+        down_grad_kernel,
+        "down_grad",
+        [block(HALF, 1024), block(HALF, 1024), block(1024, 2048)],
+        [(block(LINE, 512, 256), of(bf16, LINE, 512, 256))] * 4,
+        [pltpu.VMEM((1024, 1024), bf16)],
+        2 * 1024 * 1024 * 2048,
+        info,
+        cot_own,
+        cot_sib,
+        act,
+        grid=(4,),
+    )
+
+
+def stay(g, first):
+    return lax.max(0, lax.min(g - first, 1))
+
+
+def up_grad_kernel(info, n0_ref, n1_ref, gp_ref, far, across, beside, own, t_ref):
+    g = pl.program_id(0)
+
+    @pl.when(g == 0)
+    def _():
+        for dx in range(2):
+            for dz in range(LINE):
+                chip = lax.rem(info[0] + dz, LINE) * 2 + lax.rem(info[1] + dx, 2)
+                cols = pl.ds(pl.multiple_of(chip * 128, 128), 128)
+                rows = slice((dx * LINE + dz) * 128, (dx * LINE + dz) * 128 + 128)
+                t_ref[rows, :HALF] = n0_ref[:, cols].T
+                t_ref[rows, HALF:] = n1_ref[:, cols].T
+
+    total = dot(t_ref[...], gp_ref[...], (1, 0)).astype(bf16).reshape(8, 128, 512)
+
+    @pl.when(g < 2)
+    def _():
+        across[...] = total[:4]
+        far[...] = total[4:]
+
+    @pl.when(g >= 2)
+    def _():
+        own[...] = total[:4]
+        beside[...] = total[4:]
+
+
+def up_grad(info, nm_own, nm_sib, gp):
+    right = pl.BlockSpec((1024, 512), lambda g, s: (0, lax.rem(s[3] + 1 - g // 2, 2) * 2 + lax.rem(g, 2)))
+    return call(
+        up_grad_kernel,
+        "up_grad",
+        [block(HALF, 1024), block(HALF, 1024), right],
+        [
+            (pl.BlockSpec((LINE, 128, 512), lambda g, s, f=f: (0, 0, stay(g, f))), of(bf16, LINE, 128, 1024))
+            for f in (0, 0, 2, 2)
+        ],
+        [pltpu.VMEM((1024, 1024), bf16)],
+        2 * 1024 * 512 * 4096,
+        info,
+        nm_own,
+        nm_sib,
+        gp,
+        grid=(4,),
+    )
+
+
+def out_grad_kernel(info, l0_ref, r0_ref, l1_ref, r1_ref, keep_ref, send_ref):
+    for out, at in ((keep_ref, info[3]), (send_ref, 1 - info[3])):
+        cols = pl.ds(pl.multiple_of(at * 512, 512), 512)
+        total = dot(l0_ref[...], r0_ref[:, cols], (1, 0)) + dot(l1_ref[...], r1_ref[:, cols], (1, 0))
+        out[...] = total.astype(bf16).reshape(8, 64, 512)
+
+
+def out_grad(info, att_t, gb, att_t_sib, gb_sib):
+    return call(
+        out_grad_kernel,
+        "out_grad",
+        [block(512, HALF), block(HALF, 1024)] * 2,
+        [(block(8, 64, 512), of(bf16, 8, 64, 512))] * 2,
+        [],
+        2 * 512 * 1024 * 1024,
+        info,
+        att_t.reshape(512, HALF),
+        gb,
+        att_t_sib.reshape(512, HALF),
+        gb_sib,
+    )
+
+
+def input_back_kernel(info, d0_ref, d1_ref, *refs):
+    keep_ref, send_ref, w_ref, sems = refs[4:]
+    copies = qkv_copies(info, refs[:4], w_ref, sems, 0, 1536)
+    start(copies)
+    wait(copies)
+    for part, out in ((1, send_ref), (0, keep_ref)):
+        at = info[3] if part == 0 else 1 - info[3]
+        slots = pl.ds(pl.multiple_of(at * HALF, HALF), HALF)
+        for n in range(2):
+            dims = slice(n * 512, n * 512 + 512)
+            total = dot(d0_ref[slots, :], w_ref[dims, :768], (1, 1)) + dot(d1_ref[slots, :], w_ref[dims, 768:], (1, 1))
+            out[:, dims] = total.astype(out.dtype)
+
+
+def input_back(info, d0, d1, pieces):
+    return call(
+        input_back_kernel,
+        "input_back",
+        [block(1024, 768)] * 2 + [hbm()] * 4,
+        [(block(HALF, 1024), of(f32, HALF, 1024)), (block(HALF, 1024), of(bf16, HALF, 1024))],
+        [pltpu.VMEM((1024, 1536), bf16), pltpu.SemaphoreType.DMA((16,))],
+        2 * 1024 * 1024 * 1536,
+        info,
+        d0,
+        d1,
+        *pieces,
+    )
+
+
+def qkv_grad_kernel(info, l0_ref, r0_ref, l1_ref, r1_ref, *refs):
+    beside, own = refs[-2:]
+    total = dot(l0_ref[...], r0_ref[...], (1, 0)) + dot(l1_ref[...], r1_ref[...], (1, 0))
+    total = total.astype(bf16).reshape(8, 64, 768)
+    own[:, :, :768] = total[:4]
+    beside[:, :, :768] = total[4:]
+    if len(refs) == 4:
+        both = (refs[0][...].astype(f32) + refs[1][...].astype(f32)).astype(bf16)
+        own[:, :, 768:] = both[:4]
+        beside[:, :, 768:] = both[4:]
+
+
+def qkv_grad(info, nin_t, dproj, nin_t_sib, dproj_sib, more=()):
+    width = 768 + 512 * bool(more)
+    return call(
+        qkv_grad_kernel,
+        "qkv_grad",
+        [block(512, 1024), block(1024, 768)] * 2 + [block(8, 64, 512)] * len(more),
+        [(block(4, 64, width), of(bf16, 4, 64, width))] * 2,
+        [],
+        2 * 2048 * 512 * 768,
+        info,
+        nin_t.reshape(512, 1024),
+        dproj,
+        nin_t_sib.reshape(512, 1024),
+        dproj_sib,
+        *more,
+    )
+
+
+def input_norm_kernel(info, xo_ref, xt_ref, g_ref, own_ref, oth_ref, t_ref):
+    side = info[3]
+    for part, x_ref in ((0, xo_ref), (1, xt_ref)):
+        at = side if part == 0 else 1 - side
+        normed = (centred(x_ref[...].astype(f32))[0] * g_ref[:1]).astype(bf16)
+        t_ref[:, pl.ds(pl.multiple_of(at * HALF, HALF), HALF)] = normed.T
+    put_parities(info, t_ref, own_ref, oth_ref)
+
+
+def input_norm(info, x_own, x_other, gains):
+    return call(
+        input_norm_kernel,
+        "input_norm",
+        [block(HALF, 1024), block(HALF, 1024), block(2, 1024)],
+        [(block(8, 64, 1024), of(bf16, 8, 64, 1024))] * 2,
+        [pltpu.VMEM((1024, 1024), bf16)],
+        20 << 20,
+        info,
+        x_own,
+        x_other,
+        gains,
+    )
+
+
+def heads_kernel(info, w_ref, got_ref, gain_ref, out_ref):
+    side = info[3] == 0
+    first, middle, last = w_ref[:, :512], got_ref[:, :512], w_ref[:, 1024:]
+    q = jnp.where(side, first, middle)
+    k = jnp.where(side, last, first)
+    v = jnp.where(side, middle, last)
+    for i in range(2):
+        for j, part in enumerate((q, k, v)):
+            out_ref[:, i * 768 + j * 256 : i * 768 + j * 256 + 256] = part[:, i * 256 : i * 256 + 256]
+    lane = lax.broadcasted_iota(jnp.int32, (w_ref.shape[0], 128), 1)
+    mine = jnp.broadcast_to(gain_ref[...].astype(f32), lane.shape)
+    theirs = jnp.broadcast_to(got_ref[:, 512:513].astype(f32), lane.shape)
+    out_ref[:, 1536:] = jnp.where((lane == 0) == side, mine, theirs).astype(bf16)
+
+
+def heads_of(info, w, got, gains):
+    return call(
+        heads_kernel,
+        "heads",
+        [block(64, 1536), block(64, 640), block(64, 1)],
+        [(block(64, 1664), of(bf16, 64, 1664))],
+        [],
+        1 << 16,
+        info,
+        w,
+        got,
+        gains,
+    )[0]
+
+
+def by_core_kernel(info, up_ref, own_ref, oth_ref):
+    for ref, core in ((own_ref, info[2]), (oth_ref, 1 - info[2])):
+        for i, to in enumerate((0, 2, 1, 3)):
+            ref[:, to * 256 : to * 256 + 256] = up_ref[:, pl.ds(pl.multiple_of(i * 512 + core * 256, 256), 256)]
+
+
+def by_core(info, w_up):
+    return call(
+        by_core_kernel,
+        "by_core",
+        [block(64, 2048)],
+        [(block(64, 1024), of(bf16, 64, 1024))] * 2,
+        [],
+        1 << 16,
+        info,
+        w_up,
+    )
+
+
+def both_rows_kernel(info, own_ref, got_ref, out_ref):
+    out_ref[pl.ds(pl.multiple_of(info[2] * 64, 64), 64), :] = own_ref[...]
+    out_ref[pl.ds(pl.multiple_of((1 - info[2]) * 64, 64), 64), :] = got_ref[...]
+
+
+def both_rows(info, own, got):
+    return call(
+        both_rows_kernel,
+        "both_rows",
+        [block(64, 1024)] * 2,
+        [(block(128, 1024), of(bf16, 128, 1024))],
+        [],
+        1 << 16,
+        info,
+        own,
+        got,
+    )[0]
+
+
+def added_kernel(info, a_ref, b_ref, out_ref):
+    out_ref[...] = (a_ref[...].astype(f32) + b_ref[...].astype(f32)).astype(bf16)
+
+
+def added(info, a, b, name="added"):
+    steps = 2
+    spec = pl.BlockSpec((a.shape[0] // steps, *a.shape[1:]), lambda i, s: (i,) + (0,) * (a.ndim - 1))
+    return call(added_kernel, name, [spec, spec], [(spec, of(bf16, *a.shape))], [], 0, info, a, b, grid=(steps,))[0]
+
+
+def line_parts_kernel(info, a_ref, b_ref, c_ref, *outs):
+    for k, out in enumerate(outs):
+        out[...] = (a_ref[k].astype(f32) + b_ref[k].astype(f32) + c_ref[k].astype(f32)).astype(bf16)
+
+
+def line_parts(info, own, from_x, from_y, name):
+    spec, out = block(*own.shape), block(*own.shape[1:])
+    return call(
+        line_parts_kernel, name, [spec] * 3, [(out, of(bf16, *own.shape[1:]))] * LINE, [], 0, info, own, from_x, from_y
+    )
+
+
+def qkv_parts_kernel(info, a_ref, ax_ref, b_ref, bx_ref, *outs):
+    for k, out in enumerate(outs):
+        out[:, :1280] = (a_ref[k].astype(f32) + ax_ref[k].astype(f32)).astype(bf16)
+        out[:, 1280:] = (b_ref[k].astype(f32) + bx_ref[k].astype(f32)).astype(bf16)
+
+
+def qkv_parts(info, a, a_x, b, b_x):
+    return call(
+        qkv_parts_kernel,
+        "qkv_parts",
+        [block(4, 64, 1280)] * 2 + [block(4, 64, 768)] * 2,
+        [(block(64, 2048), of(bf16, 64, 2048))] * LINE,
+        [],
+        0,
+        info,
+        a,
+        a_x,
+        b,
+        b_x,
+    )
+
+
+def stack_kernel(info, *refs):
+    for k in range(LINE):
+        refs[LINE][k] = refs[k][...]
+
+
+def stacked(info, parts, name):
+    shape = parts[0].shape
+    return call(
+        stack_kernel, name, [block(*shape)] * LINE, [(block(LINE, *shape), of(bf16, LINE, *shape))], [], 0, info, *parts
+    )[0]
+
+
+def touch_kernel(info, a_ref, out_ref):
+    out_ref[...] = a_ref[...]
+
+
+def touch(info, a):
+    return call(touch_kernel, "touch", [block(*a.shape)], [(block(*a.shape), of(a.dtype, *a.shape))], [], 0, info, a)[0]
+
+
+def summed(refs, *at):
+    total = refs[0][at].astype(f32)
+    for ref in refs[1:]:
+        total = total + ref[at].astype(f32)
+    return total
+
+
+def down_sum_kernel(info, *refs):
+    refs[4][...] = summed(refs[:4]).T
+
+
+def down_sum(info, parts):
+    return call(
+        down_sum_kernel,
+        "down_sum",
+        [block(512, 256)] * 4,
+        [(block(256, 512), of(f32, 256, 512))],
+        [],
+        0,
+        info,
+        *parts,
+    )[0]
+
+
+def up_sum_kernel(info, *refs):
+    for out, core in ((refs[4], info[2]), (refs[5], 1 - info[2])):
+        out[...] = summed(refs[:4], pl.ds(pl.multiple_of(core * 64, 64), 64))
+
+
+def up_sum(info, parts):
+    return call(
+        up_sum_kernel,
+        "up_sum",
+        [block(128, 1024)] * 4,
+        [(block(64, 1024), of(f32, 64, 1024))] * 2,
+        [],
+        0,
+        info,
+        *parts,
+    )
+
+
+def up_whole_kernel(info, mine_ref, got_ref, w_ref, out_ref, sum_ref):
+    for ref, core in ((mine_ref, info[2]), (got_ref, 1 - info[2])):
+        for i, place in enumerate((0, 2, 1, 3)):
+            cols = pl.ds(pl.multiple_of(i * 512 + core * 256, 256), 256)
+            out_ref[:, cols] = ref[:, place * 256 : place * 256 + 256]
+    total = jnp.sum(w_ref[...].astype(f32) * out_ref[...], axis=1, keepdims=True)
+    sum_ref[...] = jnp.broadcast_to(total, sum_ref.shape)
+
+
+def up_whole(info, mine, got, w):
+    return call(
+        up_whole_kernel,
+        "up_whole",
+        [block(64, 1024)] * 2 + [block(64, 2048)],
+        [(block(64, 2048), of(f32, 64, 2048)), (block(64, 128), of(f32, 64, 128))],
+        [],
+        0,
+        info,
+        mine,
+        got,
+        w,
+    )
+
+
+def qkv_sum_kernel(info, *refs):
+    heads_ref, mid_ref, keep_ref, send_ref, out_ref = refs[4:]
+    total = summed(refs[:4])
+    out_ref[...] = total[:, 768:1280]
+    groups = (total[:, :768], total[:, 1280:])
+    q, k, v = (jnp.concatenate([g[:, j : j + 256] for g in groups], axis=1) for j in (0, 256, 512))
+    weights = heads_ref[...].astype(f32)
+    by_row = jnp.sum(weights[:, :768] * groups[0], axis=1, keepdims=True) + jnp.sum(
+        weights[:, 768:1536] * groups[1], axis=1, keepdims=True
+    )
+    both = jnp.broadcast_to(by_row, mid_ref.shape)
+    first = info[3] == 0
+    keep_ref[:, :512] = jnp.where(first, q, k)
+    keep_ref[:, 512:1024] = jnp.where(first, k, v)
+    keep_ref[:, 1024:] = jnp.where(first, both, mid_ref[...])
+    send_ref[:, :512] = jnp.where(first, v, q)
+    send_ref[:, 512:] = jnp.where(first, mid_ref[...], both)
+
+
+def qkv_sum(info, parts, heads, mid_sums):
+    return call(
+        qkv_sum_kernel,
+        "qkv_sum",
+        [block(64, 2048)] * 4 + [block(64, 1664), block(64, 128)],
+        [
+            (block(64, 1152), of(f32, 64, 1152)),
+            (block(64, 640), of(f32, 64, 640)),
+            (block(64, 512), of(f32, 64, 512)),
+        ],
+        [],
+        0,
+        info,
+        *parts,
+        heads,
+        mid_sums,
+    )
+
+
+def qkv_whole_kernel(info, keep_ref, got_ref, gain_ref, out_ref, gg_ref):
+    out_ref[:, :512] = keep_ref[:, :512]
+    out_ref[:, 512:1024] = got_ref[:, :512]
+    out_ref[:, 1024:] = keep_ref[:, 512:1024]
+    gg_ref[...] = (keep_ref[:, 1024:1025] + got_ref[:, 512:513]) / gain_ref[...].astype(f32)
+
+
+def qkv_whole(info, keep, got, gains):
+    return call(
+        qkv_whole_kernel,
+        "qkv_whole",
+        [block(64, 1152), block(64, 640), block(64, 1)],
+        [(block(64, 1536), of(f32, 64, 1536)), (block(64, 1), of(f32, 64, 1))],
+        [],
+        0,
+        info,
+        keep,
+        got,
+        gains,
+    )
+
+
+def input_grad_kernel(info, x_ref, e0_ref, e1_ref, gm_ref, g_ref, out_ref):
+    n, scale = centred(x_ref[...].astype(f32))
+    eg = (e0_ref[...] + e1_ref[...].astype(f32)) * g_ref[:1]
+    lean = eg - jnp.mean(eg, axis=-1, keepdims=True) - n * jnp.mean(eg * n, axis=-1, keepdims=True)
+    out_ref[...] = gm_ref[...] + scale * lean
+
+
+def input_grad(info, x, e_own, e_got, gm, gains):
+    rows = pl.BlockSpec((256, 1024), lambda i, s: (i, 0))
+    return call(
+        input_grad_kernel,
+        "input_grad",
+        [rows] * 4 + [block(2, 1024)],
+        [(rows, of(f32, HALF, 1024))],
+        [],
+        0,
+        info,
+        x,
+        e_own,
+        e_got,
+        gm,
+        gains,
+        grid=(2,),
+    )[0]
+
+
+def slot_bias(phones, prompts, targets):
+    places = jnp.arange(HALF, dtype=jnp.int32)
+    count = phones.shape[0]
+    segs, is_phone = [], None
+    for lengths in (phones + prompts, targets):
+        ends = jnp.stack([sum(lengths[i] for i in range(upto + 1)) for upto in range(count)])
+        seg = jnp.sum((places[:, None] >= ends[None, :]).astype(jnp.int32), axis=1)
+        segs.append(seg)
+        if is_phone is None:
+            onehot = seg[:, None] == jnp.arange(count, dtype=jnp.int32)[None, :]
+            phone_ends = jnp.sum(jnp.where(onehot, (ends - lengths + phones)[None, :], 0), axis=1)
+            is_phone = places < phone_ends
+    seg = jnp.concatenate(segs)
+    phone = jnp.concatenate([is_phone, jnp.zeros((HALF,), dtype=bool)])
+    order = jnp.arange(2 * HALF, dtype=jnp.int32)
+    allowed = (seg[:, None] == seg[None, :]) & (
+        phone[:, None] | (jnp.logical_not(phone)[None, :] & (order[:, None] <= order[None, :]))
+    )
+    allowed_t = (seg[:, None] == seg[None, :]) & (
+        phone[None, :] | (jnp.logical_not(phone)[:, None] & (order[None, :] <= order[:, None]))
+    )
+    bias = jnp.where(allowed, 0.0, NEG).astype(f32)
+    return bias, jnp.where(allowed_t, 0.0, NEG).astype(f32)
+
+
+def line_shards(tokens, cotangent, gains, w_qkv, w_out, w_up, w_down, phone_len, prompt_len, target_len):
+    r = lax.axis_index("rows")
+    side = lax.axis_index("pair")
+    core = r % 2
+    info = jnp.stack([r // 4, r // 2 % 2, core, side]).astype(jnp.int32)
+    x_own = tokens[0]
+    cot = cotangent[0]
+
+    out_all = lax.all_gather(w_out, ("pair", "rows"), axis=0, tiled=True).reshape(2, 1024, 512)
+    crossed = swap_y(jnp.concatenate([w_qkv[:, 512:1024], jnp.pad(gains, ((0, 0), (0, 127)))], axis=1))
+    x_other = swap_y(x_own)
+    heads = heads_of(info, w_qkv, crossed, gains)
+    pieces = along_line(heads)
+    up_keep, up_send = by_core(info, after(w_up, heads))
+    up_got = swap_c(up_send)
+    bias_t, bias = slot_bias(after(phone_len, up_keep)[0], prompt_len[0], target_len[0])
+    up_piece = both_rows(info, up_keep, up_got)
+    pieces, x_other, bias, bias_t, up_piece = barrier(pieces, x_other, bias, bias_t, up_piece)
+    qkv_line = stacked(info, pieces, "qkv_stack")
+    beside = swap_x(qkv_line)
+    qkv_line_sib = swap_c(qkv_line)
+    up_line = along_line(after(up_piece, qkv_line))
+    beside_sib = swap_c(beside)
+    up_line = stacked(info, up_line, "up_stack")
+    up_x, up_y = swap_x(up_line), swap_y(up_line)
+
+    qkv_pieces = (qkv_line, beside, after(qkv_line_sib, up_line), after(beside_sib, up_line))
+    projected, gain_all = project(info, x_own, x_other, qkv_pieces)
+    down_line = along_line(after(w_down, projected))
+    keep0, send0, lse0 = attend(info, projected, after(bias, out_all), 0)
+    got0 = swap_y(send0)
+    up_x, up_y = after((up_x, up_y), keep0)
+    up_far = swap_x(up_y)
+    keep1, send1, lse1 = attend(info, projected, after(bias, keep0), 1)
+    got1 = swap_y(send1)
+    down_line = stacked(info, after(down_line, keep1), "down_stack")
+    down_x = swap_x(down_line)
+    cot_sib = swap_c(after(cot, keep1))
+    nin_t, nin_t_oth = input_norm(info, after(x_own, down_line), x_other, gain_all)
+    down_y = swap_y(after(down_line, got0))
+    gain_all = touch(info, after(gain_all, nin_t, up_far, got0))
+    got1 = after(got1, gain_all)
+    mid, nm_own, att_t, att_t_oth = attention_out(info, x_own, (keep0, keep1), (got0, got1), out_all, gain_all)
+    nm_sib = swap_c(nm_own)
+    nin_t_sib = swap_c(after(nin_t_oth, nm_own))
+    att_t_sib = swap_c(att_t_oth)
+    up_pieces = (up_line, up_x, up_y, up_far, up_far)
+    down_far = [swap_y(down_x[:2]), swap_x(down_y[2:])]
+    nm_sib = after(nm_sib, touch(info, after(gain_all, nm_own, down_x, down_y)))
+    act, slope = up(info, nm_own, nm_sib, up_pieces)
+    down_pieces = (down_line, down_x, down_y, *down_far)
+    mixed_keep, mixed_send, gp = down(info, act, slope, cot, cot_sib, mid, down_pieces)
+
+    gp, nin_t_sib, att_t_sib = barrier(gp, nin_t_sib, att_t_sib)
+    mixed_got = swap_c(mixed_send)
+    e_keep, e_send = normed_back(info, gp, up_pieces)
+    e_got = swap_c(e_send)
+    far, down_across, down_beside, down_own = down_grad(info, cot, cot_sib, after(act, e_keep))
+    down_far, down_x = swap_x(far), swap_x(down_beside)
+    gm, gb, ga_keep, ga_send = middle_back(info, after(e_keep, far), after(e_got, far), cot, mid, gain_all, out_all)
+    ga_got = swap_y(ga_send)
+    gb_sib = swap_c(gb)
+    far, up_across, up_beside, up_own = up_grad(info, nm_own, nm_sib, after(gp, gb))
+    down_across = added(info, after(down_across, far), after(down_far, far))
+    down_y = swap_y(down_across)
+    up_far = swap_x(far)
+    gb_sib = after(gb_sib, down_across)
+    out_keep, out_send = out_grad(info, att_t, after(gb, down_across), att_t_sib, gb_sib)
+    out_got = swap_y(out_send)
+    ga_got = after(ga_got, out_keep)
+    dproj0 = attend_back(info, projected, after(bias_t, out_keep), lse0, ga_keep, ga_got, 0)
+    dproj0_sib = swap_c(dproj0)
+    down_x, down_y = after((down_x, down_y), dproj0)
+    down_parts = line_parts(info, down_own, down_x, down_y, "down_parts")
+    down_shift = [shift_z(down_parts[k], k) for k in range(1, LINE)]
+    up_x = swap_x(up_beside)
+    mixed = added(info, mixed_keep, after(mixed_got, out_got, down_parts), "mixed")
+    dproj0_sib = after(dproj0_sib, mixed)
+    first_beside, first_own = qkv_grad(info, nin_t, after(dproj0, mixed), nin_t_sib, dproj0_sib, (out_keep, out_got))
+    first_x = swap_x(first_beside)
+    up_across = added(info, up_across, after(up_far, first_own))
+    up_y = swap_y(up_across)
+    dproj1 = attend_back(info, projected, after(bias_t, first_own, up_across), lse1, ga_keep, ga_got, 1)
+    dproj1_sib = swap_c(dproj1)
+    g_down = down_sum(info, (after(down_parts[0], dproj1), *after(down_shift, dproj1)))
+    up_x, up_y = after((up_x, up_y), g_down)
+    up_parts = line_parts(info, up_own, up_x, up_y, "up_parts")
+    up_shift = [shift_z(up_parts[k], k) for k in range(1, LINE)]
+    dproj1_sib = after(dproj1_sib, up_parts)
+    second_beside, second_own = qkv_grad(info, nin_t, after(dproj1, up_parts), nin_t_sib, dproj1_sib)
+    second_x = swap_x(second_beside)
+    e_own, e_send = input_back(info, after(dproj0, second_own), dproj1, qkv_pieces)
+    e_got = swap_y(e_send)
+    first_x, second_x = after((first_x, second_x), e_own)
+    heads_parts = qkv_parts(info, first_own, first_x, second_own, second_x)
+    qkv_shift = [shift_z(heads_parts[k], k) for k in range(1, LINE)]
+    up_mine, up_send = up_sum(info, (after(up_parts[0], heads_parts), *up_shift))
+    up_got = swap_c(up_send)
+    grad_tokens = input_grad(info, after(x_own, up_mine), e_own, after(e_got, up_mine), gm, gain_all)
+    g_up, mid_sums = up_whole(info, up_mine, after(up_got, grad_tokens), w_up)
+    keep, send, g_out = qkv_sum(info, (after(heads_parts[0], mid_sums), *after(qkv_shift, mid_sums)), heads, mid_sums)
+    got = swap_y(send)
+    g_qkv, grad_gains = qkv_whole(info, keep, got, gains)
+    return (mixed[None], grad_tokens[None], grad_gains, g_qkv, g_out, g_up, g_down)
+
+
 def solution(mesh):
+    lined = mesh.shape["rows"] == 4 * LINE and mesh.shape["pair"] == 2
     return jax.shard_map(
-        shards,
+        line_shards if lined else shards,
         mesh=mesh,
         in_specs=(
             P("rows", "pair", None),

time: 931 us -> 422 us (0.45)
  waiting for transfers between devices: 496 us -> 75.3 us
  Pallas kernels: 0 us -> 233 us
  matrix products: 204 us -> 0 us
  other arithmetic: 82.5 us -> 8.1 us
  blocking collectives: 59 us -> 0 us
  starting transfers between devices: 7.22 us -> 56.2 us
  local copies, waits for them, and re-layouts: 57.3 us -> 24.9 us
    reduce_scatter x8 -> x0, waiting for transfers between devices: 327 us -> none  [the longest x1 108 us: shards(): lax.psum_scatter(grad_up.astype(jnp.bfloat16), 'rows', scatter_dimension=...]
    pallas_call x0 -> x36, Pallas kernels: none -> 233 us  [the longest x34 202 us: call(): pl.pallas_call(kernel, grid_spec=pltpu.PrefetchScalarGridSpec(num_scalar_...]
    dot_general x32 -> x0, matrix products: 161 us -> none  [the longest x1 27.9 us: shards(): jnp.dot(normed_mid_low, up_all, preferred_element_type=jnp.float32)]
    all_gather x6 -> x0, blocking collectives: 54 us -> none  [the longest x1 18.9 us: shards(): lax.all_gather(paired[0], 'rows', axis=0, tiled=True)]
    ppermute x2 -> x55, starting transfers between devices: 6.23 us -> 56.2 us  [the longest x18 29.2 us: shift_z(): return lax.ppermute(v, 'rows', row_pairs(lambda z, x, c: (z + k, x, c)))]
    unnamed x14 -> x1, waiting for transfers between devices: 47.5 us -> 0.68 us
    all_gather x4 -> x1, waiting for transfers between devices: 43 us -> 0.01 us  [line_shards(): lax.all_gather(w_out, ('pair', 'rows'), axis=0, tiled=True)]
    sub x8 -> x0, matrix products: 42.7 us -> none  [softmax_rows(): exponents = jnp.exp(scores - row_max)]
  transfers between devices with their start and end apart: 15 -> 56, of which waited for: 12 -> 18; matrix products, arithmetic and copies ran while one was open for 20% -> 3% of each run, Pallas kernels for 0% -> 52%
where the time goes in v3:
time: 422 us; the launch traced here: 415 us
  Pallas kernels  233 us (55%)
  waiting for transfers between devices  75.3 us (18%)
  starting transfers between devices  56.2 us (13%)
  local copies, waits for them, and re-layouts  24.9 us (6%)
  between operations  17.4 us (4%)
  other arithmetic  8.1 us (2%)
    pallas_call x34, Pallas kernels, call(): pl.pallas_call(kernel, grid_spec=pltpu.PrefetchScalarGridSpec(num_scalar_...  202 us
    ppermute x18, waiting for transfers between devices, shift_z(): return lax.ppermute(v, 'rows', row_pairs(lambda z, x, c: (z + k, x, c)))  36.1 us
    pallas_call x2, Pallas kernels, attend_back(): pl.pallas_call(attend_back_kernel, grid_spec=pltpu.PrefetchScalarGridSpec...  30.7 us
    ppermute x18, starting transfers between devices, shift_z(): return lax.ppermute(v, 'rows', row_pairs(lambda z, x, c: (z + k, x, c)))  29.2 us
    unnamed x140, local copies, waits for them, and re-layouts  21.2 us
    ppermute x11, waiting for transfers between devices, swap_x(): return lax.ppermute(v, 'rows', row_pairs(lambda z, x, c: (z, 1 - x, c)))  17.7 us
    ppermute x13, waiting for transfers between devices, swap_y(): return lax.ppermute(v, 'pair', [(0, 1), (1, 0)])  17.2 us
    ppermute x11, starting transfers between devices, swap_x(): return lax.ppermute(v, 'rows', row_pairs(lambda z, x, c: (z, 1 - x, c)))  13.3 us
  transfers between devices with their start and end apart: 56, of which 18 were waited for; matrix products, arithmetic and copies ran while one was open for 3% of the time, Pallas kernels for 52%

profile of v3, /device:TPU:8, one launch (start us, length us, event | category | flops | bytes accessed | tf_op | source)
XLA Modules:
  0.0 414.9 jit_solution(3496120750519725347)
XLA Ops:
  18.7 3.0 collective-permute-start.2
  30.1 5.1 %fusion.5 = (f32[1024,1024]{1,0:T(8,128)}, f32[1024,1024]{1,0:T(8,128)}) fusion(s32[1024]{0:T(1024)S(1)} %pad_add_fusion, pred[1024]{0:T(1024)(128)(4,1)S(1)} %get-tuple-element.285, pred[1024]{0:T(1024)(128)(4,1)S(1)} %get-tuple-element.286), kind=kLoop, calls=%fused_computation.9 | loop fusion | flops 11534336 | bytes 8394752 | tf_op jit(solution)/shard_map/jit(_where)/select_n | solution.py:1282
  38.2 2.6 collective-permute-done.1.refs_1_
  41.5 2.9 qkv_stack.1.refs_0_
  45.5 2.7 collective-permute-start.9
  49.7 6.2 %collective-permute-done.10.refs_3_ = bf16[128,1024]{1,0:T(8,128)(2,1)S(1)} collective-permute-done((bf16[128,1024]{1,0:T(8,128)(2,1)}, bf16[128,1024]{1,0:T(8,128)(2,1)S(1)}, u32[]{:S(2)}, u32[]{:S(2)}) %collective-permute-start.10) | collective-permute-done | bytes 262176 | tf_op jit(solution)/shard_map/ppermute | solution.py:322
  55.9 7.5 %collective-permute-done.9.refs_2_ = bf16[128,1024]{1,0:T(8,128)(2,1)S(1)} collective-permute-done((bf16[128,1024]{1,0:T(8,128)(2,1)}, bf16[128,1024]{1,0:T(8,128)(2,1)S(1)}, u32[]{:S(2)}, u32[]{:S(2)}) %collective-permute-start.9) | collective-permute-done | bytes 262176 | tf_op jit(solution)/shard_map/ppermute | solution.py:322
  63.4 7.5 %collective-permute-done.8.refs_1_ = bf16[128,1024]{1,0:T(8,128)(2,1)S(1)} collective-permute-done((bf16[128,1024]{1,0:T(8,128)(2,1)}, bf16[128,1024]{1,0:T(8,128)(2,1)S(1)}, u32[]{:S(2)}, u32[]{:S(2)}) %collective-permute-start.8) | collective-permute-done | bytes 262176 | tf_op jit(solution)/shard_map/ppermute | solution.py:322
  71.6 2.9 up_stack.1.refs_0_
  82.5 10.0 %project.1 = (bf16[1024,1536]{1,0:T(8,128)(2,1)}, f32[2,1024]{1,0:T(2,128)}) custom-call(s32[4]{0:T(128)} %pad_add_fusion.1.info, bf16[512,1024]{1,0:T(8,128)(2,1)} %bitcast.25, bf16[512,1024]{1,0:T(8,128)(2,1)} %copy-done.22, bf16[4,64,1664]{2,1,0:T(8,128)(2,1)} %qkv_stack.1.refs_0_, bf16[4,64,1664]{2,1,0:T(8,128)(2,1)} %copy-done.8, ...), custom_call_target="tpu_custom_call" | custom-call | flops 575000000 | bytes 65536 | tf_op jit(solution)/shard_map/project/pallas_call | solution.py:288
  92.5 6.2 %collective-permute-start.16 = (bf16[256,512]{1,0:T(8,128)(2,1)S(1)}, bf16[256,512]{1,0:T(8,128)(2,1)S(1)}, u32[]{:S(2)}, u32[]{:S(2)}) collective-permute-start(bf16[256,512]{1,0:T(8,128)(2,1)S(1)} %copy-done.39), channel_id=1, source_target_pairs={{0,24},{2,26},{4,28},{6,30},{8,0},{10,2},{12,4},{14,6},{16,8},{18,... | collective-permute-start | bytes 786440 | tf_op jit(solution)/shard_map/ppermute | solution.py:322
  100.8 11.4 %attend_0.1 = (bf16[512,256]{1,0:T(8,128)(2,1)}, bf16[512,256]{1,0:T(8,128)(2,1)}, f32[2,2,1024]{2,1,0:T(2,128)}) custom-call(s32[4]{0:T(128)} %pad_add_fusion.1.info, bf16[1024,1536]{1,0:T(8,128)(2,1)} %get-tuple-element.151.q_ref.k_ref.v_ref, bf16[1024,1536]{1,0:T(8,128)(2,1)} %get-tuple-element.151.q_ref.k_ref.v_ref, ...), custom_call_target="tpu_custom_call" | custom-call | flops 575000000 | bytes 65536 | tf_op jit(solution)/shard_map/attend_0/pallas_call | solution.py:288
  112.6 11.4 %attend_1.1 = (bf16[512,256]{1,0:T(8,128)(2,1)}, bf16[512,256]{1,0:T(8,128)(2,1)}, f32[2,2,1024]{2,1,0:T(2,128)}) custom-call(s32[4]{0:T(128)} %pad_add_fusion.1.info, bf16[1024,1536]{1,0:T(8,128)(2,1)} %get-tuple-element.151.q_ref.k_ref.v_ref, bf16[1024,1536]{1,0:T(8,128)(2,1)} %get-tuple-element.151.q_ref.k_ref.v_ref, ...), custom_call_target="tpu_custom_call" | custom-call | flops 23000000512 | bytes 65536 | tf_op jit(solution)/shard_map/attend_1/pallas_call | solution.py:288
  124.9 2.9 down_stack.1.refs_0_
  131.5 5.3 %input_norm.1 = (bf16[8,64,1024]{2,1,0:T(8,128)(2,1)}, bf16[8,64,1024]{2,1,0:T(8,128)(2,1)}) custom-call(s32[4]{0:T(128)} %pad_add_fusion.1.info, bf16[512,1024]{1,0:T(8,128)(2,1)} %bitcast.26, bf16[512,1024]{1,0:T(8,128)(2,1)} %copy-done.22, f32[2,1024]{1,0:T(2,128)} %get-tuple-element.168.g_ref.a_ref), custom_call_target="tpu_custom_call" | custom-call | flops 575000000 | bytes 65536 | tf_op jit(solution)/shard_map/input_norm/pallas_call | solution.py:288
  141.1 6.1 %attention_out.1 = (f32[512,1024]{1,0:T(8,128)}, bf16[512,1024]{1,0:T(8,128)(2,1)}, bf16[8,64,512]{2,1,0:T(8,128)(2,1)}, bf16[8,64,512]{2,1,0:T(8,128)(2,1)}) custom-call(s32[4]{0:T(128)} %pad_add_fusion.1.info, bf16[512,1024]{1,0:T(8,128)(2,1)} %bitcast.27, bf16[512,256]{1,0:T(8,128)(2,1)} %get-tuple-element.154.k0, ...), custom_call_target="tpu_custom_call" | custom-call | flops 575000000 | bytes 65536 | tf_op jit(solution)/shard_map/attention_out/pallas_call | solution.py:288
  147.8 11.6 %collective-permute-done.22.refs_1_ = bf16[4,256,512]{2,1,0:T(8,128)(2,1)S(1)} collective-permute-done((bf16[4,256,512]{2,1,0:T(8,128)(2,1)}, bf16[4,256,512]{2,1,0:T(8,128)(2,1)S(1)}, u32[]{:S(2)}, u32[]{:S(2)}) %collective-permute-start.22) | collective-permute-done | bytes 1048608 | tf_op jit(solution)/shard_map/ppermute | solution.py:326
  163.4 13.6 %up.1 = (bf16[1024,2048]{1,0:T(8,128)(2,1)}, bf16[1024,2048]{1,0:T(8,128)(2,1)}) custom-call(s32[4]{0:T(128)} %pad_add_fusion.1.info, bf16[512,1024]{1,0:T(8,128)(2,1)} %get-tuple-element.170.x0_ref.n0_ref, bf16[512,1024]{1,0:T(8,128)(2,1)} %copy-done.6, bf16[4,128,1024]{2,1,0:T(8,128)(2,1)} %up_stack.1.refs_0_, bf16[4,128,1024]{2,1,0:T(8,128)(2,1)} %copy-done.5, ...), custom_call_target="tpu_custom_call" | custom-call | flops 575000000 | bytes 65536 | tf_op jit(solution)/shard_map/up/pallas_call | solution.py:288
  178.4 19.6 %down.1 = (f32[512,1024]{1,0:T(8,128)}, bf16[512,1024]{1,0:T(8,128)(2,1)}, bf16[1024,2048]{1,0:T(8,128)(2,1)}) custom-call(s32[4]{0:T(128)} %pad_add_fusion.1.info, bf16[1024,2048]{1,0:T(8,128)(2,1)} %get-tuple-element.186.act_ref, bf16[1024,2048]{1,0:T(8,128)(2,1)} %get-tuple-element.173.slope_ref, bf16[512,1024]{1,0:T(8,128)(2,1)} %bitcast.20, ...), custom_call_target="tpu_custom_call" | custom-call | flops 575000000 | bytes 65536 | tf_op jit(solution)/shard_map/down/pallas_call | solution.py:288
  198.0 11.0 %normed_back.1 = (f32[512,1024]{1,0:T(8,128)}, bf16[512,1024]{1,0:T(8,128)(2,1)}) custom-call(s32[4]{0:T(128)} %pad_add_fusion.1.info, bf16[1024,2048]{1,0:T(8,128)(2,1)} %get-tuple-element.193.gp_ref, bf16[4,128,1024]{2,1,0:T(8,128)(2,1)} %up_stack.1.refs_0_, bf16[4,128,1024]{2,1,0:T(8,128)(2,1)} %copy-done.5, bf16[4,128,1024]{2,1,0:T(8,128)(2,1)} %copy-done.4, ...), custom_call_target="tpu_custom_call" | custom-call | flops 575000000 | bytes 65536 | tf_op jit(solution)/shard_map/normed_back/pallas_call | solution.py:288
  209.1 12.9 %down_grad.1 = (bf16[4,512,256]{2,1,0:T(8,128)(2,1)}, bf16[4,512,256]{2,1,0:T(8,128)(2,1)}, bf16[4,512,256]{2,1,0:T(8,128)(2,1)}, bf16[4,512,256]{2,1,0:T(8,128)(2,1)}) custom-call(s32[4]{0:T(128)} %pad_add_fusion.1.info, bf16[512,1024]{1,0:T(8,128)(2,1)} %bitcast.21, bf16[512,1024]{1,0:T(8,128)(2,1)} %copy-done.2, bf16[1024,2048]{1,0:T(8,128)(2,1)} %get-tuple-element.186.act_ref), custom_call_target="tpu_custom_call" | custom-call | flops 575000000 | bytes 65536 | tf_op jit(solution)/shard_map/down_grad/pallas_call | solution.py:288
  224.7 7.8 %middle_back.1 = (f32[512,1024]{1,0:T(8,128)}, bf16[512,1024]{1,0:T(8,128)(2,1)}, bf16[512,512]{1,0:T(8,128)(2,1)}, bf16[512,512]{1,0:T(8,128)(2,1)}) custom-call(s32[4]{0:T(128)} %pad_add_fusion.1.info, f32[512,1024]{1,0:T(8,128)} %get-tuple-element.188.e0_ref, bf16[512,1024]{1,0:T(8,128)(2,1)} %copy-done.16, bf16[512,1024]{1,0:T(8,128)(2,1)} %bitcast.22, ...), custom_call_target="tpu_custom_call" | custom-call | flops 575000000 | bytes 65536 | tf_op jit(solution)/shard_map/middle_back/pallas_call | solution.py:288
  233.3 10.3 %up_grad.1 = (bf16[4,128,1024]{2,1,0:T(8,128)(2,1)}, bf16[4,128,1024]{2,1,0:T(8,128)(2,1)}, bf16[4,128,1024]{2,1,0:T(8,128)(2,1)}, bf16[4,128,1024]{2,1,0:T(8,128)(2,1)}) custom-call(s32[4]{0:T(128)} %pad_add_fusion.1.info, bf16[512,1024]{1,0:T(8,128)(2,1)} %get-tuple-element.170.x0_ref.n0_ref, bf16[512,1024]{1,0:T(8,128)(2,1)} %copy-done.6, ...), custom_call_target="tpu_custom_call" | custom-call | flops 575000000 | bytes 65536 | tf_op jit(solution)/shard_map/up_grad/pallas_call | solution.py:288
  243.6 4.5 %collective-permute-done.30.b_ref = bf16[4,512,256]{2,1,0:T(8,128)(2,1)S(1)} collective-permute-done((bf16[4,512,256]{2,1,0:T(8,128)(2,1)}, bf16[4,512,256]{2,1,0:T(8,128)(2,1)S(1)}, u32[]{:S(2)}, u32[]{:S(2)}) %collective-permute-start.30) | collective-permute-done | bytes 1048608 | tf_op jit(solution)/shard_map/ppermute | solution.py:326
  249.1 3.1 added.2
  254.3 4.6 %out_grad.1 = (bf16[8,64,512]{2,1,0:T(8,128)(2,1)}, bf16[8,64,512]{2,1,0:T(8,128)(2,1)}) custom-call(s32[4]{0:T(128)} %pad_add_fusion.1.info, bf16[512,512]{1,0:T(8,128)(2,1)} %bitcast.36, bf16[512,1024]{1,0:T(8,128)(2,1)} %get-tuple-element.197.r0_ref, bf16[512,512]{1,0:T(8,128)(2,1)} %bitcast.14.l1_ref, bf16[512,1024]{1,0:T(8,128)(2,1)} %copy-done.20), custom_call_target="tpu_custom_call" | custom-call | flops 575000000 | bytes 65536 | tf_op jit(solution)/shard_map/out_grad/pallas_call | solution.py:288
  260.6 15.5 %attend_back_0.1.r0_ref.d0_ref = bf16[1024,768]{1,0:T(8,128)(2,1)} custom-call(s32[4]{0:T(128)} %pad_add_fusion.1.info, bf16[1024,1536]{1,0:T(8,128)(2,1)} %get-tuple-element.151.q_ref.k_ref.v_ref, bf16[1024,1536]{1,0:T(8,128)(2,1)} %get-tuple-element.151.q_ref.k_ref.v_ref, bf16[1024,1536]{1,0:T(8,128)(2,1)} %get-tuple-element.151.q_ref.k_ref.v_ref, ...), custom_call_target="tpu_custom_call" | custom-call | flops 23000000512 | bytes 65536 | tf_op jit(solution)/shard_map/attend_back_0/pallas_call | solution.py:534
  279.5 3.6 down_parts.1
  288.5 3.5 mixed.1
  293.9 6.4 %qkv_grad.2 = (bf16[4,64,1280]{2,1,0:T(8,128)(2,1)}, bf16[4,64,1280]{2,1,0:T(8,128)(2,1)}) custom-call(s32[4]{0:T(128)} %pad_add_fusion.1.info, bf16[512,1024]{1,0:T(8,128)(2,1)} %bitcast.31, bf16[1024,768]{1,0:T(8,128)(2,1)} %attend_back_0.1.r0_ref.d0_ref, bf16[512,1024]{1,0:T(8,128)(2,1)} %bitcast.33, bf16[1024,768]{1,0:T(8,128)(2,1)} %copy-done.13, ...), custom_call_target="tpu_custom_call" | custom-call | flops 575000000 | bytes 65536 | tf_op jit(solution)/shard_map/qkv_grad/pallas_call | solution.py:288
  301.3 3.2 added.3
  304.7 15.2 %attend_back_1.1.r0_ref.d1_ref = bf16[1024,768]{1,0:T(8,128)(2,1)} custom-call(s32[4]{0:T(128)} %pad_add_fusion.1.info, bf16[1024,1536]{1,0:T(8,128)(2,1)} %get-tuple-element.151.q_ref.k_ref.v_ref, bf16[1024,1536]{1,0:T(8,128)(2,1)} %get-tuple-element.151.q_ref.k_ref.v_ref, bf16[1024,1536]{1,0:T(8,128)(2,1)} %get-tuple-element.151.q_ref.k_ref.v_ref, ...), custom_call_target="tpu_custom_call" | custom-call | flops 575000000 | bytes 65536 | tf_op jit(solution)/shard_map/attend_back_1/pallas_call | solution.py:534
  321.9 2.8 down_sum.1
  324.8 2.7 collective-permute-done.39.c_ref
  328.6 3.7 up_parts.1
  333.5 5.8 %qkv_grad.3 = (bf16[4,64,768]{2,1,0:T(8,128)(2,1)}, bf16[4,64,768]{2,1,0:T(8,128)(2,1)}) custom-call(s32[4]{0:T(128)} %pad_add_fusion.1.info, bf16[512,1024]{1,0:T(8,128)(2,1)} %bitcast.32, bf16[1024,768]{1,0:T(8,128)(2,1)} %attend_back_1.1.r0_ref.d1_ref, bf16[512,1024]{1,0:T(8,128)(2,1)} %bitcast.34, bf16[1024,768]{1,0:T(8,128)(2,1)} %copy-done.14), custom_call_target="tpu_custom_call" | custom-call | flops 575000000 | bytes 65536 | tf_op jit(solution)/shard_map/qkv_grad/pallas_call | solution.py:288
  342.2 3.2 collective-permute-start.47
  345.6 9.4 %input_back.1 = (f32[512,1024]{1,0:T(8,128)}, bf16[512,1024]{1,0:T(8,128)(2,1)}) custom-call(s32[4]{0:T(128)} %pad_add_fusion.1.info, bf16[1024,768]{1,0:T(8,128)(2,1)} %attend_back_0.1.r0_ref.d0_ref, bf16[1024,768]{1,0:T(8,128)(2,1)} %attend_back_1.1.r0_ref.d1_ref, bf16[4,64,1664]{2,1,0:T(8,128)(2,1)} %qkv_stack.1.refs_0_, bf16[4,64,1664]{2,1,0:T(8,128)(2,1)} %copy-done.8, ...), custom_call_target="tpu_custom_call" | custom-call | flops 575000000 | bytes 65536 | tf_op jit(solution)/shard_map/input_back/pallas_call | solution.py:288
  356.1 3.3 qkv_parts.1
  359.4 2.6 collective-permute-done.47.refs_2_
  362.0 2.8 collective-permute-done.48.refs_3_
  365.5 2.7 up_sum.1
  371.6 5.2 %collective-permute-done.49.e1_ref = bf16[512,1024]{1,0:T(8,128)(2,1)S(1)} collective-permute-done((bf16[512,1024]{1,0:T(8,128)(2,1)}, bf16[512,1024]{1,0:T(8,128)(2,1)S(1)}, u32[]{:S(2)}, u32[]{:S(2)}) %collective-permute-start.49) | collective-permute-done | bytes 1048608 | tf_op jit(solution)/shard_map/ppermute | solution.py:334
  377.8 5.3 %input_grad.1 = f32[512,1024]{1,0:T(8,128)} custom-call(s32[4]{0:T(128)} %pad_add_fusion.1.info, bf16[512,1024]{1,0:T(8,128)(2,1)} %bitcast.28, f32[512,1024]{1,0:T(8,128)} %get-tuple-element.243.e0_ref, bf16[512,1024]{1,0:T(8,128)(2,1)} %copy-done.15, f32[512,1024]{1,0:T(8,128)} %get-tuple-element.255.gm_ref, f32[2,1024]{1,0:T(2,128)} %touch.2.g_ref), custom_call_target="tpu_custom_call" | custom-call | flops 575000000 | bytes 65536 | tf_op jit(solution)/shard_map/input_grad/pallas_call | solution.py:288
  383.8 2.6 up_whole.1
  386.4 5.2 %collective-permute-done.52.refs_2_ = bf16[64,2048]{1,0:T(8,128)(2,1)S(1)} collective-permute-done((bf16[64,2048]{1,0:T(8,128)(2,1)S(1)}, bf16[64,2048]{1,0:T(8,128)(2,1)S(1)}, u32[]{:S(2)}, u32[]{:S(2)}) %collective-permute-start.52) | collective-permute-done | bytes 262176 | tf_op jit(solution)/shard_map/ppermute | solution.py:322
  394.1 2.9 qkv_sum.1
  398.6 4.8 %collective-permute-done.54.got_ref = f32[64,640]{1,0:T(8,128)S(1)} collective-permute-done((f32[64,640]{1,0:T(8,128)}, f32[64,640]{1,0:T(8,128)S(1)}, u32[]{:S(2)}, u32[]{:S(2)}) %collective-permute-start.54) | collective-permute-done | bytes 163872 | tf_op jit(solution)/shard_map/ppermute | solution.py:334
  (258 shorter events, 92.5 us)
Async XLA Ops:
  7.2 93.6 %all-gather.2.cloned.1.call-start = ((), (), s32[]{:S(2)}) async-start(), calls=%async_computation | async-start | bytes 2162688 | tf_op jit(solution)/shard_map/all_gather | solution.py:1294
  11.1 29.6 %collective-permute-start.4 = (bf16[512,1024]{1,0:T(8,128)(2,1)}, bf16[512,1024]{1,0:T(8,128)(2,1)S(1)}, u32[]{:S(2)}, u32[]{:S(2)}) collective-permute-start(bf16[512,1024]{1,0:T(8,128)(2,1)} %bitcast.24), channel_id=1, source_target_pairs={{0,1},{1,0},{2,3},{3,2},{4,5},{5,4},{6,7},{7,6},{8,9},{9,8},{10,11... | collective-permute-start | bytes 3145736 | tf_op jit(solution)/shard_map/ppermute | solution.py:334
  18.7 19.5 %collective-permute-start.3 = (bf16[64,1664]{1,0:T(8,128)(2,1)}, bf16[64,1664]{1,0:T(8,128)(2,1)S(1)}, u32[]{:S(2)}, u32[]{:S(2)}) collective-permute-start(bf16[64,1664]{1,0:T(8,128)(2,1)} %heads.1.refs_0_.refs_4_), channel_id=1, source_target_pairs={{0,24},{2,26},{4,28},{6,30},{8,0},{10,2},{12,4},{14,6},{16,8},{18,... | collective-permute-start | bytes 638984 | tf_op jit(solution)/shard_map/ppermute | solution.py:322
  18.7 19.5 %collective-permute-start.2 = (bf16[64,1664]{1,0:T(8,128)(2,1)}, bf16[64,1664]{1,0:T(8,128)(2,1)S(1)}, u32[]{:S(2)}, u32[]{:S(2)}) collective-permute-start(bf16[64,1664]{1,0:T(8,128)(2,1)} %heads.1.refs_0_.refs_4_), channel_id=1, source_target_pairs={{0,16},{2,18},{4,20},{6,22},{8,24},{10,26},{12,28},{14,30},{16,0},... | collective-permute-start | bytes 638984 | tf_op jit(solution)/shard_map/ppermute | solution.py:322
  21.7 19.1 %collective-permute-start.1 = (bf16[64,1664]{1,0:T(8,128)(2,1)}, bf16[64,1664]{1,0:T(8,128)(2,1)S(1)}, u32[]{:S(2)}, u32[]{:S(2)}) collective-permute-start(bf16[64,1664]{1,0:T(8,128)(2,1)} %heads.1.refs_0_.refs_4_), channel_id=1, source_target_pairs={{0,8},{2,10},{4,12},{6,14},{8,16},{10,18},{12,20},{14,22},{16,24},... | collective-permute-start | bytes 638984 | tf_op jit(solution)/shard_map/ppermute | solution.py:322
  45.5 17.9 %collective-permute-start.9 = (bf16[128,1024]{1,0:T(8,128)(2,1)}, bf16[128,1024]{1,0:T(8,128)(2,1)S(1)}, u32[]{:S(2)}, u32[]{:S(2)}) collective-permute-start(bf16[128,1024]{1,0:T(8,128)(2,1)} %both_rows.1.refs_0_), channel_id=1, source_target_pairs={{0,16},{2,18},{4,20},{6,22},{8,24},{10,26},{12,28},{14,30},{16,0},... | collective-permute-start | bytes 786440 | tf_op jit(solution)/shard_map/ppermute | solution.py:322
  48.2 22.7 %collective-permute-start.8 = (bf16[128,1024]{1,0:T(8,128)(2,1)}, bf16[128,1024]{1,0:T(8,128)(2,1)S(1)}, u32[]{:S(2)}, u32[]{:S(2)}) collective-permute-start(bf16[128,1024]{1,0:T(8,128)(2,1)} %both_rows.1.refs_0_), channel_id=1, source_target_pairs={{0,8},{2,10},{4,12},{6,14},{8,16},{10,18},{12,20},{14,22},{16,24},... | collective-permute-start | bytes 786440 | tf_op jit(solution)/shard_map/ppermute | solution.py:322
  48.2 29.3 %collective-permute-start.6 = (bf16[4,64,1664]{2,1,0:T(8,128)(2,1)}, bf16[4,64,1664]{2,1,0:T(8,128)(2,1)S(1)}, u32[]{:S(2)}, u32[]{:S(2)}) collective-permute-start(bf16[4,64,1664]{2,1,0:T(8,128)(2,1)} %qkv_stack.1.refs_0_), channel_id=1, source_target_pairs={{0,4},{2,6},{4,0},{6,2},{8,12},{10,14},{12,8},{14,10},{16,20},{18,... | collective-permute-start | bytes 2555912 | tf_op jit(solution)/shard_map/ppermute | solution.py:326
  74.5 37.7 %collective-permute-start.18 = (bf16[4,128,1024]{2,1,0:T(8,128)(2,1)}, bf16[4,128,1024]{2,1,0:T(8,128)(2,1)S(1)}, u32[]{:S(2)}, u32[]{:S(2)}) collective-permute-start(bf16[4,128,1024]{2,1,0:T(8,128)(2,1)} %up_stack.1.refs_0_), channel_id=1, source_target_pairs={{0,1},{1,0},{2,3},{3,2},{4,5},{5,4},{6,7},{7,6},{8,9},{9,8},{10,11... | collective-permute-start | bytes 3145736 | tf_op jit(solution)/shard_map/ppermute | solution.py:334
  76.0 36.2 %collective-permute-start.17 = (bf16[4,128,1024]{2,1,0:T(8,128)(2,1)}, bf16[4,128,1024]{2,1,0:T(8,128)(2,1)S(1)}, u32[]{:S(2)}, u32[]{:S(2)}) collective-permute-start(bf16[4,128,1024]{2,1,0:T(8,128)(2,1)} %up_stack.1.refs_0_), channel_id=1, source_target_pairs={{0,4},{2,6},{4,0},{6,2},{8,12},{10,14},{12,8},{14,10},{16,20},{18,... | collective-permute-start | bytes 3145736 | tf_op jit(solution)/shard_map/ppermute | solution.py:326
  92.5 31.5 %collective-permute-start.16 = (bf16[256,512]{1,0:T(8,128)(2,1)S(1)}, bf16[256,512]{1,0:T(8,128)(2,1)S(1)}, u32[]{:S(2)}, u32[]{:S(2)}) collective-permute-start(bf16[256,512]{1,0:T(8,128)(2,1)S(1)} %copy-done.39), channel_id=1, source_target_pairs={{0,24},{2,26},{4,28},{6,30},{8,0},{10,2},{12,4},{14,6},{16,8},{18,... | collective-permute-start | bytes 786440 | tf_op jit(solution)/shard_map/ppermute | solution.py:322
  98.7 25.3 %collective-permute-start.15 = (bf16[256,512]{1,0:T(8,128)(2,1)S(1)}, bf16[256,512]{1,0:T(8,128)(2,1)S(1)}, u32[]{:S(2)}, u32[]{:S(2)}) collective-permute-start(bf16[256,512]{1,0:T(8,128)(2,1)S(1)} %copy-done.39), channel_id=1, source_target_pairs={{0,16},{2,18},{4,20},{6,22},{8,24},{10,26},{12,28},{14,30},{16,0},... | collective-permute-start | bytes 786440 | tf_op jit(solution)/shard_map/ppermute | solution.py:322
  98.7 25.3 %collective-permute-start.14 = (bf16[256,512]{1,0:T(8,128)(2,1)S(1)}, bf16[256,512]{1,0:T(8,128)(2,1)S(1)}, u32[]{:S(2)}, u32[]{:S(2)}) collective-permute-start(bf16[256,512]{1,0:T(8,128)(2,1)S(1)} %copy-done.39), channel_id=1, source_target_pairs={{0,8},{2,10},{4,12},{6,14},{8,16},{10,18},{12,20},{14,22},{16,24},... | collective-permute-start | bytes 786440 | tf_op jit(solution)/shard_map/ppermute | solution.py:322
  112.2 24.6 %collective-permute-start.12 = (bf16[512,256]{1,0:T(8,128)(2,1)}, bf16[512,256]{1,0:T(8,128)(2,1)S(1)}, u32[]{:S(2)}, u32[]{:S(2)}) collective-permute-start(bf16[512,256]{1,0:T(8,128)(2,1)} %get-tuple-element.157), channel_id=1, source_target_pairs={{0,1},{1,0},{2,3},{3,2},{4,5},{5,4},{6,7},{7,6},{8,9},{9,8},{10,11... | collective-permute-start | bytes 786440 | tf_op jit(solution)/shard_map/ppermute | solution.py:334
  112.3 26.1 %collective-permute-start.19 = (bf16[4,128,1024]{2,1,0:T(8,128)(2,1)S(1)}, bf16[4,128,1024]{2,1,0:T(8,128)(2,1)S(1)}, u32[]{:S(2)}, u32[]{:S(2)}) collective-permute-start(bf16[4,128,1024]{2,1,0:T(8,128)(2,1)S(1)} %collective-permute-done.18.refs_2_), channel_id=1, source_target_pairs={{0,4},{2,6},{4,0},{6,2},{8,12},{10,14},{12,8},{14,10},{16,20},{18,... | collective-permute-start | bytes 3145736 | tf_op jit(solution)/shard_map/ppermute | solution.py:326
  127.8 31.6 %collective-permute-start.22 = (bf16[4,256,512]{2,1,0:T(8,128)(2,1)}, bf16[4,256,512]{2,1,0:T(8,128)(2,1)S(1)}, u32[]{:S(2)}, u32[]{:S(2)}) collective-permute-start(bf16[4,256,512]{2,1,0:T(8,128)(2,1)} %down_stack.1.refs_0_), channel_id=1, source_target_pairs={{0,4},{2,6},{4,0},{6,2},{8,12},{10,14},{12,8},{14,10},{16,20},{18,... | collective-permute-start | bytes 3145736 | tf_op jit(solution)/shard_map/ppermute | solution.py:326
  136.8 24.4 %collective-permute-start.23 = (bf16[4,256,512]{2,1,0:T(8,128)(2,1)}, bf16[4,256,512]{2,1,0:T(8,128)(2,1)S(1)}, u32[]{:S(2)}, u32[]{:S(2)}) collective-permute-start(bf16[4,256,512]{2,1,0:T(8,128)(2,1)} %down_stack.1.refs_0_), channel_id=1, source_target_pairs={{0,1},{1,0},{2,3},{3,2},{4,5},{5,4},{6,7},{7,6},{8,9},{9,8},{10,11... | collective-permute-start | bytes 3145736 | tf_op jit(solution)/shard_map/ppermute | solution.py:334
  147.2 15.2 %collective-permute-start.20 = (bf16[512,1024]{1,0:T(8,128)(2,1)}, bf16[512,1024]{1,0:T(8,128)(2,1)S(1)}, u32[]{:S(2)}, u32[]{:S(2)}) collective-permute-start(bf16[512,1024]{1,0:T(8,128)(2,1)} %get-tuple-element.170.x0_ref.n0_ref), channel_id=1, source_target_pairs={{0,2},{2,0},{4,6},{6,4},{8,10},{10,8},{12,14},{14,12},{16,18},{18,... | collective-permute-start | bytes 3145736 | tf_op jit(solution)/shard_map/ppermute | solution.py:330
  147.2 29.8 %collective-permute-start.21 = (bf16[512,1024]{1,0:T(8,128)(2,1)S(1)}, bf16[512,1024]{1,0:T(8,128)(2,1)S(1)}, u32[]{:S(2)}, u32[]{:S(2)}) collective-permute-start(bf16[512,1024]{1,0:T(8,128)(2,1)S(1)} %bitcast.23), channel_id=1, source_target_pairs={{0,2},{2,0},{4,6},{6,4},{8,10},{10,8},{12,14},{14,12},{16,18},{18,... | collective-permute-start | bytes 3145736 | tf_op jit(solution)/shard_map/ppermute | solution.py:330
  147.7 50.3 %collective-permute-start.27 = (bf16[8,64,1024]{2,1,0:T(8,128)(2,1)}, bf16[8,64,1024]{2,1,0:T(8,128)(2,1)S(1)}, u32[]{:S(2)}, u32[]{:S(2)}) collective-permute-start(bf16[8,64,1024]{2,1,0:T(8,128)(2,1)} %get-tuple-element.182), channel_id=1, source_target_pairs={{0,2},{2,0},{4,6},{6,4},{8,10},{10,8},{12,14},{14,12},{16,18},{18,... | collective-permute-start | bytes 3145736 | tf_op jit(solution)/shard_map/ppermute | solution.py:330
  159.5 17.5 %collective-permute-start.24 = (bf16[2,256,512]{2,1,0:T(8,128)(2,1)S(1)}, bf16[2,256,512]{2,1,0:T(8,128)(2,1)S(1)}, u32[]{:S(2)}, u32[]{:S(2)}) collective-permute-start(bf16[2,256,512]{2,1,0:T(8,128)(2,1)S(1)} %slice.43), channel_id=1, source_target_pairs={{0,1},{1,0},{2,3},{3,2},{4,5},{5,4},{6,7},{7,6},{8,9},{9,8},{10,11... | collective-permute-start | bytes 1572872 | tf_op jit(solution)/shard_map/ppermute | solution.py:334
  162.1 14.9 %collective-permute-start.25 = (bf16[2,256,512]{2,1,0:T(8,128)(2,1)}, bf16[2,256,512]{2,1,0:T(8,128)(2,1)S(1)}, u32[]{:S(2)}, u32[]{:S(2)}) collective-permute-start(bf16[2,256,512]{2,1,0:T(8,128)(2,1)} %slice.44), channel_id=1, source_target_pairs={{0,4},{2,6},{4,0},{6,2},{8,12},{10,14},{12,8},{14,10},{16,20},{18,... | collective-permute-start | bytes 1572872 | tf_op jit(solution)/shard_map/ppermute | solution.py:326
  162.4 35.6 %collective-permute-start.28 = (bf16[8,64,512]{2,1,0:T(8,128)(2,1)}, bf16[8,64,512]{2,1,0:T(8,128)(2,1)}, u32[]{:S(2)}, u32[]{:S(2)}) collective-permute-start(bf16[8,64,512]{2,1,0:T(8,128)(2,1)} %get-tuple-element.183), channel_id=1, source_target_pairs={{0,2},{2,0},{4,6},{6,4},{8,10},{10,8},{12,14},{14,12},{16,18},{18,... | collective-permute-start | bytes 1572872 | tf_op jit(solution)/shard_map/ppermute | solution.py:330
  209.0 14.7 %collective-permute-start.29 = (bf16[512,1024]{1,0:T(8,128)(2,1)}, bf16[512,1024]{1,0:T(8,128)(2,1)S(1)}, u32[]{:S(2)}, u32[]{:S(2)}) collective-permute-start(bf16[512,1024]{1,0:T(8,128)(2,1)} %get-tuple-element.189), channel_id=1, source_target_pairs={{0,2},{2,0},{4,6},{6,4},{8,10},{10,8},{12,14},{14,12},{16,18},{18,... | collective-permute-start | bytes 3145736 | tf_op jit(solution)/shard_map/ppermute | solution.py:330
  221.9 26.2 %collective-permute-start.30 = (bf16[4,512,256]{2,1,0:T(8,128)(2,1)}, bf16[4,512,256]{2,1,0:T(8,128)(2,1)S(1)}, u32[]{:S(2)}, u32[]{:S(2)}) collective-permute-start(bf16[4,512,256]{2,1,0:T(8,128)(2,1)} %get-tuple-element.187), channel_id=1, source_target_pairs={{0,4},{2,6},{4,0},{6,2},{8,12},{10,14},{12,8},{14,10},{16,20},{18,... | collective-permute-start | bytes 3145736 | tf_op jit(solution)/shard_map/ppermute | solution.py:326
  232.5 20.1 %collective-permute-start.31 = (bf16[512,1024]{1,0:T(8,128)(2,1)}, bf16[512,1024]{1,0:T(8,128)(2,1)S(1)}, u32[]{:S(2)}, u32[]{:S(2)}) collective-permute-start(bf16[512,1024]{1,0:T(8,128)(2,1)} %get-tuple-element.197.r0_ref), channel_id=1, source_target_pairs={{0,2},{2,0},{4,6},{6,4},{8,10},{10,8},{12,14},{14,12},{16,18},{18,... | collective-permute-start | bytes 3145736 | tf_op jit(solution)/shard_map/ppermute | solution.py:330
  232.7 26.1 %collective-permute-start.35 = (bf16[512,512]{1,0:T(8,128)(2,1)}, bf16[512,512]{1,0:T(8,128)(2,1)S(1)}, u32[]{:S(2)}, u32[]{:S(2)}) collective-permute-start(bf16[512,512]{1,0:T(8,128)(2,1)} %get-tuple-element.208), channel_id=1, source_target_pairs={{0,1},{1,0},{2,3},{3,2},{4,5},{5,4},{6,7},{7,6},{8,9},{9,8},{10,11... | collective-permute-start | bytes 1572872 | tf_op jit(solution)/shard_map/ppermute | solution.py:334
  233.0 43.0 %collective-permute-start.33 = (bf16[4,512,256]{2,1,0:T(8,128)(2,1)}, bf16[4,512,256]{2,1,0:T(8,128)(2,1)S(1)}, u32[]{:S(2)}, u32[]{:S(2)}) collective-permute-start(bf16[4,512,256]{2,1,0:T(8,128)(2,1)} %get-tuple-element.202), channel_id=1, source_target_pairs={{0,4},{2,6},{4,0},{6,2},{8,12},{10,14},{12,8},{14,10},{16,20},{18,... | collective-permute-start | bytes 3145736 | tf_op jit(solution)/shard_map/ppermute | solution.py:326
  233.3 51.5 %collective-permute-start.26 = (bf16[512,1024]{1,0:T(8,128)(2,1)S(1)}, bf16[512,1024]{1,0:T(8,128)(2,1)S(1)}, u32[]{:S(2)}, u32[]{:S(2)}) collective-permute-start(bf16[512,1024]{1,0:T(8,128)(2,1)S(1)} %copy-done.32), channel_id=1, source_target_pairs={{0,2},{2,0},{4,6},{6,4},{8,10},{10,8},{12,14},{14,12},{16,18},{18,... | collective-permute-start | bytes 3145736 | tf_op jit(solution)/shard_map/ppermute | solution.py:330
  252.2 26.3 %collective-permute-start.34 = (bf16[4,512,256]{2,1,0:T(8,128)(2,1)}, bf16[4,512,256]{2,1,0:T(8,128)(2,1)S(1)}, u32[]{:S(2)}, u32[]{:S(2)}) collective-permute-start(bf16[4,512,256]{2,1,0:T(8,128)(2,1)} %added.2), channel_id=1, source_target_pairs={{0,1},{1,0},{2,3},{3,2},{4,5},{5,4},{6,7},{7,6},{8,9},{9,8},{10,11... | collective-permute-start | bytes 3145736 | tf_op jit(solution)/shard_map/ppermute | solution.py:334
  252.5 47.8 %collective-permute-start.37 = (bf16[4,128,1024]{2,1,0:T(8,128)(2,1)}, bf16[4,128,1024]{2,1,0:T(8,128)(2,1)S(1)}, u32[]{:S(2)}, u32[]{:S(2)}) collective-permute-start(bf16[4,128,1024]{2,1,0:T(8,128)(2,1)} %get-tuple-element.194), channel_id=1, source_target_pairs={{0,4},{2,6},{4,0},{6,2},{8,12},{10,14},{12,8},{14,10},{16,20},{18,... | collective-permute-start | bytes 3145736 | tf_op jit(solution)/shard_map/ppermute | solution.py:326
  258.8 29.2 %collective-permute-start.32 = (bf16[8,64,512]{2,1,0:T(8,128)(2,1)}, bf16[8,64,512]{2,1,0:T(8,128)(2,1)S(1)}, u32[]{:S(2)}, u32[]{:S(2)}) collective-permute-start(bf16[8,64,512]{2,1,0:T(8,128)(2,1)} %get-tuple-element.200), channel_id=1, source_target_pairs={{0,1},{1,0},{2,3},{3,2},{4,5},{5,4},{6,7},{7,6},{8,9},{9,8},{10,11... | collective-permute-start | bytes 1572872 | tf_op jit(solution)/shard_map/ppermute | solution.py:334
  276.1 16.0 %collective-permute-start.38 = (bf16[1024,768]{1,0:T(8,128)(2,1)}, bf16[1024,768]{1,0:T(8,128)(2,1)S(1)}, u32[]{:S(2)}, u32[]{:S(2)}) collective-permute-start(bf16[1024,768]{1,0:T(8,128)(2,1)} %attend_back_0.1.r0_ref.d0_ref), channel_id=1, source_target_pairs={{0,2},{2,0},{4,6},{6,4},{8,10},{10,8},{12,14},{14,12},{16,18},{18,... | collective-permute-start | bytes 4718600 | tf_op jit(solution)/shard_map/ppermute | solution.py:330
  283.1 36.8 %collective-permute-start.40 = (bf16[512,256]{1,0:T(8,128)(2,1)}, bf16[512,256]{1,0:T(8,128)(2,1)S(1)}, u32[]{:S(2)}, u32[]{:S(2)}) collective-permute-start(bf16[512,256]{1,0:T(8,128)(2,1)} %get-tuple-element.213), channel_id=1, source_target_pairs={{0,8},{2,10},{4,12},{6,14},{8,16},{10,18},{12,20},{14,22},{16,24},... | collective-permute-start | bytes 786440 | tf_op jit(solution)/shard_map/ppermute | solution.py:322
  284.8 35.3 %collective-permute-start.41 = (bf16[512,256]{1,0:T(8,128)(2,1)}, bf16[512,256]{1,0:T(8,128)(2,1)S(1)}, u32[]{:S(2)}, u32[]{:S(2)}) collective-permute-start(bf16[512,256]{1,0:T(8,128)(2,1)} %get-tuple-element.214), channel_id=1, source_target_pairs={{0,16},{2,18},{4,20},{6,22},{8,24},{10,26},{12,28},{14,30},{16,0},... | collective-permute-start | bytes 786440 | tf_op jit(solution)/shard_map/ppermute | solution.py:322
  288.0 32.0 %collective-permute-start.42 = (bf16[512,256]{1,0:T(8,128)(2,1)}, bf16[512,256]{1,0:T(8,128)(2,1)S(1)}, u32[]{:S(2)}, u32[]{:S(2)}) collective-permute-start(bf16[512,256]{1,0:T(8,128)(2,1)} %get-tuple-element.215), channel_id=1, source_target_pairs={{0,24},{2,26},{4,28},{6,30},{8,0},{10,2},{12,4},{14,6},{16,8},{18,... | collective-permute-start | bytes 786440 | tf_op jit(solution)/shard_map/ppermute | solution.py:322
  292.1 32.7 %collective-permute-start.36 = (bf16[4,128,1024]{2,1,0:T(8,128)(2,1)S(1)}, bf16[4,128,1024]{2,1,0:T(8,128)(2,1)S(1)}, u32[]{:S(2)}, u32[]{:S(2)}) collective-permute-start(bf16[4,128,1024]{2,1,0:T(8,128)(2,1)S(1)} %copy-done.31), channel_id=1, source_target_pairs={{0,4},{2,6},{4,0},{6,2},{8,12},{10,14},{12,8},{14,10},{16,20},{18,... | collective-permute-start | bytes 3145736 | tf_op jit(solution)/shard_map/ppermute | solution.py:326
  304.4 23.1 %collective-permute-start.39 = (bf16[4,128,1024]{2,1,0:T(8,128)(2,1)}, bf16[4,128,1024]{2,1,0:T(8,128)(2,1)S(1)}, u32[]{:S(2)}, u32[]{:S(2)}) collective-permute-start(bf16[4,128,1024]{2,1,0:T(8,128)(2,1)} %added.3), channel_id=1, source_target_pairs={{0,1},{1,0},{2,3},{3,2},{4,5},{5,4},{6,7},{7,6},{8,9},{9,8},{10,11... | collective-permute-start | bytes 3145736 | tf_op jit(solution)/shard_map/ppermute | solution.py:334
  320.9 34.1 %collective-permute-start.43 = (bf16[4,64,1280]{2,1,0:T(8,128)(2,1)S(1)}, bf16[4,64,1280]{2,1,0:T(8,128)(2,1)S(1)}, u32[]{:S(2)}, u32[]{:S(2)}) collective-permute-start(bf16[4,64,1280]{2,1,0:T(8,128)(2,1)S(1)} %copy-done.36), channel_id=1, source_target_pairs={{0,4},{2,6},{4,0},{6,2},{8,12},{10,14},{12,8},{14,10},{16,20},{18,... | collective-permute-start | bytes 1966088 | tf_op jit(solution)/shard_map/ppermute | solution.py:326
  339.3 16.1 %collective-permute-start.45 = (bf16[4,64,768]{2,1,0:T(8,128)(2,1)}, bf16[4,64,768]{2,1,0:T(8,128)(2,1)S(1)}, u32[]{:S(2)}, u32[]{:S(2)}) collective-permute-start(bf16[4,64,768]{2,1,0:T(8,128)(2,1)} %get-tuple-element.240), channel_id=1, source_target_pairs={{0,4},{2,6},{4,0},{6,2},{8,12},{10,14},{12,8},{14,10},{16,20},{18,... | collective-permute-start | bytes 1179656 | tf_op jit(solution)/shard_map/ppermute | solution.py:326
  340.6 18.8 %collective-permute-start.46 = (bf16[128,1024]{1,0:T(8,128)(2,1)S(1)}, bf16[128,1024]{1,0:T(8,128)(2,1)S(1)}, u32[]{:S(2)}, u32[]{:S(2)}) collective-permute-start(bf16[128,1024]{1,0:T(8,128)(2,1)S(1)} %copy-done.46), channel_id=1, source_target_pairs={{0,8},{2,10},{4,12},{6,14},{8,16},{10,18},{12,20},{14,22},{16,24},... | collective-permute-start | bytes 786440 | tf_op jit(solution)/shard_map/ppermute | solution.py:322
  342.2 19.8 %collective-permute-start.47 = (bf16[128,1024]{1,0:T(8,128)(2,1)S(1)}, bf16[128,1024]{1,0:T(8,128)(2,1)S(1)}, u32[]{:S(2)}, u32[]{:S(2)}) collective-permute-start(bf16[128,1024]{1,0:T(8,128)(2,1)S(1)} %copy-done.44), channel_id=1, source_target_pairs={{0,16},{2,18},{4,20},{6,22},{8,24},{10,26},{12,28},{14,30},{16,0},... | collective-permute-start | bytes 786440 | tf_op jit(solution)/shard_map/ppermute | solution.py:322
  345.4 19.4 %collective-permute-start.48 = (bf16[128,1024]{1,0:T(8,128)(2,1)S(1)}, bf16[128,1024]{1,0:T(8,128)(2,1)S(1)}, u32[]{:S(2)}, u32[]{:S(2)}) collective-permute-start(bf16[128,1024]{1,0:T(8,128)(2,1)S(1)} %copy-done.41), channel_id=1, source_target_pairs={{0,24},{2,26},{4,28},{6,30},{8,0},{10,2},{12,4},{14,6},{16,8},{18,... | collective-permute-start | bytes 786440 | tf_op jit(solution)/shard_map/ppermute | solution.py:322
  355.0 21.9 %collective-permute-start.49 = (bf16[512,1024]{1,0:T(8,128)(2,1)}, bf16[512,1024]{1,0:T(8,128)(2,1)S(1)}, u32[]{:S(2)}, u32[]{:S(2)}) collective-permute-start(bf16[512,1024]{1,0:T(8,128)(2,1)} %get-tuple-element.253), channel_id=1, source_target_pairs={{0,1},{1,0},{2,3},{3,2},{4,5},{5,4},{6,7},{7,6},{8,9},{9,8},{10,11... | collective-permute-start | bytes 3145736 | tf_op jit(solution)/shard_map/ppermute | solution.py:334
  368.2 14.9 %collective-permute-start.50 = (f32[64,1024]{1,0:T(8,128)}, f32[64,1024]{1,0:T(8,128)S(1)}, u32[]{:S(2)}, u32[]{:S(2)}) collective-permute-start(f32[64,1024]{1,0:T(8,128)} %get-tuple-element.256), channel_id=1, source_target_pairs={{0,2},{2,0},{4,6},{6,4},{8,10},{10,8},{12,14},{14,12},{16,18},{18,... | collective-permute-start | bytes 786440 | tf_op jit(solution)/shard_map/ppermute | solution.py:330
  368.2 18.2 %collective-permute-start.51 = (bf16[64,2048]{1,0:T(8,128)(2,1)S(1)}, bf16[64,2048]{1,0:T(8,128)(2,1)S(1)}, u32[]{:S(2)}, u32[]{:S(2)}) collective-permute-start(bf16[64,2048]{1,0:T(8,128)(2,1)S(1)} %copy-done.47), channel_id=1, source_target_pairs={{0,8},{2,10},{4,12},{6,14},{8,16},{10,18},{12,20},{14,22},{16,24},... | collective-permute-start | bytes 786440 | tf_op jit(solution)/shard_map/ppermute | solution.py:322
  368.3 23.3 %collective-permute-start.52 = (bf16[64,2048]{1,0:T(8,128)(2,1)S(1)}, bf16[64,2048]{1,0:T(8,128)(2,1)S(1)}, u32[]{:S(2)}, u32[]{:S(2)}) collective-permute-start(bf16[64,2048]{1,0:T(8,128)(2,1)S(1)} %copy-done.45), channel_id=1, source_target_pairs={{0,16},{2,18},{4,20},{6,22},{8,24},{10,26},{12,28},{14,30},{16,0},... | collective-permute-start | bytes 786440 | tf_op jit(solution)/shard_map/ppermute | solution.py:322
  369.6 23.7 %collective-permute-start.53 = (bf16[64,2048]{1,0:T(8,128)(2,1)S(1)}, bf16[64,2048]{1,0:T(8,128)(2,1)S(1)}, u32[]{:S(2)}, u32[]{:S(2)}) collective-permute-start(bf16[64,2048]{1,0:T(8,128)(2,1)S(1)} %copy-done.42), channel_id=1, source_target_pairs={{0,24},{2,26},{4,28},{6,30},{8,0},{10,2},{12,4},{14,6},{16,8},{18,... | collective-permute-start | bytes 786440 | tf_op jit(solution)/shard_map/ppermute | solution.py:322
  (77 other events, 456.2 us)
Sparse Core Ops, SparseCore 0:
  10.9 70.7 all-gather.1

commit v4 on v3

--- a/solution.py
+++ b/solution.py
@@ -262,14 +262,17 @@
 NEG = -1e30
 bf16 = jnp.bfloat16
 f32 = jnp.float32
-VMEM_LIMIT = 56 * 1024 * 1024
-
-
-def params(limit=VMEM_LIMIT):
-    return pltpu.CompilerParams(vmem_limit_bytes=limit)
-
-
-PLACES = dict(up_stack=20, attend_1=20, touch=20, attend_back_0=20, mixed=20, down_sum=20, up_parts=20, up_sum=20)
+VMEM = dict(
+    down=24, up=20, normed_back=20, down_grad=20, up_grad=16, middle_back=20, project=20, input_back=18, attend_0=12, attend_1=12,
+    attend_back_0=14, attend_back_1=14, attention_out=16, qkv_grad=16, out_grad=10, input_norm=18, input_grad=14
+)
+
+
+def params(name):
+    return pltpu.CompilerParams(vmem_limit_bytes=VMEM.get(name, 10) * 1024 * 1024)
+
+
+PLACES = dict(attend_1=20, touch=20, attend_back_0=20, down_sum=20, up_parts=20, up_sum=20)
 
 
 def cost(name):
@@ -295,7 +298,7 @@
             scratch_shapes=scratch,
         ),
         out_shape=[shape for _, shape in outs],
-        compiler_params=params(),
+        compiler_params=params(name),
         cost_estimate=cost(name),
         name=name,
     )(*args)
@@ -547,7 +550,7 @@
             scratch_shapes=[pltpu.VMEM((1024, 128), f32), pltpu.VMEM((1024, 128), f32)],
         ),
         out_shape=jax.ShapeDtypeStruct((1024, 768), bf16),
-        compiler_params=params(),
+        compiler_params=params(f"attend_back_{group}"),
         cost_estimate=cost(f"attend_back_{group}"),
         name=f"attend_back_{group}",
     )(info, projected, projected, projected, bias, lse, keep, other)
@@ -1306,13 +1309,14 @@
     qkv_line_sib = swap_c(qkv_line)
     up_line = along_line(after(up_piece, qkv_line))
     beside_sib = swap_c(beside)
-    up_line = stacked(info, up_line, "up_stack")
+    heads = touch(info, after(heads, up_line))
+    up_line = stacked(info, after(up_line, heads, beside_sib, qkv_line_sib), "up_stack")
     up_x, up_y = swap_x(up_line), swap_y(up_line)
 
     qkv_pieces = (qkv_line, beside, after(qkv_line_sib, up_line), after(beside_sib, up_line))
     projected, gain_all = project(info, x_own, x_other, qkv_pieces)
     down_line = along_line(after(w_down, projected))
-    keep0, send0, lse0 = attend(info, projected, after(bias, out_all), 0)
+    keep0, send0, lse0 = attend(info, projected, bias, 0)
     got0 = swap_y(send0)
     up_x, up_y = after((up_x, up_y), keep0)
     up_far = swap_x(up_y)
@@ -1323,7 +1327,7 @@
     cot_sib = swap_c(after(cot, keep1))
     nin_t, nin_t_oth = input_norm(info, after(x_own, down_line), x_other, gain_all)
     down_y = swap_y(after(down_line, got0))
-    gain_all = touch(info, after(gain_all, nin_t, up_far, got0))
+    gain_all = touch(info, after(gain_all, nin_t, up_far, got0, out_all))
     got1 = after(got1, gain_all)
     mid, nm_own, att_t, att_t_oth = attention_out(info, x_own, (keep0, keep1), (got0, got1), out_all, gain_all)
     nm_sib = swap_c(nm_own)
@@ -1331,7 +1335,8 @@
     att_t_sib = swap_c(att_t_oth)
     up_pieces = (up_line, up_x, up_y, up_far, up_far)
     down_far = [swap_y(down_x[:2]), swap_x(down_y[2:])]
-    nm_sib = after(nm_sib, touch(info, after(gain_all, nm_own, down_x, down_y)))
+    gain_all = touch(info, after(gain_all, nm_own, down_x, down_y))
+    nm_sib = after(nm_sib, gain_all)
     act, slope = up(info, nm_own, nm_sib, up_pieces)
     down_pieces = (down_line, down_x, down_y, *down_far)
     mixed_keep, mixed_send, gp = down(info, act, slope, cot, cot_sib, mid, down_pieces)
@@ -1359,9 +1364,9 @@
     down_parts = line_parts(info, down_own, down_x, down_y, "down_parts")
     down_shift = [shift_z(down_parts[k], k) for k in range(1, LINE)]
     up_x = swap_x(up_beside)
-    mixed = added(info, mixed_keep, after(mixed_got, out_got, down_parts), "mixed")
-    dproj0_sib = after(dproj0_sib, mixed)
-    first_beside, first_own = qkv_grad(info, nin_t, after(dproj0, mixed), nin_t_sib, dproj0_sib, (out_keep, out_got))
+    gain_all = touch(info, after(gain_all, out_got, down_parts))
+    dproj0_sib = after(dproj0_sib, gain_all)
+    first_beside, first_own = qkv_grad(info, nin_t, after(dproj0, gain_all), nin_t_sib, dproj0_sib, (out_keep, out_got))
     first_x = swap_x(first_beside)
     up_across = added(info, up_across, after(up_far, first_own))
     up_y = swap_y(up_across)
@@ -1381,7 +1386,8 @@
     qkv_shift = [shift_z(heads_parts[k], k) for k in range(1, LINE)]
     up_mine, up_send = up_sum(info, (after(up_parts[0], heads_parts), *up_shift))
     up_got = swap_c(up_send)
-    grad_tokens = input_grad(info, after(x_own, up_mine), e_own, after(e_got, up_mine), gm, gain_all)
+    mixed = added(info, mixed_keep, after(mixed_got, up_mine), "mixed")
+    grad_tokens = input_grad(info, after(x_own, mixed), e_own, after(e_got, mixed), gm, gain_all)
     g_up, mid_sums = up_whole(info, up_mine, after(up_got, grad_tokens), w_up)
     keep, send, g_out = qkv_sum(info, (after(heads_parts[0], mid_sums), *after(qkv_shift, mid_sums)), heads, mid_sums)
     got = swap_y(send)

time: 422 us -> 366 us (0.87)
  Pallas kernels: 233 us -> 135 us
  waiting for transfers between devices: 75.3 us -> 128 us
  local copies, waits for them, and re-layouts: 24.9 us -> 16.8 us
    pallas_call x34 -> x37, Pallas kernels: 202 us -> 112 us  [call(): pl.pallas_call(kernel, grid_spec=pltpu.PrefetchScalarGridSpec(num_scalar_...]
    ppermute x11, waiting for transfers between devices: 17.7 us -> 54.3 us  [swap_x(): return lax.ppermute(v, 'rows', row_pairs(lambda z, x, c: (z, 1 - x, c)))]
    ppermute x13, waiting for transfers between devices: 17.2 us -> 33.3 us  [swap_y(): return lax.ppermute(v, 'pair', [(0, 1), (1, 0)])]
    unnamed x140 -> x100, local copies, waits for them, and re-layouts: 21.2 us -> 11.9 us
    pallas_call x2, Pallas kernels: 30.7 us -> 23.2 us  [attend_back(): pl.pallas_call(attend_back_kernel, grid_spec=pltpu.PrefetchScalarGridSpec...]
  transfers between devices with their start and end apart: 56 -> 56, of which waited for: 18 -> 25; matrix products, arithmetic and copies ran while one was open for 3% -> 3% of each run, Pallas kernels for 52% -> 35%
where the time goes in v4:
time: 366 us; the launch traced here: 359 us
  Pallas kernels  135 us (37%)
  waiting for transfers between devices  128 us (35%)
  starting transfers between devices  54.2 us (15%)
  between operations  17.9 us (5%)
  local copies, waits for them, and re-layouts  16.8 us (5%)
  other arithmetic  7.55 us (2%)
    pallas_call x37, Pallas kernels, call(): pl.pallas_call(kernel, grid_spec=pltpu.PrefetchScalarGridSpec(num_scalar_...  112 us
    ppermute x11, waiting for transfers between devices, swap_x(): return lax.ppermute(v, 'rows', row_pairs(lambda z, x, c: (z, 1 - x, c)))  54.3 us
    ppermute x18, waiting for transfers between devices, shift_z(): return lax.ppermute(v, 'rows', row_pairs(lambda z, x, c: (z + k, x, c)))  39.1 us
    ppermute x13, waiting for transfers between devices, swap_y(): return lax.ppermute(v, 'pair', [(0, 1), (1, 0)])  33.3 us
    ppermute x18, starting transfers between devices, shift_z(): return lax.ppermute(v, 'rows', row_pairs(lambda z, x, c: (z + k, x, c)))  28.9 us
    pallas_call x2, Pallas kernels, attend_back(): pl.pallas_call(attend_back_kernel, grid_spec=pltpu.PrefetchScalarGridSpec...  23.2 us
    ppermute x13, starting transfers between devices, swap_y(): return lax.ppermute(v, 'pair', [(0, 1), (1, 0)])  13.7 us
    unnamed x100, local copies, waits for them, and re-layouts  11.9 us
  transfers between devices with their start and end apart: 56, of which 25 were waited for; matrix products, arithmetic and copies ran while one was open for 3% of the time, Pallas kernels for 35%

profile of v4, /device:TPU:8, one launch (start us, length us, event | category | flops | bytes accessed | tf_op | source)
XLA Modules:
  0.0 359.4 jit_solution(4745899677649770336)
XLA Ops:
  16.0 3.0 collective-permute-start.2
  19.0 2.5 collective-permute-start.1
  26.6 5.1 %fusion.5 = (f32[1024,1024]{1,0:T(8,128)}, f32[1024,1024]{1,0:T(8,128)}) fusion(s32[1024]{0:T(1024)S(1)} %pad_add_fusion, pred[1024]{0:T(1024)(128)(4,1)S(1)} %get-tuple-element.299, pred[1024]{0:T(1024)(128)(4,1)S(1)} %get-tuple-element.300), kind=kLoop, calls=%fused_computation.9 | loop fusion | flops 11534336 | bytes 8394752 | tf_op jit(solution)/shard_map/jit(_where)/select_n | solution.py:1285
  32.8 3.6 collective-permute-done.1.refs_1_
  40.7 2.8 collective-permute-start.9
  44.6 16.7 %collective-permute-done.10.refs_3_ = bf16[128,1024]{1,0:T(8,128)(2,1)S(1)} collective-permute-done((bf16[128,1024]{1,0:T(8,128)(2,1)S(1)}, bf16[128,1024]{1,0:T(8,128)(2,1)S(1)}, u32[]{:S(2)}, u32[]{:S(2)}) %collective-permute-start.10) | collective-permute-done | bytes 262176 | tf_op jit(solution)/shard_map/ppermute | solution.py:325
  61.4 4.0 %collective-permute-done.8.refs_1_ = bf16[128,1024]{1,0:T(8,128)(2,1)S(1)} collective-permute-done((bf16[128,1024]{1,0:T(8,128)(2,1)S(1)}, bf16[128,1024]{1,0:T(8,128)(2,1)S(1)}, u32[]{:S(2)}, u32[]{:S(2)}) %collective-permute-start.8) | collective-permute-done | bytes 262176 | tf_op jit(solution)/shard_map/ppermute | solution.py:325
  72.3 6.0 %project.1 = (bf16[1024,1536]{1,0:T(8,128)(2,1)S(1)}, f32[2,1024]{1,0:T(2,128)S(1)}) custom-call(s32[4]{0:T(128)S(1)} %pad_add_fusion.1.info, bf16[512,1024]{1,0:T(8,128)(2,1)S(1)} %bitcast.25, bf16[512,1024]{1,0:T(8,128)(2,1)S(1)} %copy-done.26, bf16[4,64,1664]{2,1,0:T(8,128)(2,1)S(1)} %copy-done.16, bf16[4,64,1664]{2,1,0:T(8,128)(2,1)S(1)} %copy-done.19, ...), custom_call_target="tpu_custom_call" | custom-call | flops 575000000 | bytes 65536 | tf_op jit(solution)/shard_map/project/pallas_call | solution.py:291
  78.3 2.3 collective-permute-start.16
  82.5 8.5 %attend_0.1 = (bf16[512,256]{1,0:T(8,128)(2,1)S(1)}, bf16[512,256]{1,0:T(8,128)(2,1)S(1)}, f32[2,2,1024]{2,1,0:T(2,128)S(1)}) custom-call(s32[4]{0:T(128)S(1)} %pad_add_fusion.1.info, bf16[1024,1536]{1,0:T(8,128)(2,1)S(1)} %get-tuple-element.163.q_ref.k_ref.v_ref, bf16[1024,1536]{1,0:T(8,128)(2,1)S(1)} %get-tuple-element.163.q_ref.k_ref.v_ref, ...), custom_call_target="tpu_custom_call" | custom-call | flops 575000000 | bytes 65536 | tf_op jit(solution)/shard_map/attend_0/pallas_call | solution.py:291
  91.1 3.6 %collective-permute-done.18.refs_2_ = bf16[4,128,1024]{2,1,0:T(8,128)(2,1)} collective-permute-done((bf16[4,128,1024]{2,1,0:T(8,128)(2,1)S(1)}, bf16[4,128,1024]{2,1,0:T(8,128)(2,1)}, u32[]{:S(2)}, u32[]{:S(2)}) %collective-permute-start.18) | collective-permute-done | bytes 1048608 | tf_op jit(solution)/shard_map/ppermute | solution.py:337
  96.7 9.1 %attend_1.1 = (bf16[512,256]{1,0:T(8,128)(2,1)S(1)}, bf16[512,256]{1,0:T(8,128)(2,1)}, f32[2,2,1024]{2,1,0:T(2,128)S(1)}) custom-call(s32[4]{0:T(128)S(1)} %pad_add_fusion.1.info, bf16[1024,1536]{1,0:T(8,128)(2,1)S(1)} %get-tuple-element.163.q_ref.k_ref.v_ref, bf16[1024,1536]{1,0:T(8,128)(2,1)S(1)} %get-tuple-element.163.q_ref.k_ref.v_ref, ...), custom_call_target="tpu_custom_call" | custom-call | flops 23000000512 | bytes 65536 | tf_op jit(solution)/shard_map/attend_1/pallas_call | solution.py:291
  111.8 2.3 input_norm.1
  116.2 10.1 %collective-permute-done.19.refs_3_.refs_4_ = bf16[4,128,1024]{2,1,0:T(8,128)(2,1)} collective-permute-done((bf16[4,128,1024]{2,1,0:T(8,128)(2,1)}, bf16[4,128,1024]{2,1,0:T(8,128)(2,1)}, u32[]{:S(2)}, u32[]{:S(2)}) %collective-permute-start.19) | collective-permute-done | bytes 1048608 | tf_op jit(solution)/shard_map/ppermute | solution.py:329
  128.3 3.3 attention_out.1
  132.2 3.6 collective-permute-done.22.refs_2_
  138.2 10.6 %collective-permute-done.21.refs_1_ = bf16[4,256,512]{2,1,0:T(8,128)(2,1)} collective-permute-done((bf16[4,256,512]{2,1,0:T(8,128)(2,1)}, bf16[4,256,512]{2,1,0:T(8,128)(2,1)}, u32[]{:S(2)}, u32[]{:S(2)}) %collective-permute-start.21) | collective-permute-done | bytes 1048608 | tf_op jit(solution)/shard_map/ppermute | solution.py:329
  152.9 9.4 %up.1 = (bf16[1024,2048]{1,0:T(8,128)(2,1)S(1)}, bf16[1024,2048]{1,0:T(8,128)(2,1)S(1)}) custom-call(s32[4]{0:T(128)S(1)} %pad_add_fusion.1.info, bf16[512,1024]{1,0:T(8,128)(2,1)S(1)} %get-tuple-element.181.x0_ref.n0_ref, bf16[512,1024]{1,0:T(8,128)(2,1)S(1)} %collective-permute-done.20.x1_ref.n1_ref, bf16[4,128,1024]{2,1,0:T(8,128)(2,1)S(1)} %copy-done.10, ...), custom_call_target="tpu_custom_call" | custom-call | flops 575000000 | bytes 65536 | tf_op jit(solution)/shard_map/up/pallas_call | solution.py:291
  162.3 13.9 %down.1 = (f32[512,1024]{1,0:T(8,128)S(1)}, bf16[512,1024]{1,0:T(8,128)(2,1)S(1)}, bf16[1024,2048]{1,0:T(8,128)(2,1)S(1)}) custom-call(s32[4]{0:T(128)S(1)} %pad_add_fusion.1.info, bf16[1024,2048]{1,0:T(8,128)(2,1)S(1)} %get-tuple-element.198.act_ref, bf16[1024,2048]{1,0:T(8,128)(2,1)S(1)} %get-tuple-element.187.slope_ref, bf16[512,1024]{1,0:T(8,128)(2,1)S(1)} %bitcast.21, ...), custom_call_target="tpu_custom_call" | custom-call | flops 575000000 | bytes 65536 | tf_op jit(solution)/shard_map/down/pallas_call | solution.py:291
  176.2 7.1 %normed_back.1 = (f32[512,1024]{1,0:T(8,128)S(1)}, bf16[512,1024]{1,0:T(8,128)(2,1)S(1)}) custom-call(s32[4]{0:T(128)S(1)} %pad_add_fusion.1.info, bf16[1024,2048]{1,0:T(8,128)(2,1)S(1)} %get-tuple-element.204.gp_ref, bf16[4,128,1024]{2,1,0:T(8,128)(2,1)S(1)} %copy-done.10, bf16[4,128,1024]{2,1,0:T(8,128)(2,1)S(1)} %copy-done.12, ...), custom_call_target="tpu_custom_call" | custom-call | flops 575000000 | bytes 65536 | tf_op jit(solution)/shard_map/normed_back/pallas_call | solution.py:291
  183.4 7.7 %down_grad.1 = (bf16[4,512,256]{2,1,0:T(8,128)(2,1)S(1)}, bf16[4,512,256]{2,1,0:T(8,128)(2,1)S(1)}, bf16[4,512,256]{2,1,0:T(8,128)(2,1)S(1)}, bf16[4,512,256]{2,1,0:T(8,128)(2,1)S(1)}) custom-call(s32[4]{0:T(128)S(1)} %pad_add_fusion.1.info, bf16[512,1024]{1,0:T(8,128)(2,1)S(1)} %bitcast.22, bf16[512,1024]{1,0:T(8,128)(2,1)S(1)} %collective-permute-done.23.c1_ref, ...), custom_call_target="tpu_custom_call" | custom-call | flops 575000000 | bytes 65536 | tf_op jit(solution)/shard_map/down_grad/pallas_call | solution.py:291
  191.7 3.0 middle_back.1
  197.6 7.5 %up_grad.1 = (bf16[4,128,1024]{2,1,0:T(8,128)(2,1)S(1)}, bf16[4,128,1024]{2,1,0:T(8,128)(2,1)S(1)}, bf16[4,128,1024]{2,1,0:T(8,128)(2,1)S(1)}, bf16[4,128,1024]{2,1,0:T(8,128)(2,1)S(1)}) custom-call(s32[4]{0:T(128)S(1)} %pad_add_fusion.1.info, bf16[512,1024]{1,0:T(8,128)(2,1)S(1)} %get-tuple-element.181.x0_ref.n0_ref, bf16[512,1024]{1,0:T(8,128)(2,1)S(1)} %copy-done.14, ...), custom_call_target="tpu_custom_call" | custom-call | flops 575000000 | bytes 65536 | tf_op jit(solution)/shard_map/up_grad/pallas_call | solution.py:291
  205.1 12.1 %collective-permute-done.32.b_ref = bf16[4,512,256]{2,1,0:T(8,128)(2,1)S(1)} collective-permute-done((bf16[4,512,256]{2,1,0:T(8,128)(2,1)S(1)}, bf16[4,512,256]{2,1,0:T(8,128)(2,1)S(1)}, u32[]{:S(2)}, u32[]{:S(2)}) %collective-permute-start.32) | collective-permute-done | bytes 1048608 | tf_op jit(solution)/shard_map/ppermute | solution.py:329
  219.6 1.8 out_grad.1
  222.5 11.7 %attend_back_0.1.r0_ref.d0_ref = bf16[1024,768]{1,0:T(8,128)(2,1)S(1)} custom-call(s32[4]{0:T(128)S(1)} %pad_add_fusion.1.info, bf16[1024,1536]{1,0:T(8,128)(2,1)S(1)} %get-tuple-element.163.q_ref.k_ref.v_ref, bf16[1024,1536]{1,0:T(8,128)(2,1)S(1)} %get-tuple-element.163.q_ref.k_ref.v_ref, bf16[1024,1536]{1,0:T(8,128)(2,1)S(1)} %get-tuple-element.163.q_ref.k_ref.v_ref, ...), custom_call_target="tpu_custom_call" | custom-call | flops 23000000512 | bytes 65536 | tf_op jit(solution)/shard_map/attend_back_0/pallas_call | solution.py:537
  234.3 5.4 %collective-permute-done.36.b_ref = bf16[4,512,256]{2,1,0:T(8,128)(2,1)S(1)} collective-permute-done((bf16[4,512,256]{2,1,0:T(8,128)(2,1)S(1)}, bf16[4,512,256]{2,1,0:T(8,128)(2,1)S(1)}, u32[]{:S(2)}, u32[]{:S(2)}) %collective-permute-start.36) | collective-permute-done | bytes 1048608 | tf_op jit(solution)/shard_map/ppermute | solution.py:329
  239.6 4.5 %collective-permute-done.37.c_ref = bf16[4,512,256]{2,1,0:T(8,128)(2,1)S(1)} collective-permute-done((bf16[4,512,256]{2,1,0:T(8,128)(2,1)S(1)}, bf16[4,512,256]{2,1,0:T(8,128)(2,1)S(1)}, u32[]{:S(2)}, u32[]{:S(2)}) %collective-permute-start.37) | collective-permute-done | bytes 1048608 | tf_op jit(solution)/shard_map/ppermute | solution.py:337
  245.1 2.5 collective-permute-start.40
  249.2 4.5 %collective-permute-done.35.refs_1_ = bf16[8,64,512]{2,1,0:T(8,128)(2,1)S(1)} collective-permute-done((bf16[8,64,512]{2,1,0:T(8,128)(2,1)S(1)}, bf16[8,64,512]{2,1,0:T(8,128)(2,1)S(1)}, u32[]{:S(2)}, u32[]{:S(2)}) %collective-permute-start.35) | collective-permute-done | bytes 524320 | tf_op jit(solution)/shard_map/ppermute | solution.py:337
  256.6 2.5 qkv_grad.2
  259.2 2.9 collective-permute-done.31.b_ref
  264.3 11.5 %attend_back_1.1.r0_ref.d1_ref = bf16[1024,768]{1,0:T(8,128)(2,1)S(1)} custom-call(s32[4]{0:T(128)S(1)} %pad_add_fusion.1.info, bf16[1024,1536]{1,0:T(8,128)(2,1)S(1)} %get-tuple-element.163.q_ref.k_ref.v_ref, bf16[1024,1536]{1,0:T(8,128)(2,1)S(1)} %get-tuple-element.163.q_ref.k_ref.v_ref, bf16[1024,1536]{1,0:T(8,128)(2,1)S(1)} %get-tuple-element.163.q_ref.k_ref.v_ref, ...), custom_call_target="tpu_custom_call" | custom-call | flops 575000000 | bytes 65536 | tf_op jit(solution)/shard_map/attend_back_1/pallas_call | solution.py:537
  278.0 6.6 %collective-permute-done.30.b_ref = bf16[4,128,1024]{2,1,0:T(8,128)(2,1)S(1)} collective-permute-done((bf16[4,128,1024]{2,1,0:T(8,128)(2,1)S(1)}, bf16[4,128,1024]{2,1,0:T(8,128)(2,1)S(1)}, u32[]{:S(2)}, u32[]{:S(2)}) %collective-permute-start.30) | collective-permute-done | bytes 1048608 | tf_op jit(solution)/shard_map/ppermute | solution.py:329
  284.6 3.1 collective-permute-done.39.c_ref
  288.6 2.3 qkv_grad.3
  291.5 2.5 collective-permute-start.46
  295.6 4.8 %input_back.1 = (f32[512,1024]{1,0:T(8,128)S(1)}, bf16[512,1024]{1,0:T(8,128)(2,1)S(1)}) custom-call(s32[4]{0:T(128)S(1)} %pad_add_fusion.1.info, bf16[1024,768]{1,0:T(8,128)(2,1)S(1)} %attend_back_0.1.r0_ref.d0_ref, bf16[1024,768]{1,0:T(8,128)(2,1)S(1)} %attend_back_1.1.r0_ref.d1_ref, bf16[4,64,1664]{2,1,0:T(8,128)(2,1)S(1)} %copy-done.17, ...), custom_call_target="tpu_custom_call" | custom-call | flops 575000000 | bytes 65536 | tf_op jit(solution)/shard_map/input_back/pallas_call | solution.py:291
  300.5 6.1 %collective-permute-done.45.bx_ref = bf16[4,64,768]{2,1,0:T(8,128)(2,1)S(1)} collective-permute-done((bf16[4,64,768]{2,1,0:T(8,128)(2,1)S(1)}, bf16[4,64,768]{2,1,0:T(8,128)(2,1)S(1)}, u32[]{:S(2)}, u32[]{:S(2)}) %collective-permute-start.45) | collective-permute-done | bytes 393248 | tf_op jit(solution)/shard_map/ppermute | solution.py:329
  308.5 3.0 collective-permute-done.46.refs_1_
  311.4 3.3 collective-permute-done.47.refs_2_
  316.8 2.2 collective-permute-start.52
  319.0 1.9 collective-permute-start.53
  322.6 8.9 %collective-permute-done.49.e1_ref = bf16[512,1024]{1,0:T(8,128)(2,1)S(1)} collective-permute-done((bf16[512,1024]{1,0:T(8,128)(2,1)S(1)}, bf16[512,1024]{1,0:T(8,128)(2,1)S(1)}, u32[]{:S(2)}, u32[]{:S(2)}) %collective-permute-start.49) | collective-permute-done | bytes 1048608 | tf_op jit(solution)/shard_map/ppermute | solution.py:337
  331.4 3.1 input_grad.1
  336.0 4.1 %collective-permute-done.52.refs_2_ = bf16[64,2048]{1,0:T(8,128)(2,1)S(1)} collective-permute-done((bf16[64,2048]{1,0:T(8,128)(2,1)S(1)}, bf16[64,2048]{1,0:T(8,128)(2,1)S(1)}, u32[]{:S(2)}, u32[]{:S(2)}) %collective-permute-start.52) | collective-permute-done | bytes 262176 | tf_op jit(solution)/shard_map/ppermute | solution.py:325
  340.1 2.7 collective-permute-done.53.refs_3_
  345.1 5.1 %collective-permute-done.54.got_ref = f32[64,640]{1,0:T(8,128)S(1)} collective-permute-done((f32[64,640]{1,0:T(8,128)S(1)}, f32[64,640]{1,0:T(8,128)S(1)}, u32[]{:S(2)}, u32[]{:S(2)}) %collective-permute-start.54) | collective-permute-done | bytes 163872 | tf_op jit(solution)/shard_map/ppermute | solution.py:337
  (221 shorter events, 76.8 us)
Async XLA Ops:
  7.2 109.0 %all-gather.2.cloned.1.call-start = ((), (), s32[]{:S(2)}) async-start(), calls=%async_computation | async-start | bytes 2162688 | tf_op jit(solution)/shard_map/all_gather | solution.py:1297
  10.4 25.9 %collective-permute-start.4 = (bf16[512,1024]{1,0:T(8,128)(2,1)}, bf16[512,1024]{1,0:T(8,128)(2,1)S(1)}, u32[]{:S(2)}, u32[]{:S(2)}) collective-permute-start(bf16[512,1024]{1,0:T(8,128)(2,1)} %bitcast.24), channel_id=1, source_target_pairs={{0,1},{1,0},{2,3},{3,2},{4,5},{5,4},{6,7},{7,6},{8,9},{9,8},{10,11... | collective-permute-start | bytes 3145736 | tf_op jit(solution)/shard_map/ppermute | solution.py:337
  15.9 16.9 %collective-permute-start.3 = (bf16[64,1664]{1,0:T(8,128)(2,1)S(1)}, bf16[64,1664]{1,0:T(8,128)(2,1)S(1)}, u32[]{:S(2)}, u32[]{:S(2)}) collective-permute-start(bf16[64,1664]{1,0:T(8,128)(2,1)S(1)} %heads.1.refs_0_.a_ref), channel_id=1, source_target_pairs={{0,24},{2,26},{4,28},{6,30},{8,0},{10,2},{12,4},{14,6},{16,8},{18,... | collective-permute-start | bytes 638984 | tf_op jit(solution)/shard_map/ppermute | solution.py:325
  16.0 16.8 %collective-permute-start.2 = (bf16[64,1664]{1,0:T(8,128)(2,1)S(1)}, bf16[64,1664]{1,0:T(8,128)(2,1)S(1)}, u32[]{:S(2)}, u32[]{:S(2)}) collective-permute-start(bf16[64,1664]{1,0:T(8,128)(2,1)S(1)} %heads.1.refs_0_.a_ref), channel_id=1, source_target_pairs={{0,16},{2,18},{4,20},{6,22},{8,24},{10,26},{12,28},{14,30},{16,0},... | collective-permute-start | bytes 638984 | tf_op jit(solution)/shard_map/ppermute | solution.py:325
  19.0 17.4 %collective-permute-start.1 = (bf16[64,1664]{1,0:T(8,128)(2,1)S(1)}, bf16[64,1664]{1,0:T(8,128)(2,1)S(1)}, u32[]{:S(2)}, u32[]{:S(2)}) collective-permute-start(bf16[64,1664]{1,0:T(8,128)(2,1)S(1)} %heads.1.refs_0_.a_ref), channel_id=1, source_target_pairs={{0,8},{2,10},{4,12},{6,14},{8,16},{10,18},{12,20},{14,22},{16,24},... | collective-permute-start | bytes 638984 | tf_op jit(solution)/shard_map/ppermute | solution.py:325
  38.0 27.4 %collective-permute-start.6 = (bf16[4,64,1664]{2,1,0:T(8,128)(2,1)S(1)}, bf16[4,64,1664]{2,1,0:T(8,128)(2,1)S(1)}, u32[]{:S(2)}, u32[]{:S(2)}) collective-permute-start(bf16[4,64,1664]{2,1,0:T(8,128)(2,1)S(1)} %qkv_stack.1.refs_0_), channel_id=1, source_target_pairs={{0,4},{2,6},{4,0},{6,2},{8,12},{10,14},{12,8},{14,10},{16,20},{18,... | collective-permute-start | bytes 2555912 | tf_op jit(solution)/shard_map/ppermute | solution.py:329
  39.5 21.8 %collective-permute-start.10 = (bf16[128,1024]{1,0:T(8,128)(2,1)S(1)}, bf16[128,1024]{1,0:T(8,128)(2,1)S(1)}, u32[]{:S(2)}, u32[]{:S(2)}) collective-permute-start(bf16[128,1024]{1,0:T(8,128)(2,1)S(1)} %both_rows.1.refs_0_), channel_id=1, source_target_pairs={{0,24},{2,26},{4,28},{6,30},{8,0},{10,2},{12,4},{14,6},{16,8},{18,... | collective-permute-start | bytes 786440 | tf_op jit(solution)/shard_map/ppermute | solution.py:325
  40.7 20.7 %collective-permute-start.9 = (bf16[128,1024]{1,0:T(8,128)(2,1)S(1)}, bf16[128,1024]{1,0:T(8,128)(2,1)S(1)}, u32[]{:S(2)}, u32[]{:S(2)}) collective-permute-start(bf16[128,1024]{1,0:T(8,128)(2,1)S(1)} %both_rows.1.refs_0_), channel_id=1, source_target_pairs={{0,16},{2,18},{4,20},{6,22},{8,24},{10,26},{12,28},{14,30},{16,0},... | collective-permute-start | bytes 786440 | tf_op jit(solution)/shard_map/ppermute | solution.py:325
  43.5 21.9 %collective-permute-start.8 = (bf16[128,1024]{1,0:T(8,128)(2,1)S(1)}, bf16[128,1024]{1,0:T(8,128)(2,1)S(1)}, u32[]{:S(2)}, u32[]{:S(2)}) collective-permute-start(bf16[128,1024]{1,0:T(8,128)(2,1)S(1)} %both_rows.1.refs_0_), channel_id=1, source_target_pairs={{0,8},{2,10},{4,12},{6,14},{8,16},{10,18},{12,20},{14,22},{16,24},... | collective-permute-start | bytes 786440 | tf_op jit(solution)/shard_map/ppermute | solution.py:325
  44.5 21.7 %collective-permute-start.7 = (bf16[4,64,1664]{2,1,0:T(8,128)(2,1)S(1)}, bf16[4,64,1664]{2,1,0:T(8,128)(2,1)S(1)}, u32[]{:S(2)}, u32[]{:S(2)}) collective-permute-start(bf16[4,64,1664]{2,1,0:T(8,128)(2,1)S(1)} %qkv_stack.1.refs_0_), channel_id=1, source_target_pairs={{0,2},{2,0},{4,6},{6,4},{8,10},{10,8},{12,14},{14,12},{16,18},{18,... | collective-permute-start | bytes 2555912 | tf_op jit(solution)/shard_map/ppermute | solution.py:333
  68.4 26.3 %collective-permute-start.18 = (bf16[4,128,1024]{2,1,0:T(8,128)(2,1)S(1)}, bf16[4,128,1024]{2,1,0:T(8,128)(2,1)}, u32[]{:S(2)}, u32[]{:S(2)}) collective-permute-start(bf16[4,128,1024]{2,1,0:T(8,128)(2,1)S(1)} %up_stack.1.refs_0_), channel_id=1, source_target_pairs={{0,1},{1,0},{2,3},{3,2},{4,5},{5,4},{6,7},{7,6},{8,9},{9,8},{10,11... | collective-permute-start | bytes 3145736 | tf_op jit(solution)/shard_map/ppermute | solution.py:337
  69.4 26.8 %collective-permute-start.17 = (bf16[4,128,1024]{2,1,0:T(8,128)(2,1)S(1)}, bf16[4,128,1024]{2,1,0:T(8,128)(2,1)S(1)}, u32[]{:S(2)}, u32[]{:S(2)}) collective-permute-start(bf16[4,128,1024]{2,1,0:T(8,128)(2,1)S(1)} %up_stack.1.refs_0_), channel_id=1, source_target_pairs={{0,4},{2,6},{4,0},{6,2},{8,12},{10,14},{12,8},{14,10},{16,20},{18,... | collective-permute-start | bytes 3145736 | tf_op jit(solution)/shard_map/ppermute | solution.py:329
  78.3 27.5 %collective-permute-start.16 = (bf16[256,512]{1,0:T(8,128)(2,1)S(1)}, bf16[256,512]{1,0:T(8,128)(2,1)S(1)}, u32[]{:S(2)}, u32[]{:S(2)}) collective-permute-start(bf16[256,512]{1,0:T(8,128)(2,1)S(1)} %copy-done.42), channel_id=1, source_target_pairs={{0,24},{2,26},{4,28},{6,30},{8,0},{10,2},{12,4},{14,6},{16,8},{18,... | collective-permute-start | bytes 786440 | tf_op jit(solution)/shard_map/ppermute | solution.py:325
  80.6 26.3 %collective-permute-start.15 = (bf16[256,512]{1,0:T(8,128)(2,1)S(1)}, bf16[256,512]{1,0:T(8,128)(2,1)S(1)}, u32[]{:S(2)}, u32[]{:S(2)}) collective-permute-start(bf16[256,512]{1,0:T(8,128)(2,1)S(1)} %copy-done.42), channel_id=1, source_target_pairs={{0,16},{2,18},{4,20},{6,22},{8,24},{10,26},{12,28},{14,30},{16,0},... | collective-permute-start | bytes 786440 | tf_op jit(solution)/shard_map/ppermute | solution.py:325
  82.3 24.6 %collective-permute-start.14 = (bf16[256,512]{1,0:T(8,128)(2,1)S(1)}, bf16[256,512]{1,0:T(8,128)(2,1)S(1)}, u32[]{:S(2)}, u32[]{:S(2)}) collective-permute-start(bf16[256,512]{1,0:T(8,128)(2,1)S(1)} %copy-done.42), channel_id=1, source_target_pairs={{0,8},{2,10},{4,12},{6,14},{8,16},{10,18},{12,20},{14,22},{16,24},... | collective-permute-start | bytes 786440 | tf_op jit(solution)/shard_map/ppermute | solution.py:325
  96.2 30.1 %collective-permute-start.19 = (bf16[4,128,1024]{2,1,0:T(8,128)(2,1)}, bf16[4,128,1024]{2,1,0:T(8,128)(2,1)}, u32[]{:S(2)}, u32[]{:S(2)}) collective-permute-start(bf16[4,128,1024]{2,1,0:T(8,128)(2,1)} %collective-permute-done.18.refs_2_), channel_id=1, source_target_pairs={{0,4},{2,6},{4,0},{6,2},{8,12},{10,14},{12,8},{14,10},{16,20},{18,... | collective-permute-start | bytes 3145736 | tf_op jit(solution)/shard_map/ppermute | solution.py:329
  105.8 21.1 %collective-permute-start.13 = (bf16[512,256]{1,0:T(8,128)(2,1)}, bf16[512,256]{1,0:T(8,128)(2,1)}, u32[]{:S(2)}, u32[]{:S(2)}) collective-permute-start(bf16[512,256]{1,0:T(8,128)(2,1)} %get-tuple-element.169), channel_id=1, source_target_pairs={{0,1},{1,0},{2,3},{3,2},{4,5},{5,4},{6,7},{7,6},{8,9},{9,8},{10,11... | collective-permute-start | bytes 786440 | tf_op jit(solution)/shard_map/ppermute | solution.py:337
  108.6 40.2 %collective-permute-start.21 = (bf16[4,256,512]{2,1,0:T(8,128)(2,1)}, bf16[4,256,512]{2,1,0:T(8,128)(2,1)}, u32[]{:S(2)}, u32[]{:S(2)}) collective-permute-start(bf16[4,256,512]{2,1,0:T(8,128)(2,1)} %down_stack.1.refs_0_), channel_id=1, source_target_pairs={{0,4},{2,6},{4,0},{6,2},{8,12},{10,14},{12,8},{14,10},{16,20},{18,... | collective-permute-start | bytes 3145736 | tf_op jit(solution)/shard_map/ppermute | solution.py:329
  110.8 24.9 %collective-permute-start.22 = (bf16[4,256,512]{2,1,0:T(8,128)(2,1)}, bf16[4,256,512]{2,1,0:T(8,128)(2,1)}, u32[]{:S(2)}, u32[]{:S(2)}) collective-permute-start(bf16[4,256,512]{2,1,0:T(8,128)(2,1)} %down_stack.1.refs_0_), channel_id=1, source_target_pairs={{0,1},{1,0},{2,3},{3,2},{4,5},{5,4},{6,7},{7,6},{8,9},{9,8},{10,11... | collective-permute-start | bytes 3145736 | tf_op jit(solution)/shard_map/ppermute | solution.py:337
  131.6 19.3 %collective-permute-start.20 = (bf16[512,1024]{1,0:T(8,128)(2,1)S(1)}, bf16[512,1024]{1,0:T(8,128)(2,1)S(1)}, u32[]{:S(2)}, u32[]{:S(2)}) collective-permute-start(bf16[512,1024]{1,0:T(8,128)(2,1)S(1)} %get-tuple-element.181.x0_ref.n0_ref), channel_id=1, source_target_pairs={{0,2},{2,0},{4,6},{6,4},{8,10},{10,8},{12,14},{14,12},{16,18},{18,... | collective-permute-start | bytes 3145736 | tf_op jit(solution)/shard_map/ppermute | solution.py:333
  131.7 30.6 %collective-permute-start.23 = (bf16[512,1024]{1,0:T(8,128)(2,1)S(1)}, bf16[512,1024]{1,0:T(8,128)(2,1)S(1)}, u32[]{:S(2)}, u32[]{:S(2)}) collective-permute-start(bf16[512,1024]{1,0:T(8,128)(2,1)S(1)} %bitcast.20), channel_id=1, source_target_pairs={{0,2},{2,0},{4,6},{6,4},{8,10},{10,8},{12,14},{14,12},{16,18},{18,... | collective-permute-start | bytes 3145736 | tf_op jit(solution)/shard_map/ppermute | solution.py:333
  136.8 25.4 %collective-permute-start.25 = (bf16[2,256,512]{2,1,0:T(8,128)(2,1)S(1)}, bf16[2,256,512]{2,1,0:T(8,128)(2,1)S(1)}, u32[]{:S(2)}, u32[]{:S(2)}) collective-permute-start(bf16[2,256,512]{2,1,0:T(8,128)(2,1)S(1)} %slice.44), channel_id=1, source_target_pairs={{0,4},{2,6},{4,0},{6,2},{8,12},{10,14},{12,8},{14,10},{16,20},{18,... | collective-permute-start | bytes 1572872 | tf_op jit(solution)/shard_map/ppermute | solution.py:329
  150.9 25.3 %collective-permute-start.28 = (bf16[8,64,512]{2,1,0:T(8,128)(2,1)S(1)}, bf16[8,64,512]{2,1,0:T(8,128)(2,1)S(1)}, u32[]{:S(2)}, u32[]{:S(2)}) collective-permute-start(bf16[8,64,512]{2,1,0:T(8,128)(2,1)S(1)} %get-tuple-element.195), channel_id=1, source_target_pairs={{0,2},{2,0},{4,6},{6,4},{8,10},{10,8},{12,14},{14,12},{16,18},{18,... | collective-permute-start | bytes 1572872 | tf_op jit(solution)/shard_map/ppermute | solution.py:333
  151.0 25.3 %collective-permute-start.27 = (bf16[8,64,1024]{2,1,0:T(8,128)(2,1)S(1)}, bf16[8,64,1024]{2,1,0:T(8,128)(2,1)S(1)}, u32[]{:S(2)}, u32[]{:S(2)}) collective-permute-start(bf16[8,64,1024]{2,1,0:T(8,128)(2,1)S(1)} %copy-done.41), channel_id=1, source_target_pairs={{0,2},{2,0},{4,6},{6,4},{8,10},{10,8},{12,14},{14,12},{16,18},{18,... | collective-permute-start | bytes 3145736 | tf_op jit(solution)/shard_map/ppermute | solution.py:333
  191.2 26.0 %collective-permute-start.32 = (bf16[4,512,256]{2,1,0:T(8,128)(2,1)S(1)}, bf16[4,512,256]{2,1,0:T(8,128)(2,1)S(1)}, u32[]{:S(2)}, u32[]{:S(2)}) collective-permute-start(bf16[4,512,256]{2,1,0:T(8,128)(2,1)S(1)} %get-tuple-element.199), channel_id=1, source_target_pairs={{0,4},{2,6},{4,0},{6,2},{8,12},{10,14},{12,8},{14,10},{16,20},{18,... | collective-permute-start | bytes 3145736 | tf_op jit(solution)/shard_map/ppermute | solution.py:329
  194.7 24.8 %collective-permute-start.33 = (bf16[512,1024]{1,0:T(8,128)(2,1)S(1)}, bf16[512,1024]{1,0:T(8,128)(2,1)S(1)}, u32[]{:S(2)}, u32[]{:S(2)}) collective-permute-start(bf16[512,1024]{1,0:T(8,128)(2,1)S(1)} %get-tuple-element.214.r0_ref), channel_id=1, source_target_pairs={{0,2},{2,0},{4,6},{6,4},{8,10},{10,8},{12,14},{14,12},{16,18},{18,... | collective-permute-start | bytes 3145736 | tf_op jit(solution)/shard_map/ppermute | solution.py:333
  195.0 26.4 %collective-permute-start.34 = (bf16[512,512]{1,0:T(8,128)(2,1)S(1)}, bf16[512,512]{1,0:T(8,128)(2,1)S(1)}, u32[]{:S(2)}, u32[]{:S(2)}) collective-permute-start(bf16[512,512]{1,0:T(8,128)(2,1)S(1)} %get-tuple-element.221), channel_id=1, source_target_pairs={{0,1},{1,0},{2,3},{3,2},{4,5},{5,4},{6,7},{7,6},{8,9},{9,8},{10,11... | collective-permute-start | bytes 1572872 | tf_op jit(solution)/shard_map/ppermute | solution.py:337
  196.0 43.6 %collective-permute-start.36 = (bf16[4,512,256]{2,1,0:T(8,128)(2,1)S(1)}, bf16[4,512,256]{2,1,0:T(8,128)(2,1)S(1)}, u32[]{:S(2)}, u32[]{:S(2)}) collective-permute-start(bf16[4,512,256]{2,1,0:T(8,128)(2,1)S(1)} %get-tuple-element.225), channel_id=1, source_target_pairs={{0,4},{2,6},{4,0},{6,2},{8,12},{10,14},{12,8},{14,10},{16,20},{18,... | collective-permute-start | bytes 3145736 | tf_op jit(solution)/shard_map/ppermute | solution.py:329
  218.0 26.2 %collective-permute-start.37 = (bf16[4,512,256]{2,1,0:T(8,128)(2,1)S(1)}, bf16[4,512,256]{2,1,0:T(8,128)(2,1)S(1)}, u32[]{:S(2)}, u32[]{:S(2)}) collective-permute-start(bf16[4,512,256]{2,1,0:T(8,128)(2,1)S(1)} %added.2), channel_id=1, source_target_pairs={{0,1},{1,0},{2,3},{3,2},{4,5},{5,4},{6,7},{7,6},{8,9},{9,8},{10,11... | collective-permute-start | bytes 3145736 | tf_op jit(solution)/shard_map/ppermute | solution.py:337
  219.1 43.0 %collective-permute-start.31 = (bf16[4,128,1024]{2,1,0:T(8,128)(2,1)S(1)}, bf16[4,128,1024]{2,1,0:T(8,128)(2,1)S(1)}, u32[]{:S(2)}, u32[]{:S(2)}) collective-permute-start(bf16[4,128,1024]{2,1,0:T(8,128)(2,1)S(1)} %get-tuple-element.208), channel_id=1, source_target_pairs={{0,4},{2,6},{4,0},{6,2},{8,12},{10,14},{12,8},{14,10},{16,20},{18,... | collective-permute-start | bytes 3145736 | tf_op jit(solution)/shard_map/ppermute | solution.py:329
  221.4 32.3 %collective-permute-start.35 = (bf16[8,64,512]{2,1,0:T(8,128)(2,1)S(1)}, bf16[8,64,512]{2,1,0:T(8,128)(2,1)S(1)}, u32[]{:S(2)}, u32[]{:S(2)}) collective-permute-start(bf16[8,64,512]{2,1,0:T(8,128)(2,1)S(1)} %get-tuple-element.223), channel_id=1, source_target_pairs={{0,1},{1,0},{2,3},{3,2},{4,5},{5,4},{6,7},{7,6},{8,9},{9,8},{10,11... | collective-permute-start | bytes 1572872 | tf_op jit(solution)/shard_map/ppermute | solution.py:337
  234.2 21.8 %collective-permute-start.38 = (bf16[1024,768]{1,0:T(8,128)(2,1)S(1)}, bf16[1024,768]{1,0:T(8,128)(2,1)S(1)}, u32[]{:S(2)}, u32[]{:S(2)}) collective-permute-start(bf16[1024,768]{1,0:T(8,128)(2,1)S(1)} %attend_back_0.1.r0_ref.d0_ref), channel_id=1, source_target_pairs={{0,2},{2,0},{4,6},{6,4},{8,10},{10,8},{12,14},{14,12},{16,18},{18,... | collective-permute-start | bytes 4718600 | tf_op jit(solution)/shard_map/ppermute | solution.py:333
  245.1 30.7 %collective-permute-start.40 = (bf16[512,256]{1,0:T(8,128)(2,1)S(1)}, bf16[512,256]{1,0:T(8,128)(2,1)S(1)}, u32[]{:S(2)}, u32[]{:S(2)}) collective-permute-start(bf16[512,256]{1,0:T(8,128)(2,1)S(1)} %get-tuple-element.229), channel_id=1, source_target_pairs={{0,8},{2,10},{4,12},{6,14},{8,16},{10,18},{12,20},{14,22},{16,24},... | collective-permute-start | bytes 786440 | tf_op jit(solution)/shard_map/ppermute | solution.py:325
  247.6 28.3 %collective-permute-start.41 = (bf16[512,256]{1,0:T(8,128)(2,1)S(1)}, bf16[512,256]{1,0:T(8,128)(2,1)S(1)}, u32[]{:S(2)}, u32[]{:S(2)}) collective-permute-start(bf16[512,256]{1,0:T(8,128)(2,1)S(1)} %get-tuple-element.230), channel_id=1, source_target_pairs={{0,16},{2,18},{4,20},{6,22},{8,24},{10,26},{12,28},{14,30},{16,0},... | collective-permute-start | bytes 786440 | tf_op jit(solution)/shard_map/ppermute | solution.py:325
  253.7 22.2 %collective-permute-start.42 = (bf16[512,256]{1,0:T(8,128)(2,1)S(1)}, bf16[512,256]{1,0:T(8,128)(2,1)S(1)}, u32[]{:S(2)}, u32[]{:S(2)}) collective-permute-start(bf16[512,256]{1,0:T(8,128)(2,1)S(1)} %get-tuple-element.231), channel_id=1, source_target_pairs={{0,24},{2,26},{4,28},{6,30},{8,0},{10,2},{12,4},{14,6},{16,8},{18,... | collective-permute-start | bytes 786440 | tf_op jit(solution)/shard_map/ppermute | solution.py:325
  256.0 28.6 %collective-permute-start.30 = (bf16[4,128,1024]{2,1,0:T(8,128)(2,1)S(1)}, bf16[4,128,1024]{2,1,0:T(8,128)(2,1)S(1)}, u32[]{:S(2)}, u32[]{:S(2)}) collective-permute-start(bf16[4,128,1024]{2,1,0:T(8,128)(2,1)S(1)} %get-tuple-element.206), channel_id=1, source_target_pairs={{0,4},{2,6},{4,0},{6,2},{8,12},{10,14},{12,8},{14,10},{16,20},{18,... | collective-permute-start | bytes 3145736 | tf_op jit(solution)/shard_map/ppermute | solution.py:329
  263.2 24.4 %collective-permute-start.39 = (bf16[4,128,1024]{2,1,0:T(8,128)(2,1)S(1)}, bf16[4,128,1024]{2,1,0:T(8,128)(2,1)S(1)}, u32[]{:S(2)}, u32[]{:S(2)}) collective-permute-start(bf16[4,128,1024]{2,1,0:T(8,128)(2,1)S(1)} %added.3), channel_id=1, source_target_pairs={{0,1},{1,0},{2,3},{3,2},{4,5},{5,4},{6,7},{7,6},{8,9},{9,8},{10,11... | collective-permute-start | bytes 3145736 | tf_op jit(solution)/shard_map/ppermute | solution.py:337
  275.9 24.5 %collective-permute-start.43 = (bf16[4,64,1280]{2,1,0:T(8,128)(2,1)S(1)}, bf16[4,64,1280]{2,1,0:T(8,128)(2,1)S(1)}, u32[]{:S(2)}, u32[]{:S(2)}) collective-permute-start(bf16[4,64,1280]{2,1,0:T(8,128)(2,1)S(1)} %get-tuple-element.247), channel_id=1, source_target_pairs={{0,4},{2,6},{4,0},{6,2},{8,12},{10,14},{12,8},{14,10},{16,20},{18,... | collective-permute-start | bytes 1966088 | tf_op jit(solution)/shard_map/ppermute | solution.py:329
  291.0 15.7 %collective-permute-start.45 = (bf16[4,64,768]{2,1,0:T(8,128)(2,1)S(1)}, bf16[4,64,768]{2,1,0:T(8,128)(2,1)S(1)}, u32[]{:S(2)}, u32[]{:S(2)}) collective-permute-start(bf16[4,64,768]{2,1,0:T(8,128)(2,1)S(1)} %get-tuple-element.253), channel_id=1, source_target_pairs={{0,4},{2,6},{4,0},{6,2},{8,12},{10,14},{12,8},{14,10},{16,20},{18,... | collective-permute-start | bytes 1179656 | tf_op jit(solution)/shard_map/ppermute | solution.py:329
  291.5 19.9 %collective-permute-start.46 = (bf16[128,1024]{1,0:T(8,128)(2,1)S(1)}, bf16[128,1024]{1,0:T(8,128)(2,1)S(1)}, u32[]{:S(2)}, u32[]{:S(2)}) collective-permute-start(bf16[128,1024]{1,0:T(8,128)(2,1)S(1)} %get-tuple-element.248), channel_id=1, source_target_pairs={{0,8},{2,10},{4,12},{6,14},{8,16},{10,18},{12,20},{14,22},{16,24},... | collective-permute-start | bytes 786440 | tf_op jit(solution)/shard_map/ppermute | solution.py:325
  294.0 20.7 %collective-permute-start.47 = (bf16[128,1024]{1,0:T(8,128)(2,1)S(1)}, bf16[128,1024]{1,0:T(8,128)(2,1)S(1)}, u32[]{:S(2)}, u32[]{:S(2)}) collective-permute-start(bf16[128,1024]{1,0:T(8,128)(2,1)S(1)} %get-tuple-element.249), channel_id=1, source_target_pairs={{0,16},{2,18},{4,20},{6,22},{8,24},{10,26},{12,28},{14,30},{16,0},... | collective-permute-start | bytes 786440 | tf_op jit(solution)/shard_map/ppermute | solution.py:325
  295.6 20.3 %collective-permute-start.48 = (bf16[128,1024]{1,0:T(8,128)(2,1)S(1)}, bf16[128,1024]{1,0:T(8,128)(2,1)S(1)}, u32[]{:S(2)}, u32[]{:S(2)}) collective-permute-start(bf16[128,1024]{1,0:T(8,128)(2,1)S(1)} %get-tuple-element.250), channel_id=1, source_target_pairs={{0,24},{2,26},{4,28},{6,30},{8,0},{10,2},{12,4},{14,6},{16,8},{18,... | collective-permute-start | bytes 786440 | tf_op jit(solution)/shard_map/ppermute | solution.py:325
  300.4 18.6 %collective-permute-start.26 = (bf16[512,1024]{1,0:T(8,128)(2,1)S(1)}, bf16[512,1024]{1,0:T(8,128)(2,1)S(1)}, u32[]{:S(2)}, u32[]{:S(2)}) collective-permute-start(bf16[512,1024]{1,0:T(8,128)(2,1)S(1)} %copy-done.39), channel_id=1, source_target_pairs={{0,2},{2,0},{4,6},{6,4},{8,10},{10,8},{12,14},{14,12},{16,18},{18,... | collective-permute-start | bytes 3145736 | tf_op jit(solution)/shard_map/ppermute | solution.py:333
  306.7 24.8 %collective-permute-start.49 = (bf16[512,1024]{1,0:T(8,128)(2,1)S(1)}, bf16[512,1024]{1,0:T(8,128)(2,1)S(1)}, u32[]{:S(2)}, u32[]{:S(2)}) collective-permute-start(bf16[512,1024]{1,0:T(8,128)(2,1)S(1)} %get-tuple-element.267), channel_id=1, source_target_pairs={{0,1},{1,0},{2,3},{3,2},{4,5},{5,4},{6,7},{7,6},{8,9},{9,8},{10,11... | collective-permute-start | bytes 3145736 | tf_op jit(solution)/shard_map/ppermute | solution.py:337
  316.6 17.9 %collective-permute-start.50 = (f32[64,1024]{1,0:T(8,128)S(1)}, f32[64,1024]{1,0:T(8,128)S(1)}, u32[]{:S(2)}, u32[]{:S(2)}) collective-permute-start(f32[64,1024]{1,0:T(8,128)S(1)} %get-tuple-element.270), channel_id=1, source_target_pairs={{0,2},{2,0},{4,6},{6,4},{8,10},{10,8},{12,14},{14,12},{16,18},{18,... | collective-permute-start | bytes 786440 | tf_op jit(solution)/shard_map/ppermute | solution.py:333
  316.7 19.3 %collective-permute-start.51 = (bf16[64,2048]{1,0:T(8,128)(2,1)S(1)}, bf16[64,2048]{1,0:T(8,128)(2,1)S(1)}, u32[]{:S(2)}, u32[]{:S(2)}) collective-permute-start(bf16[64,2048]{1,0:T(8,128)(2,1)S(1)} %get-tuple-element.260), channel_id=1, source_target_pairs={{0,8},{2,10},{4,12},{6,14},{8,16},{10,18},{12,20},{14,22},{16,24},... | collective-permute-start | bytes 786440 | tf_op jit(solution)/shard_map/ppermute | solution.py:325
  316.8 23.3 %collective-permute-start.52 = (bf16[64,2048]{1,0:T(8,128)(2,1)S(1)}, bf16[64,2048]{1,0:T(8,128)(2,1)S(1)}, u32[]{:S(2)}, u32[]{:S(2)}) collective-permute-start(bf16[64,2048]{1,0:T(8,128)(2,1)S(1)} %get-tuple-element.261), channel_id=1, source_target_pairs={{0,16},{2,18},{4,20},{6,22},{8,24},{10,26},{12,28},{14,30},{16,0},... | collective-permute-start | bytes 786440 | tf_op jit(solution)/shard_map/ppermute | solution.py:325
  319.0 23.7 %collective-permute-start.53 = (bf16[64,2048]{1,0:T(8,128)(2,1)S(1)}, bf16[64,2048]{1,0:T(8,128)(2,1)S(1)}, u32[]{:S(2)}, u32[]{:S(2)}) collective-permute-start(bf16[64,2048]{1,0:T(8,128)(2,1)S(1)} %get-tuple-element.262), channel_id=1, source_target_pairs={{0,24},{2,26},{4,28},{6,30},{8,0},{10,2},{12,4},{14,6},{16,8},{18,... | collective-permute-start | bytes 786440 | tf_op jit(solution)/shard_map/ppermute | solution.py:325
  (57 other events, 559.5 us)
Sparse Core Ops, SparseCore 0:
  44.6 71.4 all-gather.1

commit v5 on v4

--- a/solution.py
+++ b/solution.py
@@ -1151,32 +1151,36 @@
     )
 
 
-def up_whole_kernel(info, mine_ref, got_ref, w_ref, out_ref, sum_ref):
+def up_whole_kernel(info, mine_ref, got_ref, w_ref, in_ref, out_ref, own_ref, send_ref):
     for ref, core in ((mine_ref, info[2]), (got_ref, 1 - info[2])):
         for i, place in enumerate((0, 2, 1, 3)):
             cols = pl.ds(pl.multiple_of(i * 512 + core * 256, 256), 256)
             out_ref[:, cols] = ref[:, place * 256 : place * 256 + 256]
     total = jnp.sum(w_ref[...].astype(f32) * out_ref[...], axis=1, keepdims=True)
-    sum_ref[...] = jnp.broadcast_to(total, sum_ref.shape)
-
-
-def up_whole(info, mine, got, w):
+    mid = jnp.broadcast_to(total, in_ref.shape)
+    first = info[3] == 0
+    own_ref[...] = jnp.where(first, in_ref[...], mid)
+    send_ref[...] = jnp.where(first, mid, in_ref[...])
+
+
+def up_whole(info, mine, got, w, in_sums):
     return call(
         up_whole_kernel,
         "up_whole",
-        [block(64, 1024)] * 2 + [block(64, 2048)],
-        [(block(64, 2048), of(f32, 64, 2048)), (block(64, 128), of(f32, 64, 128))],
+        [block(64, 1024)] * 2 + [block(64, 2048), block(64, 128)],
+        [(block(64, 2048), of(f32, 64, 2048))] + [(block(64, 128), of(f32, 64, 128))] * 2,
         [],
         0,
         info,
         mine,
         got,
         w,
+        in_sums,
     )
 
 
 def qkv_sum_kernel(info, *refs):
-    heads_ref, mid_ref, keep_ref, send_ref, out_ref = refs[4:]
+    heads_ref, keep_ref, send_ref, sum_ref, out_ref = refs[4:]
     total = summed(refs[:4])
     out_ref[...] = total[:, 768:1280]
     groups = (total[:, :768], total[:, 1280:])
@@ -1185,52 +1189,47 @@
     by_row = jnp.sum(weights[:, :768] * groups[0], axis=1, keepdims=True) + jnp.sum(
         weights[:, 768:1536] * groups[1], axis=1, keepdims=True
     )
-    both = jnp.broadcast_to(by_row, mid_ref.shape)
+    sum_ref[...] = jnp.broadcast_to(by_row, sum_ref.shape)
     first = info[3] == 0
     keep_ref[:, :512] = jnp.where(first, q, k)
-    keep_ref[:, 512:1024] = jnp.where(first, k, v)
-    keep_ref[:, 1024:] = jnp.where(first, both, mid_ref[...])
-    send_ref[:, :512] = jnp.where(first, v, q)
-    send_ref[:, 512:] = jnp.where(first, mid_ref[...], both)
-
-
-def qkv_sum(info, parts, heads, mid_sums):
+    keep_ref[:, 512:] = jnp.where(first, k, v)
+    send_ref[...] = jnp.where(first, v, q)
+
+
+def qkv_sum(info, parts, heads):
     return call(
         qkv_sum_kernel,
         "qkv_sum",
-        [block(64, 2048)] * 4 + [block(64, 1664), block(64, 128)],
-        [
-            (block(64, 1152), of(f32, 64, 1152)),
-            (block(64, 640), of(f32, 64, 640)),
-            (block(64, 512), of(f32, 64, 512)),
-        ],
+        [block(64, 2048)] * 4 + [block(64, 1664)],
+        [(block(64, n), of(f32, 64, n)) for n in (1024, 512, 128, 512)],
         [],
         0,
         info,
         *parts,
         heads,
-        mid_sums,
-    )
-
-
-def qkv_whole_kernel(info, keep_ref, got_ref, gain_ref, out_ref, gg_ref):
+    )
+
+
+def qkv_whole_kernel(info, keep_ref, got_ref, own_ref, other_ref, gain_ref, out_ref, gg_ref):
     out_ref[:, :512] = keep_ref[:, :512]
-    out_ref[:, 512:1024] = got_ref[:, :512]
-    out_ref[:, 1024:] = keep_ref[:, 512:1024]
-    gg_ref[...] = (keep_ref[:, 1024:1025] + got_ref[:, 512:513]) / gain_ref[...].astype(f32)
-
-
-def qkv_whole(info, keep, got, gains):
+    out_ref[:, 512:1024] = got_ref[...]
+    out_ref[:, 1024:] = keep_ref[:, 512:]
+    gg_ref[...] = (own_ref[:, :1] + other_ref[:, :1]) / gain_ref[...].astype(f32)
+
+
+def qkv_whole(info, keep, got, own_sums, other_sums, gains):
     return call(
         qkv_whole_kernel,
         "qkv_whole",
-        [block(64, 1152), block(64, 640), block(64, 1)],
+        [block(64, 1024), block(64, 512), block(64, 128), block(64, 128), block(64, 1)],
         [(block(64, 1536), of(f32, 64, 1536)), (block(64, 1), of(f32, 64, 1))],
         [],
         0,
         info,
         keep,
         got,
+        own_sums,
+        other_sums,
         gains,
     )
 
@@ -1388,10 +1387,11 @@
     up_got = swap_c(up_send)
     mixed = added(info, mixed_keep, after(mixed_got, up_mine), "mixed")
     grad_tokens = input_grad(info, after(x_own, mixed), e_own, after(e_got, mixed), gm, gain_all)
-    g_up, mid_sums = up_whole(info, up_mine, after(up_got, grad_tokens), w_up)
-    keep, send, g_out = qkv_sum(info, (after(heads_parts[0], mid_sums), *after(qkv_shift, mid_sums)), heads, mid_sums)
+    keep, send, in_sums, g_out = qkv_sum(info, (after(heads_parts[0], grad_tokens), *after(qkv_shift, grad_tokens)), heads)
     got = swap_y(send)
-    g_qkv, grad_gains = qkv_whole(info, keep, got, gains)
+    g_up, gain_own, gain_send = up_whole(info, up_mine, after(up_got, keep), w_up, in_sums)
+    gain_got = swap_y(gain_send)
+    g_qkv, grad_gains = qkv_whole(info, keep, after(got, g_up), gain_own, gain_got, gains)
     return (mixed[None], grad_tokens[None], grad_gains, g_qkv, g_out, g_up, g_down)
 
 

time: 366 us -> 362 us (0.989)
  waiting for transfers between devices: 128 us -> 122 us
    ppermute x13 -> x14, waiting for transfers between devices: 33.3 us -> 22.3 us  [swap_y(): return lax.ppermute(v, 'pair', [(0, 1), (1, 0)])]
    ppermute x18, waiting for transfers between devices: 39.1 us -> 43.3 us  [shift_z(): return lax.ppermute(v, 'rows', row_pairs(lambda z, x, c: (z + k, x, c)))]
    ppermute x13 -> x14, starting transfers between devices: 13.7 us -> 14.6 us  [swap_y(): return lax.ppermute(v, 'pair', [(0, 1), (1, 0)])]
  transfers between devices with their start and end apart: 56 -> 57, of which waited for: 25 -> 26; matrix products, arithmetic and copies ran while one was open for 3% -> 3% of each run, Pallas kernels for 35% -> 35%
where the time goes in v5:
time: 362 us; the launch traced here: 355 us
  Pallas kernels  135 us (37%)
  waiting for transfers between devices  122 us (34%)
  starting transfers between devices  56.8 us (16%)
  between operations  17.9 us (5%)
  local copies, waits for them, and re-layouts  16.8 us (5%)
  other arithmetic  7.56 us (2%)
    pallas_call x37, Pallas kernels, call(): pl.pallas_call(kernel, grid_spec=pltpu.PrefetchScalarGridSpec(num_scalar_...  112 us
    ppermute x11, waiting for transfers between devices, swap_x(): return lax.ppermute(v, 'rows', row_pairs(lambda z, x, c: (z, 1 - x, c)))  54.3 us
    ppermute x18, waiting for transfers between devices, shift_z(): return lax.ppermute(v, 'rows', row_pairs(lambda z, x, c: (z + k, x, c)))  43.3 us
    ppermute x18, starting transfers between devices, shift_z(): return lax.ppermute(v, 'rows', row_pairs(lambda z, x, c: (z + k, x, c)))  30.6 us
    pallas_call x2, Pallas kernels, attend_back(): pl.pallas_call(attend_back_kernel, grid_spec=pltpu.PrefetchScalarGridSpec...  23.2 us
    ppermute x14, waiting for transfers between devices, swap_y(): return lax.ppermute(v, 'pair', [(0, 1), (1, 0)])  22.3 us
    ppermute x14, starting transfers between devices, swap_y(): return lax.ppermute(v, 'pair', [(0, 1), (1, 0)])  14.6 us
    unnamed x100, local copies, waits for them, and re-layouts  11.9 us
  transfers between devices with their start and end apart: 57, of which 26 were waited for; matrix products, arithmetic and copies ran while one was open for 3% of the time, Pallas kernels for 35%

profile of v5, /device:TPU:8, one launch (start us, length us, event | category | flops | bytes accessed | tf_op | source)
XLA Modules:
  0.0 355.4 jit_solution(6798108742280132135)
XLA Ops:
  16.0 3.0 collective-permute-start.2
  19.0 2.5 collective-permute-start.1
  26.6 5.1 %fusion.5 = (f32[1024,1024]{1,0:T(8,128)}, f32[1024,1024]{1,0:T(8,128)}) fusion(s32[1024]{0:T(1024)S(1)} %pad_add_fusion, pred[1024]{0:T(1024)(128)(4,1)S(1)} %get-tuple-element.305, pred[1024]{0:T(1024)(128)(4,1)S(1)} %get-tuple-element.306), kind=kLoop, calls=%fused_computation.9 | loop fusion | flops 11534336 | bytes 8394752 | tf_op jit(solution)/shard_map/jit(_where)/select_n | solution.py:1284
  32.8 3.6 %collective-permute-done.1.refs_1_ = bf16[64,1664]{1,0:T(8,128)(2,1)S(1)} collective-permute-done((bf16[64,1664]{1,0:T(8,128)(2,1)S(1)}, bf16[64,1664]{1,0:T(8,128)(2,1)S(1)}, u32[]{:S(2)}, u32[]{:S(2)}) %collective-permute-start.1) | collective-permute-done | bytes 213024 | tf_op jit(solution)/shard_map/ppermute | solution.py:325
  40.7 2.8 collective-permute-start.9
  44.6 16.7 %collective-permute-done.10.refs_3_ = bf16[128,1024]{1,0:T(8,128)(2,1)S(1)} collective-permute-done((bf16[128,1024]{1,0:T(8,128)(2,1)S(1)}, bf16[128,1024]{1,0:T(8,128)(2,1)S(1)}, u32[]{:S(2)}, u32[]{:S(2)}) %collective-permute-start.10) | collective-permute-done | bytes 262176 | tf_op jit(solution)/shard_map/ppermute | solution.py:325
  61.4 4.0 %collective-permute-done.8.refs_1_ = bf16[128,1024]{1,0:T(8,128)(2,1)S(1)} collective-permute-done((bf16[128,1024]{1,0:T(8,128)(2,1)S(1)}, bf16[128,1024]{1,0:T(8,128)(2,1)S(1)}, u32[]{:S(2)}, u32[]{:S(2)}) %collective-permute-start.8) | collective-permute-done | bytes 262176 | tf_op jit(solution)/shard_map/ppermute | solution.py:325
  72.3 6.0 %project.1 = (bf16[1024,1536]{1,0:T(8,128)(2,1)S(1)}, f32[2,1024]{1,0:T(2,128)S(1)}) custom-call(s32[4]{0:T(128)S(1)} %pad_add_fusion.1.info, bf16[512,1024]{1,0:T(8,128)(2,1)S(1)} %bitcast.25, bf16[512,1024]{1,0:T(8,128)(2,1)S(1)} %copy-done.26, bf16[4,64,1664]{2,1,0:T(8,128)(2,1)S(1)} %copy-done.16, bf16[4,64,1664]{2,1,0:T(8,128)(2,1)S(1)} %copy-done.19, ...), custom_call_target="tpu_custom_call" | custom-call | flops 575000000 | bytes 65536 | tf_op jit(solution)/shard_map/project/pallas_call | solution.py:291
  78.3 2.3 collective-permute-start.16
  80.6 1.7 collective-permute-start.15
  82.5 8.5 %attend_0.1 = (bf16[512,256]{1,0:T(8,128)(2,1)S(1)}, bf16[512,256]{1,0:T(8,128)(2,1)S(1)}, f32[2,2,1024]{2,1,0:T(2,128)S(1)}) custom-call(s32[4]{0:T(128)S(1)} %pad_add_fusion.1.info, bf16[1024,1536]{1,0:T(8,128)(2,1)S(1)} %get-tuple-element.166.q_ref.k_ref.v_ref, bf16[1024,1536]{1,0:T(8,128)(2,1)S(1)} %get-tuple-element.166.q_ref.k_ref.v_ref, ...), custom_call_target="tpu_custom_call" | custom-call | flops 575000000 | bytes 65536 | tf_op jit(solution)/shard_map/attend_0/pallas_call | solution.py:291
  91.1 3.6 %collective-permute-done.18.refs_2_ = bf16[4,128,1024]{2,1,0:T(8,128)(2,1)} collective-permute-done((bf16[4,128,1024]{2,1,0:T(8,128)(2,1)S(1)}, bf16[4,128,1024]{2,1,0:T(8,128)(2,1)}, u32[]{:S(2)}, u32[]{:S(2)}) %collective-permute-start.18) | collective-permute-done | bytes 1048608 | tf_op jit(solution)/shard_map/ppermute | solution.py:337
  96.7 9.1 %attend_1.1 = (bf16[512,256]{1,0:T(8,128)(2,1)S(1)}, bf16[512,256]{1,0:T(8,128)(2,1)}, f32[2,2,1024]{2,1,0:T(2,128)S(1)}) custom-call(s32[4]{0:T(128)S(1)} %pad_add_fusion.1.info, bf16[1024,1536]{1,0:T(8,128)(2,1)S(1)} %get-tuple-element.166.q_ref.k_ref.v_ref, bf16[1024,1536]{1,0:T(8,128)(2,1)S(1)} %get-tuple-element.166.q_ref.k_ref.v_ref, ...), custom_call_target="tpu_custom_call" | custom-call | flops 23000000512 | bytes 65536 | tf_op jit(solution)/shard_map/attend_1/pallas_call | solution.py:291
  111.8 2.3 input_norm.1
  116.2 10.1 %collective-permute-done.19.refs_3_.refs_4_ = bf16[4,128,1024]{2,1,0:T(8,128)(2,1)} collective-permute-done((bf16[4,128,1024]{2,1,0:T(8,128)(2,1)}, bf16[4,128,1024]{2,1,0:T(8,128)(2,1)}, u32[]{:S(2)}, u32[]{:S(2)}) %collective-permute-start.19) | collective-permute-done | bytes 1048608 | tf_op jit(solution)/shard_map/ppermute | solution.py:329
  128.3 3.3 attention_out.1
  132.2 3.6 %collective-permute-done.22.refs_2_ = bf16[4,256,512]{2,1,0:T(8,128)(2,1)} collective-permute-done((bf16[4,256,512]{2,1,0:T(8,128)(2,1)}, bf16[4,256,512]{2,1,0:T(8,128)(2,1)}, u32[]{:S(2)}, u32[]{:S(2)}) %collective-permute-start.22) | collective-permute-done | bytes 1048608 | tf_op jit(solution)/shard_map/ppermute | solution.py:337
  138.2 10.6 %collective-permute-done.21.refs_1_ = bf16[4,256,512]{2,1,0:T(8,128)(2,1)} collective-permute-done((bf16[4,256,512]{2,1,0:T(8,128)(2,1)}, bf16[4,256,512]{2,1,0:T(8,128)(2,1)}, u32[]{:S(2)}, u32[]{:S(2)}) %collective-permute-start.21) | collective-permute-done | bytes 1048608 | tf_op jit(solution)/shard_map/ppermute | solution.py:329
  152.9 9.4 %up.1 = (bf16[1024,2048]{1,0:T(8,128)(2,1)S(1)}, bf16[1024,2048]{1,0:T(8,128)(2,1)S(1)}) custom-call(s32[4]{0:T(128)S(1)} %pad_add_fusion.1.info, bf16[512,1024]{1,0:T(8,128)(2,1)S(1)} %get-tuple-element.184.x0_ref.n0_ref, bf16[512,1024]{1,0:T(8,128)(2,1)S(1)} %collective-permute-done.20.x1_ref.n1_ref, bf16[4,128,1024]{2,1,0:T(8,128)(2,1)S(1)} %copy-done.10, ...), custom_call_target="tpu_custom_call" | custom-call | flops 575000000 | bytes 65536 | tf_op jit(solution)/shard_map/up/pallas_call | solution.py:291
  162.3 13.9 %down.1 = (f32[512,1024]{1,0:T(8,128)S(1)}, bf16[512,1024]{1,0:T(8,128)(2,1)S(1)}, bf16[1024,2048]{1,0:T(8,128)(2,1)S(1)}) custom-call(s32[4]{0:T(128)S(1)} %pad_add_fusion.1.info, bf16[1024,2048]{1,0:T(8,128)(2,1)S(1)} %get-tuple-element.201.act_ref, bf16[1024,2048]{1,0:T(8,128)(2,1)S(1)} %get-tuple-element.190.slope_ref, bf16[512,1024]{1,0:T(8,128)(2,1)S(1)} %bitcast.21, ...), custom_call_target="tpu_custom_call" | custom-call | flops 575000000 | bytes 65536 | tf_op jit(solution)/shard_map/down/pallas_call | solution.py:291
  176.2 7.1 %normed_back.1 = (f32[512,1024]{1,0:T(8,128)S(1)}, bf16[512,1024]{1,0:T(8,128)(2,1)S(1)}) custom-call(s32[4]{0:T(128)S(1)} %pad_add_fusion.1.info, bf16[1024,2048]{1,0:T(8,128)(2,1)S(1)} %get-tuple-element.207.gp_ref, bf16[4,128,1024]{2,1,0:T(8,128)(2,1)S(1)} %copy-done.10, bf16[4,128,1024]{2,1,0:T(8,128)(2,1)S(1)} %copy-done.12, ...), custom_call_target="tpu_custom_call" | custom-call | flops 575000000 | bytes 65536 | tf_op jit(solution)/shard_map/normed_back/pallas_call | solution.py:291
  183.4 7.7 %down_grad.1 = (bf16[4,512,256]{2,1,0:T(8,128)(2,1)S(1)}, bf16[4,512,256]{2,1,0:T(8,128)(2,1)S(1)}, bf16[4,512,256]{2,1,0:T(8,128)(2,1)S(1)}, bf16[4,512,256]{2,1,0:T(8,128)(2,1)S(1)}) custom-call(s32[4]{0:T(128)S(1)} %pad_add_fusion.1.info, bf16[512,1024]{1,0:T(8,128)(2,1)S(1)} %bitcast.22, bf16[512,1024]{1,0:T(8,128)(2,1)S(1)} %collective-permute-done.23.c1_ref, ...), custom_call_target="tpu_custom_call" | custom-call | flops 575000000 | bytes 65536 | tf_op jit(solution)/shard_map/down_grad/pallas_call | solution.py:291
  191.7 3.0 middle_back.1
  197.6 7.5 %up_grad.1 = (bf16[4,128,1024]{2,1,0:T(8,128)(2,1)S(1)}, bf16[4,128,1024]{2,1,0:T(8,128)(2,1)S(1)}, bf16[4,128,1024]{2,1,0:T(8,128)(2,1)S(1)}, bf16[4,128,1024]{2,1,0:T(8,128)(2,1)S(1)}) custom-call(s32[4]{0:T(128)S(1)} %pad_add_fusion.1.info, bf16[512,1024]{1,0:T(8,128)(2,1)S(1)} %get-tuple-element.184.x0_ref.n0_ref, bf16[512,1024]{1,0:T(8,128)(2,1)S(1)} %copy-done.14, ...), custom_call_target="tpu_custom_call" | custom-call | flops 575000000 | bytes 65536 | tf_op jit(solution)/shard_map/up_grad/pallas_call | solution.py:291
  205.1 12.1 %collective-permute-done.32.b_ref = bf16[4,512,256]{2,1,0:T(8,128)(2,1)S(1)} collective-permute-done((bf16[4,512,256]{2,1,0:T(8,128)(2,1)S(1)}, bf16[4,512,256]{2,1,0:T(8,128)(2,1)S(1)}, u32[]{:S(2)}, u32[]{:S(2)}) %collective-permute-start.32) | collective-permute-done | bytes 1048608 | tf_op jit(solution)/shard_map/ppermute | solution.py:329
  219.6 1.8 out_grad.1
  222.5 11.7 %attend_back_0.1.r0_ref.d0_ref = bf16[1024,768]{1,0:T(8,128)(2,1)S(1)} custom-call(s32[4]{0:T(128)S(1)} %pad_add_fusion.1.info, bf16[1024,1536]{1,0:T(8,128)(2,1)S(1)} %get-tuple-element.166.q_ref.k_ref.v_ref, bf16[1024,1536]{1,0:T(8,128)(2,1)S(1)} %get-tuple-element.166.q_ref.k_ref.v_ref, bf16[1024,1536]{1,0:T(8,128)(2,1)S(1)} %get-tuple-element.166.q_ref.k_ref.v_ref, ...), custom_call_target="tpu_custom_call" | custom-call | flops 23000000512 | bytes 65536 | tf_op jit(solution)/shard_map/attend_back_0/pallas_call | solution.py:537
  234.3 5.4 %collective-permute-done.36.b_ref = bf16[4,512,256]{2,1,0:T(8,128)(2,1)S(1)} collective-permute-done((bf16[4,512,256]{2,1,0:T(8,128)(2,1)S(1)}, bf16[4,512,256]{2,1,0:T(8,128)(2,1)S(1)}, u32[]{:S(2)}, u32[]{:S(2)}) %collective-permute-start.36) | collective-permute-done | bytes 1048608 | tf_op jit(solution)/shard_map/ppermute | solution.py:329
  239.6 4.5 %collective-permute-done.37.c_ref = bf16[4,512,256]{2,1,0:T(8,128)(2,1)S(1)} collective-permute-done((bf16[4,512,256]{2,1,0:T(8,128)(2,1)S(1)}, bf16[4,512,256]{2,1,0:T(8,128)(2,1)S(1)}, u32[]{:S(2)}, u32[]{:S(2)}) %collective-permute-start.37) | collective-permute-done | bytes 1048608 | tf_op jit(solution)/shard_map/ppermute | solution.py:337
  245.1 2.5 collective-permute-start.40
  249.2 4.5 %collective-permute-done.35.refs_1_ = bf16[8,64,512]{2,1,0:T(8,128)(2,1)S(1)} collective-permute-done((bf16[8,64,512]{2,1,0:T(8,128)(2,1)S(1)}, bf16[8,64,512]{2,1,0:T(8,128)(2,1)S(1)}, u32[]{:S(2)}, u32[]{:S(2)}) %collective-permute-start.35) | collective-permute-done | bytes 524320 | tf_op jit(solution)/shard_map/ppermute | solution.py:337
  253.7 1.7 collective-permute-start.42
  256.6 2.5 qkv_grad.2
  259.2 2.9 collective-permute-done.31.b_ref
  264.3 11.5 %attend_back_1.1.r0_ref.d1_ref = bf16[1024,768]{1,0:T(8,128)(2,1)S(1)} custom-call(s32[4]{0:T(128)S(1)} %pad_add_fusion.1.info, bf16[1024,1536]{1,0:T(8,128)(2,1)S(1)} %get-tuple-element.166.q_ref.k_ref.v_ref, bf16[1024,1536]{1,0:T(8,128)(2,1)S(1)} %get-tuple-element.166.q_ref.k_ref.v_ref, bf16[1024,1536]{1,0:T(8,128)(2,1)S(1)} %get-tuple-element.166.q_ref.k_ref.v_ref, ...), custom_call_target="tpu_custom_call" | custom-call | flops 575000000 | bytes 65536 | tf_op jit(solution)/shard_map/attend_back_1/pallas_call | solution.py:537
  278.0 6.6 %collective-permute-done.30.b_ref = bf16[4,128,1024]{2,1,0:T(8,128)(2,1)S(1)} collective-permute-done((bf16[4,128,1024]{2,1,0:T(8,128)(2,1)S(1)}, bf16[4,128,1024]{2,1,0:T(8,128)(2,1)S(1)}, u32[]{:S(2)}, u32[]{:S(2)}) %collective-permute-start.30) | collective-permute-done | bytes 1048608 | tf_op jit(solution)/shard_map/ppermute | solution.py:329
  284.6 3.1 collective-permute-done.39.c_ref
  288.6 2.3 qkv_grad.3
  291.5 2.5 collective-permute-start.46
  295.6 4.8 %input_back.1 = (f32[512,1024]{1,0:T(8,128)S(1)}, bf16[512,1024]{1,0:T(8,128)(2,1)S(1)}) custom-call(s32[4]{0:T(128)S(1)} %pad_add_fusion.1.info, bf16[1024,768]{1,0:T(8,128)(2,1)S(1)} %attend_back_0.1.r0_ref.d0_ref, bf16[1024,768]{1,0:T(8,128)(2,1)S(1)} %attend_back_1.1.r0_ref.d1_ref, bf16[4,64,1664]{2,1,0:T(8,128)(2,1)S(1)} %copy-done.17, ...), custom_call_target="tpu_custom_call" | custom-call | flops 575000000 | bytes 65536 | tf_op jit(solution)/shard_map/input_back/pallas_call | solution.py:291
  300.5 6.1 %collective-permute-done.45.bx_ref = bf16[4,64,768]{2,1,0:T(8,128)(2,1)S(1)} collective-permute-done((bf16[4,64,768]{2,1,0:T(8,128)(2,1)S(1)}, bf16[4,64,768]{2,1,0:T(8,128)(2,1)S(1)}, u32[]{:S(2)}, u32[]{:S(2)}) %collective-permute-start.45) | collective-permute-done | bytes 393248 | tf_op jit(solution)/shard_map/ppermute | solution.py:329
  308.5 3.0 collective-permute-done.46.refs_1_
  311.4 2.5 collective-permute-start.50
  313.9 11.6 %collective-permute-done.47.refs_2_ = bf16[128,1024]{1,0:T(8,128)(2,1)S(1)} collective-permute-done((bf16[128,1024]{1,0:T(8,128)(2,1)S(1)}, bf16[128,1024]{1,0:T(8,128)(2,1)S(1)}, u32[]{:S(2)}, u32[]{:S(2)}) %collective-permute-start.47) | collective-permute-done | bytes 262176 | tf_op jit(solution)/shard_map/ppermute | solution.py:325
  325.5 3.4 collective-permute-start.51
  331.4 3.1 input_grad.1
  334.5 2.7 collective-permute-done.51.refs_2_
  343.3 1.9 collective-permute-done.53.got_ref
  (223 shorter events, 75.5 us)
Async XLA Ops:
  7.2 109.0 %all-gather.2.cloned.1.call-start = ((), (), s32[]{:S(2)}) async-start(), calls=%async_computation | async-start | bytes 2162688 | tf_op jit(solution)/shard_map/all_gather | solution.py:1296
  10.4 25.9 %collective-permute-start.4 = (bf16[512,1024]{1,0:T(8,128)(2,1)}, bf16[512,1024]{1,0:T(8,128)(2,1)S(1)}, u32[]{:S(2)}, u32[]{:S(2)}) collective-permute-start(bf16[512,1024]{1,0:T(8,128)(2,1)} %bitcast.24), channel_id=1, source_target_pairs={{0,1},{1,0},{2,3},{3,2},{4,5},{5,4},{6,7},{7,6},{8,9},{9,8},{10,11... | collective-permute-start | bytes 3145736 | tf_op jit(solution)/shard_map/ppermute | solution.py:337
  15.9 16.9 %collective-permute-start.3 = (bf16[64,1664]{1,0:T(8,128)(2,1)S(1)}, bf16[64,1664]{1,0:T(8,128)(2,1)S(1)}, u32[]{:S(2)}, u32[]{:S(2)}) collective-permute-start(bf16[64,1664]{1,0:T(8,128)(2,1)S(1)} %heads.1.refs_0_.a_ref), channel_id=1, source_target_pairs={{0,24},{2,26},{4,28},{6,30},{8,0},{10,2},{12,4},{14,6},{16,8},{18,... | collective-permute-start | bytes 638984 | tf_op jit(solution)/shard_map/ppermute | solution.py:325
  16.0 16.8 %collective-permute-start.2 = (bf16[64,1664]{1,0:T(8,128)(2,1)S(1)}, bf16[64,1664]{1,0:T(8,128)(2,1)S(1)}, u32[]{:S(2)}, u32[]{:S(2)}) collective-permute-start(bf16[64,1664]{1,0:T(8,128)(2,1)S(1)} %heads.1.refs_0_.a_ref), channel_id=1, source_target_pairs={{0,16},{2,18},{4,20},{6,22},{8,24},{10,26},{12,28},{14,30},{16,0},... | collective-permute-start | bytes 638984 | tf_op jit(solution)/shard_map/ppermute | solution.py:325
  19.0 17.4 %collective-permute-start.1 = (bf16[64,1664]{1,0:T(8,128)(2,1)S(1)}, bf16[64,1664]{1,0:T(8,128)(2,1)S(1)}, u32[]{:S(2)}, u32[]{:S(2)}) collective-permute-start(bf16[64,1664]{1,0:T(8,128)(2,1)S(1)} %heads.1.refs_0_.a_ref), channel_id=1, source_target_pairs={{0,8},{2,10},{4,12},{6,14},{8,16},{10,18},{12,20},{14,22},{16,24},... | collective-permute-start | bytes 638984 | tf_op jit(solution)/shard_map/ppermute | solution.py:325
  38.0 27.4 %collective-permute-start.6 = (bf16[4,64,1664]{2,1,0:T(8,128)(2,1)S(1)}, bf16[4,64,1664]{2,1,0:T(8,128)(2,1)S(1)}, u32[]{:S(2)}, u32[]{:S(2)}) collective-permute-start(bf16[4,64,1664]{2,1,0:T(8,128)(2,1)S(1)} %qkv_stack.1.refs_0_), channel_id=1, source_target_pairs={{0,4},{2,6},{4,0},{6,2},{8,12},{10,14},{12,8},{14,10},{16,20},{18,... | collective-permute-start | bytes 2555912 | tf_op jit(solution)/shard_map/ppermute | solution.py:329
  39.5 21.8 %collective-permute-start.10 = (bf16[128,1024]{1,0:T(8,128)(2,1)S(1)}, bf16[128,1024]{1,0:T(8,128)(2,1)S(1)}, u32[]{:S(2)}, u32[]{:S(2)}) collective-permute-start(bf16[128,1024]{1,0:T(8,128)(2,1)S(1)} %both_rows.1.refs_0_), channel_id=1, source_target_pairs={{0,24},{2,26},{4,28},{6,30},{8,0},{10,2},{12,4},{14,6},{16,8},{18,... | collective-permute-start | bytes 786440 | tf_op jit(solution)/shard_map/ppermute | solution.py:325
  40.7 20.7 %collective-permute-start.9 = (bf16[128,1024]{1,0:T(8,128)(2,1)S(1)}, bf16[128,1024]{1,0:T(8,128)(2,1)S(1)}, u32[]{:S(2)}, u32[]{:S(2)}) collective-permute-start(bf16[128,1024]{1,0:T(8,128)(2,1)S(1)} %both_rows.1.refs_0_), channel_id=1, source_target_pairs={{0,16},{2,18},{4,20},{6,22},{8,24},{10,26},{12,28},{14,30},{16,0},... | collective-permute-start | bytes 786440 | tf_op jit(solution)/shard_map/ppermute | solution.py:325
  43.5 21.9 %collective-permute-start.8 = (bf16[128,1024]{1,0:T(8,128)(2,1)S(1)}, bf16[128,1024]{1,0:T(8,128)(2,1)S(1)}, u32[]{:S(2)}, u32[]{:S(2)}) collective-permute-start(bf16[128,1024]{1,0:T(8,128)(2,1)S(1)} %both_rows.1.refs_0_), channel_id=1, source_target_pairs={{0,8},{2,10},{4,12},{6,14},{8,16},{10,18},{12,20},{14,22},{16,24},... | collective-permute-start | bytes 786440 | tf_op jit(solution)/shard_map/ppermute | solution.py:325
  44.5 21.7 %collective-permute-start.7 = (bf16[4,64,1664]{2,1,0:T(8,128)(2,1)S(1)}, bf16[4,64,1664]{2,1,0:T(8,128)(2,1)S(1)}, u32[]{:S(2)}, u32[]{:S(2)}) collective-permute-start(bf16[4,64,1664]{2,1,0:T(8,128)(2,1)S(1)} %qkv_stack.1.refs_0_), channel_id=1, source_target_pairs={{0,2},{2,0},{4,6},{6,4},{8,10},{10,8},{12,14},{14,12},{16,18},{18,... | collective-permute-start | bytes 2555912 | tf_op jit(solution)/shard_map/ppermute | solution.py:333
  68.4 26.3 %collective-permute-start.18 = (bf16[4,128,1024]{2,1,0:T(8,128)(2,1)S(1)}, bf16[4,128,1024]{2,1,0:T(8,128)(2,1)}, u32[]{:S(2)}, u32[]{:S(2)}) collective-permute-start(bf16[4,128,1024]{2,1,0:T(8,128)(2,1)S(1)} %up_stack.1.refs_0_), channel_id=1, source_target_pairs={{0,1},{1,0},{2,3},{3,2},{4,5},{5,4},{6,7},{7,6},{8,9},{9,8},{10,11... | collective-permute-start | bytes 3145736 | tf_op jit(solution)/shard_map/ppermute | solution.py:337
  69.4 26.8 %collective-permute-start.17 = (bf16[4,128,1024]{2,1,0:T(8,128)(2,1)S(1)}, bf16[4,128,1024]{2,1,0:T(8,128)(2,1)S(1)}, u32[]{:S(2)}, u32[]{:S(2)}) collective-permute-start(bf16[4,128,1024]{2,1,0:T(8,128)(2,1)S(1)} %up_stack.1.refs_0_), channel_id=1, source_target_pairs={{0,4},{2,6},{4,0},{6,2},{8,12},{10,14},{12,8},{14,10},{16,20},{18,... | collective-permute-start | bytes 3145736 | tf_op jit(solution)/shard_map/ppermute | solution.py:329
  78.3 27.5 %collective-permute-start.16 = (bf16[256,512]{1,0:T(8,128)(2,1)S(1)}, bf16[256,512]{1,0:T(8,128)(2,1)S(1)}, u32[]{:S(2)}, u32[]{:S(2)}) collective-permute-start(bf16[256,512]{1,0:T(8,128)(2,1)S(1)} %copy-done.42), channel_id=1, source_target_pairs={{0,24},{2,26},{4,28},{6,30},{8,0},{10,2},{12,4},{14,6},{16,8},{18,... | collective-permute-start | bytes 786440 | tf_op jit(solution)/shard_map/ppermute | solution.py:325
  80.6 26.3 %collective-permute-start.15 = (bf16[256,512]{1,0:T(8,128)(2,1)S(1)}, bf16[256,512]{1,0:T(8,128)(2,1)S(1)}, u32[]{:S(2)}, u32[]{:S(2)}) collective-permute-start(bf16[256,512]{1,0:T(8,128)(2,1)S(1)} %copy-done.42), channel_id=1, source_target_pairs={{0,16},{2,18},{4,20},{6,22},{8,24},{10,26},{12,28},{14,30},{16,0},... | collective-permute-start | bytes 786440 | tf_op jit(solution)/shard_map/ppermute | solution.py:325
  82.3 24.6 %collective-permute-start.14 = (bf16[256,512]{1,0:T(8,128)(2,1)S(1)}, bf16[256,512]{1,0:T(8,128)(2,1)S(1)}, u32[]{:S(2)}, u32[]{:S(2)}) collective-permute-start(bf16[256,512]{1,0:T(8,128)(2,1)S(1)} %copy-done.42), channel_id=1, source_target_pairs={{0,8},{2,10},{4,12},{6,14},{8,16},{10,18},{12,20},{14,22},{16,24},... | collective-permute-start | bytes 786440 | tf_op jit(solution)/shard_map/ppermute | solution.py:325
  94.7 15.4 %collective-permute-start.12 = (bf16[512,256]{1,0:T(8,128)(2,1)S(1)}, bf16[512,256]{1,0:T(8,128)(2,1)S(1)}, u32[]{:S(2)}, u32[]{:S(2)}) collective-permute-start(bf16[512,256]{1,0:T(8,128)(2,1)S(1)} %get-tuple-element.171), channel_id=1, source_target_pairs={{0,1},{1,0},{2,3},{3,2},{4,5},{5,4},{6,7},{7,6},{8,9},{9,8},{10,11... | collective-permute-start | bytes 786440 | tf_op jit(solution)/shard_map/ppermute | solution.py:337
  96.2 30.1 %collective-permute-start.19 = (bf16[4,128,1024]{2,1,0:T(8,128)(2,1)}, bf16[4,128,1024]{2,1,0:T(8,128)(2,1)}, u32[]{:S(2)}, u32[]{:S(2)}) collective-permute-start(bf16[4,128,1024]{2,1,0:T(8,128)(2,1)} %collective-permute-done.18.refs_2_), channel_id=1, source_target_pairs={{0,4},{2,6},{4,0},{6,2},{8,12},{10,14},{12,8},{14,10},{16,20},{18,... | collective-permute-start | bytes 3145736 | tf_op jit(solution)/shard_map/ppermute | solution.py:329
  105.8 21.1 %collective-permute-start.13 = (bf16[512,256]{1,0:T(8,128)(2,1)}, bf16[512,256]{1,0:T(8,128)(2,1)}, u32[]{:S(2)}, u32[]{:S(2)}) collective-permute-start(bf16[512,256]{1,0:T(8,128)(2,1)} %get-tuple-element.172), channel_id=1, source_target_pairs={{0,1},{1,0},{2,3},{3,2},{4,5},{5,4},{6,7},{7,6},{8,9},{9,8},{10,11... | collective-permute-start | bytes 786440 | tf_op jit(solution)/shard_map/ppermute | solution.py:337
  108.6 40.2 %collective-permute-start.21 = (bf16[4,256,512]{2,1,0:T(8,128)(2,1)}, bf16[4,256,512]{2,1,0:T(8,128)(2,1)}, u32[]{:S(2)}, u32[]{:S(2)}) collective-permute-start(bf16[4,256,512]{2,1,0:T(8,128)(2,1)} %down_stack.1.refs_0_), channel_id=1, source_target_pairs={{0,4},{2,6},{4,0},{6,2},{8,12},{10,14},{12,8},{14,10},{16,20},{18,... | collective-permute-start | bytes 3145736 | tf_op jit(solution)/shard_map/ppermute | solution.py:329
  110.8 24.9 %collective-permute-start.22 = (bf16[4,256,512]{2,1,0:T(8,128)(2,1)}, bf16[4,256,512]{2,1,0:T(8,128)(2,1)}, u32[]{:S(2)}, u32[]{:S(2)}) collective-permute-start(bf16[4,256,512]{2,1,0:T(8,128)(2,1)} %down_stack.1.refs_0_), channel_id=1, source_target_pairs={{0,1},{1,0},{2,3},{3,2},{4,5},{5,4},{6,7},{7,6},{8,9},{9,8},{10,11... | collective-permute-start | bytes 3145736 | tf_op jit(solution)/shard_map/ppermute | solution.py:337
  131.6 19.3 %collective-permute-start.20 = (bf16[512,1024]{1,0:T(8,128)(2,1)S(1)}, bf16[512,1024]{1,0:T(8,128)(2,1)S(1)}, u32[]{:S(2)}, u32[]{:S(2)}) collective-permute-start(bf16[512,1024]{1,0:T(8,128)(2,1)S(1)} %get-tuple-element.184.x0_ref.n0_ref), channel_id=1, source_target_pairs={{0,2},{2,0},{4,6},{6,4},{8,10},{10,8},{12,14},{14,12},{16,18},{18,... | collective-permute-start | bytes 3145736 | tf_op jit(solution)/shard_map/ppermute | solution.py:333
  131.7 30.6 %collective-permute-start.23 = (bf16[512,1024]{1,0:T(8,128)(2,1)S(1)}, bf16[512,1024]{1,0:T(8,128)(2,1)S(1)}, u32[]{:S(2)}, u32[]{:S(2)}) collective-permute-start(bf16[512,1024]{1,0:T(8,128)(2,1)S(1)} %bitcast.20), channel_id=1, source_target_pairs={{0,2},{2,0},{4,6},{6,4},{8,10},{10,8},{12,14},{14,12},{16,18},{18,... | collective-permute-start | bytes 3145736 | tf_op jit(solution)/shard_map/ppermute | solution.py:333
  136.8 25.4 %collective-permute-start.25 = (bf16[2,256,512]{2,1,0:T(8,128)(2,1)S(1)}, bf16[2,256,512]{2,1,0:T(8,128)(2,1)S(1)}, u32[]{:S(2)}, u32[]{:S(2)}) collective-permute-start(bf16[2,256,512]{2,1,0:T(8,128)(2,1)S(1)} %slice.44), channel_id=1, source_target_pairs={{0,4},{2,6},{4,0},{6,2},{8,12},{10,14},{12,8},{14,10},{16,20},{18,... | collective-permute-start | bytes 1572872 | tf_op jit(solution)/shard_map/ppermute | solution.py:329
  149.9 12.4 %collective-permute-start.24 = (bf16[2,256,512]{2,1,0:T(8,128)(2,1)S(1)}, bf16[2,256,512]{2,1,0:T(8,128)(2,1)S(1)}, u32[]{:S(2)}, u32[]{:S(2)}) collective-permute-start(bf16[2,256,512]{2,1,0:T(8,128)(2,1)S(1)} %slice.43), channel_id=1, source_target_pairs={{0,1},{1,0},{2,3},{3,2},{4,5},{5,4},{6,7},{7,6},{8,9},{9,8},{10,11... | collective-permute-start | bytes 1572872 | tf_op jit(solution)/shard_map/ppermute | solution.py:337
  150.9 25.3 %collective-permute-start.28 = (bf16[8,64,512]{2,1,0:T(8,128)(2,1)S(1)}, bf16[8,64,512]{2,1,0:T(8,128)(2,1)S(1)}, u32[]{:S(2)}, u32[]{:S(2)}) collective-permute-start(bf16[8,64,512]{2,1,0:T(8,128)(2,1)S(1)} %get-tuple-element.198), channel_id=1, source_target_pairs={{0,2},{2,0},{4,6},{6,4},{8,10},{10,8},{12,14},{14,12},{16,18},{18,... | collective-permute-start | bytes 1572872 | tf_op jit(solution)/shard_map/ppermute | solution.py:333
  151.0 25.3 %collective-permute-start.27 = (bf16[8,64,1024]{2,1,0:T(8,128)(2,1)S(1)}, bf16[8,64,1024]{2,1,0:T(8,128)(2,1)S(1)}, u32[]{:S(2)}, u32[]{:S(2)}) collective-permute-start(bf16[8,64,1024]{2,1,0:T(8,128)(2,1)S(1)} %copy-done.41), channel_id=1, source_target_pairs={{0,2},{2,0},{4,6},{6,4},{8,10},{10,8},{12,14},{14,12},{16,18},{18,... | collective-permute-start | bytes 3145736 | tf_op jit(solution)/shard_map/ppermute | solution.py:333
  191.2 26.0 %collective-permute-start.32 = (bf16[4,512,256]{2,1,0:T(8,128)(2,1)S(1)}, bf16[4,512,256]{2,1,0:T(8,128)(2,1)S(1)}, u32[]{:S(2)}, u32[]{:S(2)}) collective-permute-start(bf16[4,512,256]{2,1,0:T(8,128)(2,1)S(1)} %get-tuple-element.202), channel_id=1, source_target_pairs={{0,4},{2,6},{4,0},{6,2},{8,12},{10,14},{12,8},{14,10},{16,20},{18,... | collective-permute-start | bytes 3145736 | tf_op jit(solution)/shard_map/ppermute | solution.py:329
  194.7 24.8 %collective-permute-start.33 = (bf16[512,1024]{1,0:T(8,128)(2,1)S(1)}, bf16[512,1024]{1,0:T(8,128)(2,1)S(1)}, u32[]{:S(2)}, u32[]{:S(2)}) collective-permute-start(bf16[512,1024]{1,0:T(8,128)(2,1)S(1)} %get-tuple-element.217.r0_ref), channel_id=1, source_target_pairs={{0,2},{2,0},{4,6},{6,4},{8,10},{10,8},{12,14},{14,12},{16,18},{18,... | collective-permute-start | bytes 3145736 | tf_op jit(solution)/shard_map/ppermute | solution.py:333
  195.0 26.4 %collective-permute-start.34 = (bf16[512,512]{1,0:T(8,128)(2,1)S(1)}, bf16[512,512]{1,0:T(8,128)(2,1)S(1)}, u32[]{:S(2)}, u32[]{:S(2)}) collective-permute-start(bf16[512,512]{1,0:T(8,128)(2,1)S(1)} %get-tuple-element.224), channel_id=1, source_target_pairs={{0,1},{1,0},{2,3},{3,2},{4,5},{5,4},{6,7},{7,6},{8,9},{9,8},{10,11... | collective-permute-start | bytes 1572872 | tf_op jit(solution)/shard_map/ppermute | solution.py:337
  196.0 43.6 %collective-permute-start.36 = (bf16[4,512,256]{2,1,0:T(8,128)(2,1)S(1)}, bf16[4,512,256]{2,1,0:T(8,128)(2,1)S(1)}, u32[]{:S(2)}, u32[]{:S(2)}) collective-permute-start(bf16[4,512,256]{2,1,0:T(8,128)(2,1)S(1)} %get-tuple-element.228), channel_id=1, source_target_pairs={{0,4},{2,6},{4,0},{6,2},{8,12},{10,14},{12,8},{14,10},{16,20},{18,... | collective-permute-start | bytes 3145736 | tf_op jit(solution)/shard_map/ppermute | solution.py:329
  218.0 26.2 %collective-permute-start.37 = (bf16[4,512,256]{2,1,0:T(8,128)(2,1)S(1)}, bf16[4,512,256]{2,1,0:T(8,128)(2,1)S(1)}, u32[]{:S(2)}, u32[]{:S(2)}) collective-permute-start(bf16[4,512,256]{2,1,0:T(8,128)(2,1)S(1)} %added.2), channel_id=1, source_target_pairs={{0,1},{1,0},{2,3},{3,2},{4,5},{5,4},{6,7},{7,6},{8,9},{9,8},{10,11... | collective-permute-start | bytes 3145736 | tf_op jit(solution)/shard_map/ppermute | solution.py:337
  219.1 43.0 %collective-permute-start.31 = (bf16[4,128,1024]{2,1,0:T(8,128)(2,1)S(1)}, bf16[4,128,1024]{2,1,0:T(8,128)(2,1)S(1)}, u32[]{:S(2)}, u32[]{:S(2)}) collective-permute-start(bf16[4,128,1024]{2,1,0:T(8,128)(2,1)S(1)} %get-tuple-element.211), channel_id=1, source_target_pairs={{0,4},{2,6},{4,0},{6,2},{8,12},{10,14},{12,8},{14,10},{16,20},{18,... | collective-permute-start | bytes 3145736 | tf_op jit(solution)/shard_map/ppermute | solution.py:329
  221.4 32.3 %collective-permute-start.35 = (bf16[8,64,512]{2,1,0:T(8,128)(2,1)S(1)}, bf16[8,64,512]{2,1,0:T(8,128)(2,1)S(1)}, u32[]{:S(2)}, u32[]{:S(2)}) collective-permute-start(bf16[8,64,512]{2,1,0:T(8,128)(2,1)S(1)} %get-tuple-element.226), channel_id=1, source_target_pairs={{0,1},{1,0},{2,3},{3,2},{4,5},{5,4},{6,7},{7,6},{8,9},{9,8},{10,11... | collective-permute-start | bytes 1572872 | tf_op jit(solution)/shard_map/ppermute | solution.py:337
  234.2 21.8 %collective-permute-start.38 = (bf16[1024,768]{1,0:T(8,128)(2,1)S(1)}, bf16[1024,768]{1,0:T(8,128)(2,1)S(1)}, u32[]{:S(2)}, u32[]{:S(2)}) collective-permute-start(bf16[1024,768]{1,0:T(8,128)(2,1)S(1)} %attend_back_0.1.r0_ref.d0_ref), channel_id=1, source_target_pairs={{0,2},{2,0},{4,6},{6,4},{8,10},{10,8},{12,14},{14,12},{16,18},{18,... | collective-permute-start | bytes 4718600 | tf_op jit(solution)/shard_map/ppermute | solution.py:333
  245.1 30.7 %collective-permute-start.40 = (bf16[512,256]{1,0:T(8,128)(2,1)S(1)}, bf16[512,256]{1,0:T(8,128)(2,1)S(1)}, u32[]{:S(2)}, u32[]{:S(2)}) collective-permute-start(bf16[512,256]{1,0:T(8,128)(2,1)S(1)} %get-tuple-element.232), channel_id=1, source_target_pairs={{0,8},{2,10},{4,12},{6,14},{8,16},{10,18},{12,20},{14,22},{16,24},... | collective-permute-start | bytes 786440 | tf_op jit(solution)/shard_map/ppermute | solution.py:325
  247.6 28.3 %collective-permute-start.41 = (bf16[512,256]{1,0:T(8,128)(2,1)S(1)}, bf16[512,256]{1,0:T(8,128)(2,1)S(1)}, u32[]{:S(2)}, u32[]{:S(2)}) collective-permute-start(bf16[512,256]{1,0:T(8,128)(2,1)S(1)} %get-tuple-element.233), channel_id=1, source_target_pairs={{0,16},{2,18},{4,20},{6,22},{8,24},{10,26},{12,28},{14,30},{16,0},... | collective-permute-start | bytes 786440 | tf_op jit(solution)/shard_map/ppermute | solution.py:325
  253.7 22.2 %collective-permute-start.42 = (bf16[512,256]{1,0:T(8,128)(2,1)S(1)}, bf16[512,256]{1,0:T(8,128)(2,1)S(1)}, u32[]{:S(2)}, u32[]{:S(2)}) collective-permute-start(bf16[512,256]{1,0:T(8,128)(2,1)S(1)} %get-tuple-element.234), channel_id=1, source_target_pairs={{0,24},{2,26},{4,28},{6,30},{8,0},{10,2},{12,4},{14,6},{16,8},{18,... | collective-permute-start | bytes 786440 | tf_op jit(solution)/shard_map/ppermute | solution.py:325
  256.0 28.6 %collective-permute-start.30 = (bf16[4,128,1024]{2,1,0:T(8,128)(2,1)S(1)}, bf16[4,128,1024]{2,1,0:T(8,128)(2,1)S(1)}, u32[]{:S(2)}, u32[]{:S(2)}) collective-permute-start(bf16[4,128,1024]{2,1,0:T(8,128)(2,1)S(1)} %get-tuple-element.209), channel_id=1, source_target_pairs={{0,4},{2,6},{4,0},{6,2},{8,12},{10,14},{12,8},{14,10},{16,20},{18,... | collective-permute-start | bytes 3145736 | tf_op jit(solution)/shard_map/ppermute | solution.py:329
  263.2 24.4 %collective-permute-start.39 = (bf16[4,128,1024]{2,1,0:T(8,128)(2,1)S(1)}, bf16[4,128,1024]{2,1,0:T(8,128)(2,1)S(1)}, u32[]{:S(2)}, u32[]{:S(2)}) collective-permute-start(bf16[4,128,1024]{2,1,0:T(8,128)(2,1)S(1)} %added.3), channel_id=1, source_target_pairs={{0,1},{1,0},{2,3},{3,2},{4,5},{5,4},{6,7},{7,6},{8,9},{9,8},{10,11... | collective-permute-start | bytes 3145736 | tf_op jit(solution)/shard_map/ppermute | solution.py:337
  275.8 12.8 %collective-permute-start.44 = (bf16[1024,768]{1,0:T(8,128)(2,1)S(1)}, bf16[1024,768]{1,0:T(8,128)(2,1)S(1)}, u32[]{:S(2)}, u32[]{:S(2)}) collective-permute-start(bf16[1024,768]{1,0:T(8,128)(2,1)S(1)} %attend_back_1.1.r0_ref.d1_ref), channel_id=1, source_target_pairs={{0,2},{2,0},{4,6},{6,4},{8,10},{10,8},{12,14},{14,12},{16,18},{18,... | collective-permute-start | bytes 4718600 | tf_op jit(solution)/shard_map/ppermute | solution.py:333
  275.9 24.5 %collective-permute-start.43 = (bf16[4,64,1280]{2,1,0:T(8,128)(2,1)S(1)}, bf16[4,64,1280]{2,1,0:T(8,128)(2,1)S(1)}, u32[]{:S(2)}, u32[]{:S(2)}) collective-permute-start(bf16[4,64,1280]{2,1,0:T(8,128)(2,1)S(1)} %get-tuple-element.250), channel_id=1, source_target_pairs={{0,4},{2,6},{4,0},{6,2},{8,12},{10,14},{12,8},{14,10},{16,20},{18,... | collective-permute-start | bytes 1966088 | tf_op jit(solution)/shard_map/ppermute | solution.py:329
  291.0 15.7 %collective-permute-start.45 = (bf16[4,64,768]{2,1,0:T(8,128)(2,1)S(1)}, bf16[4,64,768]{2,1,0:T(8,128)(2,1)S(1)}, u32[]{:S(2)}, u32[]{:S(2)}) collective-permute-start(bf16[4,64,768]{2,1,0:T(8,128)(2,1)S(1)} %get-tuple-element.256), channel_id=1, source_target_pairs={{0,4},{2,6},{4,0},{6,2},{8,12},{10,14},{12,8},{14,10},{16,20},{18,... | collective-permute-start | bytes 1179656 | tf_op jit(solution)/shard_map/ppermute | solution.py:329
  291.5 19.9 %collective-permute-start.46 = (bf16[128,1024]{1,0:T(8,128)(2,1)S(1)}, bf16[128,1024]{1,0:T(8,128)(2,1)S(1)}, u32[]{:S(2)}, u32[]{:S(2)}) collective-permute-start(bf16[128,1024]{1,0:T(8,128)(2,1)S(1)} %get-tuple-element.251), channel_id=1, source_target_pairs={{0,8},{2,10},{4,12},{6,14},{8,16},{10,18},{12,20},{14,22},{16,24},... | collective-permute-start | bytes 786440 | tf_op jit(solution)/shard_map/ppermute | solution.py:325
  294.0 31.5 %collective-permute-start.47 = (bf16[128,1024]{1,0:T(8,128)(2,1)S(1)}, bf16[128,1024]{1,0:T(8,128)(2,1)S(1)}, u32[]{:S(2)}, u32[]{:S(2)}) collective-permute-start(bf16[128,1024]{1,0:T(8,128)(2,1)S(1)} %get-tuple-element.252), channel_id=1, source_target_pairs={{0,16},{2,18},{4,20},{6,22},{8,24},{10,26},{12,28},{14,30},{16,0},... | collective-permute-start | bytes 786440 | tf_op jit(solution)/shard_map/ppermute | solution.py:325
  295.6 33.2 %collective-permute-start.48 = (bf16[128,1024]{1,0:T(8,128)(2,1)S(1)}, bf16[128,1024]{1,0:T(8,128)(2,1)S(1)}, u32[]{:S(2)}, u32[]{:S(2)}) collective-permute-start(bf16[128,1024]{1,0:T(8,128)(2,1)S(1)} %get-tuple-element.253), channel_id=1, source_target_pairs={{0,24},{2,26},{4,28},{6,30},{8,0},{10,2},{12,4},{14,6},{16,8},{18,... | collective-permute-start | bytes 786440 | tf_op jit(solution)/shard_map/ppermute | solution.py:325
  300.4 29.1 %collective-permute-start.26 = (bf16[512,1024]{1,0:T(8,128)(2,1)S(1)}, bf16[512,1024]{1,0:T(8,128)(2,1)S(1)}, u32[]{:S(2)}, u32[]{:S(2)}) collective-permute-start(bf16[512,1024]{1,0:T(8,128)(2,1)S(1)} %copy-done.39), channel_id=1, source_target_pairs={{0,2},{2,0},{4,6},{6,4},{8,10},{10,8},{12,14},{14,12},{16,18},{18,... | collective-permute-start | bytes 3145736 | tf_op jit(solution)/shard_map/ppermute | solution.py:333
  306.7 24.8 %collective-permute-start.49 = (bf16[512,1024]{1,0:T(8,128)(2,1)S(1)}, bf16[512,1024]{1,0:T(8,128)(2,1)S(1)}, u32[]{:S(2)}, u32[]{:S(2)}) collective-permute-start(bf16[512,1024]{1,0:T(8,128)(2,1)S(1)} %get-tuple-element.270), channel_id=1, source_target_pairs={{0,1},{1,0},{2,3},{3,2},{4,5},{5,4},{6,7},{7,6},{8,9},{9,8},{10,11... | collective-permute-start | bytes 3145736 | tf_op jit(solution)/shard_map/ppermute | solution.py:337
  311.4 23.1 %collective-permute-start.50 = (bf16[64,2048]{1,0:T(8,128)(2,1)S(1)}, bf16[64,2048]{1,0:T(8,128)(2,1)S(1)}, u32[]{:S(2)}, u32[]{:S(2)}) collective-permute-start(bf16[64,2048]{1,0:T(8,128)(2,1)S(1)} %get-tuple-element.263), channel_id=1, source_target_pairs={{0,8},{2,10},{4,12},{6,14},{8,16},{10,18},{12,20},{14,22},{16,24},... | collective-permute-start | bytes 786440 | tf_op jit(solution)/shard_map/ppermute | solution.py:325
  (58 other events, 539.6 us)
Sparse Core Ops, SparseCore 0:
  44.6 71.4 all-gather.1

commit v6 on v5

--- a/solution.py
+++ b/solution.py
@@ -264,7 +264,7 @@
 f32 = jnp.float32
 VMEM = dict(
     down=24, up=20, normed_back=20, down_grad=20, up_grad=16, middle_back=20, project=20, input_back=18, attend_0=12, attend_1=12,
-    attend_back_0=14, attend_back_1=14, attention_out=16, qkv_grad=16, out_grad=10, input_norm=18, input_grad=14
+    attend_back_0=14, attend_back_1=14, attention_out=16, qkv_grad=16, out_grad=10, input_norm=18, input_grad=14, half_added=18
 )
 
 
@@ -272,7 +272,7 @@
     return pltpu.CompilerParams(vmem_limit_bytes=VMEM.get(name, 10) * 1024 * 1024)
 
 
-PLACES = dict(attend_1=20, touch=20, attend_back_0=20, down_sum=20, up_parts=20, up_sum=20)
+PLACES = dict(half_added=8, attend_1=20, touch=20, attend_back_0=20, down_sum=20, up_parts=20, up_sum=20)
 
 
 def cost(name):
@@ -782,7 +782,7 @@
     )
 
 
-def down_grad_kernel(info, c0_ref, c1_ref, act_ref, far, across, beside, own, t_ref):
+def down_grad_kernel(info, c0_ref, c1_ref, act_ref, far_a, far_b, across, beside, own, t_ref):
     g = pl.program_id(0)
 
     @pl.when(g == 0)
@@ -798,11 +798,18 @@
         total = dot(t_ref[rows, :], act_ref[:, units], (1, 0)).astype(bf16)
         for j in range(2):
             dz = lax.rem(half * 2 + j - info[0] + LINE, LINE)
-            for at, ref in enumerate((far, across, beside, own)):
+            part = total[:, j * 256 : j * 256 + 256]
+            for at, ref in ((1, across), (2, beside), (3, own)):
 
                 @pl.when(g == at)
                 def _():
-                    ref[dz] = total[:, j * 256 : j * 256 + 256]
+                    ref[dz] = part
+
+            for ref, here in ((far_a, dz < 2), (far_b, dz >= 2)):
+
+                @pl.when((g == 0) & here)
+                def _():
+                    ref[lax.rem(dz, 2)] = part
 
 
 def down_grad(info, cot_own, cot_sib, act):
@@ -810,7 +817,7 @@
         down_grad_kernel,
         "down_grad",
         [block(HALF, 1024), block(HALF, 1024), block(1024, 2048)],
-        [(block(LINE, 512, 256), of(bf16, LINE, 512, 256))] * 4,
+        [(block(n, 512, 256), of(bf16, n, 512, 256)) for n in (2, 2, 4, 4, 4)],
         [pltpu.VMEM((1024, 1024), bf16)],
         2 * 1024 * 1024 * 2048,
         info,
@@ -1053,6 +1060,20 @@
     steps = 2
     spec = pl.BlockSpec((a.shape[0] // steps, *a.shape[1:]), lambda i, s: (i,) + (0,) * (a.ndim - 1))
     return call(added_kernel, name, [spec, spec], [(spec, of(bf16, *a.shape))], [], 0, info, a, b, grid=(steps,))[0]
+
+
+def half_added_kernel(info, a_ref, b_ref, first_ref, second_ref, a_out, b_out):
+    a_out[:2] = (a_ref[:2].astype(f32) + first_ref[...].astype(f32)).astype(bf16)
+    a_out[2:] = a_ref[2:]
+    b_out[:2] = b_ref[:2]
+    b_out[2:] = (b_ref[2:].astype(f32) + second_ref[...].astype(f32)).astype(bf16)
+
+
+def half_added(info, a, b, first, second):
+    spec, half = block(*a.shape), block(*first.shape)
+    return call(
+        half_added_kernel, "half_added", [spec, spec, half, half], [(spec, of(bf16, *a.shape))] * 2, [], 0, info, a, b, first, second
+    )
 
 
 def line_parts_kernel(info, a_ref, b_ref, c_ref, *outs):
@@ -1344,18 +1365,18 @@
     mixed_got = swap_c(mixed_send)
     e_keep, e_send = normed_back(info, gp, up_pieces)
     e_got = swap_c(e_send)
-    far, down_across, down_beside, down_own = down_grad(info, cot, cot_sib, after(act, e_keep))
-    down_far, down_x = swap_x(far), swap_x(down_beside)
+    far, far_b, down_across, down_beside, down_own = down_grad(info, cot, cot_sib, after(act, e_keep))
+    down_far = (swap_x(far), swap_y(far_b))
     gm, gb, ga_keep, ga_send = middle_back(info, after(e_keep, far), after(e_got, far), cot, mid, gain_all, out_all)
     ga_got = swap_y(ga_send)
     gb_sib = swap_c(gb)
     far, up_across, up_beside, up_own = up_grad(info, nm_own, nm_sib, after(gp, gb))
-    down_across = added(info, after(down_across, far), after(down_far, far))
-    down_y = swap_y(down_across)
-    up_far = swap_x(far)
+    down_across, down_beside = half_added(info, after(down_across, far), down_beside, *after(down_far, far))
+    down_x, down_y = swap_x(down_beside), swap_y(down_across)
     gb_sib = after(gb_sib, down_across)
     out_keep, out_send = out_grad(info, att_t, after(gb, down_across), att_t_sib, gb_sib)
     out_got = swap_y(out_send)
+    up_far = swap_x(after(far, out_keep))
     ga_got = after(ga_got, out_keep)
     dproj0 = attend_back(info, projected, after(bias_t, out_keep), lse0, ga_keep, ga_got, 0)
     dproj0_sib = swap_c(dproj0)

time: 362 us -> 356 us (0.983)
  waiting for transfers between devices: 122 us -> 115 us
    ppermute x11, waiting for transfers between devices: 54.3 us -> 33.3 us  [swap_x(): return lax.ppermute(v, 'rows', row_pairs(lambda z, x, c: (z, 1 - x, c)))]
    ppermute x14 -> x15, waiting for transfers between devices: 22.3 us -> 36.4 us  [swap_y(): return lax.ppermute(v, 'pair', [(0, 1), (1, 0)])]
    ppermute x14 -> x15, starting transfers between devices: 14.6 us -> 15.7 us  [swap_y(): return lax.ppermute(v, 'pair', [(0, 1), (1, 0)])]
    unnamed x100 -> x96, local copies, waits for them, and re-layouts: 11.9 us -> 12 us
  transfers between devices with their start and end apart: 57 -> 58, of which waited for: 26 -> 26; matrix products, arithmetic and copies ran while one was open for 3% -> 3% of each run, Pallas kernels for 35% -> 36%
where the time goes in v6:
time: 356 us; the launch traced here: 350 us
  Pallas kernels  135 us (38%)
  waiting for transfers between devices  115 us (32%)
  starting transfers between devices  58.2 us (16%)
  between operations  17.9 us (5%)
  local copies, waits for them, and re-layouts  16.9 us (5%)
  other arithmetic  7.56 us (2%)
    pallas_call x37, Pallas kernels, call(): pl.pallas_call(kernel, grid_spec=pltpu.PrefetchScalarGridSpec(num_scalar_...  112 us
    ppermute x18, waiting for transfers between devices, shift_z(): return lax.ppermute(v, 'rows', row_pairs(lambda z, x, c: (z + k, x, c)))  43.3 us
    ppermute x15, waiting for transfers between devices, swap_y(): return lax.ppermute(v, 'pair', [(0, 1), (1, 0)])  36.4 us
    ppermute x11, waiting for transfers between devices, swap_x(): return lax.ppermute(v, 'rows', row_pairs(lambda z, x, c: (z, 1 - x, c)))  33.3 us
    ppermute x18, starting transfers between devices, shift_z(): return lax.ppermute(v, 'rows', row_pairs(lambda z, x, c: (z + k, x, c)))  30.6 us
    pallas_call x2, Pallas kernels, attend_back(): pl.pallas_call(attend_back_kernel, grid_spec=pltpu.PrefetchScalarGridSpec...  23.2 us
    ppermute x15, starting transfers between devices, swap_y(): return lax.ppermute(v, 'pair', [(0, 1), (1, 0)])  15.7 us
    unnamed x96, local copies, waits for them, and re-layouts  12 us
  transfers between devices with their start and end apart: 58, of which 26 were waited for; matrix products, arithmetic and copies ran while one was open for 3% of the time, Pallas kernels for 36%

profile of v6, /device:TPU:8, one launch (start us, length us, event | category | flops | bytes accessed | tf_op | source)
XLA Modules:
  0.0 349.9 jit_solution(9398249248536270552)
XLA Ops:
  16.0 3.0 collective-permute-start.2
  19.0 2.5 collective-permute-start.1
  26.6 5.1 %fusion.5 = (f32[1024,1024]{1,0:T(8,128)}, f32[1024,1024]{1,0:T(8,128)}) fusion(s32[1024]{0:T(1024)S(1)} %pad_add_fusion, pred[1024]{0:T(1024)(128)(4,1)S(1)} %get-tuple-element.315, pred[1024]{0:T(1024)(128)(4,1)S(1)} %get-tuple-element.316), kind=kLoop, calls=%fused_computation.9 | loop fusion | flops 11534336 | bytes 8394752 | tf_op jit(solution)/shard_map/jit(_where)/select_n | solution.py:1305
  32.8 3.6 %collective-permute-done.1.refs_1_ = bf16[64,1664]{1,0:T(8,128)(2,1)S(1)} collective-permute-done((bf16[64,1664]{1,0:T(8,128)(2,1)S(1)}, bf16[64,1664]{1,0:T(8,128)(2,1)S(1)}, u32[]{:S(2)}, u32[]{:S(2)}) %collective-permute-start.1) | collective-permute-done | bytes 213024 | tf_op jit(solution)/shard_map/ppermute | solution.py:325
  40.7 2.8 collective-permute-start.9
  44.6 16.7 %collective-permute-done.10.refs_3_ = bf16[128,1024]{1,0:T(8,128)(2,1)S(1)} collective-permute-done((bf16[128,1024]{1,0:T(8,128)(2,1)S(1)}, bf16[128,1024]{1,0:T(8,128)(2,1)S(1)}, u32[]{:S(2)}, u32[]{:S(2)}) %collective-permute-start.10) | collective-permute-done | bytes 262176 | tf_op jit(solution)/shard_map/ppermute | solution.py:325
  61.4 4.0 %collective-permute-done.8.refs_1_ = bf16[128,1024]{1,0:T(8,128)(2,1)S(1)} collective-permute-done((bf16[128,1024]{1,0:T(8,128)(2,1)S(1)}, bf16[128,1024]{1,0:T(8,128)(2,1)S(1)}, u32[]{:S(2)}, u32[]{:S(2)}) %collective-permute-start.8) | collective-permute-done | bytes 262176 | tf_op jit(solution)/shard_map/ppermute | solution.py:325
  72.3 6.0 %project.1 = (bf16[1024,1536]{1,0:T(8,128)(2,1)S(1)}, f32[2,1024]{1,0:T(2,128)S(1)}) custom-call(s32[4]{0:T(128)S(1)} %pad_add_fusion.1.info, bf16[512,1024]{1,0:T(8,128)(2,1)S(1)} %bitcast.25, bf16[512,1024]{1,0:T(8,128)(2,1)S(1)} %copy-done.26, bf16[4,64,1664]{2,1,0:T(8,128)(2,1)S(1)} %copy-done.16, bf16[4,64,1664]{2,1,0:T(8,128)(2,1)S(1)} %copy-done.19, ...), custom_call_target="tpu_custom_call" | custom-call | flops 575000000 | bytes 65536 | tf_op jit(solution)/shard_map/project/pallas_call | solution.py:291
  78.3 2.3 collective-permute-start.16
  80.6 1.7 collective-permute-start.15
  82.5 8.5 %attend_0.1 = (bf16[512,256]{1,0:T(8,128)(2,1)S(1)}, bf16[512,256]{1,0:T(8,128)(2,1)S(1)}, f32[2,2,1024]{2,1,0:T(2,128)S(1)}) custom-call(s32[4]{0:T(128)S(1)} %pad_add_fusion.1.info, bf16[1024,1536]{1,0:T(8,128)(2,1)S(1)} %get-tuple-element.171.q_ref.k_ref.v_ref, bf16[1024,1536]{1,0:T(8,128)(2,1)S(1)} %get-tuple-element.171.q_ref.k_ref.v_ref, ...), custom_call_target="tpu_custom_call" | custom-call | flops 575000000 | bytes 65536 | tf_op jit(solution)/shard_map/attend_0/pallas_call | solution.py:291
  91.1 3.6 %collective-permute-done.18.refs_2_ = bf16[4,128,1024]{2,1,0:T(8,128)(2,1)} collective-permute-done((bf16[4,128,1024]{2,1,0:T(8,128)(2,1)S(1)}, bf16[4,128,1024]{2,1,0:T(8,128)(2,1)}, u32[]{:S(2)}, u32[]{:S(2)}) %collective-permute-start.18) | collective-permute-done | bytes 1048608 | tf_op jit(solution)/shard_map/ppermute | solution.py:337
  96.7 9.1 %attend_1.1 = (bf16[512,256]{1,0:T(8,128)(2,1)S(1)}, bf16[512,256]{1,0:T(8,128)(2,1)}, f32[2,2,1024]{2,1,0:T(2,128)S(1)}) custom-call(s32[4]{0:T(128)S(1)} %pad_add_fusion.1.info, bf16[1024,1536]{1,0:T(8,128)(2,1)S(1)} %get-tuple-element.171.q_ref.k_ref.v_ref, bf16[1024,1536]{1,0:T(8,128)(2,1)S(1)} %get-tuple-element.171.q_ref.k_ref.v_ref, ...), custom_call_target="tpu_custom_call" | custom-call | flops 23000000512 | bytes 65536 | tf_op jit(solution)/shard_map/attend_1/pallas_call | solution.py:291
  106.9 1.7 down_stack.1.refs_0_
  111.8 2.3 input_norm.1
  116.2 10.1 %collective-permute-done.19.refs_3_.refs_4_ = bf16[4,128,1024]{2,1,0:T(8,128)(2,1)} collective-permute-done((bf16[4,128,1024]{2,1,0:T(8,128)(2,1)}, bf16[4,128,1024]{2,1,0:T(8,128)(2,1)}, u32[]{:S(2)}, u32[]{:S(2)}) %collective-permute-start.19) | collective-permute-done | bytes 1048608 | tf_op jit(solution)/shard_map/ppermute | solution.py:329
  128.3 3.3 attention_out.1
  132.2 3.6 %collective-permute-done.22.refs_2_ = bf16[4,256,512]{2,1,0:T(8,128)(2,1)} collective-permute-done((bf16[4,256,512]{2,1,0:T(8,128)(2,1)}, bf16[4,256,512]{2,1,0:T(8,128)(2,1)}, u32[]{:S(2)}, u32[]{:S(2)}) %collective-permute-start.22) | collective-permute-done | bytes 1048608 | tf_op jit(solution)/shard_map/ppermute | solution.py:337
  138.2 10.6 %collective-permute-done.21.refs_1_ = bf16[4,256,512]{2,1,0:T(8,128)(2,1)} collective-permute-done((bf16[4,256,512]{2,1,0:T(8,128)(2,1)}, bf16[4,256,512]{2,1,0:T(8,128)(2,1)}, u32[]{:S(2)}, u32[]{:S(2)}) %collective-permute-start.21) | collective-permute-done | bytes 1048608 | tf_op jit(solution)/shard_map/ppermute | solution.py:329
  152.9 9.4 %up.1 = (bf16[1024,2048]{1,0:T(8,128)(2,1)S(1)}, bf16[1024,2048]{1,0:T(8,128)(2,1)S(1)}) custom-call(s32[4]{0:T(128)S(1)} %pad_add_fusion.1.info, bf16[512,1024]{1,0:T(8,128)(2,1)S(1)} %get-tuple-element.189.x0_ref.n0_ref, bf16[512,1024]{1,0:T(8,128)(2,1)S(1)} %collective-permute-done.20.x1_ref.n1_ref, bf16[4,128,1024]{2,1,0:T(8,128)(2,1)S(1)} %copy-done.10, ...), custom_call_target="tpu_custom_call" | custom-call | flops 575000000 | bytes 65536 | tf_op jit(solution)/shard_map/up/pallas_call | solution.py:291
  162.3 13.9 %down.1 = (f32[512,1024]{1,0:T(8,128)S(1)}, bf16[512,1024]{1,0:T(8,128)(2,1)S(1)}, bf16[1024,2048]{1,0:T(8,128)(2,1)S(1)}) custom-call(s32[4]{0:T(128)S(1)} %pad_add_fusion.1.info, bf16[1024,2048]{1,0:T(8,128)(2,1)S(1)} %get-tuple-element.206.act_ref, bf16[1024,2048]{1,0:T(8,128)(2,1)S(1)} %get-tuple-element.195.slope_ref, bf16[512,1024]{1,0:T(8,128)(2,1)S(1)} %bitcast.21, ...), custom_call_target="tpu_custom_call" | custom-call | flops 575000000 | bytes 65536 | tf_op jit(solution)/shard_map/down/pallas_call | solution.py:291
  176.2 7.1 %normed_back.1 = (f32[512,1024]{1,0:T(8,128)S(1)}, bf16[512,1024]{1,0:T(8,128)(2,1)S(1)}) custom-call(s32[4]{0:T(128)S(1)} %pad_add_fusion.1.info, bf16[1024,2048]{1,0:T(8,128)(2,1)S(1)} %get-tuple-element.212.gp_ref, bf16[4,128,1024]{2,1,0:T(8,128)(2,1)S(1)} %copy-done.10, bf16[4,128,1024]{2,1,0:T(8,128)(2,1)S(1)} %copy-done.12, ...), custom_call_target="tpu_custom_call" | custom-call | flops 575000000 | bytes 65536 | tf_op jit(solution)/shard_map/normed_back/pallas_call | solution.py:291
  183.4 7.8 %down_grad.1 = (bf16[2,512,256]{2,1,0:T(8,128)(2,1)S(1)}, bf16[2,512,256]{2,1,0:T(8,128)(2,1)S(1)}, bf16[4,512,256]{2,1,0:T(8,128)(2,1)S(1)}, bf16[4,512,256]{2,1,0:T(8,128)(2,1)S(1)}, bf16[4,512,256]{2,1,0:T(8,128)(2,1)S(1)}) custom-call(s32[4]{0:T(128)S(1)} %pad_add_fusion.1.info, bf16[512,1024]{1,0:T(8,128)(2,1)S(1)} %bitcast.22, ...), custom_call_target="tpu_custom_call" | custom-call | flops 575000000 | bytes 65536 | tf_op jit(solution)/shard_map/down_grad/pallas_call | solution.py:291
  192.8 3.0 middle_back.1
  195.9 7.5 %up_grad.1 = (bf16[4,128,1024]{2,1,0:T(8,128)(2,1)S(1)}, bf16[4,128,1024]{2,1,0:T(8,128)(2,1)S(1)}, bf16[4,128,1024]{2,1,0:T(8,128)(2,1)S(1)}, bf16[4,128,1024]{2,1,0:T(8,128)(2,1)S(1)}) custom-call(s32[4]{0:T(128)S(1)} %pad_add_fusion.1.info, bf16[512,1024]{1,0:T(8,128)(2,1)S(1)} %get-tuple-element.189.x0_ref.n0_ref, bf16[512,1024]{1,0:T(8,128)(2,1)S(1)} %copy-done.14, ...), custom_call_target="tpu_custom_call" | custom-call | flops 575000000 | bytes 65536 | tf_op jit(solution)/shard_map/up_grad/pallas_call | solution.py:291
  203.4 2.2 collective-permute-done.32.second_ref
  209.8 1.8 out_grad.1
  211.6 9.7 %collective-permute-done.35.send_ref = bf16[512,512]{1,0:T(8,128)(2,1)S(1)} collective-permute-done((bf16[512,512]{1,0:T(8,128)(2,1)S(1)}, bf16[512,512]{1,0:T(8,128)(2,1)S(1)}, u32[]{:S(2)}, u32[]{:S(2)}) %collective-permute-start.35) | collective-permute-done | bytes 524320 | tf_op jit(solution)/shard_map/ppermute | solution.py:337
  222.8 11.7 %attend_back_0.1.r0_ref.d0_ref = bf16[1024,768]{1,0:T(8,128)(2,1)S(1)} custom-call(s32[4]{0:T(128)S(1)} %pad_add_fusion.1.info, bf16[1024,1536]{1,0:T(8,128)(2,1)S(1)} %get-tuple-element.171.q_ref.k_ref.v_ref, bf16[1024,1536]{1,0:T(8,128)(2,1)S(1)} %get-tuple-element.171.q_ref.k_ref.v_ref, bf16[1024,1536]{1,0:T(8,128)(2,1)S(1)} %get-tuple-element.171.q_ref.k_ref.v_ref, ...), custom_call_target="tpu_custom_call" | custom-call | flops 23000000512 | bytes 65536 | tf_op jit(solution)/shard_map/attend_back_0/pallas_call | solution.py:537
  235.4 8.3 %collective-permute-done.38.c_ref = bf16[4,512,256]{2,1,0:T(8,128)(2,1)S(1)} collective-permute-done((bf16[4,512,256]{2,1,0:T(8,128)(2,1)S(1)}, bf16[4,512,256]{2,1,0:T(8,128)(2,1)S(1)}, u32[]{:S(2)}, u32[]{:S(2)}) %collective-permute-start.38) | collective-permute-done | bytes 1048608 | tf_op jit(solution)/shard_map/ppermute | solution.py:337
  244.6 2.5 collective-permute-start.41
  248.7 4.6 %collective-permute-done.36.refs_1_ = bf16[8,64,512]{2,1,0:T(8,128)(2,1)S(1)} collective-permute-done((bf16[8,64,512]{2,1,0:T(8,128)(2,1)S(1)}, bf16[8,64,512]{2,1,0:T(8,128)(2,1)S(1)}, u32[]{:S(2)}, u32[]{:S(2)}) %collective-permute-start.36) | collective-permute-done | bytes 524320 | tf_op jit(solution)/shard_map/ppermute | solution.py:337
  253.3 1.7 collective-permute-start.43
  256.2 2.5 qkv_grad.2
  261.0 11.5 %attend_back_1.1.r0_ref.d1_ref = bf16[1024,768]{1,0:T(8,128)(2,1)S(1)} custom-call(s32[4]{0:T(128)S(1)} %pad_add_fusion.1.info, bf16[1024,1536]{1,0:T(8,128)(2,1)S(1)} %get-tuple-element.171.q_ref.k_ref.v_ref, bf16[1024,1536]{1,0:T(8,128)(2,1)S(1)} %get-tuple-element.171.q_ref.k_ref.v_ref, bf16[1024,1536]{1,0:T(8,128)(2,1)S(1)} %get-tuple-element.171.q_ref.k_ref.v_ref, ...), custom_call_target="tpu_custom_call" | custom-call | flops 575000000 | bytes 65536 | tf_op jit(solution)/shard_map/attend_back_1/pallas_call | solution.py:537
  275.6 6.1 %collective-permute-done.30.b_ref = bf16[4,128,1024]{2,1,0:T(8,128)(2,1)S(1)} collective-permute-done((bf16[4,128,1024]{2,1,0:T(8,128)(2,1)S(1)}, bf16[4,128,1024]{2,1,0:T(8,128)(2,1)S(1)}, u32[]{:S(2)}, u32[]{:S(2)}) %collective-permute-start.30) | collective-permute-done | bytes 1048608 | tf_op jit(solution)/shard_map/ppermute | solution.py:329
  284.2 2.3 qkv_grad.3
  292.0 4.8 %input_back.1 = (f32[512,1024]{1,0:T(8,128)S(1)}, bf16[512,1024]{1,0:T(8,128)(2,1)S(1)}) custom-call(s32[4]{0:T(128)S(1)} %pad_add_fusion.1.info, bf16[1024,768]{1,0:T(8,128)(2,1)S(1)} %attend_back_0.1.r0_ref.d0_ref, bf16[1024,768]{1,0:T(8,128)(2,1)S(1)} %attend_back_1.1.r0_ref.d1_ref, bf16[4,64,1664]{2,1,0:T(8,128)(2,1)S(1)} %copy-done.17, ...), custom_call_target="tpu_custom_call" | custom-call | flops 575000000 | bytes 65536 | tf_op jit(solution)/shard_map/input_back/pallas_call | solution.py:291
  296.9 4.5 %collective-permute-done.46.bx_ref = bf16[4,64,768]{2,1,0:T(8,128)(2,1)S(1)} collective-permute-done((bf16[4,64,768]{2,1,0:T(8,128)(2,1)S(1)}, bf16[4,64,768]{2,1,0:T(8,128)(2,1)S(1)}, u32[]{:S(2)}, u32[]{:S(2)}) %collective-permute-start.46) | collective-permute-done | bytes 393248 | tf_op jit(solution)/shard_map/ppermute | solution.py:329
  303.2 2.7 collective-permute-done.47.refs_1_
  305.9 2.5 collective-permute-start.51
  308.3 11.6 %collective-permute-done.48.refs_2_ = bf16[128,1024]{1,0:T(8,128)(2,1)S(1)} collective-permute-done((bf16[128,1024]{1,0:T(8,128)(2,1)S(1)}, bf16[128,1024]{1,0:T(8,128)(2,1)S(1)}, u32[]{:S(2)}, u32[]{:S(2)}) %collective-permute-start.48) | collective-permute-done | bytes 262176 | tf_op jit(solution)/shard_map/ppermute | solution.py:325
  319.9 3.4 collective-permute-start.52
  324.1 1.6 mixed.1
  325.7 3.1 input_grad.1
  328.8 2.0 collective-permute-done.52.refs_2_
  330.8 2.2 collective-permute-done.53.refs_3_
  337.8 2.0 collective-permute-done.54.got_ref
  (221 shorter events, 77.7 us)
Async XLA Ops:
  7.2 109.0 %all-gather.2.cloned.1.call-start = ((), (), s32[]{:S(2)}) async-start(), calls=%async_computation | async-start | bytes 2162688 | tf_op jit(solution)/shard_map/all_gather | solution.py:1317
  10.4 25.9 %collective-permute-start.4 = (bf16[512,1024]{1,0:T(8,128)(2,1)}, bf16[512,1024]{1,0:T(8,128)(2,1)S(1)}, u32[]{:S(2)}, u32[]{:S(2)}) collective-permute-start(bf16[512,1024]{1,0:T(8,128)(2,1)} %bitcast.24), channel_id=1, source_target_pairs={{0,1},{1,0},{2,3},{3,2},{4,5},{5,4},{6,7},{7,6},{8,9},{9,8},{10,11... | collective-permute-start | bytes 3145736 | tf_op jit(solution)/shard_map/ppermute | solution.py:337
  15.9 16.9 %collective-permute-start.3 = (bf16[64,1664]{1,0:T(8,128)(2,1)S(1)}, bf16[64,1664]{1,0:T(8,128)(2,1)S(1)}, u32[]{:S(2)}, u32[]{:S(2)}) collective-permute-start(bf16[64,1664]{1,0:T(8,128)(2,1)S(1)} %heads.1.refs_0_.a_ref), channel_id=1, source_target_pairs={{0,24},{2,26},{4,28},{6,30},{8,0},{10,2},{12,4},{14,6},{16,8},{18,... | collective-permute-start | bytes 638984 | tf_op jit(solution)/shard_map/ppermute | solution.py:325
  16.0 16.8 %collective-permute-start.2 = (bf16[64,1664]{1,0:T(8,128)(2,1)S(1)}, bf16[64,1664]{1,0:T(8,128)(2,1)S(1)}, u32[]{:S(2)}, u32[]{:S(2)}) collective-permute-start(bf16[64,1664]{1,0:T(8,128)(2,1)S(1)} %heads.1.refs_0_.a_ref), channel_id=1, source_target_pairs={{0,16},{2,18},{4,20},{6,22},{8,24},{10,26},{12,28},{14,30},{16,0},... | collective-permute-start | bytes 638984 | tf_op jit(solution)/shard_map/ppermute | solution.py:325
  19.0 17.4 %collective-permute-start.1 = (bf16[64,1664]{1,0:T(8,128)(2,1)S(1)}, bf16[64,1664]{1,0:T(8,128)(2,1)S(1)}, u32[]{:S(2)}, u32[]{:S(2)}) collective-permute-start(bf16[64,1664]{1,0:T(8,128)(2,1)S(1)} %heads.1.refs_0_.a_ref), channel_id=1, source_target_pairs={{0,8},{2,10},{4,12},{6,14},{8,16},{10,18},{12,20},{14,22},{16,24},... | collective-permute-start | bytes 638984 | tf_op jit(solution)/shard_map/ppermute | solution.py:325
  38.0 27.4 %collective-permute-start.6 = (bf16[4,64,1664]{2,1,0:T(8,128)(2,1)S(1)}, bf16[4,64,1664]{2,1,0:T(8,128)(2,1)S(1)}, u32[]{:S(2)}, u32[]{:S(2)}) collective-permute-start(bf16[4,64,1664]{2,1,0:T(8,128)(2,1)S(1)} %qkv_stack.1.refs_0_), channel_id=1, source_target_pairs={{0,4},{2,6},{4,0},{6,2},{8,12},{10,14},{12,8},{14,10},{16,20},{18,... | collective-permute-start | bytes 2555912 | tf_op jit(solution)/shard_map/ppermute | solution.py:329
  39.5 21.8 %collective-permute-start.10 = (bf16[128,1024]{1,0:T(8,128)(2,1)S(1)}, bf16[128,1024]{1,0:T(8,128)(2,1)S(1)}, u32[]{:S(2)}, u32[]{:S(2)}) collective-permute-start(bf16[128,1024]{1,0:T(8,128)(2,1)S(1)} %both_rows.1.refs_0_), channel_id=1, source_target_pairs={{0,24},{2,26},{4,28},{6,30},{8,0},{10,2},{12,4},{14,6},{16,8},{18,... | collective-permute-start | bytes 786440 | tf_op jit(solution)/shard_map/ppermute | solution.py:325
  40.7 20.7 %collective-permute-start.9 = (bf16[128,1024]{1,0:T(8,128)(2,1)S(1)}, bf16[128,1024]{1,0:T(8,128)(2,1)S(1)}, u32[]{:S(2)}, u32[]{:S(2)}) collective-permute-start(bf16[128,1024]{1,0:T(8,128)(2,1)S(1)} %both_rows.1.refs_0_), channel_id=1, source_target_pairs={{0,16},{2,18},{4,20},{6,22},{8,24},{10,26},{12,28},{14,30},{16,0},... | collective-permute-start | bytes 786440 | tf_op jit(solution)/shard_map/ppermute | solution.py:325
  43.5 21.9 %collective-permute-start.8 = (bf16[128,1024]{1,0:T(8,128)(2,1)S(1)}, bf16[128,1024]{1,0:T(8,128)(2,1)S(1)}, u32[]{:S(2)}, u32[]{:S(2)}) collective-permute-start(bf16[128,1024]{1,0:T(8,128)(2,1)S(1)} %both_rows.1.refs_0_), channel_id=1, source_target_pairs={{0,8},{2,10},{4,12},{6,14},{8,16},{10,18},{12,20},{14,22},{16,24},... | collective-permute-start | bytes 786440 | tf_op jit(solution)/shard_map/ppermute | solution.py:325
  44.5 21.7 %collective-permute-start.7 = (bf16[4,64,1664]{2,1,0:T(8,128)(2,1)S(1)}, bf16[4,64,1664]{2,1,0:T(8,128)(2,1)S(1)}, u32[]{:S(2)}, u32[]{:S(2)}) collective-permute-start(bf16[4,64,1664]{2,1,0:T(8,128)(2,1)S(1)} %qkv_stack.1.refs_0_), channel_id=1, source_target_pairs={{0,2},{2,0},{4,6},{6,4},{8,10},{10,8},{12,14},{14,12},{16,18},{18,... | collective-permute-start | bytes 2555912 | tf_op jit(solution)/shard_map/ppermute | solution.py:333
  68.4 26.3 %collective-permute-start.18 = (bf16[4,128,1024]{2,1,0:T(8,128)(2,1)S(1)}, bf16[4,128,1024]{2,1,0:T(8,128)(2,1)}, u32[]{:S(2)}, u32[]{:S(2)}) collective-permute-start(bf16[4,128,1024]{2,1,0:T(8,128)(2,1)S(1)} %up_stack.1.refs_0_), channel_id=1, source_target_pairs={{0,1},{1,0},{2,3},{3,2},{4,5},{5,4},{6,7},{7,6},{8,9},{9,8},{10,11... | collective-permute-start | bytes 3145736 | tf_op jit(solution)/shard_map/ppermute | solution.py:337
  69.4 26.8 %collective-permute-start.17 = (bf16[4,128,1024]{2,1,0:T(8,128)(2,1)S(1)}, bf16[4,128,1024]{2,1,0:T(8,128)(2,1)S(1)}, u32[]{:S(2)}, u32[]{:S(2)}) collective-permute-start(bf16[4,128,1024]{2,1,0:T(8,128)(2,1)S(1)} %up_stack.1.refs_0_), channel_id=1, source_target_pairs={{0,4},{2,6},{4,0},{6,2},{8,12},{10,14},{12,8},{14,10},{16,20},{18,... | collective-permute-start | bytes 3145736 | tf_op jit(solution)/shard_map/ppermute | solution.py:329
  78.3 27.5 %collective-permute-start.16 = (bf16[256,512]{1,0:T(8,128)(2,1)S(1)}, bf16[256,512]{1,0:T(8,128)(2,1)S(1)}, u32[]{:S(2)}, u32[]{:S(2)}) collective-permute-start(bf16[256,512]{1,0:T(8,128)(2,1)S(1)} %copy-done.40), channel_id=1, source_target_pairs={{0,24},{2,26},{4,28},{6,30},{8,0},{10,2},{12,4},{14,6},{16,8},{18,... | collective-permute-start | bytes 786440 | tf_op jit(solution)/shard_map/ppermute | solution.py:325
  80.6 26.3 %collective-permute-start.15 = (bf16[256,512]{1,0:T(8,128)(2,1)S(1)}, bf16[256,512]{1,0:T(8,128)(2,1)S(1)}, u32[]{:S(2)}, u32[]{:S(2)}) collective-permute-start(bf16[256,512]{1,0:T(8,128)(2,1)S(1)} %copy-done.40), channel_id=1, source_target_pairs={{0,16},{2,18},{4,20},{6,22},{8,24},{10,26},{12,28},{14,30},{16,0},... | collective-permute-start | bytes 786440 | tf_op jit(solution)/shard_map/ppermute | solution.py:325
  82.3 24.6 %collective-permute-start.14 = (bf16[256,512]{1,0:T(8,128)(2,1)S(1)}, bf16[256,512]{1,0:T(8,128)(2,1)S(1)}, u32[]{:S(2)}, u32[]{:S(2)}) collective-permute-start(bf16[256,512]{1,0:T(8,128)(2,1)S(1)} %copy-done.40), channel_id=1, source_target_pairs={{0,8},{2,10},{4,12},{6,14},{8,16},{10,18},{12,20},{14,22},{16,24},... | collective-permute-start | bytes 786440 | tf_op jit(solution)/shard_map/ppermute | solution.py:325
  94.7 15.4 %collective-permute-start.12 = (bf16[512,256]{1,0:T(8,128)(2,1)S(1)}, bf16[512,256]{1,0:T(8,128)(2,1)S(1)}, u32[]{:S(2)}, u32[]{:S(2)}) collective-permute-start(bf16[512,256]{1,0:T(8,128)(2,1)S(1)} %get-tuple-element.176), channel_id=1, source_target_pairs={{0,1},{1,0},{2,3},{3,2},{4,5},{5,4},{6,7},{7,6},{8,9},{9,8},{10,11... | collective-permute-start | bytes 786440 | tf_op jit(solution)/shard_map/ppermute | solution.py:337
  96.2 30.1 %collective-permute-start.19 = (bf16[4,128,1024]{2,1,0:T(8,128)(2,1)}, bf16[4,128,1024]{2,1,0:T(8,128)(2,1)}, u32[]{:S(2)}, u32[]{:S(2)}) collective-permute-start(bf16[4,128,1024]{2,1,0:T(8,128)(2,1)} %collective-permute-done.18.refs_2_), channel_id=1, source_target_pairs={{0,4},{2,6},{4,0},{6,2},{8,12},{10,14},{12,8},{14,10},{16,20},{18,... | collective-permute-start | bytes 3145736 | tf_op jit(solution)/shard_map/ppermute | solution.py:329
  105.8 21.1 %collective-permute-start.13 = (bf16[512,256]{1,0:T(8,128)(2,1)}, bf16[512,256]{1,0:T(8,128)(2,1)}, u32[]{:S(2)}, u32[]{:S(2)}) collective-permute-start(bf16[512,256]{1,0:T(8,128)(2,1)} %get-tuple-element.177), channel_id=1, source_target_pairs={{0,1},{1,0},{2,3},{3,2},{4,5},{5,4},{6,7},{7,6},{8,9},{9,8},{10,11... | collective-permute-start | bytes 786440 | tf_op jit(solution)/shard_map/ppermute | solution.py:337
  108.6 40.2 %collective-permute-start.21 = (bf16[4,256,512]{2,1,0:T(8,128)(2,1)}, bf16[4,256,512]{2,1,0:T(8,128)(2,1)}, u32[]{:S(2)}, u32[]{:S(2)}) collective-permute-start(bf16[4,256,512]{2,1,0:T(8,128)(2,1)} %down_stack.1.refs_0_), channel_id=1, source_target_pairs={{0,4},{2,6},{4,0},{6,2},{8,12},{10,14},{12,8},{14,10},{16,20},{18,... | collective-permute-start | bytes 3145736 | tf_op jit(solution)/shard_map/ppermute | solution.py:329
  110.8 24.9 %collective-permute-start.22 = (bf16[4,256,512]{2,1,0:T(8,128)(2,1)}, bf16[4,256,512]{2,1,0:T(8,128)(2,1)}, u32[]{:S(2)}, u32[]{:S(2)}) collective-permute-start(bf16[4,256,512]{2,1,0:T(8,128)(2,1)} %down_stack.1.refs_0_), channel_id=1, source_target_pairs={{0,1},{1,0},{2,3},{3,2},{4,5},{5,4},{6,7},{7,6},{8,9},{9,8},{10,11... | collective-permute-start | bytes 3145736 | tf_op jit(solution)/shard_map/ppermute | solution.py:337
  131.6 19.4 %collective-permute-start.20 = (bf16[512,1024]{1,0:T(8,128)(2,1)S(1)}, bf16[512,1024]{1,0:T(8,128)(2,1)S(1)}, u32[]{:S(2)}, u32[]{:S(2)}) collective-permute-start(bf16[512,1024]{1,0:T(8,128)(2,1)S(1)} %get-tuple-element.189.x0_ref.n0_ref), channel_id=1, source_target_pairs={{0,2},{2,0},{4,6},{6,4},{8,10},{10,8},{12,14},{14,12},{16,18},{18,... | collective-permute-start | bytes 3145736 | tf_op jit(solution)/shard_map/ppermute | solution.py:333
  131.7 30.6 %collective-permute-start.23 = (bf16[512,1024]{1,0:T(8,128)(2,1)S(1)}, bf16[512,1024]{1,0:T(8,128)(2,1)S(1)}, u32[]{:S(2)}, u32[]{:S(2)}) collective-permute-start(bf16[512,1024]{1,0:T(8,128)(2,1)S(1)} %bitcast.20), channel_id=1, source_target_pairs={{0,2},{2,0},{4,6},{6,4},{8,10},{10,8},{12,14},{14,12},{16,18},{18,... | collective-permute-start | bytes 3145736 | tf_op jit(solution)/shard_map/ppermute | solution.py:333
  136.8 25.4 %collective-permute-start.25 = (bf16[2,256,512]{2,1,0:T(8,128)(2,1)S(1)}, bf16[2,256,512]{2,1,0:T(8,128)(2,1)S(1)}, u32[]{:S(2)}, u32[]{:S(2)}) collective-permute-start(bf16[2,256,512]{2,1,0:T(8,128)(2,1)S(1)} %slice.44), channel_id=1, source_target_pairs={{0,4},{2,6},{4,0},{6,2},{8,12},{10,14},{12,8},{14,10},{16,20},{18,... | collective-permute-start | bytes 1572872 | tf_op jit(solution)/shard_map/ppermute | solution.py:329
  149.9 12.4 %collective-permute-start.24 = (bf16[2,256,512]{2,1,0:T(8,128)(2,1)S(1)}, bf16[2,256,512]{2,1,0:T(8,128)(2,1)S(1)}, u32[]{:S(2)}, u32[]{:S(2)}) collective-permute-start(bf16[2,256,512]{2,1,0:T(8,128)(2,1)S(1)} %slice.43), channel_id=1, source_target_pairs={{0,1},{1,0},{2,3},{3,2},{4,5},{5,4},{6,7},{7,6},{8,9},{9,8},{10,11... | collective-permute-start | bytes 1572872 | tf_op jit(solution)/shard_map/ppermute | solution.py:337
  150.9 25.3 %collective-permute-start.28 = (bf16[8,64,512]{2,1,0:T(8,128)(2,1)S(1)}, bf16[8,64,512]{2,1,0:T(8,128)(2,1)S(1)}, u32[]{:S(2)}, u32[]{:S(2)}) collective-permute-start(bf16[8,64,512]{2,1,0:T(8,128)(2,1)S(1)} %get-tuple-element.203), channel_id=1, source_target_pairs={{0,2},{2,0},{4,6},{6,4},{8,10},{10,8},{12,14},{14,12},{16,18},{18,... | collective-permute-start | bytes 1572872 | tf_op jit(solution)/shard_map/ppermute | solution.py:333
  151.0 25.3 %collective-permute-start.27 = (bf16[8,64,1024]{2,1,0:T(8,128)(2,1)S(1)}, bf16[8,64,1024]{2,1,0:T(8,128)(2,1)S(1)}, u32[]{:S(2)}, u32[]{:S(2)}) collective-permute-start(bf16[8,64,1024]{2,1,0:T(8,128)(2,1)S(1)} %copy-done.39), channel_id=1, source_target_pairs={{0,2},{2,0},{4,6},{6,4},{8,10},{10,8},{12,14},{14,12},{16,18},{18,... | collective-permute-start | bytes 3145736 | tf_op jit(solution)/shard_map/ppermute | solution.py:333
  191.2 14.4 %collective-permute-start.32 = (bf16[2,512,256]{2,1,0:T(8,128)(2,1)S(1)}, bf16[2,512,256]{2,1,0:T(8,128)(2,1)S(1)}, u32[]{:S(2)}, u32[]{:S(2)}) collective-permute-start(bf16[2,512,256]{2,1,0:T(8,128)(2,1)S(1)} %get-tuple-element.221), channel_id=1, source_target_pairs={{0,1},{1,0},{2,3},{3,2},{4,5},{5,4},{6,7},{7,6},{8,9},{9,8},{10,11... | collective-permute-start | bytes 1572872 | tf_op jit(solution)/shard_map/ppermute | solution.py:337
  192.3 14.0 %collective-permute-start.31 = (bf16[2,512,256]{2,1,0:T(8,128)(2,1)S(1)}, bf16[2,512,256]{2,1,0:T(8,128)(2,1)S(1)}, u32[]{:S(2)}, u32[]{:S(2)}) collective-permute-start(bf16[2,512,256]{2,1,0:T(8,128)(2,1)S(1)} %get-tuple-element.207), channel_id=1, source_target_pairs={{0,4},{2,6},{4,0},{6,2},{8,12},{10,14},{12,8},{14,10},{16,20},{18,... | collective-permute-start | bytes 1572872 | tf_op jit(solution)/shard_map/ppermute | solution.py:329
  195.8 13.9 %collective-permute-start.33 = (bf16[512,1024]{1,0:T(8,128)(2,1)S(1)}, bf16[512,1024]{1,0:T(8,128)(2,1)S(1)}, u32[]{:S(2)}, u32[]{:S(2)}) collective-permute-start(bf16[512,1024]{1,0:T(8,128)(2,1)S(1)} %get-tuple-element.225.r0_ref), channel_id=1, source_target_pairs={{0,2},{2,0},{4,6},{6,4},{8,10},{10,8},{12,14},{14,12},{16,18},{18,... | collective-permute-start | bytes 3145736 | tf_op jit(solution)/shard_map/ppermute | solution.py:333
  206.4 14.9 %collective-permute-start.35 = (bf16[512,512]{1,0:T(8,128)(2,1)S(1)}, bf16[512,512]{1,0:T(8,128)(2,1)S(1)}, u32[]{:S(2)}, u32[]{:S(2)}) collective-permute-start(bf16[512,512]{1,0:T(8,128)(2,1)S(1)} %get-tuple-element.234), channel_id=1, source_target_pairs={{0,1},{1,0},{2,3},{3,2},{4,5},{5,4},{6,7},{7,6},{8,9},{9,8},{10,11... | collective-permute-start | bytes 1572872 | tf_op jit(solution)/shard_map/ppermute | solution.py:337
  208.2 35.5 %collective-permute-start.38 = (bf16[4,512,256]{2,1,0:T(8,128)(2,1)S(1)}, bf16[4,512,256]{2,1,0:T(8,128)(2,1)S(1)}, u32[]{:S(2)}, u32[]{:S(2)}) collective-permute-start(bf16[4,512,256]{2,1,0:T(8,128)(2,1)S(1)} %get-tuple-element.224), channel_id=1, source_target_pairs={{0,1},{1,0},{2,3},{3,2},{4,5},{5,4},{6,7},{7,6},{8,9},{9,8},{10,11... | collective-permute-start | bytes 3145736 | tf_op jit(solution)/shard_map/ppermute | solution.py:337
  209.3 26.1 %collective-permute-start.37 = (bf16[4,512,256]{2,1,0:T(8,128)(2,1)S(1)}, bf16[4,512,256]{2,1,0:T(8,128)(2,1)S(1)}, u32[]{:S(2)}, u32[]{:S(2)}) collective-permute-start(bf16[4,512,256]{2,1,0:T(8,128)(2,1)S(1)} %get-tuple-element.238), channel_id=1, source_target_pairs={{0,4},{2,6},{4,0},{6,2},{8,12},{10,14},{12,8},{14,10},{16,20},{18,... | collective-permute-start | bytes 3145736 | tf_op jit(solution)/shard_map/ppermute | solution.py:329
  221.2 32.1 %collective-permute-start.36 = (bf16[8,64,512]{2,1,0:T(8,128)(2,1)S(1)}, bf16[8,64,512]{2,1,0:T(8,128)(2,1)S(1)}, u32[]{:S(2)}, u32[]{:S(2)}) collective-permute-start(bf16[8,64,512]{2,1,0:T(8,128)(2,1)S(1)} %get-tuple-element.236), channel_id=1, source_target_pairs={{0,1},{1,0},{2,3},{3,2},{4,5},{5,4},{6,7},{7,6},{8,9},{9,8},{10,11... | collective-permute-start | bytes 1572872 | tf_op jit(solution)/shard_map/ppermute | solution.py:337
  222.2 36.5 %collective-permute-start.34 = (bf16[4,128,1024]{2,1,0:T(8,128)(2,1)S(1)}, bf16[4,128,1024]{2,1,0:T(8,128)(2,1)S(1)}, u32[]{:S(2)}, u32[]{:S(2)}) collective-permute-start(bf16[4,128,1024]{2,1,0:T(8,128)(2,1)S(1)} %get-tuple-element.229), channel_id=1, source_target_pairs={{0,4},{2,6},{4,0},{6,2},{8,12},{10,14},{12,8},{14,10},{16,20},{18,... | collective-permute-start | bytes 3145736 | tf_op jit(solution)/shard_map/ppermute | solution.py:329
  234.5 21.1 %collective-permute-start.39 = (bf16[1024,768]{1,0:T(8,128)(2,1)S(1)}, bf16[1024,768]{1,0:T(8,128)(2,1)S(1)}, u32[]{:S(2)}, u32[]{:S(2)}) collective-permute-start(bf16[1024,768]{1,0:T(8,128)(2,1)S(1)} %attend_back_0.1.r0_ref.d0_ref), channel_id=1, source_target_pairs={{0,2},{2,0},{4,6},{6,4},{8,10},{10,8},{12,14},{14,12},{16,18},{18,... | collective-permute-start | bytes 4718600 | tf_op jit(solution)/shard_map/ppermute | solution.py:333
  244.6 27.9 %collective-permute-start.41 = (bf16[512,256]{1,0:T(8,128)(2,1)S(1)}, bf16[512,256]{1,0:T(8,128)(2,1)S(1)}, u32[]{:S(2)}, u32[]{:S(2)}) collective-permute-start(bf16[512,256]{1,0:T(8,128)(2,1)S(1)} %get-tuple-element.242), channel_id=1, source_target_pairs={{0,8},{2,10},{4,12},{6,14},{8,16},{10,18},{12,20},{14,22},{16,24},... | collective-permute-start | bytes 786440 | tf_op jit(solution)/shard_map/ppermute | solution.py:325
  247.1 25.4 %collective-permute-start.42 = (bf16[512,256]{1,0:T(8,128)(2,1)S(1)}, bf16[512,256]{1,0:T(8,128)(2,1)S(1)}, u32[]{:S(2)}, u32[]{:S(2)}) collective-permute-start(bf16[512,256]{1,0:T(8,128)(2,1)S(1)} %get-tuple-element.243), channel_id=1, source_target_pairs={{0,16},{2,18},{4,20},{6,22},{8,24},{10,26},{12,28},{14,30},{16,0},... | collective-permute-start | bytes 786440 | tf_op jit(solution)/shard_map/ppermute | solution.py:325
  253.3 19.3 %collective-permute-start.43 = (bf16[512,256]{1,0:T(8,128)(2,1)S(1)}, bf16[512,256]{1,0:T(8,128)(2,1)S(1)}, u32[]{:S(2)}, u32[]{:S(2)}) collective-permute-start(bf16[512,256]{1,0:T(8,128)(2,1)S(1)} %get-tuple-element.244), channel_id=1, source_target_pairs={{0,24},{2,26},{4,28},{6,30},{8,0},{10,2},{12,4},{14,6},{16,8},{18,... | collective-permute-start | bytes 786440 | tf_op jit(solution)/shard_map/ppermute | solution.py:325
  255.5 26.2 %collective-permute-start.30 = (bf16[4,128,1024]{2,1,0:T(8,128)(2,1)S(1)}, bf16[4,128,1024]{2,1,0:T(8,128)(2,1)S(1)}, u32[]{:S(2)}, u32[]{:S(2)}) collective-permute-start(bf16[4,128,1024]{2,1,0:T(8,128)(2,1)S(1)} %get-tuple-element.214), channel_id=1, source_target_pairs={{0,4},{2,6},{4,0},{6,2},{8,12},{10,14},{12,8},{14,10},{16,20},{18,... | collective-permute-start | bytes 3145736 | tf_op jit(solution)/shard_map/ppermute | solution.py:329
  259.9 23.3 %collective-permute-start.40 = (bf16[4,128,1024]{2,1,0:T(8,128)(2,1)S(1)}, bf16[4,128,1024]{2,1,0:T(8,128)(2,1)S(1)}, u32[]{:S(2)}, u32[]{:S(2)}) collective-permute-start(bf16[4,128,1024]{2,1,0:T(8,128)(2,1)S(1)} %added.1), channel_id=1, source_target_pairs={{0,1},{1,0},{2,3},{3,2},{4,5},{5,4},{6,7},{7,6},{8,9},{9,8},{10,11... | collective-permute-start | bytes 3145736 | tf_op jit(solution)/shard_map/ppermute | solution.py:337
  272.6 24.1 %collective-permute-start.44 = (bf16[4,64,1280]{2,1,0:T(8,128)(2,1)S(1)}, bf16[4,64,1280]{2,1,0:T(8,128)(2,1)S(1)}, u32[]{:S(2)}, u32[]{:S(2)}) collective-permute-start(bf16[4,64,1280]{2,1,0:T(8,128)(2,1)S(1)} %get-tuple-element.260), channel_id=1, source_target_pairs={{0,4},{2,6},{4,0},{6,2},{8,12},{10,14},{12,8},{14,10},{16,20},{18,... | collective-permute-start | bytes 1966088 | tf_op jit(solution)/shard_map/ppermute | solution.py:329
  286.5 14.8 %collective-permute-start.46 = (bf16[4,64,768]{2,1,0:T(8,128)(2,1)S(1)}, bf16[4,64,768]{2,1,0:T(8,128)(2,1)S(1)}, u32[]{:S(2)}, u32[]{:S(2)}) collective-permute-start(bf16[4,64,768]{2,1,0:T(8,128)(2,1)S(1)} %get-tuple-element.266), channel_id=1, source_target_pairs={{0,4},{2,6},{4,0},{6,2},{8,12},{10,14},{12,8},{14,10},{16,20},{18,... | collective-permute-start | bytes 1179656 | tf_op jit(solution)/shard_map/ppermute | solution.py:329
  287.7 18.1 %collective-permute-start.47 = (bf16[128,1024]{1,0:T(8,128)(2,1)S(1)}, bf16[128,1024]{1,0:T(8,128)(2,1)S(1)}, u32[]{:S(2)}, u32[]{:S(2)}) collective-permute-start(bf16[128,1024]{1,0:T(8,128)(2,1)S(1)} %get-tuple-element.261), channel_id=1, source_target_pairs={{0,8},{2,10},{4,12},{6,14},{8,16},{10,18},{12,20},{14,22},{16,24},... | collective-permute-start | bytes 786440 | tf_op jit(solution)/shard_map/ppermute | solution.py:325
  288.8 31.1 %collective-permute-start.48 = (bf16[128,1024]{1,0:T(8,128)(2,1)S(1)}, bf16[128,1024]{1,0:T(8,128)(2,1)S(1)}, u32[]{:S(2)}, u32[]{:S(2)}) collective-permute-start(bf16[128,1024]{1,0:T(8,128)(2,1)S(1)} %get-tuple-element.262), channel_id=1, source_target_pairs={{0,16},{2,18},{4,20},{6,22},{8,24},{10,26},{12,28},{14,30},{16,0},... | collective-permute-start | bytes 786440 | tf_op jit(solution)/shard_map/ppermute | solution.py:325
  290.4 32.9 %collective-permute-start.49 = (bf16[128,1024]{1,0:T(8,128)(2,1)S(1)}, bf16[128,1024]{1,0:T(8,128)(2,1)S(1)}, u32[]{:S(2)}, u32[]{:S(2)}) collective-permute-start(bf16[128,1024]{1,0:T(8,128)(2,1)S(1)} %get-tuple-element.263), channel_id=1, source_target_pairs={{0,24},{2,26},{4,28},{6,30},{8,0},{10,2},{12,4},{14,6},{16,8},{18,... | collective-permute-start | bytes 786440 | tf_op jit(solution)/shard_map/ppermute | solution.py:325
  296.8 27.2 %collective-permute-start.26 = (bf16[512,1024]{1,0:T(8,128)(2,1)S(1)}, bf16[512,1024]{1,0:T(8,128)(2,1)S(1)}, u32[]{:S(2)}, u32[]{:S(2)}) collective-permute-start(bf16[512,1024]{1,0:T(8,128)(2,1)S(1)} %copy-done.37), channel_id=1, source_target_pairs={{0,2},{2,0},{4,6},{6,4},{8,10},{10,8},{12,14},{14,12},{16,18},{18,... | collective-permute-start | bytes 3145736 | tf_op jit(solution)/shard_map/ppermute | solution.py:333
  301.4 24.3 %collective-permute-start.50 = (bf16[512,1024]{1,0:T(8,128)(2,1)S(1)}, bf16[512,1024]{1,0:T(8,128)(2,1)S(1)}, u32[]{:S(2)}, u32[]{:S(2)}) collective-permute-start(bf16[512,1024]{1,0:T(8,128)(2,1)S(1)} %get-tuple-element.280), channel_id=1, source_target_pairs={{0,1},{1,0},{2,3},{3,2},{4,5},{5,4},{6,7},{7,6},{8,9},{9,8},{10,11... | collective-permute-start | bytes 3145736 | tf_op jit(solution)/shard_map/ppermute | solution.py:337
  305.9 22.9 %collective-permute-start.51 = (bf16[64,2048]{1,0:T(8,128)(2,1)S(1)}, bf16[64,2048]{1,0:T(8,128)(2,1)S(1)}, u32[]{:S(2)}, u32[]{:S(2)}) collective-permute-start(bf16[64,2048]{1,0:T(8,128)(2,1)S(1)} %get-tuple-element.273), channel_id=1, source_target_pairs={{0,8},{2,10},{4,12},{6,14},{8,16},{10,18},{12,20},{14,22},{16,24},... | collective-permute-start | bytes 786440 | tf_op jit(solution)/shard_map/ppermute | solution.py:325
  (57 other events, 487.1 us)
Sparse Core Ops, SparseCore 0:
  44.6 71.4 all-gather.1

commit v7 on v6

--- a/solution.py
+++ b/solution.py
@@ -381,7 +381,7 @@
         for dx in range(2):
             for dz in range(LINE):
                 chip = order(lax.rem(info[0] + LINE - dz, LINE), lax.rem(info[1] + dx, 2))
-                ref, at = ((line, dz), (beside, dz), (across, dz), (far_a, dz) if dz < 2 else (far_b, dz + far_b.shape[0] - LINE))[dx + 2 * dy]
+                ref, at = ((line, dz), (beside, dz), (across, dz), (far_a, dz) if dz < far_a.shape[0] else (far_b, dz - far_a.shape[0]))[dx + 2 * dy]
                 out[dy].append(
                     pltpu.make_async_copy(
                         ref.at[at, :, pl.ds(0, cols)],
@@ -1339,7 +1339,7 @@
     keep0, send0, lse0 = attend(info, projected, bias, 0)
     got0 = swap_y(send0)
     up_x, up_y = after((up_x, up_y), keep0)
-    up_far = swap_x(up_y)
+    up_far = [swap_y(up_x[:1]), swap_x(up_y[1:])]
     keep1, send1, lse1 = attend(info, projected, after(bias, keep0), 1)
     got1 = swap_y(send1)
     down_line = stacked(info, after(down_line, keep1), "down_stack")
@@ -1353,7 +1353,7 @@
     nm_sib = swap_c(nm_own)
     nin_t_sib = swap_c(after(nin_t_oth, nm_own))
     att_t_sib = swap_c(att_t_oth)
-    up_pieces = (up_line, up_x, up_y, up_far, up_far)
+    up_pieces = (up_line, up_x, up_y, *up_far)
     down_far = [swap_y(down_x[:2]), swap_x(down_y[2:])]
     gain_all = touch(info, after(gain_all, nm_own, down_x, down_y))
     nm_sib = after(nm_sib, gain_all)

time: 356 us -> 352 us (0.989)
  waiting for transfers between devices: 115 us -> 108 us
    ppermute x11, waiting for transfers between devices: 33.3 us -> 18.6 us  [swap_x(): return lax.ppermute(v, 'rows', row_pairs(lambda z, x, c: (z, 1 - x, c)))]
    ppermute x15 -> x16, waiting for transfers between devices: 36.4 us -> 45.4 us  [swap_y(): return lax.ppermute(v, 'pair', [(0, 1), (1, 0)])]
    ppermute x15 -> x16, starting transfers between devices: 15.7 us -> 17.6 us  [swap_y(): return lax.ppermute(v, 'pair', [(0, 1), (1, 0)])]
    unnamed x96 -> x104, local copies, waits for them, and re-layouts: 12 us -> 12.2 us
  transfers between devices with their start and end apart: 58 -> 59, of which waited for: 26 -> 25; matrix products, arithmetic and copies ran while one was open for 3% -> 4% of each run, Pallas kernels for 36% -> 36%
where the time goes in v7:
time: 352 us; the launch traced here: 345 us
  Pallas kernels  135 us (38%)
  waiting for transfers between devices  108 us (31%)
  starting transfers between devices  57.9 us (16%)
  local copies, waits for them, and re-layouts  18.8 us (5%)
  between operations  17.9 us (5%)
  other arithmetic  7.49 us (2%)
    pallas_call x37, Pallas kernels, call(): pl.pallas_call(kernel, grid_spec=pltpu.PrefetchScalarGridSpec(num_scalar_...  111 us
    ppermute x16, waiting for transfers between devices, swap_y(): return lax.ppermute(v, 'pair', [(0, 1), (1, 0)])  45.4 us
    ppermute x18, waiting for transfers between devices, shift_z(): return lax.ppermute(v, 'rows', row_pairs(lambda z, x, c: (z + k, x, c)))  43 us
    ppermute x18, starting transfers between devices, shift_z(): return lax.ppermute(v, 'rows', row_pairs(lambda z, x, c: (z + k, x, c)))  29.2 us
    pallas_call x2, Pallas kernels, attend_back(): pl.pallas_call(attend_back_kernel, grid_spec=pltpu.PrefetchScalarGridSpec...  23.2 us
    ppermute x11, waiting for transfers between devices, swap_x(): return lax.ppermute(v, 'rows', row_pairs(lambda z, x, c: (z, 1 - x, c)))  18.6 us
    ppermute x16, starting transfers between devices, swap_y(): return lax.ppermute(v, 'pair', [(0, 1), (1, 0)])  17.6 us
    unnamed x104, local copies, waits for them, and re-layouts  12.2 us
  transfers between devices with their start and end apart: 59, of which 25 were waited for; matrix products, arithmetic and copies ran while one was open for 4% of the time, Pallas kernels for 36%

profile of v7, /device:TPU:8, one launch (start us, length us, event | category | flops | bytes accessed | tf_op | source)
XLA Modules:
  0.0 345.2 jit_solution(12878517894392535847)
XLA Ops:
  16.0 3.0 collective-permute-start.2
  19.0 2.5 collective-permute-start.1
  26.6 5.0 %fusion.5 = (f32[1024,1024]{1,0:T(8,128)}, f32[1024,1024]{1,0:T(8,128)}) fusion(s32[1024]{0:T(1024)S(1)} %pad_add_fusion, pred[1024]{0:T(1024)(128)(4,1)S(1)} %get-tuple-element.315, pred[1024]{0:T(1024)(128)(4,1)S(1)} %get-tuple-element.316), kind=kLoop, calls=%fused_computation.9 | loop fusion | flops 11534336 | bytes 8394752 | tf_op jit(solution)/shard_map/jit(_where)/select_n | solution.py:1305
  32.8 3.6 %collective-permute-done.1.refs_1_ = bf16[64,1664]{1,0:T(8,128)(2,1)S(1)} collective-permute-done((bf16[64,1664]{1,0:T(8,128)(2,1)S(1)}, bf16[64,1664]{1,0:T(8,128)(2,1)S(1)}, u32[]{:S(2)}, u32[]{:S(2)}) %collective-permute-start.1) | collective-permute-done | bytes 213024 | tf_op jit(solution)/shard_map/ppermute | solution.py:325
  40.7 2.8 collective-permute-start.9
  44.6 16.7 %collective-permute-done.10.refs_3_ = bf16[128,1024]{1,0:T(8,128)(2,1)S(1)} collective-permute-done((bf16[128,1024]{1,0:T(8,128)(2,1)S(1)}, bf16[128,1024]{1,0:T(8,128)(2,1)S(1)}, u32[]{:S(2)}, u32[]{:S(2)}) %collective-permute-start.10) | collective-permute-done | bytes 262176 | tf_op jit(solution)/shard_map/ppermute | solution.py:325
  61.4 4.0 %collective-permute-done.8.refs_1_ = bf16[128,1024]{1,0:T(8,128)(2,1)S(1)} collective-permute-done((bf16[128,1024]{1,0:T(8,128)(2,1)S(1)}, bf16[128,1024]{1,0:T(8,128)(2,1)S(1)}, u32[]{:S(2)}, u32[]{:S(2)}) %collective-permute-start.8) | collective-permute-done | bytes 262176 | tf_op jit(solution)/shard_map/ppermute | solution.py:325
  72.3 6.0 %project.1 = (bf16[1024,1536]{1,0:T(8,128)(2,1)S(1)}, f32[2,1024]{1,0:T(2,128)S(1)}) custom-call(s32[4]{0:T(128)S(1)} %pad_add_fusion.1.info, bf16[512,1024]{1,0:T(8,128)(2,1)S(1)} %bitcast.25, bf16[512,1024]{1,0:T(8,128)(2,1)S(1)} %copy-done.28, bf16[4,64,1664]{2,1,0:T(8,128)(2,1)S(1)} %copy-done.18, bf16[4,64,1664]{2,1,0:T(8,128)(2,1)S(1)} %copy-done.21, ...), custom_call_target="tpu_custom_call" | custom-call | flops 575000000 | bytes 65536 | tf_op jit(solution)/shard_map/project/pallas_call | solution.py:291
  78.3 2.3 collective-permute-start.16
  80.6 1.7 collective-permute-start.15
  82.5 8.5 %attend_0.1 = (bf16[512,256]{1,0:T(8,128)(2,1)S(1)}, bf16[512,256]{1,0:T(8,128)(2,1)S(1)}, f32[2,2,1024]{2,1,0:T(2,128)S(1)}) custom-call(s32[4]{0:T(128)S(1)} %pad_add_fusion.1.info, bf16[1024,1536]{1,0:T(8,128)(2,1)S(1)} %get-tuple-element.171.q_ref.k_ref.v_ref, bf16[1024,1536]{1,0:T(8,128)(2,1)S(1)} %get-tuple-element.171.q_ref.k_ref.v_ref, ...), custom_call_target="tpu_custom_call" | custom-call | flops 575000000 | bytes 65536 | tf_op jit(solution)/shard_map/attend_0/pallas_call | solution.py:291
  91.1 3.5 %collective-permute-done.18.refs_2_ = bf16[4,128,1024]{2,1,0:T(8,128)(2,1)S(1)} collective-permute-done((bf16[4,128,1024]{2,1,0:T(8,128)(2,1)S(1)}, bf16[4,128,1024]{2,1,0:T(8,128)(2,1)S(1)}, u32[]{:S(2)}, u32[]{:S(2)}) %collective-permute-start.18) | collective-permute-done | bytes 1048608 | tf_op jit(solution)/shard_map/ppermute | solution.py:337
  99.5 9.1 %attend_1.1 = (bf16[512,256]{1,0:T(8,128)(2,1)S(1)}, bf16[512,256]{1,0:T(8,128)(2,1)}, f32[2,2,1024]{2,1,0:T(2,128)S(1)}) custom-call(s32[4]{0:T(128)S(1)} %pad_add_fusion.1.info, bf16[1024,1536]{1,0:T(8,128)(2,1)S(1)} %get-tuple-element.171.q_ref.k_ref.v_ref, bf16[1024,1536]{1,0:T(8,128)(2,1)S(1)} %get-tuple-element.171.q_ref.k_ref.v_ref, ...), custom_call_target="tpu_custom_call" | custom-call | flops 23000000512 | bytes 65536 | tf_op jit(solution)/shard_map/attend_1/pallas_call | solution.py:291
  109.6 1.6 down_stack.1.refs_0_
  114.5 2.3 input_norm.1
  118.9 3.3 collective-permute-done.20.refs_4_
  124.2 3.3 attention_out.1
  128.1 11.5 %collective-permute-done.23.refs_2_ = bf16[4,256,512]{2,1,0:T(8,128)(2,1)} collective-permute-done((bf16[4,256,512]{2,1,0:T(8,128)(2,1)}, bf16[4,256,512]{2,1,0:T(8,128)(2,1)}, u32[]{:S(2)}, u32[]{:S(2)}) %collective-permute-start.23) | collective-permute-done | bytes 1048608 | tf_op jit(solution)/shard_map/ppermute | solution.py:337
  141.3 3.4 collective-permute-done.22.refs_1_
  149.3 9.5 %up.1 = (bf16[1024,2048]{1,0:T(8,128)(2,1)S(1)}, bf16[1024,2048]{1,0:T(8,128)(2,1)S(1)}) custom-call(s32[4]{0:T(128)S(1)} %pad_add_fusion.1.info, bf16[512,1024]{1,0:T(8,128)(2,1)S(1)} %get-tuple-element.190.x0_ref.n0_ref, bf16[512,1024]{1,0:T(8,128)(2,1)S(1)} %collective-permute-done.21.x1_ref.n1_ref, bf16[4,128,1024]{2,1,0:T(8,128)(2,1)S(1)} %copy-done.12, ...), custom_call_target="tpu_custom_call" | custom-call | flops 575000000 | bytes 65536 | tf_op jit(solution)/shard_map/up/pallas_call | solution.py:291
  158.8 13.9 %down.1 = (f32[512,1024]{1,0:T(8,128)S(1)}, bf16[512,1024]{1,0:T(8,128)(2,1)S(1)}, bf16[1024,2048]{1,0:T(8,128)(2,1)S(1)}) custom-call(s32[4]{0:T(128)S(1)} %pad_add_fusion.1.info, bf16[1024,2048]{1,0:T(8,128)(2,1)S(1)} %get-tuple-element.206.act_ref, bf16[1024,2048]{1,0:T(8,128)(2,1)S(1)} %get-tuple-element.195.slope_ref, bf16[512,1024]{1,0:T(8,128)(2,1)S(1)} %bitcast.21, ...), custom_call_target="tpu_custom_call" | custom-call | flops 575000000 | bytes 65536 | tf_op jit(solution)/shard_map/down/pallas_call | solution.py:291
  172.7 6.8 %normed_back.1 = (f32[512,1024]{1,0:T(8,128)S(1)}, bf16[512,1024]{1,0:T(8,128)(2,1)S(1)}) custom-call(s32[4]{0:T(128)S(1)} %pad_add_fusion.1.info, bf16[1024,2048]{1,0:T(8,128)(2,1)S(1)} %get-tuple-element.212.gp_ref, bf16[4,128,1024]{2,1,0:T(8,128)(2,1)S(1)} %copy-done.12, bf16[4,128,1024]{2,1,0:T(8,128)(2,1)S(1)} %copy-done.10, ...), custom_call_target="tpu_custom_call" | custom-call | flops 575000000 | bytes 65536 | tf_op jit(solution)/shard_map/normed_back/pallas_call | solution.py:291
  179.7 7.8 %down_grad.1 = (bf16[2,512,256]{2,1,0:T(8,128)(2,1)S(1)}, bf16[2,512,256]{2,1,0:T(8,128)(2,1)S(1)}, bf16[4,512,256]{2,1,0:T(8,128)(2,1)S(1)}, bf16[4,512,256]{2,1,0:T(8,128)(2,1)S(1)}, bf16[4,512,256]{2,1,0:T(8,128)(2,1)S(1)}) custom-call(s32[4]{0:T(128)S(1)} %pad_add_fusion.1.info, bf16[512,1024]{1,0:T(8,128)(2,1)S(1)} %bitcast.22, ...), custom_call_target="tpu_custom_call" | custom-call | flops 575000000 | bytes 65536 | tf_op jit(solution)/shard_map/down_grad/pallas_call | solution.py:291
  188.8 3.0 middle_back.1
  191.9 7.5 %up_grad.1 = (bf16[4,128,1024]{2,1,0:T(8,128)(2,1)S(1)}, bf16[4,128,1024]{2,1,0:T(8,128)(2,1)S(1)}, bf16[4,128,1024]{2,1,0:T(8,128)(2,1)S(1)}, bf16[4,128,1024]{2,1,0:T(8,128)(2,1)S(1)}) custom-call(s32[4]{0:T(128)S(1)} %pad_add_fusion.1.info, bf16[512,1024]{1,0:T(8,128)(2,1)S(1)} %get-tuple-element.190.x0_ref.n0_ref, bf16[512,1024]{1,0:T(8,128)(2,1)S(1)} %copy-done.14, ...), custom_call_target="tpu_custom_call" | custom-call | flops 575000000 | bytes 65536 | tf_op jit(solution)/shard_map/up_grad/pallas_call | solution.py:291
  199.4 2.4 collective-permute-done.33.second_ref
  205.8 1.8 out_grad.1
  207.6 9.6 %collective-permute-done.36.send_ref = bf16[512,512]{1,0:T(8,128)(2,1)S(1)} collective-permute-done((bf16[512,512]{1,0:T(8,128)(2,1)S(1)}, bf16[512,512]{1,0:T(8,128)(2,1)S(1)}, u32[]{:S(2)}, u32[]{:S(2)}) %collective-permute-start.36) | collective-permute-done | bytes 524320 | tf_op jit(solution)/shard_map/ppermute | solution.py:337
  219.0 11.7 %attend_back_0.1.r0_ref.d0_ref = bf16[1024,768]{1,0:T(8,128)(2,1)S(1)} custom-call(s32[4]{0:T(128)S(1)} %pad_add_fusion.1.info, bf16[1024,1536]{1,0:T(8,128)(2,1)S(1)} %get-tuple-element.171.q_ref.k_ref.v_ref, bf16[1024,1536]{1,0:T(8,128)(2,1)S(1)} %get-tuple-element.171.q_ref.k_ref.v_ref, bf16[1024,1536]{1,0:T(8,128)(2,1)S(1)} %get-tuple-element.171.q_ref.k_ref.v_ref, ...), custom_call_target="tpu_custom_call" | custom-call | flops 23000000512 | bytes 65536 | tf_op jit(solution)/shard_map/attend_back_0/pallas_call | solution.py:537
  231.3 8.3 %collective-permute-done.39.c_ref = bf16[4,512,256]{2,1,0:T(8,128)(2,1)S(1)} collective-permute-done((bf16[4,512,256]{2,1,0:T(8,128)(2,1)S(1)}, bf16[4,512,256]{2,1,0:T(8,128)(2,1)S(1)}, u32[]{:S(2)}, u32[]{:S(2)}) %collective-permute-start.39) | collective-permute-done | bytes 1048608 | tf_op jit(solution)/shard_map/ppermute | solution.py:337
  240.6 1.9 collective-permute-start.42
  243.9 5.4 %collective-permute-done.37.refs_1_ = bf16[8,64,512]{2,1,0:T(8,128)(2,1)S(1)} collective-permute-done((bf16[8,64,512]{2,1,0:T(8,128)(2,1)S(1)}, bf16[8,64,512]{2,1,0:T(8,128)(2,1)S(1)}, u32[]{:S(2)}, u32[]{:S(2)}) %collective-permute-start.37) | collective-permute-done | bytes 524320 | tf_op jit(solution)/shard_map/ppermute | solution.py:337
  251.3 2.5 qkv_grad.2
  256.5 11.5 %attend_back_1.1.r0_ref.d1_ref = bf16[1024,768]{1,0:T(8,128)(2,1)S(1)} custom-call(s32[4]{0:T(128)S(1)} %pad_add_fusion.1.info, bf16[1024,1536]{1,0:T(8,128)(2,1)S(1)} %get-tuple-element.171.q_ref.k_ref.v_ref, bf16[1024,1536]{1,0:T(8,128)(2,1)S(1)} %get-tuple-element.171.q_ref.k_ref.v_ref, bf16[1024,1536]{1,0:T(8,128)(2,1)S(1)} %get-tuple-element.171.q_ref.k_ref.v_ref, ...), custom_call_target="tpu_custom_call" | custom-call | flops 575000000 | bytes 65536 | tf_op jit(solution)/shard_map/attend_back_1/pallas_call | solution.py:537
  270.9 5.9 %collective-permute-done.31.b_ref = bf16[4,128,1024]{2,1,0:T(8,128)(2,1)S(1)} collective-permute-done((bf16[4,128,1024]{2,1,0:T(8,128)(2,1)S(1)}, bf16[4,128,1024]{2,1,0:T(8,128)(2,1)S(1)}, u32[]{:S(2)}, u32[]{:S(2)}) %collective-permute-start.31) | collective-permute-done | bytes 1048608 | tf_op jit(solution)/shard_map/ppermute | solution.py:329
  279.2 2.3 qkv_grad.3
  285.5 1.8 collective-permute-start.50
  287.3 4.8 %input_back.1 = (f32[512,1024]{1,0:T(8,128)S(1)}, bf16[512,1024]{1,0:T(8,128)(2,1)S(1)}) custom-call(s32[4]{0:T(128)S(1)} %pad_add_fusion.1.info, bf16[1024,768]{1,0:T(8,128)(2,1)S(1)} %attend_back_0.1.r0_ref.d0_ref, bf16[1024,768]{1,0:T(8,128)(2,1)S(1)} %attend_back_1.1.r0_ref.d1_ref, bf16[4,64,1664]{2,1,0:T(8,128)(2,1)S(1)} %copy-done.19, ...), custom_call_target="tpu_custom_call" | custom-call | flops 575000000 | bytes 65536 | tf_op jit(solution)/shard_map/input_back/pallas_call | solution.py:291
  292.2 4.4 %collective-permute-done.47.bx_ref = bf16[4,64,768]{2,1,0:T(8,128)(2,1)S(1)} collective-permute-done((bf16[4,64,768]{2,1,0:T(8,128)(2,1)S(1)}, bf16[4,64,768]{2,1,0:T(8,128)(2,1)S(1)}, u32[]{:S(2)}, u32[]{:S(2)}) %collective-permute-start.47) | collective-permute-done | bytes 393248 | tf_op jit(solution)/shard_map/ppermute | solution.py:329
  298.6 2.3 collective-permute-done.48.refs_1_
  300.9 2.5 collective-permute-start.52
  303.4 11.6 %collective-permute-done.49.refs_2_ = bf16[128,1024]{1,0:T(8,128)(2,1)S(1)} collective-permute-done((bf16[128,1024]{1,0:T(8,128)(2,1)S(1)}, bf16[128,1024]{1,0:T(8,128)(2,1)S(1)}, u32[]{:S(2)}, u32[]{:S(2)}) %collective-permute-start.49) | collective-permute-done | bytes 262176 | tf_op jit(solution)/shard_map/ppermute | solution.py:325
  314.9 3.4 collective-permute-start.53
  319.1 1.6 mixed.1
  320.7 3.1 input_grad.1
  323.8 2.1 collective-permute-done.53.refs_2_
  325.9 2.1 collective-permute-done.54.refs_3_
  332.9 2.0 collective-permute-done.55.got_ref
  (233 shorter events, 79.6 us)
Async XLA Ops:
  7.2 111.7 %all-gather.2.cloned.1.call-start = ((), (), s32[]{:S(2)}) async-start(), calls=%async_computation | async-start | bytes 2162688 | tf_op jit(solution)/shard_map/all_gather | solution.py:1317
  10.4 25.9 %collective-permute-start.4 = (bf16[512,1024]{1,0:T(8,128)(2,1)}, bf16[512,1024]{1,0:T(8,128)(2,1)S(1)}, u32[]{:S(2)}, u32[]{:S(2)}) collective-permute-start(bf16[512,1024]{1,0:T(8,128)(2,1)} %bitcast.24), channel_id=1, source_target_pairs={{0,1},{1,0},{2,3},{3,2},{4,5},{5,4},{6,7},{7,6},{8,9},{9,8},{10,11... | collective-permute-start | bytes 3145736 | tf_op jit(solution)/shard_map/ppermute | solution.py:337
  15.9 16.9 %collective-permute-start.3 = (bf16[64,1664]{1,0:T(8,128)(2,1)S(1)}, bf16[64,1664]{1,0:T(8,128)(2,1)S(1)}, u32[]{:S(2)}, u32[]{:S(2)}) collective-permute-start(bf16[64,1664]{1,0:T(8,128)(2,1)S(1)} %heads.1.refs_0_.a_ref), channel_id=1, source_target_pairs={{0,24},{2,26},{4,28},{6,30},{8,0},{10,2},{12,4},{14,6},{16,8},{18,... | collective-permute-start | bytes 638984 | tf_op jit(solution)/shard_map/ppermute | solution.py:325
  16.0 16.8 %collective-permute-start.2 = (bf16[64,1664]{1,0:T(8,128)(2,1)S(1)}, bf16[64,1664]{1,0:T(8,128)(2,1)S(1)}, u32[]{:S(2)}, u32[]{:S(2)}) collective-permute-start(bf16[64,1664]{1,0:T(8,128)(2,1)S(1)} %heads.1.refs_0_.a_ref), channel_id=1, source_target_pairs={{0,16},{2,18},{4,20},{6,22},{8,24},{10,26},{12,28},{14,30},{16,0},... | collective-permute-start | bytes 638984 | tf_op jit(solution)/shard_map/ppermute | solution.py:325
  19.0 17.4 %collective-permute-start.1 = (bf16[64,1664]{1,0:T(8,128)(2,1)S(1)}, bf16[64,1664]{1,0:T(8,128)(2,1)S(1)}, u32[]{:S(2)}, u32[]{:S(2)}) collective-permute-start(bf16[64,1664]{1,0:T(8,128)(2,1)S(1)} %heads.1.refs_0_.a_ref), channel_id=1, source_target_pairs={{0,8},{2,10},{4,12},{6,14},{8,16},{10,18},{12,20},{14,22},{16,24},... | collective-permute-start | bytes 638984 | tf_op jit(solution)/shard_map/ppermute | solution.py:325
  38.0 27.4 %collective-permute-start.6 = (bf16[4,64,1664]{2,1,0:T(8,128)(2,1)S(1)}, bf16[4,64,1664]{2,1,0:T(8,128)(2,1)S(1)}, u32[]{:S(2)}, u32[]{:S(2)}) collective-permute-start(bf16[4,64,1664]{2,1,0:T(8,128)(2,1)S(1)} %qkv_stack.1.refs_0_), channel_id=1, source_target_pairs={{0,4},{2,6},{4,0},{6,2},{8,12},{10,14},{12,8},{14,10},{16,20},{18,... | collective-permute-start | bytes 2555912 | tf_op jit(solution)/shard_map/ppermute | solution.py:329
  39.5 21.8 %collective-permute-start.10 = (bf16[128,1024]{1,0:T(8,128)(2,1)S(1)}, bf16[128,1024]{1,0:T(8,128)(2,1)S(1)}, u32[]{:S(2)}, u32[]{:S(2)}) collective-permute-start(bf16[128,1024]{1,0:T(8,128)(2,1)S(1)} %both_rows.1.refs_0_), channel_id=1, source_target_pairs={{0,24},{2,26},{4,28},{6,30},{8,0},{10,2},{12,4},{14,6},{16,8},{18,... | collective-permute-start | bytes 786440 | tf_op jit(solution)/shard_map/ppermute | solution.py:325
  40.7 20.7 %collective-permute-start.9 = (bf16[128,1024]{1,0:T(8,128)(2,1)S(1)}, bf16[128,1024]{1,0:T(8,128)(2,1)S(1)}, u32[]{:S(2)}, u32[]{:S(2)}) collective-permute-start(bf16[128,1024]{1,0:T(8,128)(2,1)S(1)} %both_rows.1.refs_0_), channel_id=1, source_target_pairs={{0,16},{2,18},{4,20},{6,22},{8,24},{10,26},{12,28},{14,30},{16,0},... | collective-permute-start | bytes 786440 | tf_op jit(solution)/shard_map/ppermute | solution.py:325
  43.5 21.9 %collective-permute-start.8 = (bf16[128,1024]{1,0:T(8,128)(2,1)S(1)}, bf16[128,1024]{1,0:T(8,128)(2,1)S(1)}, u32[]{:S(2)}, u32[]{:S(2)}) collective-permute-start(bf16[128,1024]{1,0:T(8,128)(2,1)S(1)} %both_rows.1.refs_0_), channel_id=1, source_target_pairs={{0,8},{2,10},{4,12},{6,14},{8,16},{10,18},{12,20},{14,22},{16,24},... | collective-permute-start | bytes 786440 | tf_op jit(solution)/shard_map/ppermute | solution.py:325
  44.5 21.8 %collective-permute-start.7 = (bf16[4,64,1664]{2,1,0:T(8,128)(2,1)S(1)}, bf16[4,64,1664]{2,1,0:T(8,128)(2,1)S(1)}, u32[]{:S(2)}, u32[]{:S(2)}) collective-permute-start(bf16[4,64,1664]{2,1,0:T(8,128)(2,1)S(1)} %qkv_stack.1.refs_0_), channel_id=1, source_target_pairs={{0,2},{2,0},{4,6},{6,4},{8,10},{10,8},{12,14},{14,12},{16,18},{18,... | collective-permute-start | bytes 2555912 | tf_op jit(solution)/shard_map/ppermute | solution.py:333
  68.4 26.2 %collective-permute-start.18 = (bf16[4,128,1024]{2,1,0:T(8,128)(2,1)S(1)}, bf16[4,128,1024]{2,1,0:T(8,128)(2,1)S(1)}, u32[]{:S(2)}, u32[]{:S(2)}) collective-permute-start(bf16[4,128,1024]{2,1,0:T(8,128)(2,1)S(1)} %up_stack.1.refs_0_), channel_id=1, source_target_pairs={{0,1},{1,0},{2,3},{3,2},{4,5},{5,4},{6,7},{7,6},{8,9},{9,8},{10,11... | collective-permute-start | bytes 3145736 | tf_op jit(solution)/shard_map/ppermute | solution.py:337
  69.4 26.8 %collective-permute-start.17 = (bf16[4,128,1024]{2,1,0:T(8,128)(2,1)S(1)}, bf16[4,128,1024]{2,1,0:T(8,128)(2,1)S(1)}, u32[]{:S(2)}, u32[]{:S(2)}) collective-permute-start(bf16[4,128,1024]{2,1,0:T(8,128)(2,1)S(1)} %up_stack.1.refs_0_), channel_id=1, source_target_pairs={{0,4},{2,6},{4,0},{6,2},{8,12},{10,14},{12,8},{14,10},{16,20},{18,... | collective-permute-start | bytes 3145736 | tf_op jit(solution)/shard_map/ppermute | solution.py:329
  78.3 20.7 %collective-permute-start.16 = (bf16[256,512]{1,0:T(8,128)(2,1)S(1)}, bf16[256,512]{1,0:T(8,128)(2,1)S(1)}, u32[]{:S(2)}, u32[]{:S(2)}) collective-permute-start(bf16[256,512]{1,0:T(8,128)(2,1)S(1)} %copy-done.44), channel_id=1, source_target_pairs={{0,24},{2,26},{4,28},{6,30},{8,0},{10,2},{12,4},{14,6},{16,8},{18,... | collective-permute-start | bytes 786440 | tf_op jit(solution)/shard_map/ppermute | solution.py:325
  80.6 27.9 %collective-permute-start.15 = (bf16[256,512]{1,0:T(8,128)(2,1)S(1)}, bf16[256,512]{1,0:T(8,128)(2,1)S(1)}, u32[]{:S(2)}, u32[]{:S(2)}) collective-permute-start(bf16[256,512]{1,0:T(8,128)(2,1)S(1)} %copy-done.44), channel_id=1, source_target_pairs={{0,16},{2,18},{4,20},{6,22},{8,24},{10,26},{12,28},{14,30},{16,0},... | collective-permute-start | bytes 786440 | tf_op jit(solution)/shard_map/ppermute | solution.py:325
  82.3 27.3 %collective-permute-start.14 = (bf16[256,512]{1,0:T(8,128)(2,1)S(1)}, bf16[256,512]{1,0:T(8,128)(2,1)S(1)}, u32[]{:S(2)}, u32[]{:S(2)}) collective-permute-start(bf16[256,512]{1,0:T(8,128)(2,1)S(1)} %copy-done.44), channel_id=1, source_target_pairs={{0,8},{2,10},{4,12},{6,14},{8,16},{10,18},{12,20},{14,22},{16,24},... | collective-permute-start | bytes 786440 | tf_op jit(solution)/shard_map/ppermute | solution.py:325
  94.6 18.2 %collective-permute-start.12 = (bf16[512,256]{1,0:T(8,128)(2,1)S(1)}, bf16[512,256]{1,0:T(8,128)(2,1)S(1)}, u32[]{:S(2)}, u32[]{:S(2)}) collective-permute-start(bf16[512,256]{1,0:T(8,128)(2,1)S(1)} %get-tuple-element.176), channel_id=1, source_target_pairs={{0,1},{1,0},{2,3},{3,2},{4,5},{5,4},{6,7},{7,6},{8,9},{9,8},{10,11... | collective-permute-start | bytes 786440 | tf_op jit(solution)/shard_map/ppermute | solution.py:337
  97.0 21.9 %collective-permute-start.19 = (bf16[1,128,1024]{2,1,0:T(8,128)(2,1)}, bf16[1,128,1024]{2,1,0:T(8,128)(2,1)S(1)}, u32[]{:S(2)}, u32[]{:S(2)}) collective-permute-start(bf16[1,128,1024]{2,1,0:T(8,128)(2,1)} %slice.47), channel_id=1, source_target_pairs={{0,1},{1,0},{2,3},{3,2},{4,5},{5,4},{6,7},{7,6},{8,9},{9,8},{10,11... | collective-permute-start | bytes 786440 | tf_op jit(solution)/shard_map/ppermute | solution.py:337
  98.9 23.2 %collective-permute-start.20 = (bf16[3,128,1024]{2,1,0:T(8,128)(2,1)}, bf16[3,128,1024]{2,1,0:T(8,128)(2,1)}, u32[]{:S(2)}, u32[]{:S(2)}) collective-permute-start(bf16[3,128,1024]{2,1,0:T(8,128)(2,1)} %slice.48), channel_id=1, source_target_pairs={{0,4},{2,6},{4,0},{6,2},{8,12},{10,14},{12,8},{14,10},{16,20},{18,... | collective-permute-start | bytes 2359304 | tf_op jit(solution)/shard_map/ppermute | solution.py:329
  108.6 14.2 %collective-permute-start.13 = (bf16[512,256]{1,0:T(8,128)(2,1)}, bf16[512,256]{1,0:T(8,128)(2,1)}, u32[]{:S(2)}, u32[]{:S(2)}) collective-permute-start(bf16[512,256]{1,0:T(8,128)(2,1)} %get-tuple-element.177), channel_id=1, source_target_pairs={{0,1},{1,0},{2,3},{3,2},{4,5},{5,4},{6,7},{7,6},{8,9},{9,8},{10,11... | collective-permute-start | bytes 786440 | tf_op jit(solution)/shard_map/ppermute | solution.py:337
  111.3 33.3 %collective-permute-start.22 = (bf16[4,256,512]{2,1,0:T(8,128)(2,1)}, bf16[4,256,512]{2,1,0:T(8,128)(2,1)}, u32[]{:S(2)}, u32[]{:S(2)}) collective-permute-start(bf16[4,256,512]{2,1,0:T(8,128)(2,1)} %down_stack.1.refs_0_), channel_id=1, source_target_pairs={{0,4},{2,6},{4,0},{6,2},{8,12},{10,14},{12,8},{14,10},{16,20},{18,... | collective-permute-start | bytes 3145736 | tf_op jit(solution)/shard_map/ppermute | solution.py:329
  113.5 26.1 %collective-permute-start.23 = (bf16[4,256,512]{2,1,0:T(8,128)(2,1)}, bf16[4,256,512]{2,1,0:T(8,128)(2,1)}, u32[]{:S(2)}, u32[]{:S(2)}) collective-permute-start(bf16[4,256,512]{2,1,0:T(8,128)(2,1)} %down_stack.1.refs_0_), channel_id=1, source_target_pairs={{0,1},{1,0},{2,3},{3,2},{4,5},{5,4},{6,7},{7,6},{8,9},{9,8},{10,11... | collective-permute-start | bytes 3145736 | tf_op jit(solution)/shard_map/ppermute | solution.py:337
  127.5 19.6 %collective-permute-start.21 = (bf16[512,1024]{1,0:T(8,128)(2,1)S(1)}, bf16[512,1024]{1,0:T(8,128)(2,1)S(1)}, u32[]{:S(2)}, u32[]{:S(2)}) collective-permute-start(bf16[512,1024]{1,0:T(8,128)(2,1)S(1)} %get-tuple-element.190.x0_ref.n0_ref), channel_id=1, source_target_pairs={{0,2},{2,0},{4,6},{6,4},{8,10},{10,8},{12,14},{14,12},{16,18},{18,... | collective-permute-start | bytes 3145736 | tf_op jit(solution)/shard_map/ppermute | solution.py:333
  127.6 31.2 %collective-permute-start.24 = (bf16[512,1024]{1,0:T(8,128)(2,1)S(1)}, bf16[512,1024]{1,0:T(8,128)(2,1)S(1)}, u32[]{:S(2)}, u32[]{:S(2)}) collective-permute-start(bf16[512,1024]{1,0:T(8,128)(2,1)S(1)} %bitcast.20), channel_id=1, source_target_pairs={{0,2},{2,0},{4,6},{6,4},{8,10},{10,8},{12,14},{14,12},{16,18},{18,... | collective-permute-start | bytes 3145736 | tf_op jit(solution)/shard_map/ppermute | solution.py:333
  140.7 18.1 %collective-permute-start.26 = (bf16[2,256,512]{2,1,0:T(8,128)(2,1)S(1)}, bf16[2,256,512]{2,1,0:T(8,128)(2,1)S(1)}, u32[]{:S(2)}, u32[]{:S(2)}) collective-permute-start(bf16[2,256,512]{2,1,0:T(8,128)(2,1)S(1)} %slice.52), channel_id=1, source_target_pairs={{0,4},{2,6},{4,0},{6,2},{8,12},{10,14},{12,8},{14,10},{16,20},{18,... | collective-permute-start | bytes 1572872 | tf_op jit(solution)/shard_map/ppermute | solution.py:329
  147.1 25.7 %collective-permute-start.29 = (bf16[8,64,512]{2,1,0:T(8,128)(2,1)S(1)}, bf16[8,64,512]{2,1,0:T(8,128)(2,1)S(1)}, u32[]{:S(2)}, u32[]{:S(2)}) collective-permute-start(bf16[8,64,512]{2,1,0:T(8,128)(2,1)S(1)} %get-tuple-element.203), channel_id=1, source_target_pairs={{0,2},{2,0},{4,6},{6,4},{8,10},{10,8},{12,14},{14,12},{16,18},{18,... | collective-permute-start | bytes 1572872 | tf_op jit(solution)/shard_map/ppermute | solution.py:333
  147.1 25.6 %collective-permute-start.28 = (bf16[8,64,1024]{2,1,0:T(8,128)(2,1)S(1)}, bf16[8,64,1024]{2,1,0:T(8,128)(2,1)S(1)}, u32[]{:S(2)}, u32[]{:S(2)}) collective-permute-start(bf16[8,64,1024]{2,1,0:T(8,128)(2,1)S(1)} %copy-done.43), channel_id=1, source_target_pairs={{0,2},{2,0},{4,6},{6,4},{8,10},{10,8},{12,14},{14,12},{16,18},{18,... | collective-permute-start | bytes 3145736 | tf_op jit(solution)/shard_map/ppermute | solution.py:333
  187.5 14.4 %collective-permute-start.33 = (bf16[2,512,256]{2,1,0:T(8,128)(2,1)S(1)}, bf16[2,512,256]{2,1,0:T(8,128)(2,1)S(1)}, u32[]{:S(2)}, u32[]{:S(2)}) collective-permute-start(bf16[2,512,256]{2,1,0:T(8,128)(2,1)S(1)} %get-tuple-element.221), channel_id=1, source_target_pairs={{0,1},{1,0},{2,3},{3,2},{4,5},{5,4},{6,7},{7,6},{8,9},{9,8},{10,11... | collective-permute-start | bytes 1572872 | tf_op jit(solution)/shard_map/ppermute | solution.py:337
  188.3 14.0 %collective-permute-start.32 = (bf16[2,512,256]{2,1,0:T(8,128)(2,1)S(1)}, bf16[2,512,256]{2,1,0:T(8,128)(2,1)S(1)}, u32[]{:S(2)}, u32[]{:S(2)}) collective-permute-start(bf16[2,512,256]{2,1,0:T(8,128)(2,1)S(1)} %get-tuple-element.207), channel_id=1, source_target_pairs={{0,4},{2,6},{4,0},{6,2},{8,12},{10,14},{12,8},{14,10},{16,20},{18,... | collective-permute-start | bytes 1572872 | tf_op jit(solution)/shard_map/ppermute | solution.py:329
  191.8 13.9 %collective-permute-start.34 = (bf16[512,1024]{1,0:T(8,128)(2,1)S(1)}, bf16[512,1024]{1,0:T(8,128)(2,1)S(1)}, u32[]{:S(2)}, u32[]{:S(2)}) collective-permute-start(bf16[512,1024]{1,0:T(8,128)(2,1)S(1)} %get-tuple-element.225.r0_ref), channel_id=1, source_target_pairs={{0,2},{2,0},{4,6},{6,4},{8,10},{10,8},{12,14},{14,12},{16,18},{18,... | collective-permute-start | bytes 3145736 | tf_op jit(solution)/shard_map/ppermute | solution.py:333
  202.3 14.9 %collective-permute-start.36 = (bf16[512,512]{1,0:T(8,128)(2,1)S(1)}, bf16[512,512]{1,0:T(8,128)(2,1)S(1)}, u32[]{:S(2)}, u32[]{:S(2)}) collective-permute-start(bf16[512,512]{1,0:T(8,128)(2,1)S(1)} %get-tuple-element.234), channel_id=1, source_target_pairs={{0,1},{1,0},{2,3},{3,2},{4,5},{5,4},{6,7},{7,6},{8,9},{9,8},{10,11... | collective-permute-start | bytes 1572872 | tf_op jit(solution)/shard_map/ppermute | solution.py:337
  204.4 35.2 %collective-permute-start.39 = (bf16[4,512,256]{2,1,0:T(8,128)(2,1)S(1)}, bf16[4,512,256]{2,1,0:T(8,128)(2,1)S(1)}, u32[]{:S(2)}, u32[]{:S(2)}) collective-permute-start(bf16[4,512,256]{2,1,0:T(8,128)(2,1)S(1)} %get-tuple-element.224), channel_id=1, source_target_pairs={{0,1},{1,0},{2,3},{3,2},{4,5},{5,4},{6,7},{7,6},{8,9},{9,8},{10,11... | collective-permute-start | bytes 3145736 | tf_op jit(solution)/shard_map/ppermute | solution.py:337
  205.2 26.1 %collective-permute-start.38 = (bf16[4,512,256]{2,1,0:T(8,128)(2,1)S(1)}, bf16[4,512,256]{2,1,0:T(8,128)(2,1)S(1)}, u32[]{:S(2)}, u32[]{:S(2)}) collective-permute-start(bf16[4,512,256]{2,1,0:T(8,128)(2,1)S(1)} %get-tuple-element.238), channel_id=1, source_target_pairs={{0,4},{2,6},{4,0},{6,2},{8,12},{10,14},{12,8},{14,10},{16,20},{18,... | collective-permute-start | bytes 3145736 | tf_op jit(solution)/shard_map/ppermute | solution.py:329
  217.2 32.1 %collective-permute-start.37 = (bf16[8,64,512]{2,1,0:T(8,128)(2,1)S(1)}, bf16[8,64,512]{2,1,0:T(8,128)(2,1)S(1)}, u32[]{:S(2)}, u32[]{:S(2)}) collective-permute-start(bf16[8,64,512]{2,1,0:T(8,128)(2,1)S(1)} %get-tuple-element.236), channel_id=1, source_target_pairs={{0,1},{1,0},{2,3},{3,2},{4,5},{5,4},{6,7},{7,6},{8,9},{9,8},{10,11... | collective-permute-start | bytes 1572872 | tf_op jit(solution)/shard_map/ppermute | solution.py:337
  218.5 35.4 %collective-permute-start.35 = (bf16[4,128,1024]{2,1,0:T(8,128)(2,1)S(1)}, bf16[4,128,1024]{2,1,0:T(8,128)(2,1)S(1)}, u32[]{:S(2)}, u32[]{:S(2)}) collective-permute-start(bf16[4,128,1024]{2,1,0:T(8,128)(2,1)S(1)} %get-tuple-element.229), channel_id=1, source_target_pairs={{0,4},{2,6},{4,0},{6,2},{8,12},{10,14},{12,8},{14,10},{16,20},{18,... | collective-permute-start | bytes 3145736 | tf_op jit(solution)/shard_map/ppermute | solution.py:329
  230.7 19.9 %collective-permute-start.40 = (bf16[1024,768]{1,0:T(8,128)(2,1)S(1)}, bf16[1024,768]{1,0:T(8,128)(2,1)S(1)}, u32[]{:S(2)}, u32[]{:S(2)}) collective-permute-start(bf16[1024,768]{1,0:T(8,128)(2,1)S(1)} %attend_back_0.1.r0_ref.d0_ref), channel_id=1, source_target_pairs={{0,2},{2,0},{4,6},{6,4},{8,10},{10,8},{12,14},{14,12},{16,18},{18,... | collective-permute-start | bytes 4718600 | tf_op jit(solution)/shard_map/ppermute | solution.py:333
  240.6 27.4 %collective-permute-start.42 = (bf16[512,256]{1,0:T(8,128)(2,1)S(1)}, bf16[512,256]{1,0:T(8,128)(2,1)S(1)}, u32[]{:S(2)}, u32[]{:S(2)}) collective-permute-start(bf16[512,256]{1,0:T(8,128)(2,1)S(1)} %get-tuple-element.242), channel_id=1, source_target_pairs={{0,8},{2,10},{4,12},{6,14},{8,16},{10,18},{12,20},{14,22},{16,24},... | collective-permute-start | bytes 786440 | tf_op jit(solution)/shard_map/ppermute | solution.py:325
  242.4 25.7 %collective-permute-start.43 = (bf16[512,256]{1,0:T(8,128)(2,1)S(1)}, bf16[512,256]{1,0:T(8,128)(2,1)S(1)}, u32[]{:S(2)}, u32[]{:S(2)}) collective-permute-start(bf16[512,256]{1,0:T(8,128)(2,1)S(1)} %get-tuple-element.243), channel_id=1, source_target_pairs={{0,16},{2,18},{4,20},{6,22},{8,24},{10,26},{12,28},{14,30},{16,0},... | collective-permute-start | bytes 786440 | tf_op jit(solution)/shard_map/ppermute | solution.py:325
  249.3 18.8 %collective-permute-start.44 = (bf16[512,256]{1,0:T(8,128)(2,1)S(1)}, bf16[512,256]{1,0:T(8,128)(2,1)S(1)}, u32[]{:S(2)}, u32[]{:S(2)}) collective-permute-start(bf16[512,256]{1,0:T(8,128)(2,1)S(1)} %get-tuple-element.244), channel_id=1, source_target_pairs={{0,24},{2,26},{4,28},{6,30},{8,0},{10,2},{12,4},{14,6},{16,8},{18,... | collective-permute-start | bytes 786440 | tf_op jit(solution)/shard_map/ppermute | solution.py:325
  250.7 26.2 %collective-permute-start.31 = (bf16[4,128,1024]{2,1,0:T(8,128)(2,1)S(1)}, bf16[4,128,1024]{2,1,0:T(8,128)(2,1)S(1)}, u32[]{:S(2)}, u32[]{:S(2)}) collective-permute-start(bf16[4,128,1024]{2,1,0:T(8,128)(2,1)S(1)} %get-tuple-element.214), channel_id=1, source_target_pairs={{0,4},{2,6},{4,0},{6,2},{8,12},{10,14},{12,8},{14,10},{16,20},{18,... | collective-permute-start | bytes 3145736 | tf_op jit(solution)/shard_map/ppermute | solution.py:329
  255.0 23.3 %collective-permute-start.41 = (bf16[4,128,1024]{2,1,0:T(8,128)(2,1)S(1)}, bf16[4,128,1024]{2,1,0:T(8,128)(2,1)S(1)}, u32[]{:S(2)}, u32[]{:S(2)}) collective-permute-start(bf16[4,128,1024]{2,1,0:T(8,128)(2,1)S(1)} %added.1), channel_id=1, source_target_pairs={{0,1},{1,0},{2,3},{3,2},{4,5},{5,4},{6,7},{7,6},{8,9},{9,8},{10,11... | collective-permute-start | bytes 3145736 | tf_op jit(solution)/shard_map/ppermute | solution.py:337
  268.1 24.0 %collective-permute-start.45 = (bf16[4,64,1280]{2,1,0:T(8,128)(2,1)S(1)}, bf16[4,64,1280]{2,1,0:T(8,128)(2,1)S(1)}, u32[]{:S(2)}, u32[]{:S(2)}) collective-permute-start(bf16[4,64,1280]{2,1,0:T(8,128)(2,1)S(1)} %get-tuple-element.260), channel_id=1, source_target_pairs={{0,4},{2,6},{4,0},{6,2},{8,12},{10,14},{12,8},{14,10},{16,20},{18,... | collective-permute-start | bytes 1966088 | tf_op jit(solution)/shard_map/ppermute | solution.py:329
  281.6 15.0 %collective-permute-start.47 = (bf16[4,64,768]{2,1,0:T(8,128)(2,1)S(1)}, bf16[4,64,768]{2,1,0:T(8,128)(2,1)S(1)}, u32[]{:S(2)}, u32[]{:S(2)}) collective-permute-start(bf16[4,64,768]{2,1,0:T(8,128)(2,1)S(1)} %get-tuple-element.266), channel_id=1, source_target_pairs={{0,4},{2,6},{4,0},{6,2},{8,12},{10,14},{12,8},{14,10},{16,20},{18,... | collective-permute-start | bytes 1179656 | tf_op jit(solution)/shard_map/ppermute | solution.py:329
  282.8 18.1 %collective-permute-start.48 = (bf16[128,1024]{1,0:T(8,128)(2,1)S(1)}, bf16[128,1024]{1,0:T(8,128)(2,1)S(1)}, u32[]{:S(2)}, u32[]{:S(2)}) collective-permute-start(bf16[128,1024]{1,0:T(8,128)(2,1)S(1)} %get-tuple-element.261), channel_id=1, source_target_pairs={{0,8},{2,10},{4,12},{6,14},{8,16},{10,18},{12,20},{14,22},{16,24},... | collective-permute-start | bytes 786440 | tf_op jit(solution)/shard_map/ppermute | solution.py:325
  284.1 30.9 %collective-permute-start.49 = (bf16[128,1024]{1,0:T(8,128)(2,1)S(1)}, bf16[128,1024]{1,0:T(8,128)(2,1)S(1)}, u32[]{:S(2)}, u32[]{:S(2)}) collective-permute-start(bf16[128,1024]{1,0:T(8,128)(2,1)S(1)} %get-tuple-element.262), channel_id=1, source_target_pairs={{0,16},{2,18},{4,20},{6,22},{8,24},{10,26},{12,28},{14,30},{16,0},... | collective-permute-start | bytes 786440 | tf_op jit(solution)/shard_map/ppermute | solution.py:325
  285.5 32.9 %collective-permute-start.50 = (bf16[128,1024]{1,0:T(8,128)(2,1)S(1)}, bf16[128,1024]{1,0:T(8,128)(2,1)S(1)}, u32[]{:S(2)}, u32[]{:S(2)}) collective-permute-start(bf16[128,1024]{1,0:T(8,128)(2,1)S(1)} %get-tuple-element.263), channel_id=1, source_target_pairs={{0,24},{2,26},{4,28},{6,30},{8,0},{10,2},{12,4},{14,6},{16,8},{18,... | collective-permute-start | bytes 786440 | tf_op jit(solution)/shard_map/ppermute | solution.py:325
  292.1 26.9 %collective-permute-start.27 = (bf16[512,1024]{1,0:T(8,128)(2,1)S(1)}, bf16[512,1024]{1,0:T(8,128)(2,1)S(1)}, u32[]{:S(2)}, u32[]{:S(2)}) collective-permute-start(bf16[512,1024]{1,0:T(8,128)(2,1)S(1)} %copy-done.41), channel_id=1, source_target_pairs={{0,2},{2,0},{4,6},{6,4},{8,10},{10,8},{12,14},{14,12},{16,18},{18,... | collective-permute-start | bytes 3145736 | tf_op jit(solution)/shard_map/ppermute | solution.py:333
  296.6 24.2 %collective-permute-start.51 = (bf16[512,1024]{1,0:T(8,128)(2,1)S(1)}, bf16[512,1024]{1,0:T(8,128)(2,1)S(1)}, u32[]{:S(2)}, u32[]{:S(2)}) collective-permute-start(bf16[512,1024]{1,0:T(8,128)(2,1)S(1)} %get-tuple-element.280), channel_id=1, source_target_pairs={{0,1},{1,0},{2,3},{3,2},{4,5},{5,4},{6,7},{7,6},{8,9},{9,8},{10,11... | collective-permute-start | bytes 3145736 | tf_op jit(solution)/shard_map/ppermute | solution.py:337
  300.9 22.9 %collective-permute-start.52 = (bf16[64,2048]{1,0:T(8,128)(2,1)S(1)}, bf16[64,2048]{1,0:T(8,128)(2,1)S(1)}, u32[]{:S(2)}, u32[]{:S(2)}) collective-permute-start(bf16[64,2048]{1,0:T(8,128)(2,1)S(1)} %get-tuple-element.273), channel_id=1, source_target_pairs={{0,8},{2,10},{4,12},{6,14},{8,16},{10,18},{12,20},{14,22},{16,24},... | collective-permute-start | bytes 786440 | tf_op jit(solution)/shard_map/ppermute | solution.py:325
  (62 other events, 539.0 us)
Sparse Core Ops, SparseCore 0:
  44.6 71.3 all-gather.1
